TPU v7x, 32 devices: a whole 2x2x4 slice. The times are simulated.
32 devices in a mesh: section: 2 (over core), ctx: 4 (over z), fsdp: 4 (over y, x).
Axes of the slice: x: 2, y: 2, z: 4, core: 2. Of those that a mesh axis runs over, the one named last changes fastest.
Arguments:
- tokens: bfloat16 [2, 4, 1024, 768], P(None, 'fsdp', 'ctx'), may hold values from -6 to 6
- cotangent: bfloat16 [2, 4, 1024, 768], P(None, 'fsdp', 'ctx'), may hold values from -6 to 6
- span_order: int32 [4], replicated, may hold values from 0 to 3, each once
- w_qkv: bfloat16 [2, 768, 2304], P('section', 'fsdp'), may hold values from -0.21875 to 0.21875
- w_out: bfloat16 [2, 768, 768], P('section', 'fsdp'), may hold values from -1.25 to 1.25
- w_up: bfloat16 [2, 768, 3072], P('section', 'fsdp'), may hold values from -0.3125 to 0.3125
- w_down: bfloat16 [2, 3072, 768], P('section', 'fsdp'), may hold values from -0.21875 to 0.21875
- norm_gains: bfloat16 [2, 2, 768], P('section', None, 'fsdp'), may hold values from 0.25 to 1.75
- bias_rows: bfloat16 [2, 6, 768], P('section', None, 'fsdp'), may hold values from -3 to 3
- bias_hidden: bfloat16 [2, 3072], P('section', 'fsdp'), may hold values from -3 to 3
Outputs:
- layer_outputs: bfloat16 [2, 2, 4, 1024, 768], P('section', None, 'fsdp', 'ctx')
- input_grads: float32 [2, 2, 4, 1024, 768], P('section', None, 'fsdp', 'ctx')
- grad_w_qkv: float32 [2, 768, 2304], P('section', 'fsdp')
- grad_w_out: float32 [2, 768, 768], P('section', 'fsdp')
- grad_w_up: float32 [2, 768, 3072], P('section', 'fsdp')
- grad_w_down: float32 [2, 3072, 768], P('section', 'fsdp')
- grad_norm_gains: float32 [2, 2, 768], P('section', None, 'fsdp')
- grad_bias_rows: float32 [2, 6, 768], P('section', None, 'fsdp')
- grad_bias_hidden: float32 [2, 3072], P('section', 'fsdp')
Inputs may be any that keep to these rules, and one draw needn't show every extreme that they name: Ctx index c holds, in this order, span number span_order[c] and span number 2 * 4 - 1 - span_order[c] of 128 tokens of every sequence; each value appears once.
All inputs are finite; a program needn't handle non-finite values.
Results may differ from a plain program's by a relative error of at most 0.019.
Values may be sent and summed in bfloat16 or wider, within the bound.
No kernel may reach another device: no remote copies, remote signals or barrier semaphores. Data moves between devices by JAX's collectives and lax.ppermute only.
A program may use at most 192 MiB of HBM per device.

v0:
```python
import jax
import jax.numpy as jnp
from jax import lax
from jax.sharding import PartitionSpec as P

HEADS = 12


epsilon = 1e-05


def shifted(value, axis, steps):
    count = lax.axis_size(axis)
    pairs = [(source, (source + steps) % count) for source in range(count)]
    return lax.ppermute(value, axis, pairs)


def from_behind(value, axis, steps):
    count = lax.axis_size(axis)
    leading, last = (max(0, -steps), min(count, count - steps))
    return lax.ppermute(value, axis, [(source, source + steps) for source in range(leading, last)])


def positions(row_ids, span_order, span_len):
    cycle_size = span_order.shape[0]
    holder = row_ids // (2 * span_len)
    second = row_ids // span_len % 2
    lookup = jnp.sum(
        jnp.where(
            holder[:, None] == jnp.arange(cycle_size, dtype=jnp.int32)[None, :],
            span_order[None, :],
            0,
        ),
        axis=1,
    )
    span_ids = jnp.where(second == 0, lookup, 2 * cycle_size - 1 - lookup)
    return span_ids * span_len + row_ids % span_len


def layer_norm(values, gain_row, shift_row):
    centred = values - jnp.mean(values, axis=-1, keepdims=True)
    spread = jnp.mean(centred * centred, axis=-1, keepdims=True)
    return centred * lax.rsqrt(spread + epsilon) * gain_row + shift_row


def gelu_tanh(values):
    return jax.nn.gelu(values, approximate=True)


def back_dot(left, weight):
    return lax.dot_general(
        left, weight, (((1,), (1,)), ((), ())), preferred_element_type=jnp.float32
    )


def grad_dot(left, right):
    return lax.dot_general(
        left, right, (((0,), (0,)), ((), ())), preferred_element_type=jnp.float32
    )


def make_absorb(queries, local_pos, span_order, span_len):

    def absorb(carried, pieces, first_row):
        run_max, run_sum, run_acc = carried
        key_part, value_part = pieces
        key_pos = positions(jnp.arange(key_part.shape[0], dtype=jnp.int32), span_order, span_len)
        scores = (
            jnp.einsum("qhd,khd->hqk", queries, key_part, preferred_element_type=jnp.float32)
            * 0.125
        )
        allowed = key_pos[None, None, :] <= local_pos[None, :, None]
        new_max = jnp.maximum(run_max, jnp.max(jnp.where(allowed, scores, -1e30), axis=-1))
        weights = jnp.where(allowed, jnp.exp(scores - new_max[:, :, None]), 0.0)
        factor = jnp.exp(run_max - new_max)
        run_sum = jnp.sum(weights, axis=-1)
        added = jnp.einsum(
            "hqk,khd->hqd",
            weights.astype(jnp.bfloat16),
            value_part,
            preferred_element_type=jnp.float32,
        )
        run_acc = added
        return (new_max, run_sum, run_acc)

    return absorb


def attend_forward(queries, key_rows, value_rows, local_pos, span_order, span_len):
    row_count, head_count, head_size = queries.shape
    absorb = make_absorb(queries, local_pos, span_order, span_len)
    initial = (
        jnp.full((head_count, row_count), -1e30, jnp.float32),
        jnp.zeros((head_count, row_count), jnp.float32),
        jnp.zeros((head_count, row_count, head_size), jnp.float32),
    )
    run_max, run_sum, run_acc = absorb(
        initial,
        (
            lax.all_gather(key_rows, "ctx", axis=0, tiled=True),
            lax.all_gather(value_rows, "ctx", axis=0, tiled=True),
        ),
        jnp.int32(0),
    )
    kept_kv = (key_rows, value_rows)
    mixed_heads = run_acc / run_sum[:, :, None]
    mixed_out = (
        jnp.transpose(mixed_heads, (1, 0, 2))
        .reshape(row_count, head_count * head_size)
        .astype(jnp.bfloat16)
    )
    return (mixed_out, run_max + jnp.log(run_sum), kept_kv)


def block_grads(
    query_part, key_part, value_part, dout_part, lse_part, delta_part, query_pos, key_pos
):
    scores = (
        jnp.einsum("qhd,khd->hqk", query_part, key_part, preferred_element_type=jnp.float32) * 0.125
    )
    allowed = key_pos[None, None, :] <= query_pos[None, :, None]
    attn_probs = jnp.where(allowed, jnp.exp(scores - lse_part[:, :, None]), 0.0)
    grad_probs = jnp.einsum(
        "qhd,khd->hqk", dout_part, value_part, preferred_element_type=jnp.float32
    )
    grad_scores = (attn_probs * (grad_probs - delta_part[:, :, None])).astype(jnp.bfloat16)
    part_dq = (
        jnp.einsum("hqk,khd->qhd", grad_scores, key_part, preferred_element_type=jnp.float32)
        * 0.125
    )
    part_dk = (
        jnp.einsum("hqk,qhd->khd", grad_scores, query_part, preferred_element_type=jnp.float32)
        * 0.125
    )
    part_dv = jnp.einsum(
        "hqk,qhd->khd",
        attn_probs.astype(jnp.bfloat16),
        dout_part,
        preferred_element_type=jnp.float32,
    )
    return (part_dq, part_dk, part_dv)


def attend_backward(
    queries,
    kept_kv,
    grad_mixed,
    log_sum,
    delta,
    local_pos,
    span_order,
    span_len,
    ctx_index,
    ctx_count,
):
    row_count = queries.shape[0]
    local_ids = jnp.arange(row_count, dtype=jnp.int32)
    zero_heads = jnp.zeros(queries.shape, jnp.float32)
    key_rows, value_rows = kept_kv

    def visit_step(step_num, carried):
        key_part, value_part, grad_k, grad_v, grad_q = carried
        anchor = (ctx_index - step_num) % ctx_count
        key_pos = positions(anchor * row_count + local_ids, span_order, span_len)
        part_dq, part_dk, part_dv = block_grads(
            queries, key_part, value_part, grad_mixed, log_sum, delta, local_pos, key_pos
        )
        key_part, value_part = shifted((key_part, value_part), "ctx", 1)
        grad_k, grad_v = (
            shifted((grad_k + part_dk).astype(jnp.bfloat16), "ctx", 1).astype(jnp.float32),
            shifted((grad_v + part_dv).astype(jnp.bfloat16), "ctx", 1).astype(jnp.float32),
        )
        return (key_part, value_part, grad_k, grad_v, grad_q + part_dq)

    initial = (key_rows, value_rows, zero_heads, zero_heads, zero_heads)
    finished = lax.fori_loop(0, ctx_count, visit_step, initial)
    grad_k, grad_v, grad_q = (finished[2], finished[3], finished[4])
    width = queries.shape[1] * queries.shape[2]
    return tuple(
        (part.reshape(row_count, width).astype(jnp.bfloat16) for part in (grad_q, grad_k, grad_v))
    )


def layer_forward(
    layer_in, matrices, gain_rows, shift_rows, hidden_bias, local_pos, span_order, span_len
):
    w_qkv, w_out, w_up, w_down = matrices
    row_count, width = layer_in.shape
    head_size = width // HEADS
    normed = layer_norm(layer_in, gain_rows[0], shift_rows[0]).astype(jnp.bfloat16)
    qkv_bias = jnp.concatenate([shift_rows[1], jnp.zeros_like(shift_rows[1]), shift_rows[2]])
    projected = (jnp.dot(normed, w_qkv, preferred_element_type=jnp.float32) + qkv_bias).astype(
        jnp.bfloat16
    )
    queries = projected[:, :width].reshape(row_count, HEADS, head_size)
    key_rows = projected[:, width : 2 * width].reshape(row_count, HEADS, head_size)
    value_rows = projected[:, 2 * width :].reshape(row_count, HEADS, head_size)
    mixed_out, log_sum, kept_kv = attend_forward(
        queries, key_rows, value_rows, local_pos, span_order, span_len
    )
    inner_sum = (
        layer_in + jnp.dot(mixed_out, w_out, preferred_element_type=jnp.float32) + shift_rows[3]
    )
    middle = layer_norm(inner_sum, gain_rows[1], shift_rows[4]).astype(jnp.bfloat16)
    hidden_pre = jnp.dot(middle, w_up, preferred_element_type=jnp.float32) + hidden_bias
    activated = gelu_tanh(hidden_pre).astype(jnp.bfloat16)
    result = (
        inner_sum + jnp.dot(activated, w_down, preferred_element_type=jnp.float32) + shift_rows[5]
    ).astype(jnp.bfloat16)
    return (result, (layer_in, queries, kept_kv, mixed_out, log_sum, inner_sum, hidden_pre))


def layer_backward(
    saved,
    grad_y,
    matrices,
    gain_rows,
    shift_rows,
    local_pos,
    span_order,
    span_len,
    ctx_index,
    ctx_count,
):
    w_qkv, w_out, w_up, w_down = matrices
    layer_in, queries, kept_kv, mixed_out, log_sum, inner_sum, hidden_pre = saved
    grad_low = grad_y.astype(jnp.bfloat16)
    activated = gelu_tanh(hidden_pre).astype(jnp.bfloat16)
    grad_act = back_dot(grad_low, w_down)
    ignored, gelu_pull = jax.vjp(gelu_tanh, hidden_pre)
    grad_hid = gelu_pull(grad_act)[0].astype(jnp.bfloat16)
    up_mid = back_dot(grad_hid, w_up)
    middle_f, norm_pull = jax.vjp(layer_norm, inner_sum, gain_rows[1], shift_rows[4])
    grad_in_mid, grad_gain_mid, grad_shift_mid = norm_pull(up_mid)
    grad_inner = grad_y + grad_in_mid
    grad_attn = grad_inner.astype(jnp.bfloat16)
    grad_mixed = back_dot(grad_attn, w_out).astype(jnp.bfloat16).reshape(queries.shape)
    mixed_heads = mixed_out.reshape(queries.shape)
    delta = jnp.einsum("qhd,qhd->hq", grad_mixed, mixed_heads, preferred_element_type=jnp.float32)
    grad_q, grad_k, grad_v = attend_backward(
        queries,
        kept_kv,
        grad_mixed,
        log_sum,
        delta,
        local_pos,
        span_order,
        span_len,
        ctx_index,
        ctx_count,
    )
    grad_qkv = jnp.concatenate([grad_q, grad_k, grad_v], axis=1)
    up_norm = back_dot(grad_qkv, w_qkv)
    normed_f, norm_pull_first = jax.vjp(layer_norm, layer_in, gain_rows[0], shift_rows[0])
    grad_in_first, grad_gain_first, grad_shift_first = norm_pull_first(up_norm)
    grad_x = grad_inner + grad_in_first
    grads = (
        grad_dot(normed_f.astype(jnp.bfloat16), grad_qkv),
        grad_dot(mixed_out, grad_attn),
        grad_dot(middle_f.astype(jnp.bfloat16), grad_hid),
        grad_dot(activated, grad_low),
        jnp.stack([grad_gain_first, grad_gain_mid]),
        jnp.stack(
            [
                grad_shift_first,
                jnp.sum(grad_q, axis=0, dtype=jnp.float32),
                jnp.sum(grad_v, axis=0, dtype=jnp.float32),
                jnp.sum(grad_attn, axis=0, dtype=jnp.float32),
                grad_shift_mid,
                jnp.sum(grad_low, axis=0, dtype=jnp.float32),
            ]
        ),
        jnp.sum(grad_hid, axis=0, dtype=jnp.float32),
    )
    return (grad_x, grads)


def body(
    tokens, cotangent, span_order, w_qkv, w_out, w_up, w_down, norm_gains, bias_rows, bias_hidden
):
    gathered = (
        lax.all_gather(w_qkv, "fsdp", axis=1, tiled=True),
        lax.all_gather(w_out, "fsdp", axis=1, tiled=True),
        lax.all_gather(w_up, "fsdp", axis=1, tiled=True),
        lax.all_gather(w_down, "fsdp", axis=1, tiled=True),
        lax.all_gather(norm_gains, "fsdp", axis=2, tiled=True),
        lax.all_gather(bias_rows, "fsdp", axis=2, tiled=True),
        lax.all_gather(bias_hidden, "fsdp", axis=1, tiled=True),
    )
    matrices = (gathered[0][0], gathered[1][0], gathered[2][0], gathered[3][0])
    gain_rows = gathered[4][0].astype(jnp.float32)
    shift_rows = gathered[5][0].astype(jnp.float32)
    hidden_bias = gathered[6][0].astype(jnp.float32)
    section_id = lax.axis_index("section")
    ctx_count = lax.axis_size("ctx")
    ctx_index = lax.axis_index("ctx")
    micro_count = tokens.shape[0]
    row_count = tokens.shape[2]
    width = tokens.shape[3]
    span_len = row_count // 2
    local_pos = positions(
        ctx_index * row_count + jnp.arange(row_count, dtype=jnp.int32), span_order, span_len
    )
    incoming = jnp.zeros((row_count, width), jnp.bfloat16)
    saved_list = []
    produced = []
    for tick_num in range(micro_count + 1):
        own_input = tokens[min(tick_num, micro_count - 1), 0].astype(jnp.float32)
        layer_in = jnp.where(section_id == 0, own_input, incoming.astype(jnp.float32))
        result, saved = layer_forward(
            layer_in, matrices, gain_rows, shift_rows, hidden_bias, local_pos, span_order, span_len
        )
        saved_list.append(saved)
        produced.append(result)
        if tick_num < micro_count:
            incoming = from_behind(result, "section", 1)
    saved_stack = jax.tree.map(lambda *leaves: jnp.stack(leaves), *saved_list)
    own_cots = cotangent[:, 0]
    received = jnp.zeros((row_count, width), jnp.bfloat16)
    totals = None
    grads_in = []
    for tick_num in range(micro_count + 1):
        micro_num = tick_num - 1 + section_id
        in_use = (micro_num >= 0) & (micro_num < micro_count)
        own_cot = lax.dynamic_index_in_dim(
            own_cots, jnp.clip(micro_num, 0, micro_count - 1), 0, keepdims=False
        ).astype(jnp.float32)
        grad_y = jnp.where(section_id == 1, own_cot, received.astype(jnp.float32))
        grad_y = jnp.where(in_use, grad_y, 0.0)
        source = jnp.clip(tick_num - 1 + 2 * section_id, 0, micro_count)
        saved = jax.tree.map(
            lambda stacked: lax.dynamic_index_in_dim(stacked, source, 0, keepdims=False),
            saved_stack,
        )
        grad_x, layer_grads = layer_backward(
            saved,
            grad_y,
            matrices,
            gain_rows,
            shift_rows,
            local_pos,
            span_order,
            span_len,
            ctx_index,
            ctx_count,
        )
        totals = layer_grads if tick_num == 0 else jax.tree.map(jnp.add, totals, layer_grads)
        grads_in.append(grad_x)
        if tick_num < micro_count:
            received = from_behind(grad_x.astype(jnp.bfloat16), "section", -1)
    layer_outputs = jnp.stack(
        [
            jnp.where(section_id == 0, produced[micro_num], produced[micro_num + 1])
            for micro_num in range(micro_count)
        ]
    )
    input_grads = jnp.stack(
        [
            jnp.where(section_id == 1, grads_in[micro_num], grads_in[micro_num + 1])
            for micro_num in range(micro_count)
        ]
    )
    scattered = (
        lax.psum_scatter(
            totals[0][None].astype(jnp.bfloat16), "fsdp", scatter_dimension=1, tiled=True
        ).astype(jnp.float32),
        lax.psum_scatter(
            totals[1][None].astype(jnp.bfloat16), "fsdp", scatter_dimension=1, tiled=True
        ).astype(jnp.float32),
        lax.psum_scatter(
            totals[2][None].astype(jnp.bfloat16), "fsdp", scatter_dimension=1, tiled=True
        ).astype(jnp.float32),
        lax.psum_scatter(
            totals[3][None].astype(jnp.bfloat16), "fsdp", scatter_dimension=1, tiled=True
        ).astype(jnp.float32),
        lax.psum_scatter(
            totals[4][None].astype(jnp.bfloat16), "fsdp", scatter_dimension=2, tiled=True
        ).astype(jnp.float32),
        lax.psum_scatter(
            totals[5][None].astype(jnp.bfloat16), "fsdp", scatter_dimension=2, tiled=True
        ).astype(jnp.float32),
        lax.psum_scatter(
            totals[6][None].astype(jnp.bfloat16), "fsdp", scatter_dimension=1, tiled=True
        ).astype(jnp.float32),
    )
    summed = (
        lax.psum(scattered[0].astype(jnp.bfloat16), "ctx").astype(jnp.float32),
        lax.psum(scattered[1].astype(jnp.bfloat16), "ctx").astype(jnp.float32),
        lax.psum(scattered[2].astype(jnp.bfloat16), "ctx").astype(jnp.float32),
        lax.psum(scattered[3].astype(jnp.bfloat16), "ctx").astype(jnp.float32),
        lax.psum(scattered[4].astype(jnp.bfloat16), "ctx").astype(jnp.float32),
        lax.psum(scattered[5].astype(jnp.bfloat16), "ctx").astype(jnp.float32),
        lax.psum(scattered[6].astype(jnp.bfloat16), "ctx").astype(jnp.float32),
    )
    return (
        layer_outputs[None, :, None],
        input_grads[None, :, None],
        summed[0],
        summed[1],
        summed[2],
        summed[3],
        summed[4],
        summed[5],
        summed[6],
    )


def solution(mesh):
    return jax.shard_map(
        body,
        mesh=mesh,
        in_specs=(
            P(None, "fsdp", "ctx", None),
            P(None, "fsdp", "ctx", None),
            P(),
            P("section", "fsdp", None),
            P("section", "fsdp", None),
            P("section", "fsdp", None),
            P("section", "fsdp", None),
            P("section", None, "fsdp"),
            P("section", None, "fsdp"),
            P("section", "fsdp"),
        ),
        out_specs=(
            P("section", None, "fsdp", "ctx", None),
            P("section", None, "fsdp", "ctx", None),
            P("section", "fsdp", None),
            P("section", "fsdp", None),
            P("section", "fsdp", None),
            P("section", "fsdp", None),
            P("section", None, "fsdp"),
            P("section", None, "fsdp"),
            P("section", "fsdp"),
        ),
        check_vma=False,
    )
```

profile of v0, /device:TPU:1, one launch (start us, length us, event | category | flops | bytes accessed | tf_op | source)
XLA Modules:
  0.0 1539.4 jit_solution(5364431452849128275)
XLA Ops:
  18.4 11.4 all_gather.39
  30.2 12.8 slice_reduce_fusion
  48.9 13.2 all-gather.11.cloned.1.call-done
  77.7 25.1 %all-gather.13.cloned.1.call-done = bf16[1024,12,64]{0,2,1:T(8,128)(2,1)} async-done(((bf16[256,12,64]{0,2,1:T(8,128)(2,1)}), bf16[1024,12,64]{0,2,1:T(8,128)(2,1)}) %all-gather.13.cloned.1.call-update) | async-done | bytes 1572880 | tf_op jit(solution)/shard_map/all_gather | solution.py:100
  114.9 26.0 %all-gather.15.cloned.1.call-done = bf16[1024,12,64]{0,2,1:T(8,128)(2,1)} async-done(((bf16[256,12,64]{0,2,1:T(8,128)(2,1)}), bf16[1024,12,64]{0,2,1:T(8,128)(2,1)}) %all-gather.15.cloned.1.call-update) | async-done | bytes 1572880 | tf_op jit(solution)/shard_map/all_gather | solution.py:101
  148.5 21.5 %all-gather.17.cloned.1.call-done = bf16[1,768,768]{2,1,0:T(8,128)(2,1)} async-done(((bf16[1,192,768]{2,1,0:T(8,128)(2,1)}), bf16[1,768,768]{2,1,0:T(8,128)(2,1)}) %all-gather.17.cloned.1.call-update) | async-done | bytes 1179664 | tf_op jit(solution)/shard_map/all_gather | solution.py:283
  172.1 56.7 %all-gather.19.cloned.1.call-done = bf16[1,768,3072]{2,1,0:T(8,128)(2,1)} async-done(((bf16[1,192,3072]{2,1,0:T(8,128)(2,1)}), bf16[1,768,3072]{2,1,0:T(8,128)(2,1)}) %all-gather.19.cloned.1.call-update) | async-done | bytes 4718608 | tf_op jit(solution)/shard_map/all_gather | solution.py:284
  234.2 53.3 %all-gather.21.cloned.1.call-done = bf16[1,3072,768]{2,1,0:T(8,128)(2,1)} async-done(((bf16[1,768,768]{2,1,0:T(8,128)(2,1)}), bf16[1,3072,768]{2,1,0:T(8,128)(2,1)}) %all-gather.21.cloned.1.call-update) | async-done | bytes 4718608 | tf_op jit(solution)/shard_map/all_gather | solution.py:285
  301.3 34.8 %all-gather.23.cloned.1.call-done = bf16[1024,12,64]{0,2,1:T(8,128)(2,1)} async-done(((bf16[256,12,64]{0,2,1:T(8,128)(2,1)}), bf16[1024,12,64]{0,2,1:T(8,128)(2,1)}) %all-gather.23.cloned.1.call-update) | async-done | bytes 1572880 | tf_op jit(solution)/shard_map/all_gather | solution.py:100
  348.3 25.4 %all-gather.25.cloned.1.call-done = bf16[1024,12,64]{0,2,1:T(8,128)(2,1)} async-done(((bf16[256,12,64]{0,2,1:T(8,128)(2,1)}), bf16[1024,12,64]{0,2,1:T(8,128)(2,1)}) %all-gather.25.cloned.1.call-update) | async-done | bytes 1572880 | tf_op jit(solution)/shard_map/all_gather | solution.py:101
  410.8 21.9 %all-gather.27.cloned.1.call-done = bf16[1024,12,64]{0,2,1:T(8,128)(2,1)} async-done(((bf16[256,12,64]{0,2,1:T(8,128)(2,1)}), bf16[1024,12,64]{0,2,1:T(8,128)(2,1)}) %all-gather.27.cloned.1.call-update) | async-done | bytes 1572880 | tf_op jit(solution)/shard_map/all_gather | solution.py:100
  441.0 29.1 %all-gather.29.cloned.1.call-done = bf16[1024,12,64]{0,2,1:T(8,128)(2,1)} async-done(((bf16[256,12,64]{0,2,1:T(8,128)(2,1)}), bf16[1024,12,64]{0,2,1:T(8,128)(2,1)}) %all-gather.29.cloned.1.call-update) | async-done | bytes 1572880 | tf_op jit(solution)/shard_map/all_gather | solution.py:101
  490.6 9.2 convert_reduce_fusion.2
  516.3 170.6 %while.75 = (s32[]{:T(128)}, bf16[256,12,64]{0,2,1:T(8,128)(2,1)}, bf16[256,12,64]{0,2,1:T(8,128)(2,1)}, f32[256,12,64]{0,2,1:T(8,128)}, f32[256,12,64]{0,2,1:T(...) while((s32[]{:T(128)}, bf16[256,12,64]{0,2,1:T(8,128)(2,1)}, ...), condition=%wide.region_26.27_spmd.clone, body=%wide.region_24.26_spmd.clone.sunk | while | flops 513621760 | bytes 37695064 | solution.py:176
  724.9 180.2 %while.76 = (s32[]{:T(128)}, bf16[256,12,64]{0,2,1:T(8,128)(2,1)}, bf16[256,12,64]{0,2,1:T(8,128)(2,1)}, f32[256,12,64]{0,2,1:T(8,128)S(1)}, f32[256,12,64]{0,2,...) while((s32[]{:T(128)}, bf16[256,12,64]{0,2,1:T(8,128)(2,1)}, ...), condition=%wide.region_37.38_spmd.clone, body=%wide.region_35.37_spmd.clone.sunk | while | flops 513621760 | bytes 40742464 | solution.py:176
  942.5 173.1 %while.77 = (s32[]{:T(128)}, bf16[256,12,64]{0,2,1:T(8,128)(2,1)S(1)}, bf16[256,12,64]{0,2,1:T(8,128)(2,1)}, f32[256,12,64]{0,2,1:T(8,128)S(1)}, f32[256,12,64]{...) while((s32[]{:T(128)}, ...), condition=%wide.region_48.49_spmd.clone, body=%wide.region_46.48_spmd.clone.sunk | while | flops 513621760 | bytes 42413716 | solution.py:176
  1159.4 9.5 fusion.130
  1205.9 37.4 %reduce-scatter.18.cloned.1.call-done = bf16[1,192,3072]{2,1,0:T(8,128)(2,1)} async-done(((bf16[1,768,3072]{2,1,0:T(8,128)(2,1)}), bf16[1,192,3072]{2,1,0:T(8,128)(2,1)}) %reduce-scatter.18.cloned.1.call-update) | async-done | bytes 1179664 | tf_op jit(solution)/shard_map/reduce_scatter | solution.py:370
  1243.3 60.0 %reduce-scatter.20.cloned.1.call-done = bf16[1,768,768]{2,1,0:T(8,128)(2,1)} async-done(((bf16[1,3072,768]{2,1,0:T(8,128)(2,1)}), bf16[1,768,768]{2,1,0:T(8,128)(2,1)}) %reduce-scatter.20.cloned.1.call-update) | async-done | bytes 1179664 | tf_op jit(solution)/shard_map/reduce_scatter | solution.py:373
  1313.2 16.8 %reduce-scatter.22.cloned.1.call-done = bf16[192,2]{1,0:T(8,128)(2,1)} async-done(((bf16[768,2]{1,0:T(8,128)(2,1)}), bf16[192,2]{1,0:T(8,128)(2,1)}) %reduce-scatter.22.cloned.1.call-update) | async-done | bytes 784
  1331.0 28.9 %reduce-scatter.26.cloned.1.call-done = bf16[768,1]{1,0:T(8,128)(2,1)} async-done(((bf16[3072,1]{1,0:T(8,128)(2,1)}), bf16[768,1]{1,0:T(8,128)(2,1)}) %reduce-scatter.26.cloned.1.call-update) | async-done | bytes 1552
  1360.9 25.7 %reduce-scatter.24.cloned.1.call-done = bf16[192,6]{1,0:T(8,128)(2,1)} async-done(((bf16[768,6]{1,0:T(8,128)(2,1)}), bf16[192,6]{1,0:T(8,128)(2,1)}) %reduce-scatter.24.cloned.1.call-update) | async-done | bytes 2320
  1388.0 15.4 %all-reduce = (bf16[1,2,192]{2,1,0:T(2,128)(2,1)S(1)}, bf16[1,6,192]{2,0,1:T(2,128)(2,1)S(1)}, bf16[1,768]{1,0:T(2,128)(2,1)S(1)}) all-reduce(bf16[1,2,192]{2,1,0:T(2,128)(2,1)S(1)} %copy.165, bf16[1,6,192]{2,0,1:T(2,128)(2,1)S(1)} %copy.167, bf16[1,768]{1,0:T(2,128)(2,1)S(1)} %copy.169), channel_id=1, replica_groups=mesh['section'=2,'ctx'=4,'fsdp'=4] {'ctx'}, use_global_device_ids=true, to_apply=%region_68.69 | all-reduce | flops 2304 | bytes 9216 | tf_op jit(solution)/shard_map/psum | solution.py:391
  1405.1 119.5 %all-reduce.4.cloned.1.call-done = (bf16[1,192,2304]{2,1,0:T(8,128)(2,1)}, bf16[1,192,768]{2,1,0:T(8,128)(2,1)}, bf16[1,192,3072]{2,1,0:T(8,128)(2,1)}, bf16[1,768,768]{2,1,0:T(8,128)(2,1)}) async-done(((bf16[1,192,2304]{2,1,0:T(8,128)(2,1)}, bf16[1,192,768]{2,1,0:T(8,128)(2,1)}, bf16[1,192,3072]{2,1,0:T(8,128)(2,1)}, bf16[1,768,768]{2,1,0:T(8,128)(2,1)}), (bf16[1,192,2304]{2,1,0:T(8,128)(2,1)}, ...) | async-done | bytes 3538960 | tf_op jit(solution)/shard_map/psum | solution.py:387
  (957 shorter events, 868.3 us)
Async XLA Ops:
  7.2 54.8 %all-gather.11.cloned.1.call-start = ((), (), s32[]{:S(2)}) async-start(), calls=%async_computation.7 | async-start | bytes 4423680 | tf_op jit(solution)/shard_map/all_gather | solution.py:282
  7.9 94.9 %all-gather.13.cloned.1.call-start = ((), (), s32[]{:S(2)}) async-start(), calls=%async_computation.8 | async-start | bytes 1966080 | tf_op jit(solution)/shard_map/all_gather | solution.py:100
  66.3 74.6 %all-gather.15.cloned.1.call-start = ((), (), s32[]{:S(2)}) async-start(), calls=%async_computation.9 | async-start | bytes 1966080 | tf_op jit(solution)/shard_map/all_gather | solution.py:101
  67.3 102.7 %all-gather.17.cloned.1.call-start = ((), (), s32[]{:S(2)}) async-start(), calls=%async_computation.10 | async-start | bytes 1474560 | tf_op jit(solution)/shard_map/all_gather | solution.py:283
  67.9 160.9 %all-gather.19.cloned.1.call-start = ((), (), s32[]{:S(2)}) async-start(), calls=%async_computation.11 | async-start | bytes 5898240 | tf_op jit(solution)/shard_map/all_gather | solution.py:284
  68.4 219.1 %all-gather.21.cloned.1.call-start = ((), (), s32[]{:S(2)}) async-start(), calls=%async_computation.12 | async-start | bytes 5898240 | tf_op jit(solution)/shard_map/all_gather | solution.py:285
  69.0 267.1 %all-gather.23.cloned.1.call-start = ((), (), s32[]{:S(2)}) async-start(), calls=%async_computation.13 | async-start | bytes 1966080 | tf_op jit(solution)/shard_map/all_gather | solution.py:100
  300.1 73.5 %all-gather.25.cloned.1.call-start = ((), (), s32[]{:S(2)}) async-start(), calls=%async_computation.14 | async-start | bytes 1966080 | tf_op jit(solution)/shard_map/all_gather | solution.py:101
  301.1 131.6 %all-gather.27.cloned.1.call-start = ((), (), s32[]{:S(2)}) async-start(), calls=%async_computation.15 | async-start | bytes 1966080 | tf_op jit(solution)/shard_map/all_gather | solution.py:100
  397.9 72.3 %all-gather.29.cloned.1.call-start = ((), (), s32[]{:S(2)}) async-start(), calls=%async_computation.16 | async-start | bytes 1966080 | tf_op jit(solution)/shard_map/all_gather | solution.py:101
  406.2 799.7 %reduce-scatter.16.cloned.1.call-start = ((), (), s32[]{:S(2)}) async-start(), calls=%async_computation.18 | async-start | bytes 1474560 | tf_op jit(solution)/shard_map/reduce_scatter | solution.py:367
  735.4 35.5 %collective-permute-start.5 = (bf16[256,12,64]{0,2,1:T(8,128)(2,1)}, bf16[256,12,64]{0,2,1:T(8,128)(2,1)}, u32[]{:S(2)}, u32[]{:S(2)}) collective-permute-start(bf16[256,12,64]{0,2,1:T(8,128)(2,1)} %copy.202), channel_id=1, source_target_pairs={{0,4},{4,8},{8,12},{12,0},{1,5},{5,9},{9,13},{13,1},{2,6},{6,10},{... | collective-permute-start | bytes 1179656 | tf_op jit(solution)/shard_map/while/body/eval_jaxpr/ppermute | solution.py:15
  781.5 35.0 %collective-permute-start.5 = (bf16[256,12,64]{0,2,1:T(8,128)(2,1)}, bf16[256,12,64]{0,2,1:T(8,128)(2,1)}, u32[]{:S(2)}, u32[]{:S(2)}) collective-permute-start(bf16[256,12,64]{0,2,1:T(8,128)(2,1)} %copy.202), channel_id=1, source_target_pairs={{0,4},{4,8},{8,12},{12,0},{1,5},{5,9},{9,13},{13,1},{2,6},{6,10},{... | collective-permute-start | bytes 1179656 | tf_op jit(solution)/shard_map/while/body/eval_jaxpr/ppermute | solution.py:15
  827.2 34.1 %collective-permute-start.5 = (bf16[256,12,64]{0,2,1:T(8,128)(2,1)}, bf16[256,12,64]{0,2,1:T(8,128)(2,1)}, u32[]{:S(2)}, u32[]{:S(2)}) collective-permute-start(bf16[256,12,64]{0,2,1:T(8,128)(2,1)} %copy.202), channel_id=1, source_target_pairs={{0,4},{4,8},{8,12},{12,0},{1,5},{5,9},{9,13},{13,1},{2,6},{6,10},{... | collective-permute-start | bytes 1179656 | tf_op jit(solution)/shard_map/while/body/eval_jaxpr/ppermute | solution.py:15
  940.8 265.1 %reduce-scatter.14.cloned.1.call-start = ((), (), s32[]{:S(2)}) async-start(), calls=%async_computation.17 | async-start | bytes 4423680 | tf_op jit(solution)/shard_map/reduce_scatter | solution.py:364
  951.4 35.5 %collective-permute-start.9 = (bf16[256,12,64]{0,2,1:T(8,128)(2,1)}, bf16[256,12,64]{0,2,1:T(8,128)(2,1)}, u32[]{:S(2)}, u32[]{:S(2)}) collective-permute-start(bf16[256,12,64]{0,2,1:T(8,128)(2,1)} %copy-done.34), channel_id=1, source_target_pairs={{0,4},{4,8},{8,12},{12,0},{1,5},{5,9},{9,13},{13,1},{2,6},{6,10},{... | collective-permute-start | bytes 1179656 | tf_op jit(solution)/shard_map/while/body/eval_jaxpr/ppermute | solution.py:15
  995.7 35.0 %collective-permute-start.9 = (bf16[256,12,64]{0,2,1:T(8,128)(2,1)}, bf16[256,12,64]{0,2,1:T(8,128)(2,1)}, u32[]{:S(2)}, u32[]{:S(2)}) collective-permute-start(bf16[256,12,64]{0,2,1:T(8,128)(2,1)} %copy-done.34), channel_id=1, source_target_pairs={{0,4},{4,8},{8,12},{12,0},{1,5},{5,9},{9,13},{13,1},{2,6},{6,10},{... | collective-permute-start | bytes 1179656 | tf_op jit(solution)/shard_map/while/body/eval_jaxpr/ppermute | solution.py:15
  1039.6 34.1 %collective-permute-start.9 = (bf16[256,12,64]{0,2,1:T(8,128)(2,1)}, bf16[256,12,64]{0,2,1:T(8,128)(2,1)}, u32[]{:S(2)}, u32[]{:S(2)}) collective-permute-start(bf16[256,12,64]{0,2,1:T(8,128)(2,1)} %copy-done.34), channel_id=1, source_target_pairs={{0,4},{4,8},{8,12},{12,0},{1,5},{5,9},{9,13},{13,1},{2,6},{6,10},{... | collective-permute-start | bytes 1179656 | tf_op jit(solution)/shard_map/while/body/eval_jaxpr/ppermute | solution.py:15
  1128.8 114.5 %reduce-scatter.18.cloned.1.call-start = ((), (), s32[]{:S(2)}) async-start(), calls=%async_computation.19 | async-start | bytes 5898240 | tf_op jit(solution)/shard_map/reduce_scatter | solution.py:370
  1146.0 157.2 %reduce-scatter.20.cloned.1.call-start = ((), (), s32[]{:S(2)}) async-start(), calls=%async_computation.20 | async-start | bytes 5898240 | tf_op jit(solution)/shard_map/reduce_scatter | solution.py:373
  1168.9 161.1 %reduce-scatter.22.cloned.1.call-start = ((), (), s32[]{:S(2)}) async-start(), calls=%async_computation.21 | async-start | bytes 245760
  1198.4 161.5 %reduce-scatter.26.cloned.1.call-start = ((), (), s32[]{:S(2)}) async-start(), calls=%async_computation.23 | async-start | bytes 983040
  1202.6 184.0 %reduce-scatter.24.cloned.1.call-start = ((), (), s32[]{:S(2)}) async-start(), calls=%async_computation.22 | async-start | bytes 245760
  1205.8 318.8 %all-reduce.4.cloned.1.call-start = ((), (), s32[]{:S(2)}) async-start(), calls=%async_computation.24 | async-start | bytes 7077888 | tf_op jit(solution)/shard_map/psum | solution.py:387
  (259 other events, 4054.1 us)
Sparse Core Ops, SparseCore 0:
  9.9 52.1 all-gather.10
  66.4 36.3 all-gather.12
  104.9 35.9 all-gather.14
  142.6 27.3 all-gather.16
  171.6 57.0 all-gather.18
  230.4 57.0 all-gather.20
  300.2 35.8 all-gather.22
  337.7 35.9 all-gather.24
  398.0 34.6 all-gather.26
  434.1 35.9 all-gather.28
  940.9 32.6 reduce-scatter.15
  1128.9 54.2 reduce-scatter.13
  1186.2 57.0 reduce-scatter.17
  1246.1 57.0 reduce-scatter.19
  1306.4 23.5 reduce-scatter.21
  1333.3 26.5 reduce-scatter.25
  1363.1 23.5 reduce-scatter.23
  1389.1 135.4 all-reduce.3
where the time goes:
time: 1550 us; the launch traced here: 1540 us
  waiting for transfers between devices  900 us (58%)
  matrix products  271 us (17%)
  other arithmetic  130 us (8%)
  local copies, waits for them, and re-layouts  118 us (8%)
  starting transfers between devices  62.9 us (4%)
  blocking collectives  41.5 us (3%)
  between operations  16.7 us (1%)
    ppermute x48, waiting for transfers between devices, shifted(): return lax.ppermute(value, axis, pairs)  297 us
    psum x1, waiting for transfers between devices, body(): lax.psum(scattered[0].astype(jnp.bfloat16), 'ctx').astype(jnp.float32)  120 us
    all_gather x3, waiting for transfers between devices, attend_forward(): lax.all_gather(key_rows, 'ctx', axis=0, tiled=True)  81.8 us
    all_gather x3, waiting for transfers between devices, attend_forward(): lax.all_gather(value_rows, 'ctx', axis=0, tiled=True)  80.5 us
    unnamed x21, waiting for transfers between devices  73.9 us
    dot_general x12, matrix products, grad_dot(): lax.dot_general(left, right, (((0,), (0,)), ((), ())), preferred_element_...  62.3 us
    reduce_scatter x1, waiting for transfers between devices, body(): lax.psum_scatter(totals[3][None].astype(jnp.bfloat16), 'fsdp', scatter_di...  60 us
    all_gather x1, waiting for transfers between devices, body(): lax.all_gather(w_up, 'fsdp', axis=1, tiled=True)  56.7 us
  transfers between devices with their start and end apart: 70, of which 64 were waited for; matrix products, arithmetic and copies ran while one was open for 19% of the time, Pallas kernels for 0%

commit v1 on v0

v1 whole, which is shorter than its diff:
```python
import functools

import jax
import jax.numpy as jnp
from jax import lax
from jax.experimental import pallas as pl
from jax.experimental.pallas import tpu as pltpu
from jax.sharding import PartitionSpec as P

HEADS = 12
EPS = 1e-05
GELU_C = 0.7978845608
GELU_A = 0.044715
LANES = 128
BF = jnp.bfloat16
F32 = jnp.float32


def dot(a, b, ca, cb):
    return lax.dot_general(a, b, (((ca,), (cb,)), ((), ())), preferred_element_type=F32)


def swap_cores(value):
    count = lax.axis_size("section")
    return lax.ppermute(value, "section", [(s, count - 1 - s) for s in range(count)])


def move_spans(order_ref, ctx, span, copy):
    for c in range(ctx):
        first = order_ref[c]
        for half, span_id in ((0, first), (1, 2 * ctx - 1 - first)):
            copy(c, half, pl.multiple_of(span_id * span, span))


def causal(scores, width, fill):
    depth = scores.shape[0]
    keys = lax.broadcasted_iota(jnp.int32, (width, width), 0)
    rows = lax.broadcasted_iota(jnp.int32, (width, width), 1)
    last = jnp.where(keys <= rows, scores[depth - width :], fill)
    if depth == width:
        return last
    return jnp.concatenate([scores[: depth - width], last], axis=0)


def attn_fwd_kernel(order_ref, qkv_ref, mixed_ref, sorted_ref, out_ref, lse_ref, *, heads, size, block):
    ctx, _, rows = qkv_ref.shape
    span = rows // 2
    feats = heads * size
    seq = ctx * rows

    def bring(c, half, place):
        sorted_ref[:, pl.ds(place, span)] = qkv_ref[c, :, half * span : (half + 1) * span]

    move_spans(order_ref, ctx, span, bring)
    lse_ref[...] = jnp.zeros_like(lse_ref)
    for h in range(heads):
        for start in range(0, seq, block):
            end = start + block
            q = sorted_ref[h * size : (h + 1) * size, start:end]
            k = sorted_ref[feats + h * size : feats + (h + 1) * size, :end]
            v = sorted_ref[2 * feats + h * size : 2 * feats + (h + 1) * size, :end]
            scores = causal(dot(k, q, 0, 0) * 0.125, block, -1e30)
            top = jnp.max(scores, axis=0, keepdims=True)
            weights = jnp.exp(scores - top)
            total = jnp.sum(weights, axis=0, keepdims=True)
            mixed = dot(v, weights.astype(BF), 1, 0) / total
            out_ref[h * size : (h + 1) * size, start:end] = mixed.astype(BF)
            lse_ref[h : h + 1, start:end] = top + jnp.log(total)

    def give(c, half, place):
        mixed_ref[c, :, half * span : (half + 1) * span] = out_ref[:, pl.ds(place, span)]

    move_spans(order_ref, ctx, span, give)


def attn_bwd_kernel(
    order_ref, dout_ref, sorted_ref, out_ref, lse_ref, grad_ref, dsort, gsort, gk, gv, *, heads, size, block
):
    ctx, _, rows = dout_ref.shape
    span = rows // 2
    feats = heads * size
    seq = ctx * rows

    def bring(c, half, place):
        dsort[:, pl.ds(place, span)] = dout_ref[c, :, half * span : (half + 1) * span]

    move_spans(order_ref, ctx, span, bring)
    for h in range(heads):
        own = slice(h * size, (h + 1) * size)
        gk[...] = jnp.zeros_like(gk)
        gv[...] = jnp.zeros_like(gv)
        for start in range(0, seq, block):
            end = start + block
            q = sorted_ref[own, start:end]
            k = sorted_ref[feats + h * size : feats + (h + 1) * size, :end]
            v = sorted_ref[2 * feats + h * size : 2 * feats + (h + 1) * size, :end]
            dout = dsort[own, start:end]
            delta = jnp.sum(
                dout.astype(F32) * out_ref[own, start:end].astype(F32), axis=0, keepdims=True
            )
            scores = dot(k, q, 0, 0) * 0.125 - lse_ref[h : h + 1, start:end]
            probs = jnp.exp(causal(scores, block, -1e30))
            dprobs = dot(v, dout, 0, 0)
            dscores = (probs * (dprobs - delta)).astype(BF)
            gsort[own, start:end] = (dot(k, dscores, 1, 0) * 0.125).astype(BF)
            gk[:, :end] += dot(q, dscores, 1, 1)
            gv[:, :end] += dot(dout, probs.astype(BF), 1, 1)
        gsort[feats + h * size : feats + (h + 1) * size, :] = (gk[...] * 0.125).astype(BF)
        gsort[2 * feats + h * size : 2 * feats + (h + 1) * size, :] = gv[...].astype(BF)

    def give(c, half, place):
        grad_ref[c, :, half * span : (half + 1) * span] = gsort[:, pl.ds(place, span)]

    move_spans(order_ref, ctx, span, give)


VMEM = pl.BlockSpec(memory_space=pltpu.VMEM)
SMEM = pl.BlockSpec(memory_space=pltpu.SMEM)
PARAMS = pltpu.CompilerParams(vmem_limit_bytes=48 * 1024 * 1024)


def widen(received, span_order):
    ctx, feats, rows = received.shape
    span = rows // 2
    holder = jnp.concatenate([span_order, 2 * ctx - 1 - span_order])
    source = jnp.concatenate([2 * jnp.arange(ctx), 2 * jnp.arange(ctx) + 1])
    place = jnp.zeros((2 * ctx,), jnp.int32).at[holder].set(source.astype(jnp.int32))
    flat = received.reshape(ctx, feats, 2, span).transpose(1, 0, 2, 3).reshape(feats, 2 * ctx, span)
    return jnp.take(flat, place, axis=1).reshape(1, feats, ctx * rows)


def narrow(wide, span_order, ctx):
    feats, seq = wide.shape[1:]
    span = seq // (2 * ctx)
    holder = jnp.stack([span_order, 2 * ctx - 1 - span_order], axis=1).reshape(-1)
    flat = jnp.take(wide.reshape(feats, 2 * ctx, span), holder, axis=1)
    return flat.reshape(feats, ctx, 2 * span).transpose(1, 0, 2)


def attention_forward(received, span_order, heads, size):
    ctx, _, rows = received.shape
    seq = ctx * rows
    narrow_spans = (rows // 2) % LANES != 0
    order = span_order
    if narrow_spans:
        received, order = widen(received, span_order), jnp.zeros((1,), jnp.int32)
    block = min(256, seq // 2)
    mixed, kept, out, lse = pl.pallas_call(
        functools.partial(attn_fwd_kernel, heads=heads, size=size, block=block),
        in_specs=[SMEM, VMEM],
        out_specs=[VMEM] * 4,
        out_shape=[
            jax.ShapeDtypeStruct((received.shape[0], heads * size, received.shape[2]), BF),
            jax.ShapeDtypeStruct((3 * heads * size, seq), BF),
            jax.ShapeDtypeStruct((heads * size, seq), BF),
            jax.ShapeDtypeStruct((8 * pl.cdiv(heads, 8), seq), F32),
        ],
        compiler_params=PARAMS,
        name="attn_fwd",
    )(order, received)
    if narrow_spans:
        mixed = narrow(mixed, span_order, ctx)
    return mixed, (kept, out, lse)


def attention_backward(dout, saved, span_order, heads, size):
    ctx, _, rows = dout.shape
    seq = ctx * rows
    kept, out, lse = saved
    narrow_spans = (rows // 2) % LANES != 0
    order = span_order
    if narrow_spans:
        dout, order = widen(dout, span_order), jnp.zeros((1,), jnp.int32)
    block = min(256, seq // 2)
    grad = pl.pallas_call(
        functools.partial(attn_bwd_kernel, heads=heads, size=size, block=block),
        in_specs=[SMEM, VMEM, VMEM, VMEM, VMEM],
        out_specs=VMEM,
        out_shape=jax.ShapeDtypeStruct((dout.shape[0], 3 * heads * size, dout.shape[2]), BF),
        scratch_shapes=[
            pltpu.VMEM((heads * size, seq), BF),
            pltpu.VMEM((3 * heads * size, seq), BF),
            pltpu.VMEM((size, seq), F32),
            pltpu.VMEM((size, seq), F32),
        ],
        compiler_params=PARAMS,
        name="attn_bwd",
    )(order, dout, kept, out, lse)
    if narrow_spans:
        grad = narrow(grad, span_order, ctx)
    return grad


def exchange(value):
    return lax.all_to_all(value, "ctx", split_axis=0, concat_axis=0, tiled=True)


def to_heads(value, blocks, ctx):
    rows = value.shape[1]
    size = value.shape[0] // (blocks * HEADS)
    held = pl.cdiv(HEADS, ctx)
    value = value.reshape(blocks, HEADS, size, rows)
    if held * ctx != HEADS:
        value = jnp.pad(value, ((0, 0), (0, held * ctx - HEADS), (0, 0), (0, 0)))
    value = value.reshape(blocks, ctx, held * size, rows).transpose(1, 0, 2, 3)
    return value.reshape(ctx, blocks * held * size, rows)


def from_heads(value, blocks, size):
    ctx, _, rows = value.shape
    held = pl.cdiv(HEADS, ctx)
    value = value.reshape(ctx, blocks, held * size, rows).transpose(1, 0, 2, 3)
    value = value.reshape(blocks, ctx * held, size, rows)[:, :HEADS]
    return value.reshape(blocks * HEADS * size, rows)


def normalised(values):
    centred = values - jnp.mean(values, axis=-1, keepdims=True)
    scale = lax.rsqrt(jnp.mean(centred * centred, axis=-1, keepdims=True) + EPS)
    return centred * scale, scale


def norm_back(unit, scale, upstream, gain):
    w = upstream * gain
    return (
        w - jnp.mean(w, axis=-1, keepdims=True) - unit * jnp.mean(w * unit, axis=-1, keepdims=True)
    ) * scale


def layer_forward(x, weights, vectors, span_order, ctx):
    w_qkv, w_out, w_up, w_down = weights
    gains, shifts, hidden_bias = vectors
    width = x.shape[1]
    size = width // HEADS
    held = pl.cdiv(HEADS, ctx)
    unit, scale = normalised(x)
    normed = (unit * gains[0] + shifts[0]).astype(BF)
    qkv_bias = jnp.concatenate([shifts[1], jnp.zeros_like(shifts[1]), shifts[2]])
    projected = (dot(w_qkv, normed, 0, 1) + qkv_bias[:, None]).astype(BF)
    received = exchange(to_heads(projected, 3, ctx))
    mixed, attn_saved = attention_forward(received, span_order, held, size)
    mixed = from_heads(exchange(mixed), 1, size)
    inner = x + dot(mixed, w_out, 0, 0) + shifts[3]
    unit2, scale2 = normalised(inner)
    middle = (unit2 * gains[1] + shifts[4]).astype(BF)
    hidden = dot(middle, w_up, 1, 0) + hidden_bias
    activated = (0.5 * hidden * (1.0 + jnp.tanh(GELU_C * (hidden + GELU_A * hidden**3)))).astype(BF)
    result = (inner + dot(activated, w_down, 1, 0) + shifts[5]).astype(BF)
    return result, (x, normed, attn_saved, mixed, inner, middle, hidden, activated)


def layer_backward(saved, grad_y, weights, vectors, span_order, ctx):
    x, normed, attn_saved, mixed, inner, middle, hidden, activated = saved
    w_qkv, w_out, w_up, w_down = weights
    gains, shifts, hidden_bias = vectors
    size = x.shape[1] // HEADS
    held = pl.cdiv(HEADS, ctx)
    grad_low = grad_y.astype(BF)
    grad_act = dot(grad_low, w_down, 1, 1)
    th = jnp.tanh(GELU_C * (hidden + GELU_A * hidden**3))
    slope = 0.5 * (1.0 + th) + 0.5 * hidden * (1.0 - th * th) * GELU_C * (
        1.0 + 3.0 * GELU_A * hidden * hidden
    )
    grad_hid = (grad_act * slope).astype(BF)
    up_mid = dot(grad_hid, w_up, 1, 1)
    unit2, scale2 = normalised(inner)
    grad_inner = grad_y + norm_back(unit2, scale2, up_mid, gains[1])
    grad_attn = grad_inner.astype(BF)
    grad_mixed = dot(w_out, grad_attn, 1, 1).astype(BF)
    dout = exchange(to_heads(grad_mixed, 1, ctx))
    grad_up = dot(middle, grad_hid, 0, 0)
    grad_down = dot(activated, grad_low, 0, 0)
    grad_out = dot(mixed, grad_attn, 1, 0)
    grad = exchange(attention_backward(dout, attn_saved, span_order, held, size))
    grad_qkv = from_heads(grad, 3, size)
    up_norm = dot(grad_qkv, w_qkv, 0, 1)
    unit, scale = normalised(x)
    grad_x = grad_inner + norm_back(unit, scale, up_norm, gains[0])
    grad_w_qkv = dot(normed, grad_qkv, 0, 1)
    width = x.shape[1]
    row_sums = jnp.sum(grad_qkv.astype(F32), axis=1)
    small = jnp.stack(
        [
            jnp.sum(up_norm * unit, axis=0),
            jnp.sum(up_mid * unit2, axis=0),
            jnp.sum(up_norm, axis=0),
            row_sums[:width],
            row_sums[2 * width :],
            jnp.sum(grad_attn.astype(F32), axis=0),
            jnp.sum(up_mid, axis=0),
            jnp.sum(grad_low.astype(F32), axis=0),
        ]
    )
    small_hidden = jnp.sum(grad_hid.astype(F32), axis=0)
    return grad_x, (grad_w_qkv, grad_out, grad_up, grad_down, small, small_hidden)


def columns_of_rows(value, parts):
    depth = value.shape[0] // parts
    return jnp.concatenate([value[i * depth : (i + 1) * depth] for i in range(parts)], axis=1)


def rows_of_columns(value, parts):
    width = value.shape[1] // parts
    return jnp.concatenate([value[:, i * width : (i + 1) * width] for i in range(parts)], axis=0)


def gather_weights(w_qkv, w_out, w_up, w_down, norm_gains, bias_rows, bias_hidden):
    axes = ("section", "fsdp")
    depth = w_qkv.shape[1]
    ratio = bias_hidden.shape[1] // depth
    small = jnp.concatenate([norm_gains[0], bias_rows[0], bias_hidden[0].reshape(ratio, depth)]).T
    small = jnp.pad(small, ((0, 0), (0, LANES - small.shape[1])))
    first = lax.all_gather(jnp.concatenate([w_qkv[0], small], axis=1), axes)
    second = lax.all_gather(jnp.concatenate([w_out[0], w_up[0]], axis=1), axes)
    third = lax.all_gather(w_down[0], axes)
    layers = w_qkv.shape[0] * lax.axis_size("section")
    fsdp = lax.axis_size("fsdp")
    width = depth * fsdp
    wide = w_qkv.shape[2]
    first = first.reshape(layers, width, -1)
    second = second.reshape(layers, width, -1)
    third = third.reshape(layers, -1, width)
    weights, vectors = [], []
    for s in range(layers):
        weights.append(
            (first[s, :, :wide], second[s, :, :width], second[s, :, width:], third[s])
        )
        table = first[s, :, wide:].T.astype(F32)
        gain_count, shift_count = norm_gains.shape[1], bias_rows.shape[1]
        hidden = table[gain_count + shift_count : gain_count + shift_count + ratio]
        hidden = hidden.reshape(ratio, fsdp, depth).transpose(1, 0, 2).reshape(-1)
        vectors.append(
            (table[:gain_count], table[gain_count : gain_count + shift_count], hidden)
        )
    return weights, vectors


def half(value, core):
    width = value.shape[-1] // 2
    return jnp.where(core == 0, value[..., :width], value[..., width:])


def reduce_pack(pack, small, core):
    kept, sent = half(pack, core), half(pack, 1 - core)
    if small is not None:
        kept = jnp.concatenate([kept, small], axis=1)
        sent = jnp.concatenate([sent, small], axis=1)
    total = kept + swap_cores(sent.astype(BF)).astype(F32)
    part = lax.psum_scatter(total.astype(BF), "fsdp", scatter_dimension=0, tiled=True)
    return lax.psum(part, "ctx")


def arranged_down(value, fsdp, ratio):
    full, width = value.shape
    depth = full // (fsdp * ratio)
    value = value.reshape(fsdp, ratio, depth, 2, width // 2).transpose(0, 2, 3, 1, 4)
    return value.reshape(fsdp * depth, ratio * width)


def body(
    tokens, cotangent, span_order, w_qkv, w_out, w_up, w_down, norm_gains, bias_rows, bias_hidden
):
    core = lax.axis_index("section")
    ctx = lax.axis_size("ctx")
    fsdp = lax.axis_size("fsdp")
    weights, vectors = gather_weights(
        w_qkv, w_out, w_up, w_down, norm_gains, bias_rows, bias_hidden
    )
    depth = w_qkv.shape[1]
    ratio = bias_hidden.shape[1] // depth
    own_tokens = jnp.where(core == 0, tokens[0, 0], tokens[1, 0]).astype(F32)
    own_cot = jnp.where(core == 0, cotangent[0, 0], cotangent[1, 0]).astype(F32)
    out0, saved0 = layer_forward(own_tokens, weights[0], vectors[0], span_order, ctx)
    out1, saved1 = layer_forward(out0.astype(F32), weights[1], vectors[1], span_order, ctx)
    other_out = swap_cores(jnp.where(core == 0, out1, out0))
    layer_outputs = jnp.where(
        core == 0, jnp.stack([out0, other_out]), jnp.stack([other_out, out1])
    )

    def reduced(grads):
        grad_w_qkv, grad_out, grad_up, grad_down, small, small_hidden = grads
        small_hidden = small_hidden.reshape(fsdp, ratio, depth).transpose(0, 2, 1)
        small = jnp.concatenate([small.T, small_hidden.reshape(fsdp * depth, ratio)], axis=1)
        count = small.shape[1]
        small = jnp.pad(small, ((0, 0), (0, LANES - count)))
        down = arranged_down(grad_down, fsdp, ratio)
        mid = down.shape[1] // 2
        up_mid = grad_up.shape[1] // 2
        early = jnp.concatenate(
            [grad_up[:, :up_mid], down[:, :mid], grad_up[:, up_mid:], down[:, mid:]], axis=1
        )
        q_mid, o_mid = grad_w_qkv.shape[1] // 2, grad_out.shape[1] // 2
        late = jnp.concatenate(
            [grad_w_qkv[:, :q_mid], grad_out[:, :o_mid], grad_w_qkv[:, q_mid:], grad_out[:, o_mid:]],
            axis=1,
        )
        return reduce_pack(early, None, core), reduce_pack(late, small, core)

    grad1, grads1 = layer_backward(saved1, own_cot, weights[1], vectors[1], span_order, ctx)
    early1, late1 = reduced(grads1)
    grad0, grads0 = layer_backward(
        saved0, grad1.astype(BF).astype(F32), weights[0], vectors[0], span_order, ctx
    )
    early0, late0 = reduced(grads0)
    other_grad = swap_cores(jnp.where(core == 0, grad1, grad0))
    input_grads = jnp.where(
        core == 0, jnp.stack([grad0, other_grad]), jnp.stack([other_grad, grad1])
    )
    own_early = jnp.where(core == 0, early0, early1)
    own_late = jnp.where(core == 0, late0, late1)
    other_early = swap_cores(jnp.where(core == 0, early1, early0))
    other_late = swap_cores(jnp.where(core == 0, late1, late0))

    def joined(own, other):
        return jnp.where(
            core == 0,
            jnp.concatenate([own, other], axis=1),
            jnp.concatenate([other, own], axis=1),
        ).astype(F32)

    up_half = w_up.shape[2] // 2
    qkv_half = w_qkv.shape[2] // 2
    out_half = w_out.shape[2] // 2
    late_half = qkv_half + out_half
    final_qkv = joined(own_late[:, :qkv_half], other_late[:, :qkv_half])
    final_out = joined(own_late[:, qkv_half:late_half], other_late[:, qkv_half:late_half])
    final_up = joined(own_early[:, :up_half], other_early[:, :up_half])
    final_down = joined(
        rows_of_columns(own_early[:, up_half:], ratio),
        rows_of_columns(other_early[:, up_half:], ratio),
    )
    table = own_late[:, late_half:].T.astype(F32)
    gain_count, shift_count = norm_gains.shape[1], bias_rows.shape[1]
    return (
        layer_outputs[None, :, None],
        input_grads[None, :, None],
        final_qkv[None],
        final_out[None],
        final_up[None],
        final_down[None],
        table[None, :gain_count],
        table[None, gain_count : gain_count + shift_count],
        table[gain_count + shift_count : gain_count + shift_count + ratio].reshape(1, -1),
    )


def solution(mesh):
    return jax.shard_map(
        body,
        mesh=mesh,
        in_specs=(
            P(None, "fsdp", "ctx", None),
            P(None, "fsdp", "ctx", None),
            P(),
            P("section", "fsdp", None),
            P("section", "fsdp", None),
            P("section", "fsdp", None),
            P("section", "fsdp", None),
            P("section", None, "fsdp"),
            P("section", None, "fsdp"),
            P("section", "fsdp"),
        ),
        out_specs=(
            P("section", None, "fsdp", "ctx", None),
            P("section", None, "fsdp", "ctx", None),
            P("section", "fsdp", None),
            P("section", "fsdp", None),
            P("section", "fsdp", None),
            P("section", "fsdp", None),
            P("section", None, "fsdp"),
            P("section", None, "fsdp"),
            P("section", "fsdp"),
        ),
        check_vma=False,
    )
```

time: 1550 us -> 817 us (0.53)
  waiting for transfers between devices: 900 us -> 378 us
  matrix products: 271 us -> 80.1 us
  other arithmetic: 130 us -> 67.9 us
  starting transfers between devices: 62.9 us -> 26.4 us
  blocking collectives: 41.5 us -> 77.3 us
  Pallas kernels: 0 us -> 30.3 us
    ppermute x52 -> x8, waiting for transfers between devices: 302 us -> 9.26 us  [swap_cores(): lax.ppermute(value, 'section', [(s, count - 1 - s) for s in range(count)])]
    dot_general x102 -> x24, matrix products: 271 us -> 80.1 us  [dot(): lax.dot_general(a, b, (((ca,), (cb,)), ((), ())), preferred_element_type=...]
    all_gather x10 -> x3, waiting for transfers between devices: 307 us -> 126 us  [the longest x1 63.2 us: gather_weights(): second = lax.all_gather(jnp.concatenate([w_out[0], w_up[0]], axis=1), axes)]
    all_to_all x0 -> x3, blocking collectives: none -> 77.3 us  [exchange(): return lax.all_to_all(value, 'ctx', split_axis=0, concat_axis=0, tiled=True)]
    unnamed x21 -> x8, waiting for transfers between devices: 73.9 us -> 0.81 us
    ppermute x52 -> x8, starting transfers between devices: 61.6 us -> 4.76 us  [swap_cores(): lax.ppermute(value, 'section', [(s, count - 1 - s) for s in range(count)])]
    reshape x0 -> x15, local copies, waits for them, and re-layouts: none -> 53.5 us  [the longest x2 26.4 us: arranged_down(): value.reshape(fsdp, ratio, depth, 2, width // 2).transpose(0, 2, 3, 1, 4)]
    reduce_sum x43 -> x11, other arithmetic: 45.5 us -> 7.32 us  [the longest x2 3.25 us: layer_backward(): jnp.sum(grad_low.astype(F32), axis=0)]
  transfers between devices with their start and end apart: 70 -> 21, of which waited for: 64 -> 10; matrix products, arithmetic and copies ran while one was open for 19% -> 25% of each run, Pallas kernels for 0% -> 2%
where the time goes in v1:
time: 817 us; the launch traced here: 809 us
  waiting for transfers between devices  378 us (46%)
  local copies, waits for them, and re-layouts  133 us (16%)
  matrix products  80.1 us (10%)
  blocking collectives  77.3 us (9%)
  other arithmetic  67.9 us (8%)
  Pallas kernels  30.3 us (4%)
  starting transfers between devices  26.4 us (3%)
  between operations  15.8 us (2%)
    psum x1, waiting for transfers between devices, reduce_pack(): return lax.psum(part, 'ctx')  129 us
    reduce_scatter x4, waiting for transfers between devices, reduce_pack(): lax.psum_scatter(total.astype(BF), 'fsdp', scatter_dimension=0, tiled=True)  84.9 us
    dot_general x24, matrix products, dot(): lax.dot_general(a, b, (((ca,), (cb,)), ((), ())), preferred_element_type=...  80.1 us
    all_to_all x3, blocking collectives, exchange(): return lax.all_to_all(value, 'ctx', split_axis=0, concat_axis=0, tiled=True)  77.3 us
    all_gather x1, waiting for transfers between devices, gather_weights(): second = lax.all_gather(jnp.concatenate([w_out[0], w_up[0]], axis=1), axes)  63.2 us
    all_gather x1, waiting for transfers between devices, gather_weights(): first = lax.all_gather(jnp.concatenate([w_qkv[0], small], axis=1), axes)  50.6 us
    all_to_all x5, waiting for transfers between devices, exchange(): return lax.all_to_all(value, 'ctx', split_axis=0, concat_axis=0, tiled=True)  28.4 us
    reshape x2, local copies, waits for them, and re-layouts, arranged_down(): value.reshape(fsdp, ratio, depth, 2, width // 2).transpose(0, 2, 3, 1, 4)  26.4 us
  transfers between devices with their start and end apart: 21, of which 10 were waited for; matrix products, arithmetic and copies ran while one was open for 25% of the time, Pallas kernels for 2%

profile of v1, /device:TPU:1, one launch (start us, length us, event | category | flops | bytes accessed | tf_op | source)
XLA Modules:
  0.0 809.0 jit_solution(1838424702845613881)
XLA Ops:
  13.7 50.6 %all-gather.8.cloned.1.call-done = bf16[1536,2432]{1,0:T(8,128)(2,1)} async-done(((bf16[192,2432]{1,0:T(8,128)(2,1)}), bf16[1536,2432]{1,0:T(8,128)(2,1)}) %all-gather.8.cloned.1.call-update) | async-done | bytes 7471120 | tf_op jit(solution)/shard_map/all_gather | solution.py:314
  70.0 32.2 %all_to_all.40.qkv_ref = bf16[4,576,256]{2,1,0:T(8,128)(2,1)S(1)} all-to-all(bf16[4,576,256]{2,1,0:T(8,128)(2,1)S(1)} %bitcast.222), channel_id=1, replica_groups=mesh['section'=2,'ctx'=4,'fsdp'=4] {'ctx'}, dimensions={0} | all-to-all | bytes 2359296 | tf_op jit(solution)/shard_map/all_to_all | solution.py:195
  102.3 7.3 attn_fwd.2
  113.4 11.7 %all-gather.6.cloned.1.call-done = bf16[8,768,768]{2,1,0:T(8,128)(2,1)} async-done(((bf16[1,768,768]{2,1,0:T(8,128)(2,1)}), bf16[8,768,768]{2,1,0:T(8,128)(2,1)}) %all-gather.6.cloned.1.call-update) | async-done | bytes 9437200 | tf_op jit(solution)/shard_map/all_gather | solution.py:316
  125.1 8.1 fusion.114
  133.1 63.2 %all-gather.10.cloned.1.call-done = bf16[1536,3840]{1,0:T(8,128)(2,1)} async-done(((bf16[192,3840]{1,0:T(8,128)(2,1)}), bf16[1536,3840]{1,0:T(8,128)(2,1)}) %all-gather.10.cloned.1.call-update) | async-done | bytes 11796496 | tf_op jit(solution)/shard_map/all_gather | solution.py:315
  207.6 32.2 %all_to_all.41.qkv_ref = bf16[4,576,256]{2,1,0:T(8,128)(2,1)S(1)} all-to-all(bf16[4,576,256]{2,1,0:T(8,128)(2,1)S(1)} %bitcast.223), channel_id=1, replica_groups=mesh['section'=2,'ctx'=4,'fsdp'=4] {'ctx'}, dimensions={0} | all-to-all | bytes 2359296 | tf_op jit(solution)/shard_map/all_to_all | solution.py:195
  253.6 7.7 all-to-all-done.3
  276.1 12.9 %all_to_all.42.dout_ref = bf16[4,192,256]{2,1,0:T(8,128)(2,1)S(1)} all-to-all(bf16[4,192,256]{2,1,0:T(8,128)(2,1)S(1)} %bitcast.245), channel_id=1, replica_groups=mesh['section'=2,'ctx'=4,'fsdp'=4] {'ctx'}, dimensions={0} | all-to-all | bytes 786432 | tf_op jit(solution)/shard_map/all_to_all | solution.py:195
  288.9 7.9 attn_bwd.2
  309.0 20.7 %all-to-all-done.5 = bf16[4,576,256]{2,1,0:T(8,128)(2,1)} async-done(((bf16[4,576,256]{2,1,0:T(8,128)(2,1)}), bf16[4,576,256]{2,1,0:T(8,128)(2,1)}, u32[]{:S(2)}, u32[]{:S(2)}) %all-to-all-start.5) | async-done | bytes 1179680 | tf_op jit(solution)/shard_map/all_to_all | solution.py:195
  364.5 7.9 attn_bwd.3
  383.9 13.5 %copy.112 = f32[4,192,2,4,384]{4,3,2,1,0:T(4,128)} copy(f32[4,192,2,4,384]{4,1,2,3,0:T(8,128)} %convolution_bitcast_fusion) | data formatting | bytes 18874368 | tf_op jit(solution)/shard_map/transpose | solution.py:357
  397.4 12.3 %reshape.596 = f32[768,3072]{1,0:T(8,128)} reshape(f32[4,192,2,4,384]{4,3,2,1,0:T(4,128)} %copy.112) | data formatting | bytes 18874368 | tf_op jit(solution)/shard_map/reshape | solution.py:358
  447.8 8.1 %fusion.112 = (f32[768,1536]{1,0:T(8,128)S(1)}, f32[768,1536]{1,0:T(8,128)S(1)}) fusion(f32[768,3072]{1,0:T(8,128)} %fusion.106), kind=kLoop, calls=%fused_computation.248 | loop fusion | bytes 18874368 | tf_op jit(solution)/shard_map/slice | solution.py:391
  470.2 11.1 %add_convert_fusion = bf16[768,3072]{1,0:T(8,128)(2,1)} fusion(bf16[768,3072]{1,0:T(8,128)(2,1)} %collective-permute-done.6, f32[768,1536]{1,0:T(8,128)} %copy-done.2, f32[768,1536]{1,0:T(8,128)} %copy-done.4, f32[768,1536]{1,0:T(8,128)} %copy-done.1, f32[768,1536]{1,0:T(8,128)} %copy-done.3, pred[]{:T(512)S(6)} %eq.4), kind=kLoop, calls=%fused_computation.5 | loop fusion | flops 14155776 | bytes 28311552 | tf_op jit(solution)/shard_map/convert_element_type | solution.py:350
  489.2 13.0 %reshape.594 = f32[4,4,192,2,384]{4,3,2,1,0:T(2,128)} reshape(f32[3072,768]{1,0:T(8,128)} %fusion.107) | data formatting | bytes 18874368 | tf_op jit(solution)/shard_map/reshape | solution.py:357
  502.1 13.5 %copy.129 = f32[4,4,192,2,384]{4,1,3,2,0:T(4,128)} copy(f32[4,4,192,2,384]{4,3,2,1,0:T(2,128)} %reshape.594) | data formatting | bytes 18874368 | tf_op jit(solution)/shard_map/reshape | solution.py:357
  515.6 12.1 %reshape.595 = f32[768,3072]{1,0:T(8,128)} reshape(f32[4,192,2,4,384]{4,3,2,1,0:T(4,128)} %bitcast.212) | data formatting | bytes 18874368 | tf_op jit(solution)/shard_map/reshape | solution.py:358
  527.7 7.6 fusion.105
  542.8 7.9 collective-permute-done.5
  554.6 24.8 %reduce-scatter.11.cloned.1.call-done = bf16[192,3072]{1,0:T(8,128)(2,1)} async-done(((bf16[768,3072]{1,0:T(8,128)(2,1)}), bf16[192,3072]{1,0:T(8,128)(2,1)}) %reduce-scatter.11.cloned.1.call-update) | async-done | bytes 1179664 | tf_op jit(solution)/shard_map/reduce_scatter | solution.py:350
  579.4 60.1 %reduce-scatter.9.cloned.1.call-done = bf16[192,3072]{1,0:T(8,128)(2,1)} async-done(((bf16[768,3072]{1,0:T(8,128)(2,1)}), bf16[192,3072]{1,0:T(8,128)(2,1)}) %reduce-scatter.9.cloned.1.call-update) | async-done | bytes 1179664 | tf_op jit(solution)/shard_map/reduce_scatter | solution.py:350
  650.8 129.4 %all-reduce.6.cloned.1.call-done = (bf16[192,1664]{1,0:T(8,128)(2,1)}, bf16[192,1664]{1,0:T(8,128)(2,1)}, bf16[192,3072]{1,0:T(8,128)(2,1)}, bf16[192,3072]{1,0:T(8,128)(2,1)}) async-done(((bf16[192,1664]{1,0:T(8,128)(2,1)}, bf16[192,1664]{1,0:T(8,128)(2,1)}, bf16[192,3072]{1,0:T(8,128)(2,1)}, bf16[192,3072]{1,0:T(8,128)(2,1)}), (bf16[192,1664]{1,0:T(8,128)(2,1)}, bf16[192,1664]{1,0:T(8,128)(2,1)}, ...) | async-done | bytes 3637264 | tf_op jit(solution)/shard_map/psum | solution.py:351
  (365 shorter events, 217.5 us)
Async XLA Ops:
  7.2 57.1 %all-gather.8.cloned.1.call-start = ((), (), s32[]{:S(2)}) async-start(), calls=%async_computation.17 | async-start | bytes 8404992 | tf_op jit(solution)/shard_map/all_gather | solution.py:314
  11.2 113.9 %all-gather.6.cloned.1.call-start = ((), (), s32[]{:S(2)}) async-start(), calls=%async_computation.12 | async-start | bytes 10616832 | tf_op jit(solution)/shard_map/all_gather | solution.py:316
  11.9 184.5 %all-gather.10.cloned.1.call-start = ((), (), s32[]{:S(2)}) async-start(), calls=%async_computation.18 | async-start | bytes 13271040 | tf_op jit(solution)/shard_map/all_gather | solution.py:315
  13.4 182.9 %copy-start.16 = (bf16[1,1,256,768]{3,2,1,0:T(8,128)(2,1)}, bf16[1,1,256,768]{3,2,1,0:T(8,128)(2,1)S(1)}, u32[]{:S(2)}) copy-start(bf16[1,1,256,768]{3,2,1,0:T(8,128)(2,1)S(1)} %get-tuple-element.109) | copy-start | bytes 1179652
  13.7 423.8 %copy-start.53 = (f32[256]{0:T(256)}, f32[256]{0:T(256)S(1)}, u32[]{:S(2)}) copy-start(f32[256]{0:T(256)S(1)} %add_rsqrt_fusion.3) | copy-start | bytes 3076
  109.5 23.6 %all-to-all-start.1 = ((bf16[4,192,256]{2,1,0:T(8,128)(2,1)}), bf16[4,192,256]{2,1,0:T(8,128)(2,1)S(1)}, u32[]{:S(2)}, u32[]{:S(2)}) async-start(bf16[4,192,256]{2,1,0:T(8,128)(2,1)} %get-tuple-element.17), calls=%async_computation.1 | async-start | bytes 786432 | tf_op jit(solution)/shard_map/all_to_all | solution.py:195
  198.5 148.9 %copy-start.55 = (f32[256]{0:T(256)}, f32[256]{0:T(256)S(1)}, u32[]{:S(2)}) copy-start(f32[256]{0:T(256)S(1)} %add_rsqrt_fusion.2) | copy-start | bytes 3076
  247.1 14.2 %all-to-all-start.3 = ((bf16[4,192,256]{2,1,0:T(8,128)(2,1)}), bf16[4,192,256]{2,1,0:T(8,128)(2,1)}, u32[]{:S(2)}, u32[]{:S(2)}) async-start(bf16[4,192,256]{2,1,0:T(8,128)(2,1)} %get-tuple-element.18), calls=%async_computation.3 | async-start | bytes 786432 | tf_op jit(solution)/shard_map/all_to_all | solution.py:195
  296.8 32.9 %all-to-all-start.5 = ((bf16[4,576,256]{2,1,0:T(8,128)(2,1)}), bf16[4,576,256]{2,1,0:T(8,128)(2,1)}, u32[]{:S(2)}, u32[]{:S(2)}) async-start(bf16[4,576,256]{2,1,0:T(8,128)(2,1)} %attn_bwd.2), calls=%async_computation.5 | async-start | bytes 2359296 | tf_op jit(solution)/shard_map/all_to_all | solution.py:195
  349.9 14.6 %all-to-all-start.6 = ((bf16[4,192,256]{2,1,0:T(8,128)(2,1)}), bf16[4,192,256]{2,1,0:T(8,128)(2,1)S(1)}, u32[]{:S(2)}, u32[]{:S(2)}) async-start(bf16[4,192,256]{2,1,0:T(8,128)(2,1)} %bitcast.244), calls=%async_computation.6 | async-start | bytes 786432 | tf_op jit(solution)/shard_map/all_to_all | solution.py:195
  363.1 68.9 %collective-permute-start.3 = (bf16[768,1664]{1,0:T(8,128)(2,1)}, bf16[768,1664]{1,0:T(8,128)(2,1)}, u32[]{:S(2)}, u32[]{:S(2)}) collective-permute-start(bf16[768,1664]{1,0:T(8,128)(2,1)} %pad_maximum_fusion.9), channel_id=1, source_target_pairs={{0,16},{16,0},{1,17},{17,1},{2,18},{18,2},{3,19},{19,3},{4,20},{20... | collective-permute-start | bytes 7667720 | tf_op jit(solution)/shard_map/ppermute | solution.py:25
  372.4 53.1 %all-to-all-start.7 = ((bf16[4,576,256]{2,1,0:T(8,128)(2,1)}), bf16[4,576,256]{2,1,0:T(8,128)(2,1)S(1)}, u32[]{:S(2)}, u32[]{:S(2)}) async-start(bf16[4,576,256]{2,1,0:T(8,128)(2,1)} %attn_bwd.3), calls=%async_computation.7 | async-start | bytes 2359296 | tf_op jit(solution)/shard_map/all_to_all | solution.py:195
  377.2 177.4 %reduce-scatter.7.cloned.1.call-start = ((), (), s32[]{:S(2)}) async-start(), calls=%async_computation.14 | async-start | bytes 3194880 | tf_op jit(solution)/shard_map/reduce_scatter | solution.py:350
  437.4 117.2 %reduce-scatter.5.cloned.1.call-start = ((), (), s32[]{:S(2)}) async-start(), calls=%async_computation.13 | async-start | bytes 3194880 | tf_op jit(solution)/shard_map/reduce_scatter | solution.py:350
  445.7 20.5 %collective-permute-start.2 = (bf16[768,1664]{1,0:T(8,128)(2,1)}, bf16[768,1664]{1,0:T(8,128)(2,1)}, u32[]{:S(2)}, u32[]{:S(2)}) collective-permute-start(bf16[768,1664]{1,0:T(8,128)(2,1)} %pad_maximum_fusion.8), channel_id=1, source_target_pairs={{0,16},{16,0},{1,17},{17,1},{2,18},{18,2},{3,19},{19,3},{4,20},{20... | collective-permute-start | bytes 7667720 | tf_op jit(solution)/shard_map/ppermute | solution.py:25
  461.1 9.1 %collective-permute-start.6 = (bf16[768,3072]{1,0:T(8,128)(2,1)}, bf16[768,3072]{1,0:T(8,128)(2,1)}, u32[]{:S(2)}, u32[]{:S(2)}) collective-permute-start(bf16[768,3072]{1,0:T(8,128)(2,1)} %select_convert_fusion), channel_id=1, source_target_pairs={{0,16},{16,0},{1,17},{17,1},{2,18},{18,2},{3,19},{19,3},{4,20},{20... | collective-permute-start | bytes 14155784 | tf_op jit(solution)/shard_map/ppermute | solution.py:25
  470.1 109.3 %reduce-scatter.11.cloned.1.call-start = ((), (), s32[]{:S(2)}) async-start(), calls=%async_computation.16 | async-start | bytes 5898240 | tf_op jit(solution)/shard_map/reduce_scatter | solution.py:350
  481.4 158.2 %reduce-scatter.9.cloned.1.call-start = ((), (), s32[]{:S(2)}) async-start(), calls=%async_computation.15 | async-start | bytes 5898240 | tf_op jit(solution)/shard_map/reduce_scatter | solution.py:350
  542.7 8.0 collective-permute-start.5
  554.5 225.6 %all-reduce.6.cloned.1.call-start = ((), (), s32[]{:S(2)}) async-start(), calls=%async_computation.19 | async-start | bytes 7274496 | tf_op jit(solution)/shard_map/psum | solution.py:351
  641.3 8.2 %collective-permute-start.1 = (f32[256,768]{1,0:T(8,128)S(1)}, f32[256,768]{1,0:T(8,128)S(1)}, u32[]{:S(2)}, u32[]{:S(2)}) collective-permute-start(f32[256,768]{1,0:T(8,128)S(1)} %get-tuple-element.106), channel_id=1, source_target_pairs={{0,16},{16,0},{1,17},{17,1},{2,18},{18,2},{3,19},{19,3},{4,20},{20... | collective-permute-start | bytes 2359304 | tf_op jit(solution)/shard_map/ppermute | solution.py:25
  646.4 2.1 collective-permute-start
  782.5 8.4 %collective-permute-start.4 = (bf16[192,1664]{1,0:T(8,128)(2,1)S(1)}, bf16[192,1664]{1,0:T(8,128)(2,1)}, u32[]{:S(2)}, u32[]{:S(2)}) collective-permute-start(bf16[192,1664]{1,0:T(8,128)(2,1)S(1)} %get-tuple-element.133), channel_id=1, source_target_pairs={{0,16},{16,0},{1,17},{17,1},{2,18},{18,2},{3,19},{19,3},{4,20},{20... | collective-permute-start | bytes 1916936 | tf_op jit(solution)/shard_map/ppermute | solution.py:25
  783.4 12.8 %collective-permute-start.7 = (bf16[192,3072]{1,0:T(8,128)(2,1)S(1)}, bf16[192,3072]{1,0:T(8,128)(2,1)}, u32[]{:S(2)}, u32[]{:S(2)}) collective-permute-start(bf16[192,3072]{1,0:T(8,128)(2,1)S(1)} %get-tuple-element.127), channel_id=1, source_target_pairs={{0,16},{16,0},{1,17},{17,1},{2,18},{18,2},{3,19},{19,3},{4,20},{20... | collective-permute-start | bytes 3538952 | tf_op jit(solution)/shard_map/ppermute | solution.py:25
  (77 other events, 1125.9 us)
Sparse Core Ops, SparseCore 0:
  11.3 53.0 all-gather.7
  66.2 58.8 all-gather.5
  127.5 68.7 all-gather.9
  437.5 39.8 reduce-scatter.6
  480.4 38.9 reduce-scatter.4
  522.3 57.0 reduce-scatter.10
  582.4 57.0 reduce-scatter.8
  642.2 137.9 all-reduce.5

commit v2 on v1

v2 whole, which is shorter than its diff:
```python
import functools

import jax
import jax.numpy as jnp
from jax import lax
from jax.experimental import pallas as pl
from jax.experimental.pallas import tpu as pltpu
from jax.sharding import PartitionSpec as P

HEADS = 12
EPS = 1e-05
GELU_C = 0.7978845608
GELU_A = 0.044715
LANES = 128
BF = jnp.bfloat16
F32 = jnp.float32
VMEM = pl.BlockSpec(memory_space=pltpu.VMEM)
SMEM = pl.BlockSpec(memory_space=pltpu.SMEM)
HBM = pl.BlockSpec(memory_space=pl.ANY)
PARAMS = pltpu.CompilerParams(vmem_limit_bytes=56 * 1024 * 1024)
GROUP = ("section", "ctx")
SHARDS = ("fsdp", "section")


def dot(a, b, ca, cb):
    return lax.dot_general(a, b, (((ca,), (cb,)), ((), ())), preferred_element_type=F32)


def shape(dims, dtype):
    return jax.ShapeDtypeStruct(dims, dtype)


def place_of(core, ctx_index):
    return core * lax.axis_size("ctx") + ctx_index


def exchange(pieces):
    ctx, cores = lax.axis_size("ctx"), lax.axis_size("section")
    half = ctx // cores
    moved = [pieces[0]]
    for d in range(1, ctx):
        pairs = []
        for base in range(cores):
            for g in range(ctx):
                t = (g + d) % ctx
                pairs.append(
                    (
                        place_of(g // half, base * half + g % half),
                        place_of(t // half, base * half + t % half),
                    )
                )
        moved.append(lax.ppermute(pieces[d], GROUP, pairs))
    return moved


def bring_rows(both, core, base):
    ctx, cores = lax.axis_size("ctx"), lax.axis_size("section")
    half = ctx // cores
    pairs = [
        (place_of(c, c * half + i), place_of(c, (1 - c) * half + i))
        for c in range(cores)
        for i in range(half)
    ]
    received = lax.ppermute(jnp.where(core == 0, both[1], both[0]), GROUP, pairs)
    own = jnp.where(core == 0, both[0], both[1])
    return jnp.where(core == base, own, received)


def return_rows(value, layer):
    ctx, cores = lax.axis_size("ctx"), lax.axis_size("section")
    half = ctx // cores
    return [
        lax.ppermute(
            value,
            GROUP,
            [(place_of(z // half, m * half + z % half), place_of(layer, z)) for z in range(ctx)],
        )
        for m in range(cores)
    ]


def normalised(values):
    centred = values - jnp.mean(values, axis=-1, keepdims=True)
    scale = lax.rsqrt(jnp.mean(centred * centred, axis=-1, keepdims=True) + EPS)
    return centred * scale, scale


def norm_back(unit, scale, upstream, gain):
    w = upstream * gain
    return (
        w - jnp.mean(w, axis=-1, keepdims=True) - unit * jnp.mean(w * unit, axis=-1, keepdims=True)
    ) * scale


def qkv_kernel(ids_ref, x_ref, vec_ref, pack_ref, *refs, parts, size):
    outs, (weight, whole, sem) = refs[:parts], refs[parts:]
    width = x_ref.shape[1]
    copy = pltpu.make_async_copy(pack_ref.at[:, : 3 * width], weight, sem.at[0])
    copy.start()
    unit, _ = normalised(x_ref[...].astype(F32))
    normed = (unit * vec_ref[0:1] + vec_ref[2:3]).astype(BF)
    copy.wait()
    held = outs[0].shape[0] // 3
    if parts * held != width:
        whole[...] = jnp.zeros_like(whole)
    for b in range(3):
        block = dot(normed, weight[:, b * width : (b + 1) * width], 1, 0)
        if b == 0:
            block = block + vec_ref[3:4]
        if b == 2:
            block = block + vec_ref[4:5]
        whole[b * parts * held : b * parts * held + width] = block.T.astype(BF)
    for d in range(parts):
        for b in range(3):
            first = pl.multiple_of(b * parts * held + ids_ref[d] * held, size)
            outs[d][b * held : (b + 1) * held] = whole[pl.ds(first, held)]


def qkv_project(ids, x, vec, pack, parts, size):
    rows, width = x.shape
    held = pl.cdiv(HEADS, parts) * size
    return pl.pallas_call(
        functools.partial(qkv_kernel, parts=parts, size=size),
        in_specs=[SMEM, VMEM, VMEM, HBM],
        out_specs=[VMEM] * parts,
        out_shape=[shape((3 * held, rows), BF)] * parts,
        scratch_shapes=[
            pltpu.VMEM((width, 3 * width), BF),
            pltpu.VMEM((3 * parts * held, rows), BF),
            pltpu.SemaphoreType.DMA((1,)),
        ],
        compiler_params=PARAMS,
        name="qkv_project",
    )(ids, x, vec, pack)


def spans_of(order_ref, which, count, span):
    first = order_ref[which]
    return (
        (0, pl.multiple_of(first * span, span)),
        (1, pl.multiple_of((2 * count - 1 - first) * span, span)),
    )


def causal(scores, width, fill):
    depth = scores.shape[0]
    keys = lax.broadcasted_iota(jnp.int32, (width, width), 0)
    rows = lax.broadcasted_iota(jnp.int32, (width, width), 1)
    last = jnp.where(keys <= rows, scores[depth - width :], fill)
    if depth == width:
        return last
    return jnp.concatenate([scores[: depth - width], last], axis=0)


def sort_in(order_ref, pieces, target):
    count = len(pieces)
    span = pieces[0].shape[1] // 2
    for d in range(count):
        for side, place in spans_of(order_ref, d, count, span):
            target[:, pl.ds(place, span)] = pieces[d][:, side * span : (side + 1) * span]


def sort_out(order_ref, source, pieces):
    count = len(pieces)
    span = pieces[0].shape[1] // 2
    for d in range(count):
        for side, place in spans_of(order_ref, count + d, count, span):
            pieces[d][:, side * span : (side + 1) * span] = source[:, pl.ds(place, span)]


def attn_fwd_kernel(order_ref, *refs, parts, heads, size, block):
    pieces, mixed, (sorted_ref, out_ref, lse_ref) = refs[:parts], refs[parts : 2 * parts], refs[2 * parts :]
    feats = heads * size
    seq = sorted_ref.shape[1]
    sort_in(order_ref, pieces, sorted_ref)
    lse_ref[...] = jnp.zeros_like(lse_ref)
    for h in range(heads):
        for start in range(0, seq, block):
            end = start + block
            q = sorted_ref[h * size : (h + 1) * size, start:end]
            k = sorted_ref[feats + h * size : feats + (h + 1) * size, :end]
            v = sorted_ref[2 * feats + h * size : 2 * feats + (h + 1) * size, :end]
            scores = causal(dot(k, q, 0, 0) * 0.125, block, -1e30)
            top = jnp.max(scores, axis=0, keepdims=True)
            weights = jnp.exp(scores - top)
            total = jnp.sum(weights, axis=0, keepdims=True)
            mixed_part = dot(v, weights.astype(BF), 1, 0) / total
            out_ref[h * size : (h + 1) * size, start:end] = mixed_part.astype(BF)
            lse_ref[h : h + 1, start:end] = top + jnp.log(total)
    sort_out(order_ref, out_ref, mixed)


def attn_bwd_kernel(order_ref, *refs, parts, heads, size, block):
    pieces, (sorted_ref, out_ref, lse_ref) = refs[:parts], refs[parts : parts + 3]
    grads, (dsort, gsort, gk, gv) = refs[parts + 3 : 2 * parts + 3], refs[2 * parts + 3 :]
    feats = heads * size
    seq = sorted_ref.shape[1]
    sort_in(order_ref, pieces, dsort)
    for h in range(heads):
        own = slice(h * size, (h + 1) * size)
        gk[...] = jnp.zeros_like(gk)
        gv[...] = jnp.zeros_like(gv)
        for start in range(0, seq, block):
            end = start + block
            q = sorted_ref[own, start:end]
            k = sorted_ref[feats + h * size : feats + (h + 1) * size, :end]
            v = sorted_ref[2 * feats + h * size : 2 * feats + (h + 1) * size, :end]
            dout = dsort[own, start:end]
            delta = jnp.sum(
                dout.astype(F32) * out_ref[own, start:end].astype(F32), axis=0, keepdims=True
            )
            scores = dot(k, q, 0, 0) * 0.125 - lse_ref[h : h + 1, start:end]
            probs = jnp.exp(causal(scores, block, -1e30))
            dprobs = dot(v, dout, 0, 0)
            dscores = (probs * (dprobs - delta)).astype(BF)
            gsort[own, start:end] = (dot(k, dscores, 1, 0) * 0.125).astype(BF)
            gk[:, :end] += dot(q, dscores, 1, 1)
            gv[:, :end] += dot(dout, probs.astype(BF), 1, 1)
        gsort[feats + h * size : feats + (h + 1) * size, :] = (gk[...] * 0.125).astype(BF)
        gsort[2 * feats + h * size : 2 * feats + (h + 1) * size, :] = gv[...].astype(BF)
    sort_out(order_ref, gsort, grads)


def widen(pieces, order):
    count = len(pieces)
    span = pieces[0].shape[1] // 2
    came = order[:count]
    holder = jnp.stack([came, 2 * count - 1 - came], axis=1).reshape(-1)
    place = jnp.argsort(holder)
    flat = jnp.concatenate(pieces, axis=1).reshape(-1, 2 * count, span)
    return [jnp.take(flat, place, axis=1).reshape(flat.shape[0], -1)]


def narrow(wide, order, count):
    feats, seq = wide.shape
    span = seq // (2 * count)
    goes = order[count:]
    holder = jnp.stack([goes, 2 * count - 1 - goes], axis=1).reshape(-1)
    flat = jnp.take(wide.reshape(feats, 2 * count, span), holder, axis=1)
    flat = flat.reshape(feats, count, 2 * span)
    return [flat[:, d] for d in range(count)]


def attention_forward(pieces, order, size):
    parts, rows = len(pieces), pieces[0].shape[1]
    seq = parts * rows
    heads = pieces[0].shape[0] // (3 * size)
    narrow_spans = (rows // 2) % LANES != 0
    ids, given = order, parts
    if narrow_spans:
        pieces, ids, given = widen(pieces, order), jnp.zeros((2,), jnp.int32), 1
    results = pl.pallas_call(
        functools.partial(
            attn_fwd_kernel, parts=given, heads=heads, size=size, block=min(256, seq // 2)
        ),
        in_specs=[SMEM] + [VMEM] * given,
        out_specs=[VMEM] * (given + 3),
        out_shape=[shape((heads * size, pieces[0].shape[1]), BF)] * given
        + [
            shape((3 * heads * size, seq), BF),
            shape((heads * size, seq), BF),
            shape((8 * pl.cdiv(heads, 8), seq), F32),
        ],
        compiler_params=PARAMS,
        name="attn_fwd",
    )(ids, *pieces)
    mixed = results[:given]
    if narrow_spans:
        mixed = narrow(mixed[0], order, parts)
    return mixed, tuple(results[given:])


def attention_backward(pieces, saved, order, size):
    parts, rows = len(pieces), pieces[0].shape[1]
    seq = parts * rows
    heads = pieces[0].shape[0] // size
    narrow_spans = (rows // 2) % LANES != 0
    ids, given = order, parts
    if narrow_spans:
        pieces, ids, given = widen(pieces, order), jnp.zeros((2,), jnp.int32), 1
    grads = pl.pallas_call(
        functools.partial(
            attn_bwd_kernel, parts=given, heads=heads, size=size, block=min(256, seq // 2)
        ),
        in_specs=[SMEM] + [VMEM] * (given + 3),
        out_specs=[VMEM] * given,
        out_shape=[shape((3 * heads * size, pieces[0].shape[1]), BF)] * given,
        scratch_shapes=[
            pltpu.VMEM((heads * size, seq), BF),
            pltpu.VMEM((3 * heads * size, seq), BF),
            pltpu.VMEM((size, seq), F32),
            pltpu.VMEM((size, seq), F32),
        ],
        compiler_params=PARAMS,
        name="attn_bwd",
    )(ids, *pieces, *saved)
    if narrow_spans:
        grads = narrow(grads[0], order, parts)
    return grads


def down_blocks(shards, ratio, depth):
    width = shards * depth
    for f in range(shards):
        for j in range(ratio):
            first = (f * ratio + j) * depth
            yield slice(first, first + depth), slice(f * depth, (f + 1) * depth), j * width


def rest_copies(pack, w_out, w_up, w_down, sems, shards, ratio):
    width = w_out.shape[0]
    depth = width // shards
    hidden = w_up.shape[1]
    out = [pltpu.make_async_copy(pack.at[:, :width], w_out, sems.at[0])]
    up = [pltpu.make_async_copy(pack.at[:, width : width + hidden], w_up, sems.at[1])]
    down = []
    for i, (rows, packed, column) in enumerate(down_blocks(shards, ratio, depth)):
        start = width + hidden + column
        down.append(
            pltpu.make_async_copy(
                pack.at[packed, start : start + width], w_down.at[rows], sems.at[2 + i]
            )
        )
    return out, up, down


def put_pieces(ids_ref, first, pieces, target):
    held = pieces[0].shape[0]
    for d, piece in enumerate(pieces):
        place = pl.multiple_of(ids_ref[first + d] * held, held)
        target[pl.ds(place, held)] = piece[...]


def mlp_kernel(ids_ref, x_ref, vec_ref, bias_ref, pack_ref, *refs, parts, shards, ratio):
    pieces = refs[:parts]
    result_ref, inner_ref, hidden_ref, mixed_ref = refs[parts : parts + 4]
    w_out, w_up, w_down, whole, sems = refs[parts + 4 :]
    width = x_ref.shape[1]
    out, up, down = rest_copies(pack_ref, w_out, w_up, w_down, sems, shards, ratio)
    for copy in out + up + down:
        copy.start()
    put_pieces(ids_ref, parts, pieces, whole)
    mixed_ref[...] = whole[:width]
    out[0].wait()
    inner = x_ref[...].astype(F32) + dot(whole[:width], w_out[...], 0, 0) + vec_ref[5:6]
    inner_ref[...] = inner
    unit, _ = normalised(inner)
    middle = (unit * vec_ref[1:2] + vec_ref[6:7]).astype(BF)
    up[0].wait()
    for copy in down:
        copy.wait()
    total = inner + vec_ref[7:8]
    for start in range(0, w_up.shape[1], width):
        cols = slice(start, start + width)
        hidden = dot(middle, w_up[:, cols], 1, 0) + bias_ref[:, cols]
        hidden_ref[:, cols] = hidden
        act = 0.5 * hidden * (1.0 + jnp.tanh(GELU_C * (hidden + GELU_A * hidden * hidden * hidden)))
        total = total + dot(act.astype(BF), w_down[cols], 1, 0)
    result_ref[...] = total.astype(BF)


def rest_scratch(width, hidden, shards, ratio):
    return [
        pltpu.VMEM((width, width), BF),
        pltpu.VMEM((width, hidden), BF),
        pltpu.VMEM((hidden, width), BF),
    ]


def mlp_forward(ids, x, vec, bias, pack, pieces, shards, ratio):
    parts = len(pieces)
    rows, width = x.shape
    hidden = ratio * width
    return pl.pallas_call(
        functools.partial(mlp_kernel, parts=parts, shards=shards, ratio=ratio),
        in_specs=[SMEM, VMEM, VMEM, VMEM, HBM] + [VMEM] * parts,
        out_specs=[VMEM] * 4,
        out_shape=[
            shape((rows, width), BF),
            shape((rows, width), F32),
            shape((rows, hidden), F32),
            shape((width, rows), BF),
        ],
        scratch_shapes=rest_scratch(width, hidden, shards, ratio)
        + [
            pltpu.VMEM((parts * pieces[0].shape[0], rows), BF),
            pltpu.SemaphoreType.DMA((2 + shards * ratio,)),
        ],
        compiler_params=PARAMS,
        name="mlp_forward",
    )(ids, x, vec, bias, pack, *pieces)


def mlp_back_kernel(
    ids_ref, grad_ref, inner_ref, hidden_ref, vec_ref, pack_ref, *refs, parts, shards, ratio
):
    outs = refs[:parts]
    ginner_ref, gattn_ref, ghid_ref, act_ref, middle_ref, small_ref, sbias_ref = refs[
        parts : parts + 7
    ]
    w_out, w_up, w_down, whole, sems = refs[parts + 7 :]
    width = grad_ref.shape[1]
    out, up, down = rest_copies(pack_ref, w_out, w_up, w_down, sems, shards, ratio)
    for copy in down + up + out:
        copy.start()
    grad_low = grad_ref[...].astype(BF)
    unit, scale = normalised(inner_ref[...])
    middle_ref[...] = (unit * vec_ref[1:2] + vec_ref[6:7]).astype(BF)
    for copy in down:
        copy.wait()
    up[0].wait()
    up_mid = jnp.zeros(unit.shape, F32)
    for start in range(0, w_up.shape[1], width):
        cols = slice(start, start + width)
        hidden = hidden_ref[:, cols]
        th = jnp.tanh(GELU_C * (hidden + GELU_A * hidden * hidden * hidden))
        act_ref[:, cols] = (0.5 * hidden * (1.0 + th)).astype(BF)
        slope = 0.5 * (1.0 + th) + 0.5 * hidden * (1.0 - th * th) * GELU_C * (
            1.0 + 3.0 * GELU_A * hidden * hidden
        )
        grad_hid = (dot(grad_low, w_down[cols], 1, 1) * slope).astype(BF)
        ghid_ref[:, cols] = grad_hid
        sbias_ref[:, cols] = jnp.sum(grad_hid.astype(F32), axis=0, keepdims=True)
        up_mid = up_mid + dot(grad_hid, w_up[:, cols], 1, 1)
    grad_inner = grad_ref[...].astype(F32) + norm_back(unit, scale, up_mid, vec_ref[1:2])
    ginner_ref[...] = grad_inner
    grad_attn = grad_inner.astype(BF)
    gattn_ref[...] = grad_attn
    out[0].wait()
    held = outs[0].shape[0]
    if parts * held != width:
        whole[...] = jnp.zeros_like(whole)
    whole[:width] = dot(w_out[...], grad_attn, 1, 1).astype(BF)
    for d in range(parts):
        outs[d][...] = whole[pl.ds(pl.multiple_of(ids_ref[d] * held, held), held)]
    small_ref[...] = jnp.concatenate(
        [
            jnp.sum(up_mid * unit, axis=0, keepdims=True),
            jnp.sum(grad_attn.astype(F32), axis=0, keepdims=True),
            jnp.sum(up_mid, axis=0, keepdims=True),
            jnp.sum(grad_low.astype(F32), axis=0, keepdims=True),
            jnp.zeros((4, width), F32),
        ],
        axis=0,
    )


def mlp_backward(ids, grad, inner, hidden, vec, pack, parts, size, shards, ratio):
    rows, width = inner.shape
    held = pl.cdiv(HEADS, parts) * size
    wide = ratio * width
    results = pl.pallas_call(
        functools.partial(mlp_back_kernel, parts=parts, shards=shards, ratio=ratio),
        in_specs=[SMEM, VMEM, VMEM, VMEM, VMEM, HBM],
        out_specs=[VMEM] * (parts + 7),
        out_shape=[shape((held, rows), BF)] * parts
        + [
            shape((rows, width), F32),
            shape((rows, width), BF),
            shape((rows, wide), BF),
            shape((rows, wide), BF),
            shape((rows, width), BF),
            shape((8, width), F32),
            shape((1, wide), F32),
        ],
        scratch_shapes=rest_scratch(width, wide, shards, ratio)
        + [
            pltpu.VMEM((parts * held, rows), BF),
            pltpu.SemaphoreType.DMA((2 + shards * ratio,)),
        ],
        compiler_params=PARAMS,
        name="mlp_backward",
    )(ids, grad, inner, hidden, vec, pack)
    return results[:parts], results[parts:]


def early_kernel(
    middle_ref, ghid_ref, act_ref, glow_ref, mixed_ref, gattn_ref, pack_ref, scratch, sems, *, shards, ratio
):
    width = middle_ref.shape[1]
    depth = width // shards
    hidden = ratio * width
    copies = []
    glow = glow_ref[...].astype(BF)

    def send(columns, i):
        copy = pltpu.make_async_copy(scratch.at[:, columns], pack_ref.at[:, columns], sems.at[i])
        copy.start()
        copies.append(copy)

    scratch[:, :width] = dot(mixed_ref[...], gattn_ref[...], 1, 0).astype(BF)
    send(slice(0, width), 0)
    for i in range(ratio):
        cols = slice(i * width, (i + 1) * width)
        block = dot(middle_ref[...], ghid_ref[:, cols], 0, 0).astype(BF)
        scratch[:, (i + 1) * width : (i + 2) * width] = block
        send(slice((i + 1) * width, (i + 2) * width), 1 + i)
    for f in range(shards):
        block = dot(act_ref[:, f * ratio * depth : (f + 1) * ratio * depth], glow, 0, 0).astype(BF)
        for j in range(ratio):
            start = width + hidden + j * width
            scratch[f * depth : (f + 1) * depth, start : start + width] = block[
                j * depth : (j + 1) * depth
            ]
    send(slice(width + hidden, width + 2 * hidden), 1 + ratio)
    for copy in copies:
        copy.wait()


def early_grads(middle, ghid, act, glow, mixed, gattn, shards, ratio):
    width = middle.shape[1]
    total = width * (1 + 2 * ratio)
    return pl.pallas_call(
        functools.partial(early_kernel, shards=shards, ratio=ratio),
        in_specs=[VMEM] * 6,
        out_specs=HBM,
        out_shape=shape((width, total), BF),
        scratch_shapes=[
            pltpu.VMEM((width, total), BF),
            pltpu.SemaphoreType.DMA((2 + ratio,)),
        ],
        compiler_params=PARAMS,
        name="early_grads",
    )(middle, ghid, act, glow, mixed, gattn)


def qkv_back_kernel(
    ids_ref, x_ref, ginner_ref, vec_ref, pack_ref, *refs, parts
):
    pieces = refs[:parts]
    gx_ref, small_ref, whole_ref = refs[parts : parts + 3]
    weight, whole, sem = refs[parts + 3 :]
    width = x_ref.shape[1]
    copy = pltpu.make_async_copy(pack_ref.at[:, : 3 * width], weight, sem.at[0])
    copy.start()
    held = pieces[0].shape[0] // 3
    for d, piece in enumerate(pieces):
        for b in range(3):
            place = pl.multiple_of(b * parts * held + ids_ref[parts + d] * held, held)
            whole[pl.ds(place, held)] = piece[b * held : (b + 1) * held]
    for b in range(3):
        whole_ref[b * width : (b + 1) * width] = whole[b * parts * held : b * parts * held + width]
    unit, scale = normalised(x_ref[...].astype(F32))
    copy.wait()
    up_norm = dot(weight[...], whole_ref[...], 1, 0).T
    gx_ref[...] = ginner_ref[...] + norm_back(unit, scale, up_norm, vec_ref[0:1])
    small_ref[...] = jnp.concatenate(
        [
            jnp.sum(up_norm * unit, axis=0, keepdims=True),
            jnp.sum(up_norm, axis=0, keepdims=True),
            jnp.zeros((6, width), F32),
        ],
        axis=0,
    )


def qkv_backward(ids, x, ginner, vec, pack, pieces):
    parts = len(pieces)
    rows, width = x.shape
    return pl.pallas_call(
        functools.partial(qkv_back_kernel, parts=parts),
        in_specs=[SMEM, VMEM, VMEM, VMEM, HBM] + [VMEM] * parts,
        out_specs=[VMEM] * 3,
        out_shape=[shape((rows, width), F32), shape((8, width), F32), shape((3 * width, rows), BF)],
        scratch_shapes=[
            pltpu.VMEM((width, 3 * width), BF),
            pltpu.VMEM((parts * pieces[0].shape[0], rows), BF),
            pltpu.SemaphoreType.DMA((1,)),
        ],
        compiler_params=PARAMS,
        name="qkv_backward",
    )(ids, x, ginner, vec, pack, *pieces)


def late_kernel(x_ref, vec_ref, grad_ref, small_ref, pack_ref, scratch, sems):
    width = x_ref.shape[1]
    copies = []
    unit, _ = normalised(x_ref[...].astype(F32))
    normed = (unit * vec_ref[0:1] + vec_ref[2:3]).T.astype(BF)
    for b in range(3):
        cols = slice(b * width, (b + 1) * width)
        rows = grad_ref[cols]
        scratch[:, cols] = dot(normed, rows, 1, 1).astype(BF)
        copy = pltpu.make_async_copy(scratch.at[:, cols], pack_ref.at[:, cols], sems.at[b])
        copy.start()
        copies.append(copy)
    last = slice(3 * width, 3 * width + LANES)
    scratch[:, last] = small_ref[...].astype(BF)
    copy = pltpu.make_async_copy(scratch.at[:, last], pack_ref.at[:, last], sems.at[3])
    copy.start()
    copies.append(copy)
    for copy in copies:
        copy.wait()


def late_grads(x, vec, grad_qkv, small):
    width = x.shape[1]
    return pl.pallas_call(
        late_kernel,
        in_specs=[VMEM] * 4,
        out_specs=HBM,
        out_shape=shape((width, 3 * width + LANES), BF),
        scratch_shapes=[
            pltpu.VMEM((width, 3 * width + LANES), BF),
            pltpu.SemaphoreType.DMA((4,)),
        ],
        compiler_params=PARAMS,
        name="late_grads",
    )(x, vec, grad_qkv, small)


def layer_forward(x, packs, vec, bias, ids, order, parts, size, shards, ratio):
    sent = qkv_project(ids, x, vec, packs[0], parts, size)
    mixed, attn_saved = attention_forward(exchange(sent), order, size)
    result, inner, hidden, mixed = mlp_forward(
        ids, x, vec, bias, packs[1], exchange(mixed), shards, ratio
    )
    return result, (x, attn_saved, inner, hidden, mixed)


def layer_backward(saved, grad, packs, vec, ids, order, parts, size, shards, ratio):
    x, attn_saved, inner, hidden, mixed = saved
    width = x.shape[1]
    depth = width // shards
    sent, (ginner, gattn, ghid, act, middle, small, sbias) = mlp_backward(
        ids, grad, inner, hidden, vec, packs[1], parts, size, shards, ratio
    )
    early = early_grads(middle, ghid, act, grad, mixed, gattn, shards, ratio)
    received = exchange(sent)
    *received, early = lax.optimization_barrier((*received, early))
    reduced = lax.psum_scatter(early, SHARDS, scatter_dimension=0, tiled=True)
    sent = attention_backward(received, attn_saved, order, size)
    grad_x, small2, grad_qkv = qkv_backward(ids, x, ginner, vec, packs[0], exchange(sent))
    sums = jnp.sum(grad_qkv.reshape(3, width, -1).astype(F32), axis=2)
    table = jnp.concatenate(
        [
            jnp.stack([small2[0], small[0], small2[1], sums[0], sums[2], small[1], small[2], small[3]]),
            sbias.reshape(shards, ratio, depth).transpose(1, 0, 2).reshape(ratio, width),
        ]
    )
    table = jnp.pad(table, ((0, LANES - table.shape[0]), (0, 0))).T
    late = late_grads(x, vec, grad_qkv, table)
    return grad_x, reduced, late


def blocks_to_columns(value, parts):
    depth = value.shape[0] // parts
    return [value[i * depth : (i + 1) * depth] for i in range(parts)]


def split_layers(pack, core):
    rows = pack.shape[0] // 2
    first, second = pack[:rows], pack[rows:]
    other = lax.ppermute(jnp.where(core == 0, second, first), "section", [(0, 1), (1, 0)])
    return jnp.where(core == 0, first, other), jnp.where(core == 0, other, second)


def gather(part):
    return lax.all_gather(part, SHARDS, axis=0, tiled=True)


def sum_over_ctx(value):
    count = lax.axis_size("ctx")
    index = lax.axis_index("ctx")
    rows = value.shape[0] // count
    pieces = value.reshape(count, rows, -1)

    def turned(d):
        return [(i, (i + d) % count) for i in range(count)]

    total = lax.dynamic_index_in_dim(pieces, index, 0, keepdims=False).astype(F32)
    for d in range(1, count):
        piece = lax.dynamic_index_in_dim(pieces, (index + d) % count, 0, keepdims=False)
        total = total + lax.ppermute(piece, "ctx", turned(d)).astype(F32)
    total = total.astype(BF)
    came = [lax.ppermute(total, "ctx", turned(d)) for d in range(count - 1, 0, -1)] + [total]
    ring = jnp.stack(came + came)
    start = (2 * count - 1 - index) % count
    return lax.dynamic_slice_in_dim(ring, start, count, 0).reshape(value.shape)


def body(
    tokens, cotangent, span_order, w_qkv, w_out, w_up, w_down, norm_gains, bias_rows, bias_hidden
):
    core = lax.axis_index("section")
    ctx = lax.axis_size("ctx")
    cores = lax.axis_size("section")
    shards = lax.axis_size("fsdp")
    half = ctx // cores
    base = lax.axis_index("ctx") // half
    member = core * half + lax.axis_index("ctx") % half
    depth = w_qkv.shape[1]
    width = depth * shards
    ratio = bias_hidden.shape[1] // depth
    size = width // HEADS
    gain_count, shift_count = norm_gains.shape[1], bias_rows.shape[1]

    steps = jnp.arange(ctx, dtype=jnp.int32)
    came, goes = (member - steps) % ctx, (member + steps) % ctx
    ids = jnp.concatenate([goes, came]).astype(jnp.int32)
    order = jnp.concatenate([span_order[came], span_order[goes]])

    small = jnp.concatenate([norm_gains[0], bias_rows[0], bias_hidden[0].reshape(ratio, depth)]).T
    small = jnp.pad(small, ((0, 0), (0, LANES - small.shape[1])))
    first = jnp.concatenate([w_qkv[0], small], axis=1)
    rest = jnp.concatenate([w_out[0], w_up[0]] + blocks_to_columns(w_down[0], ratio), axis=1)
    first0, first1 = split_layers(first, core)
    x = bring_rows(tokens[:, 0], core, base)
    rest0, rest1 = split_layers(rest, core)
    packs = []
    for a, b in ((first0, rest0), (first1, rest1)):
        packs.append((gather(a), gather(b)))
    vecs, biases = [], []
    for a, _ in packs:
        table = a[:, 3 * width :].T.astype(F32)
        vecs.append(table[:16])
        hidden = table[gain_count + shift_count : gain_count + shift_count + ratio]
        biases.append(hidden.reshape(ratio, shards, depth).transpose(1, 0, 2).reshape(1, -1))

    out0, saved0 = layer_forward(
        x, packs[0], vecs[0], biases[0], ids, order, ctx, size, shards, ratio
    )
    out1, saved1 = layer_forward(
        out0, packs[1], vecs[1], biases[1], ids, order, ctx, size, shards, ratio
    )
    cot = bring_rows(cotangent[:, 0], core, base)
    grad1, early1, late1 = layer_backward(
        saved1, cot, packs[1], vecs[1], ids, order, ctx, size, shards, ratio
    )
    late1 = lax.psum_scatter(late1, SHARDS, scatter_dimension=0, tiled=True)
    grad1_low = grad1.astype(BF)
    grad0, early0, late0 = layer_backward(
        saved0, grad1_low, packs[0], vecs[0], ids, order, ctx, size, shards, ratio
    )
    late0 = lax.psum_scatter(late0, SHARDS, scatter_dimension=0, tiled=True)

    def own_layer(value0, value1):
        return [
            jnp.where(core == 0, a, b)
            for a, b in zip(return_rows(value0, 0), return_rows(value1, 1))
        ]

    layer_outputs = jnp.stack(own_layer(out0, out1))
    input_grads = jnp.stack(own_layer(grad0.astype(BF), grad1_low)).astype(F32)

    def joined(part0, part1):
        part0, part1 = sum_over_ctx(part0), sum_over_ctx(part1)
        other = jnp.where(
            core == 0,
            lax.ppermute(part0, "section", [(1, 0)]),
            lax.ppermute(part1, "section", [(0, 1)]),
        )
        own = jnp.where(core == 0, part0, part1)
        return jnp.where(
            core == 0, jnp.concatenate([own, other]), jnp.concatenate([other, own])
        ).astype(F32)

    early = joined(early0, early1)
    late = joined(late0, late1)
    down = early[:, width * (1 + ratio) :]
    table = late[:, 3 * width :].T
    return (
        layer_outputs[None, :, None],
        input_grads[None, :, None],
        late[None, :, : 3 * width],
        early[None, :, :width],
        early[None, :, width : width * (1 + ratio)],
        jnp.concatenate([down[:, j * width : (j + 1) * width] for j in range(ratio)])[None],
        table[None, :gain_count],
        table[None, gain_count : gain_count + shift_count],
        table[gain_count + shift_count : gain_count + shift_count + ratio].reshape(1, -1),
    )


def solution(mesh):
    return jax.shard_map(
        body,
        mesh=mesh,
        in_specs=(
            P(None, "fsdp", "ctx", None),
            P(None, "fsdp", "ctx", None),
            P(),
            P("section", "fsdp", None),
            P("section", "fsdp", None),
            P("section", "fsdp", None),
            P("section", "fsdp", None),
            P("section", None, "fsdp"),
            P("section", None, "fsdp"),
            P("section", "fsdp"),
        ),
        out_specs=(
            P("section", None, "fsdp", "ctx", None),
            P("section", None, "fsdp", "ctx", None),
            P("section", "fsdp", None),
            P("section", "fsdp", None),
            P("section", "fsdp", None),
            P("section", "fsdp", None),
            P("section", None, "fsdp"),
            P("section", None, "fsdp"),
            P("section", "fsdp"),
        ),
        check_vma=False,
    )
```

time: 817 us -> 670 us (0.82)
  local copies, waits for them, and re-layouts: 133 us -> 30 us
  Pallas kernels: 30.3 us -> 127 us
  matrix products: 80.1 us -> 0 us
  blocking collectives: 77.3 us -> 0 us
  starting transfers between devices: 26.4 us -> 103 us
  other arithmetic: 67.9 us -> 24.6 us
  waiting for transfers between devices: 378 us -> 362 us
    ppermute x8 -> x64, waiting for transfers between devices: 9.26 us -> 169 us  [the longest x12 50.7 us: sum_over_ctx(): total = total + lax.ppermute(piece, 'ctx', turned(d)).astype(F32)]
    psum x1 -> x0, waiting for transfers between devices: 129 us -> none  [reduce_pack(): return lax.psum(part, 'ctx')]
    ppermute x8 -> x64, starting transfers between devices: 4.76 us -> 103 us  [the longest x12 28.6 us: sum_over_ctx(): lax.ppermute(total, 'ctx', turned(d))]
    pallas_call x4 -> x16, Pallas kernels: 30.3 us -> 127 us  [the longest x2 26.3 us: mlp_backward(): pl.pallas_call(functools.partial(mlp_back_kernel, parts=parts, shards=sha...]
    dot_general x24 -> x0, matrix products: 80.1 us -> none  [dot(): lax.dot_general(a, b, (((ca,), (cb,)), ((), ())), preferred_element_type=...]
    all_to_all x3 -> x0, blocking collectives: 77.3 us -> none  [exchange(): return lax.all_to_all(value, 'ctx', split_axis=0, concat_axis=0, tiled=True)]
    reshape x14 -> x8, local copies, waits for them, and re-layouts: 52.8 us -> 1.89 us  [the longest x4 1.56 us: body(): hidden.reshape(ratio, shards, depth).transpose(1, 0, 2).reshape(1, -1)]
    convert_element_type x13 -> x11, other arithmetic: 36.4 us -> 7.16 us  [the longest x4 4.27 us: sum_over_ctx(): total = total.astype(BF)]
  transfers between devices with their start and end apart: 21 -> 72, of which waited for: 10 -> 34; matrix products, arithmetic and copies ran while one was open for 25% -> 5% of each run, Pallas kernels for 2% -> 13%
where the time goes in v2:
time: 670 us; the launch traced here: 662 us
  waiting for transfers between devices  362 us (54%)
  Pallas kernels  127 us (19%)
  starting transfers between devices  103 us (15%)
  local copies, waits for them, and re-layouts  30 us (4%)
  other arithmetic  24.6 us (4%)
  between operations  15.7 us (2%)
    all_gather x4, waiting for transfers between devices, gather(): return lax.all_gather(part, SHARDS, axis=0, tiled=True)  108 us
    reduce_scatter x2, waiting for transfers between devices, layer_backward(): reduced = lax.psum_scatter(early, SHARDS, scatter_dimension=0, tiled=True)  82.4 us
    ppermute x12, waiting for transfers between devices, sum_over_ctx(): total = total + lax.ppermute(piece, 'ctx', turned(d)).astype(F32)  50.7 us
    ppermute x12, waiting for transfers between devices, sum_over_ctx(): lax.ppermute(total, 'ctx', turned(d))  42.5 us
    ppermute x24, waiting for transfers between devices, exchange(): moved.append(lax.ppermute(pieces[d], GROUP, pairs))  40.8 us
    ppermute x12, starting transfers between devices, sum_over_ctx(): lax.ppermute(total, 'ctx', turned(d))  28.6 us
    ppermute x12, starting transfers between devices, sum_over_ctx(): total = total + lax.ppermute(piece, 'ctx', turned(d)).astype(F32)  26.8 us
    pallas_call x2, Pallas kernels, mlp_backward(): pl.pallas_call(functools.partial(mlp_back_kernel, parts=parts, shards=sha...  26.3 us
  transfers between devices with their start and end apart: 72, of which 34 were waited for; matrix products, arithmetic and copies ran while one was open for 5% of the time, Pallas kernels for 13%

profile of v2, /device:TPU:1, one launch (start us, length us, event | category | flops | bytes accessed | tf_op | source)
XLA Modules:
  0.0 661.9 jit_solution(6189758650751903389)
XLA Ops:
  23.7 15.0 %collective-permute-done = bf16[256,768]{1,0:T(8,128)(2,1)S(1)} collective-permute-done((bf16[256,768]{1,0:T(8,128)(2,1)S(1)}, bf16[256,768]{1,0:T(8,128)(2,1)S(1)}, u32[]{:S(2)}, u32[]{:S(2)}) %collective-permute-start) | collective-permute-done | bytes 393248 | tf_op jit(solution)/shard_map/ppermute | solution.py:64
  39.5 11.1 %all-gather.5.cloned.1.call-done.pack_ref = bf16[768,2432]{1,0:T(8,128)(2,1)} async-done(((bf16[96,2432]{1,0:T(8,128)(2,1)}), bf16[768,2432]{1,0:T(8,128)(2,1)}) %all-gather.5.cloned.1.call-update) | async-done | bytes 3735568 | tf_op jit(solution)/shard_map/all_gather | solution.py:659
  61.5 26.4 %all-gather.9.cloned.1.call-done.pack_ref = bf16[768,2432]{1,0:T(8,128)(2,1)} async-done(((bf16[96,2432]{1,0:T(8,128)(2,1)}), bf16[768,2432]{1,0:T(8,128)(2,1)}) %all-gather.9.cloned.1.call-update) | async-done | bytes 3735568 | tf_op jit(solution)/shard_map/all_gather | solution.py:659
  89.9 8.4 %attn_fwd.2 = (bf16[192,256]{1,0:T(8,128)(2,1)}, bf16[192,256]{1,0:T(8,128)(2,1)}, bf16[192,256]{1,0:T(8,128)(2,1)}, bf16[192,256]{1,0:T(8,128)(2,1)}, bf16[576,...) custom-call(s32[8]{0:T(128)} %pad_add_fusion.1.order_ref, ...), custom_call_target="tpu_custom_call" | custom-call | tf_op jit(solution)/shard_map/attn_fwd/pallas_call | solution.py:252
  105.3 48.9 %all-gather.7.cloned.1.call-done.pack_ref = bf16[768,6912]{1,0:T(8,128)(2,1)} async-done(((bf16[96,6912]{1,0:T(8,128)(2,1)}), bf16[768,6912]{1,0:T(8,128)(2,1)}) %all-gather.7.cloned.1.call-update) | async-done | bytes 10616848 | tf_op jit(solution)/shard_map/all_gather | solution.py:659
  154.2 9.7 %mlp_forward.2 = (bf16[256,768]{1,0:T(8,128)(2,1)}, f32[256,768]{1,0:T(8,128)}, f32[256,3072]{1,0:T(8,128)}, bf16[768,256]{1,0:T(8,128)(2,1)}) custom-call(s32[8]{0:T(128)} %pad_add_fusion.ids_ref, bf16[256,768]{1,0:T(8,128)(2,1)} %bitcast_select_fusion.1.x_ref, f32[16,768]{1,0:T(8,128)} %slice.222.vec_ref, f32[1,3072]{1,0:T(1,128)} %reshape.235.bias_ref, ...), custom_call_target="tpu_custom_call" | custom-call | tf_op jit(solution)/shard_map/mlp_forward/pallas_call | solution.py:374
  171.7 7.9 %collective-permute-done.10.refs_1_ = bf16[576,256]{1,0:T(8,128)(2,1)S(1)} collective-permute-done((bf16[576,256]{1,0:T(8,128)(2,1)}, bf16[576,256]{1,0:T(8,128)(2,1)S(1)}, u32[]{:S(2)}, u32[]{:S(2)}) %collective-permute-start.10) | collective-permute-done | bytes 294944 | tf_op jit(solution)/shard_map/ppermute | solution.py:52
  185.7 8.4 %attn_fwd.3 = (bf16[192,256]{1,0:T(8,128)(2,1)}, bf16[192,256]{1,0:T(8,128)(2,1)}, bf16[192,256]{1,0:T(8,128)(2,1)}, bf16[192,256]{1,0:T(8,128)(2,1)}, bf16[576,...) custom-call(s32[8]{0:T(128)} %pad_add_fusion.1.order_ref, ...), custom_call_target="tpu_custom_call" | custom-call | tf_op jit(solution)/shard_map/attn_fwd/pallas_call | solution.py:252
  198.4 22.0 %all-gather.11.cloned.1.call-done.pack_ref = bf16[768,6912]{1,0:T(8,128)(2,1)} async-done(((bf16[96,6912]{1,0:T(8,128)(2,1)}), bf16[768,6912]{1,0:T(8,128)(2,1)}) %all-gather.11.cloned.1.call-update) | async-done | bytes 10616848 | tf_op jit(solution)/shard_map/all_gather | solution.py:659
  221.1 9.7 %mlp_forward.3 = (bf16[256,768]{1,0:T(8,128)(2,1)}, f32[256,768]{1,0:T(8,128)}, f32[256,3072]{1,0:T(8,128)}, bf16[768,256]{1,0:T(8,128)(2,1)}) custom-call(s32[8]{0:T(128)} %pad_add_fusion.ids_ref, bf16[256,768]{1,0:T(8,128)(2,1)} %get-tuple-element.93.x_ref, f32[16,768]{1,0:T(8,128)} %slice.227.vec_ref, f32[1,3072]{1,0:T(1,128)} %reshape.237.bias_ref, ...), custom_call_target="tpu_custom_call" | custom-call | tf_op jit(solution)/shard_map/mlp_forward/pallas_call | solution.py:374
  230.8 12.8 %mlp_backward.2 = (bf16[192,256]{1,0:T(8,128)(2,1)}, bf16[192,256]{1,0:T(8,128)(2,1)}, bf16[192,256]{1,0:T(8,128)(2,1)}, bf16[192,256]{1,0:T(8,128)(2,1)}, f32[2...) custom-call(s32[8]{0:T(128)} %pad_add_fusion.ids_ref, ...), custom_call_target="tpu_custom_call" | custom-call | tf_op jit(solution)/shard_map/mlp_backward/pallas_call | solution.py:452
  254.4 8.6 %attn_bwd.2 = (bf16[576,256]{1,0:T(8,128)(2,1)}, bf16[576,256]{1,0:T(8,128)(2,1)}, bf16[576,256]{1,0:T(8,128)(2,1)}, bf16[576,256]{1,0:T(8,128)(2,1)}) custom-call(s32[8]{0:T(128)} %pad_add_fusion.1.order_ref, bf16[192,256]{1,0:T(8,128)(2,1)} %get-tuple-element.115.refs_0_, bf16[192,256]{1,0:T(8,128)(2,1)} %copy-done.30, bf16[192,256]{1,0:T(8,128)(2,1)} %copy-done.32, ...), custom_call_target="tpu_custom_call" | custom-call | tf_op jit(solution)/shard_map/attn_bwd/pallas_call | solution.py:281
  295.1 13.5 %mlp_backward.3 = (bf16[192,256]{1,0:T(8,128)(2,1)}, bf16[192,256]{1,0:T(8,128)(2,1)}, bf16[192,256]{1,0:T(8,128)(2,1)}, bf16[192,256]{1,0:T(8,128)(2,1)}, f32[2...) custom-call(s32[8]{0:T(128)} %pad_add_fusion.ids_ref, ...), custom_call_target="tpu_custom_call" | custom-call | tf_op jit(solution)/shard_map/mlp_backward/pallas_call | solution.py:452
  311.1 7.7 %early_grads.3 = bf16[768,6912]{1,0:T(8,128)(2,1)} custom-call(bf16[256,768]{1,0:T(8,128)(2,1)} %get-tuple-element.134.middle_ref, bf16[256,3072]{1,0:T(8,128)(2,1)} %get-tuple-element.135.ghid_ref, bf16[256,3072]{1,0:T(8,128)(2,1)} %get-tuple-element.136.act_ref, bf16[256,768]{1,0:T(8,128)(2,1)} %convert_element_type.123.grad_ref.glow_ref, ...), custom_call_target="tpu_custom_call" | custom-call | tf_op jit(solution)/shard_map/early_grads/pallas_call | solution.py:513
  319.6 8.7 %attn_bwd.3 = (bf16[576,256]{1,0:T(8,128)(2,1)}, bf16[576,256]{1,0:T(8,128)(2,1)}, bf16[576,256]{1,0:T(8,128)(2,1)}, bf16[576,256]{1,0:T(8,128)(2,1)}) custom-call(s32[8]{0:T(128)} %pad_add_fusion.1.order_ref, bf16[192,256]{1,0:T(8,128)(2,1)} %get-tuple-element.139.refs_0_, bf16[192,256]{1,0:T(8,128)(2,1)} %copy-done.29, bf16[192,256]{1,0:T(8,128)(2,1)} %copy-done.31, ...), custom_call_target="tpu_custom_call" | custom-call | tf_op jit(solution)/shard_map/attn_bwd/pallas_call | solution.py:281
  377.9 10.2 %collective-permute-done.18 = bf16[256,768]{1,0:T(8,128)(2,1)S(1)} collective-permute-done((bf16[256,768]{1,0:T(8,128)(2,1)}, bf16[256,768]{1,0:T(8,128)(2,1)S(1)}, u32[]{:S(2)}, u32[]{:S(2)}) %collective-permute-start.18) | collective-permute-done | bytes 393248 | tf_op jit(solution)/shard_map/ppermute | solution.py:73
  392.0 9.0 %collective-permute-start.42 = (bf16[24,2432]{1,0:T(8,128)(2,1)S(1)}, bf16[24,2432]{1,0:T(8,128)(2,1)S(1)}, u32[]{:S(2)}, u32[]{:S(2)}) collective-permute-start(bf16[24,2432]{1,0:T(8,128)(2,1)S(1)} %get-tuple-element.221), channel_id=1, source_target_pairs={{0,4},{4,8},{8,12},{12,0},{1,5},{5,9},{9,13},{13,1},{2,6},{6,10},{... | collective-permute-start | bytes 350216 | tf_op jit(solution)/shard_map/ppermute | solution.py:674
  403.3 7.6 %collective-permute-done.43 = bf16[24,2432]{1,0:T(8,128)(2,1)S(1)} collective-permute-done((bf16[24,2432]{1,0:T(8,128)(2,1)S(1)}, bf16[24,2432]{1,0:T(8,128)(2,1)S(1)}, u32[]{:S(2)}, u32[]{:S(2)}) %collective-permute-start.43) | collective-permute-done | bytes 116768 | tf_op jit(solution)/shard_map/ppermute | solution.py:674
  443.6 9.3 %collective-permute-done.40 = bf16[24,2432]{1,0:T(8,128)(2,1)S(1)} collective-permute-done((bf16[24,2432]{1,0:T(8,128)(2,1)S(1)}, bf16[24,2432]{1,0:T(8,128)(2,1)S(1)}, u32[]{:S(2)}, u32[]{:S(2)}) %collective-permute-start.40) | collective-permute-done | bytes 116768 | tf_op jit(solution)/shard_map/ppermute | solution.py:676
  458.6 33.7 %reduce-scatter.11.cloned.1.call-done = bf16[96,6912]{1,0:T(8,128)(2,1)} async-done(((bf16[768,6912]{1,0:T(8,128)(2,1)}), bf16[96,6912]{1,0:T(8,128)(2,1)}) %reduce-scatter.11.cloned.1.call-update) | async-done | bytes 1327120 | tf_op jit(solution)/shard_map/reduce_scatter | solution.py:631
  504.1 15.2 %collective-permute-done.57 = bf16[24,6912]{1,0:T(8,128)(2,1)S(1)} collective-permute-done((bf16[24,6912]{1,0:T(8,128)(2,1)S(1)}, bf16[24,6912]{1,0:T(8,128)(2,1)S(1)}, u32[]{:S(2)}, u32[]{:S(2)}) %collective-permute-start.57) | collective-permute-done | bytes 331808 | tf_op jit(solution)/shard_map/ppermute | solution.py:674
  529.2 48.8 %reduce-scatter.9.cloned.1.call-done = bf16[96,6912]{1,0:T(8,128)(2,1)} async-done(((bf16[768,6912]{1,0:T(8,128)(2,1)}), bf16[96,6912]{1,0:T(8,128)(2,1)}) %reduce-scatter.9.cloned.1.call-update) | async-done | bytes 1327120 | tf_op jit(solution)/shard_map/reduce_scatter | solution.py:631
  589.8 15.2 %collective-permute-done.51 = bf16[24,6912]{1,0:T(8,128)(2,1)S(1)} collective-permute-done((bf16[24,6912]{1,0:T(8,128)(2,1)S(1)}, bf16[24,6912]{1,0:T(8,128)(2,1)S(1)}, u32[]{:S(2)}, u32[]{:S(2)}) %collective-permute-start.51) | collective-permute-done | bytes 331808 | tf_op jit(solution)/shard_map/ppermute | solution.py:674
  621.4 22.2 %collective-permute-done.54 = bf16[24,6912]{1,0:T(8,128)(2,1)S(1)} collective-permute-done((bf16[24,6912]{1,0:T(8,128)(2,1)S(1)}, bf16[24,6912]{1,0:T(8,128)(2,1)S(1)}, u32[]{:S(2)}, u32[]{:S(2)}) %collective-permute-start.54) | collective-permute-done | bytes 331808 | tf_op jit(solution)/shard_map/ppermute | solution.py:676
  (364 shorter events, 256.3 us)
Async XLA Ops:
  7.2 43.4 %all-gather.5.cloned.1.call-start = ((), (), s32[]{:S(2)}) async-start(), calls=%async_computation.4 | async-start | bytes 4202496 | tf_op jit(solution)/shard_map/all_gather | solution.py:659
  13.1 74.8 %all-gather.9.cloned.1.call-start = ((), (), s32[]{:S(2)}) async-start(), calls=%async_computation.6 | async-start | bytes 4202496 | tf_op jit(solution)/shard_map/all_gather | solution.py:659
  13.9 140.3 %all-gather.7.cloned.1.call-start = ((), (), s32[]{:S(2)}) async-start(), calls=%async_computation.5 | async-start | bytes 11943936 | tf_op jit(solution)/shard_map/all_gather | solution.py:659
  19.2 201.2 %all-gather.11.cloned.1.call-start = ((), (), s32[]{:S(2)}) async-start(), calls=%async_computation.7 | async-start | bytes 11943936 | tf_op jit(solution)/shard_map/all_gather | solution.py:659
  19.8 371.2 %reduce-scatter.7.cloned.1.call-start = ((), (), s32[]{:S(2)}) async-start(), calls=%async_computation.9 | async-start | bytes 4202496 | tf_op jit(solution)/shard_map/reduce_scatter | solution.py:730
  21.7 175.1 %collective-permute-start.19 = (bf16[256,768]{1,0:T(8,128)(2,1)S(1)}, bf16[256,768]{1,0:T(8,128)(2,1)S(1)}, u32[]{:S(2)}, u32[]{:S(2)}) collective-permute-start(bf16[256,768]{1,0:T(8,128)(2,1)S(1)} %select_bitcast_fusion.2), channel_id=1, source_target_pairs={{0,8},{4,12},{24,16},{28,20},{1,9},{5,13},{25,17},{29,21},{2,10},{... | collective-permute-start | bytes 1179656 | tf_op jit(solution)/shard_map/ppermute | solution.py:64
  57.5 31.5 %collective-permute-start.3 = (bf16[576,256]{1,0:T(8,128)(2,1)}, bf16[576,256]{1,0:T(8,128)(2,1)S(1)}, u32[]{:S(2)}, u32[]{:S(2)}) collective-permute-start(bf16[576,256]{1,0:T(8,128)(2,1)} %get-tuple-element.86), channel_id=1, source_target_pairs={{0,4},{4,16},{16,20},{20,0},{8,12},{12,24},{24,28},{28,8},{1,5},{5... | collective-permute-start | bytes 884744 | tf_op jit(solution)/shard_map/ppermute | solution.py:52
  58.8 30.2 %collective-permute-start.4 = (bf16[576,256]{1,0:T(8,128)(2,1)}, bf16[576,256]{1,0:T(8,128)(2,1)S(1)}, u32[]{:S(2)}, u32[]{:S(2)}) collective-permute-start(bf16[576,256]{1,0:T(8,128)(2,1)} %get-tuple-element.87), channel_id=1, source_target_pairs={{0,16},{4,20},{16,0},{20,4},{8,24},{12,28},{24,8},{28,12},{1,17},{... | collective-permute-start | bytes 884744 | tf_op jit(solution)/shard_map/ppermute | solution.py:52
  59.3 29.7 %collective-permute-start.5 = (bf16[576,256]{1,0:T(8,128)(2,1)}, bf16[576,256]{1,0:T(8,128)(2,1)S(1)}, u32[]{:S(2)}, u32[]{:S(2)}) collective-permute-start(bf16[576,256]{1,0:T(8,128)(2,1)} %get-tuple-element.88), channel_id=1, source_target_pairs={{0,20},{4,0},{16,4},{20,16},{8,28},{12,8},{24,12},{28,24},{1,21},{... | collective-permute-start | bytes 884744 | tf_op jit(solution)/shard_map/ppermute | solution.py:52
  194.1 26.3 %collective-permute-start.13 = (bf16[192,256]{1,0:T(8,128)(2,1)}, bf16[192,256]{1,0:T(8,128)(2,1)S(1)}, u32[]{:S(2)}, u32[]{:S(2)}) collective-permute-start(bf16[192,256]{1,0:T(8,128)(2,1)} %get-tuple-element.99), channel_id=1, source_target_pairs={{0,4},{4,16},{16,20},{20,0},{8,12},{12,24},{24,28},{28,8},{1,5},{5... | collective-permute-start | bytes 294920 | tf_op jit(solution)/shard_map/ppermute | solution.py:52
  195.2 25.2 %collective-permute-start.14 = (bf16[192,256]{1,0:T(8,128)(2,1)}, bf16[192,256]{1,0:T(8,128)(2,1)S(1)}, u32[]{:S(2)}, u32[]{:S(2)}) collective-permute-start(bf16[192,256]{1,0:T(8,128)(2,1)} %get-tuple-element.100), channel_id=1, source_target_pairs={{0,16},{4,20},{16,0},{20,4},{8,24},{12,28},{24,8},{28,12},{1,17},{... | collective-permute-start | bytes 294920 | tf_op jit(solution)/shard_map/ppermute | solution.py:52
  195.5 24.9 %collective-permute-start.15 = (bf16[192,256]{1,0:T(8,128)(2,1)}, bf16[192,256]{1,0:T(8,128)(2,1)S(1)}, u32[]{:S(2)}, u32[]{:S(2)}) collective-permute-start(bf16[192,256]{1,0:T(8,128)(2,1)} %get-tuple-element.101), channel_id=1, source_target_pairs={{0,20},{4,0},{16,4},{20,16},{8,28},{12,8},{24,12},{28,24},{1,21},{... | collective-permute-start | bytes 294920 | tf_op jit(solution)/shard_map/ppermute | solution.py:52
  293.1 129.8 %reduce-scatter.5.cloned.1.call-start = ((), (), s32[]{:S(2)}) async-start(), calls=%async_computation.8 | async-start | bytes 4202496 | tf_op jit(solution)/shard_map/reduce_scatter | solution.py:735
  357.6 134.7 %reduce-scatter.11.cloned.1.call-start = ((), (), s32[]{:S(2)}) async-start(), calls=%async_computation.11 | async-start | bytes 11943936 | tf_op jit(solution)/shard_map/reduce_scatter | solution.py:631
  358.3 219.7 %reduce-scatter.9.cloned.1.call-start = ((), (), s32[]{:S(2)}) async-start(), calls=%async_computation.10 | async-start | bytes 11943936 | tf_op jit(solution)/shard_map/reduce_scatter | solution.py:631
  370.0 33.2 %collective-permute-start.35 = (bf16[256,768]{1,0:T(8,128)(2,1)S(1)}, bf16[256,768]{1,0:T(8,128)(2,1)S(1)}, u32[]{:S(2)}, u32[]{:S(2)}) collective-permute-start(bf16[256,768]{1,0:T(8,128)(2,1)S(1)} %copy-done.3), channel_id=1, source_target_pairs={{8,16},{12,20},{24,24},{28,28},{9,17},{13,21},{25,25},{29,29},{10,... | collective-permute-start | bytes 1179656 | tf_op jit(solution)/shard_map/ppermute | solution.py:73
  494.8 24.6 %collective-permute-start.57 = (bf16[24,6912]{1,0:T(8,128)(2,1)S(1)}, bf16[24,6912]{1,0:T(8,128)(2,1)S(1)}, u32[]{:S(2)}, u32[]{:S(2)}) collective-permute-start(bf16[24,6912]{1,0:T(8,128)(2,1)S(1)} %get-tuple-element.217), channel_id=1, source_target_pairs={{0,8},{4,12},{8,0},{12,4},{1,9},{5,13},{9,1},{13,5},{2,10},{6,14},... | collective-permute-start | bytes 995336 | tf_op jit(solution)/shard_map/ppermute | solution.py:674
  520.5 62.2 %collective-permute-start.59 = (bf16[24,6912]{1,0:T(8,128)(2,1)S(1)}, bf16[24,6912]{1,0:T(8,128)(2,1)S(1)}, u32[]{:S(2)}, u32[]{:S(2)}) collective-permute-start(bf16[24,6912]{1,0:T(8,128)(2,1)S(1)} %fusion.6), channel_id=1, source_target_pairs={{0,12},{4,0},{8,4},{12,8},{1,13},{5,1},{9,5},{13,9},{2,14},{6,2},{... | collective-permute-start | bytes 995336 | tf_op jit(solution)/shard_map/ppermute | solution.py:676
  527.8 56.0 %collective-permute-start.60 = (bf16[24,6912]{1,0:T(8,128)(2,1)S(1)}, bf16[24,6912]{1,0:T(8,128)(2,1)S(1)}, u32[]{:S(2)}, u32[]{:S(2)}) collective-permute-start(bf16[24,6912]{1,0:T(8,128)(2,1)S(1)} %fusion.6), channel_id=1, source_target_pairs={{0,8},{4,12},{8,0},{12,4},{1,9},{5,13},{9,1},{13,5},{2,10},{6,14},... | collective-permute-start | bytes 995336 | tf_op jit(solution)/shard_map/ppermute | solution.py:676
  529.2 54.6 %collective-permute-start.61 = (bf16[24,6912]{1,0:T(8,128)(2,1)S(1)}, bf16[24,6912]{1,0:T(8,128)(2,1)S(1)}, u32[]{:S(2)}, u32[]{:S(2)}) collective-permute-start(bf16[24,6912]{1,0:T(8,128)(2,1)S(1)} %fusion.6), channel_id=1, source_target_pairs={{0,4},{4,8},{8,12},{12,0},{1,5},{5,9},{9,13},{13,1},{2,6},{6,10},{... | collective-permute-start | bytes 995336 | tf_op jit(solution)/shard_map/ppermute | solution.py:676
  580.5 24.6 %collective-permute-start.51 = (bf16[24,6912]{1,0:T(8,128)(2,1)S(1)}, bf16[24,6912]{1,0:T(8,128)(2,1)S(1)}, u32[]{:S(2)}, u32[]{:S(2)}) collective-permute-start(bf16[24,6912]{1,0:T(8,128)(2,1)S(1)} %get-tuple-element.220), channel_id=1, source_target_pairs={{0,8},{4,12},{8,0},{12,4},{1,9},{5,13},{9,1},{13,5},{2,10},{6,14},... | collective-permute-start | bytes 995336 | tf_op jit(solution)/shard_map/ppermute | solution.py:674
  613.6 33.9 %collective-permute-start.63 = (bf16[96,6912]{1,0:T(8,128)(2,1)S(1)}, bf16[96,6912]{1,0:T(8,128)(2,1)S(1)}, u32[]{:S(2)}, u32[]{:S(2)}) collective-permute-start(bf16[96,6912]{1,0:T(8,128)(2,1)S(1)} %bitcast.162), channel_id=1, source_target_pairs={{0,16},{1,17},{2,18},{3,19},{4,20},{5,21},{6,22},{7,23},{8,24},{9,... | collective-permute-start | bytes 3981320 | tf_op jit(solution)/shard_map/ppermute | solution.py:751
  614.9 28.7 %collective-permute-start.54 = (bf16[24,6912]{1,0:T(8,128)(2,1)S(1)}, bf16[24,6912]{1,0:T(8,128)(2,1)S(1)}, u32[]{:S(2)}, u32[]{:S(2)}) collective-permute-start(bf16[24,6912]{1,0:T(8,128)(2,1)S(1)} %fusion.9), channel_id=1, source_target_pairs={{0,8},{4,12},{8,0},{12,4},{1,9},{5,13},{9,1},{13,5},{2,10},{6,14},... | collective-permute-start | bytes 995336 | tf_op jit(solution)/shard_map/ppermute | solution.py:676
  616.3 27.3 %collective-permute-start.55 = (bf16[24,6912]{1,0:T(8,128)(2,1)S(1)}, bf16[24,6912]{1,0:T(8,128)(2,1)S(1)}, u32[]{:S(2)}, u32[]{:S(2)}) collective-permute-start(bf16[24,6912]{1,0:T(8,128)(2,1)S(1)} %fusion.9), channel_id=1, source_target_pairs={{0,4},{4,8},{8,12},{12,0},{1,5},{5,9},{9,13},{13,1},{2,6},{6,10},{... | collective-permute-start | bytes 995336 | tf_op jit(solution)/shard_map/ppermute | solution.py:676
  (87 other events, 860.4 us)
Sparse Core Ops, SparseCore 0:
  13.3 37.2 all-gather.4
  53.1 34.8 all-gather.8
  90.4 63.8 all-gather.6
  156.5 63.8 all-gather.10
  293.3 48.4 reduce-scatter.6
  357.7 48.7 reduce-scatter.4
  410.0 82.1 reduce-scatter.10
  495.8 82.1 reduce-scatter.8

commit v3 on v2

--- a/solution.py
+++ b/solution.py
@@ -92,46 +92,86 @@
     ) * scale
 
 
-def qkv_kernel(ids_ref, x_ref, vec_ref, pack_ref, *refs, parts, size):
-    outs, (weight, whole, sem) = refs[:parts], refs[parts:]
+def piece_places(ids_ref, parts, depth, slots):
+    first = 2 * parts
+    rows = depth // 2
+    places = []
+    for side in range(2):
+        core = ids_ref[first + slots + side]
+        for slot, start, count in (
+            (0, 0, rows),
+            (1, 0, rows),
+            (2, 0, rows),
+            (3, 0, rows // 2),
+            (3, rows // 2, rows // 2),
+        ):
+            place = ids_ref[first + slot] * depth + core * rows + start
+            places.append((pl.multiple_of(place, 16), count))
+    return places
+
+
+def qkv_kernel(ids_ref, x_ref, *refs, parts, size, shards):
+    packs, refs = refs[:10], refs[10:]
+    outs, (weight_ref, vec_ref), refs = refs[:parts], refs[parts : parts + 2], refs[parts + 2 :]
+    weight, small, whole, sems = refs
     width = x_ref.shape[1]
-    copy = pltpu.make_async_copy(pack_ref.at[:, : 3 * width], weight, sem.at[0])
-    copy.start()
+    copies = []
+    for i, (place, count) in enumerate(piece_places(ids_ref, parts, width // shards, shards)):
+        for j, target, cols in (
+            (0, small, slice(3 * width, 3 * width + LANES)),
+            (1, weight, slice(0, 3 * width)),
+        ):
+            copies.append(
+                pltpu.make_async_copy(
+                    packs[i].at[:, cols], target.at[pl.ds(place, count)], sems.at[2 * i + j]
+                )
+            )
+    for copy in copies:
+        copy.start()
     unit, _ = normalised(x_ref[...].astype(F32))
-    normed = (unit * vec_ref[0:1] + vec_ref[2:3]).astype(BF)
-    copy.wait()
+    for copy in copies:
+        copy.wait()
+    keep = pltpu.make_async_copy(weight, weight_ref, sems.at[20])
+    keep.start()
+    vec = small[...].astype(F32).T
+    vec_ref[...] = vec[:16]
+    normed = (unit * vec[0:1] + vec[2:3]).astype(BF)
     held = outs[0].shape[0] // 3
     if parts * held != width:
         whole[...] = jnp.zeros_like(whole)
     for b in range(3):
         block = dot(normed, weight[:, b * width : (b + 1) * width], 1, 0)
         if b == 0:
-            block = block + vec_ref[3:4]
+            block = block + vec[3:4]
         if b == 2:
-            block = block + vec_ref[4:5]
+            block = block + vec[4:5]
         whole[b * parts * held : b * parts * held + width] = block.T.astype(BF)
     for d in range(parts):
         for b in range(3):
             first = pl.multiple_of(b * parts * held + ids_ref[d] * held, size)
             outs[d][b * held : (b + 1) * held] = whole[pl.ds(first, held)]
-
-
-def qkv_project(ids, x, vec, pack, parts, size):
+    keep.wait()
+
+
+def qkv_project(ids, x, packs, parts, size, shards):
     rows, width = x.shape
     held = pl.cdiv(HEADS, parts) * size
-    return pl.pallas_call(
-        functools.partial(qkv_kernel, parts=parts, size=size),
-        in_specs=[SMEM, VMEM, VMEM, HBM],
-        out_specs=[VMEM] * parts,
-        out_shape=[shape((3 * held, rows), BF)] * parts,
+    results = pl.pallas_call(
+        functools.partial(qkv_kernel, parts=parts, size=size, shards=shards),
+        in_specs=[SMEM, VMEM] + [HBM] * 10,
+        out_specs=[VMEM] * parts + [HBM, VMEM],
+        out_shape=[shape((3 * held, rows), BF)] * parts
+        + [shape((width, 3 * width), BF), shape((16, width), F32)],
         scratch_shapes=[
             pltpu.VMEM((width, 3 * width), BF),
+            pltpu.VMEM((width, LANES), BF),
             pltpu.VMEM((3 * parts * held, rows), BF),
-            pltpu.SemaphoreType.DMA((1,)),
+            pltpu.SemaphoreType.DMA((21,)),
         ],
         compiler_params=PARAMS,
         name="qkv_project",
-    )(ids, x, vec, pack)
+    )(ids, x, *packs)
+    return results[:parts], results[parts], results[parts + 1]
 
 
 def spans_of(order_ref, which, count, span):
@@ -395,10 +435,8 @@
     ids_ref, grad_ref, inner_ref, hidden_ref, vec_ref, pack_ref, *refs, parts, shards, ratio
 ):
     outs = refs[:parts]
-    ginner_ref, gattn_ref, ghid_ref, act_ref, middle_ref, small_ref, sbias_ref = refs[
-        parts : parts + 7
-    ]
-    w_out, w_up, w_down, whole, sems = refs[parts + 7 :]
+    ginner_ref, gattn_ref, ghid_ref, act_ref, middle_ref, table_ref = refs[parts : parts + 6]
+    w_out, w_up, w_down, whole, sems = refs[parts + 6 :]
     width = grad_ref.shape[1]
     out, up, down = rest_copies(pack_ref, w_out, w_up, w_down, sems, shards, ratio)
     for copy in down + up + out:
@@ -410,6 +448,8 @@
         copy.wait()
     up[0].wait()
     up_mid = jnp.zeros(unit.shape, F32)
+    depth = width // shards
+    table_ref[...] = jnp.zeros_like(table_ref)
     for start in range(0, w_up.shape[1], width):
         cols = slice(start, start + width)
         hidden = hidden_ref[:, cols]
@@ -420,7 +460,10 @@
         )
         grad_hid = (dot(grad_low, w_down[cols], 1, 1) * slope).astype(BF)
         ghid_ref[:, cols] = grad_hid
-        sbias_ref[:, cols] = jnp.sum(grad_hid.astype(F32), axis=0, keepdims=True)
+        sums = jnp.sum(grad_hid.astype(F32), axis=0, keepdims=True)
+        for i in range(width // depth):
+            f, j = divmod(start // depth + i, ratio)
+            table_ref[8 + j : 9 + j, f * depth : (f + 1) * depth] = sums[:, i * depth : (i + 1) * depth]
         up_mid = up_mid + dot(grad_hid, w_up[:, cols], 1, 1)
     grad_inner = grad_ref[...].astype(F32) + norm_back(unit, scale, up_mid, vec_ref[1:2])
     ginner_ref[...] = grad_inner
@@ -433,16 +476,10 @@
     whole[:width] = dot(w_out[...], grad_attn, 1, 1).astype(BF)
     for d in range(parts):
         outs[d][...] = whole[pl.ds(pl.multiple_of(ids_ref[d] * held, held), held)]
-    small_ref[...] = jnp.concatenate(
-        [
-            jnp.sum(up_mid * unit, axis=0, keepdims=True),
-            jnp.sum(grad_attn.astype(F32), axis=0, keepdims=True),
-            jnp.sum(up_mid, axis=0, keepdims=True),
-            jnp.sum(grad_low.astype(F32), axis=0, keepdims=True),
-            jnp.zeros((4, width), F32),
-        ],
-        axis=0,
-    )
+    table_ref[1:2] = jnp.sum(up_mid * unit, axis=0, keepdims=True)
+    table_ref[5:6] = jnp.sum(grad_attn.astype(F32), axis=0, keepdims=True)
+    table_ref[6:7] = jnp.sum(up_mid, axis=0, keepdims=True)
+    table_ref[7:8] = jnp.sum(grad_low.astype(F32), axis=0, keepdims=True)
 
 
 def mlp_backward(ids, grad, inner, hidden, vec, pack, parts, size, shards, ratio):
@@ -452,7 +489,7 @@
     results = pl.pallas_call(
         functools.partial(mlp_back_kernel, parts=parts, shards=shards, ratio=ratio),
         in_specs=[SMEM, VMEM, VMEM, VMEM, VMEM, HBM],
-        out_specs=[VMEM] * (parts + 7),
+        out_specs=[VMEM] * (parts + 6),
         out_shape=[shape((held, rows), BF)] * parts
         + [
             shape((rows, width), F32),
@@ -460,8 +497,7 @@
             shape((rows, wide), BF),
             shape((rows, wide), BF),
             shape((rows, width), BF),
-            shape((8, width), F32),
-            shape((1, wide), F32),
+            shape((LANES, width), F32),
         ],
         scratch_shapes=rest_scratch(width, wide, shards, ratio)
         + [
@@ -474,14 +510,49 @@
     return results[:parts], results[parts:]
 
 
+def write_down(act_ref, glow_ref, pack, start, shards, ratio):
+    width = glow_ref.shape[1]
+    depth = width // shards
+    glow = glow_ref[...].astype(BF)
+    for f in range(shards):
+        block = dot(act_ref[:, f * ratio * depth : (f + 1) * ratio * depth], glow, 0, 0).astype(BF)
+        for j in range(ratio):
+            first = start + j * width
+            pack[f * depth : (f + 1) * depth, first : first + width] = block[
+                j * depth : (j + 1) * depth
+            ]
+
+
+def send_sides(ids_ref, first, pack, start, count, targets, sems, offset, shards):
+    depth = pack.shape[0] // shards
+    rows = depth // 2
+    copies = []
+    for side in range(2):
+        core = ids_ref[first + shards + side]
+        for k in range(shards):
+            place = pl.multiple_of(ids_ref[first + k] * depth + core * rows, 16)
+            copies.append(
+                pltpu.make_async_copy(
+                    pack.at[pl.ds(place, rows), start : start + count],
+                    targets[side].at[k],
+                    sems.at[offset + side * shards + k],
+                )
+            )
+    for copy in copies:
+        copy.start()
+    return copies
+
+
 def early_kernel(
-    middle_ref, ghid_ref, act_ref, glow_ref, mixed_ref, gattn_ref, pack_ref, scratch, sems, *, shards, ratio
+    ids_ref, middle_ref, ghid_ref, mixed_ref, gattn_ref, act_ref, glow_ref, *refs, parts, shards, ratio, apart
 ):
+    if apart:
+        outs, (scratch, sems) = refs[:4], refs[4:]
+    else:
+        pack_ref, scratch, sems = refs
     width = middle_ref.shape[1]
-    depth = width // shards
-    hidden = ratio * width
+    main = (1 + ratio) * width
     copies = []
-    glow = glow_ref[...].astype(BF)
 
     def send(columns, i):
         copy = pltpu.make_async_copy(scratch.at[:, columns], pack_ref.at[:, columns], sems.at[i])
@@ -489,158 +560,154 @@
         copies.append(copy)
 
     scratch[:, :width] = dot(mixed_ref[...], gattn_ref[...], 1, 0).astype(BF)
-    send(slice(0, width), 0)
     for i in range(ratio):
         cols = slice(i * width, (i + 1) * width)
         block = dot(middle_ref[...], ghid_ref[:, cols], 0, 0).astype(BF)
         scratch[:, (i + 1) * width : (i + 2) * width] = block
-        send(slice((i + 1) * width, (i + 2) * width), 1 + i)
-    for f in range(shards):
-        block = dot(act_ref[:, f * ratio * depth : (f + 1) * ratio * depth], glow, 0, 0).astype(BF)
-        for j in range(ratio):
-            start = width + hidden + j * width
-            scratch[f * depth : (f + 1) * depth, start : start + width] = block[
-                j * depth : (j + 1) * depth
-            ]
-    send(slice(width + hidden, width + 2 * hidden), 1 + ratio)
+    if apart:
+        copies += send_sides(
+            ids_ref, 2 * parts, scratch, 0, main, outs[:2], sems, 0, shards
+        )
+    else:
+        send(slice(0, main), 0)
+    write_down(act_ref, glow_ref, scratch, main, shards, ratio)
+    if apart:
+        copies += send_sides(
+            ids_ref, 2 * parts, scratch, main, ratio * width, outs[2:], sems, 2 * shards, shards
+        )
+    else:
+        send(slice(main, main + ratio * width), 1)
     for copy in copies:
         copy.wait()
 
 
-def early_grads(middle, ghid, act, glow, mixed, gattn, shards, ratio):
+def early_grads(ids, middle, ghid, mixed, gattn, act, grad, parts, shards, ratio, apart):
     width = middle.shape[1]
-    total = width * (1 + 2 * ratio)
+    main, hidden = (1 + ratio) * width, ratio * width
+    rows = width // shards // 2
+    up, down = shape((shards, rows, main), BF), shape((shards, rows, hidden), BF)
     return pl.pallas_call(
-        functools.partial(early_kernel, shards=shards, ratio=ratio),
-        in_specs=[VMEM] * 6,
-        out_specs=HBM,
-        out_shape=shape((width, total), BF),
+        functools.partial(early_kernel, parts=parts, shards=shards, ratio=ratio, apart=apart),
+        in_specs=[SMEM] + [VMEM] * 6,
+        out_specs=[HBM] * (4 if apart else 1),
+        out_shape=[up, up, down, down] if apart else [shape((width, main + hidden), BF)],
         scratch_shapes=[
-            pltpu.VMEM((width, total), BF),
-            pltpu.SemaphoreType.DMA((2 + ratio,)),
+            pltpu.VMEM((width, main + hidden), BF),
+            pltpu.SemaphoreType.DMA((4 * shards,)),
         ],
         compiler_params=PARAMS,
         name="early_grads",
-    )(middle, ghid, act, glow, mixed, gattn)
+    )(ids, middle, ghid, mixed, gattn, act, grad)
 
 
 def qkv_back_kernel(
-    ids_ref, x_ref, ginner_ref, vec_ref, pack_ref, *refs, parts
+    ids_ref, x_ref, ginner_ref, vec_ref, table_ref, weight_hbm, *refs, parts, shards
 ):
-    pieces = refs[:parts]
-    gx_ref, small_ref, whole_ref = refs[parts : parts + 3]
-    weight, whole, sem = refs[parts + 3 :]
+    pieces, refs = refs[:parts], refs[parts:]
+    gx_ref, keep_ref, send_ref, weight, whole, pack, sem = refs
     width = x_ref.shape[1]
-    copy = pltpu.make_async_copy(pack_ref.at[:, : 3 * width], weight, sem.at[0])
+    main = 3 * width + LANES
+    copies = []
+    copy = pltpu.make_async_copy(weight_hbm, weight, sem.at[0])
     copy.start()
     held = pieces[0].shape[0] // 3
+    padded = parts * held
     for d, piece in enumerate(pieces):
         for b in range(3):
-            place = pl.multiple_of(b * parts * held + ids_ref[parts + d] * held, held)
+            place = pl.multiple_of(b * padded + ids_ref[parts + d] * held, held)
             whole[pl.ds(place, held)] = piece[b * held : (b + 1) * held]
+    unit, scale = normalised(x_ref[...].astype(F32))
+    normed = (unit * vec_ref[0:1] + vec_ref[2:3]).T.astype(BF)
+    copy.wait()
+    up_norm = jnp.zeros((width, x_ref.shape[0]), F32)
+    sums = []
     for b in range(3):
-        whole_ref[b * width : (b + 1) * width] = whole[b * parts * held : b * parts * held + width]
-    unit, scale = normalised(x_ref[...].astype(F32))
-    copy.wait()
-    up_norm = dot(weight[...], whole_ref[...], 1, 0).T
-    gx_ref[...] = ginner_ref[...] + norm_back(unit, scale, up_norm, vec_ref[0:1])
-    small_ref[...] = jnp.concatenate(
-        [
-            jnp.sum(up_norm * unit, axis=0, keepdims=True),
-            jnp.sum(up_norm, axis=0, keepdims=True),
-            jnp.zeros((6, width), F32),
-        ],
-        axis=0,
+        grads = whole[b * padded : b * padded + width]
+        cols = slice(b * width, (b + 1) * width)
+        up_norm = up_norm + dot(weight[:, cols], grads, 1, 0)
+        pack[:, cols] = dot(normed, grads, 1, 1).astype(BF)
+        sums.append(jnp.sum(grads.astype(F32), axis=1, keepdims=True))
+    up_norm = up_norm.T
+    gx_ref[...] = (ginner_ref[...] + norm_back(unit, scale, up_norm, vec_ref[0:1])).astype(BF)
+    line = lax.broadcasted_iota(jnp.int32, table_ref.shape, 0)
+    table = jnp.where(
+        line == 0,
+        jnp.sum(up_norm * unit, axis=0, keepdims=True),
+        jnp.where(line == 2, jnp.sum(up_norm, axis=0, keepdims=True), table_ref[...]),
+    ).T
+    lane = lax.broadcasted_iota(jnp.int32, table.shape, 1)
+    table = jnp.where(lane == 3, sums[0], jnp.where(lane == 4, sums[2], table))
+    pack[:, 3 * width : main] = table.astype(BF)
+    copies += send_sides(
+        ids_ref, 2 * parts, pack, 0, main, (keep_ref, send_ref), sem, 1, shards
     )
-
-
-def qkv_backward(ids, x, ginner, vec, pack, pieces):
+    for copy in copies:
+        copy.wait()
+
+
+def qkv_backward(ids, x, ginner, vec, table, weight, pieces, shards):
     parts = len(pieces)
     rows, width = x.shape
+    total = 3 * width + LANES
+    part = shape((shards, width // shards // 2, total), BF)
     return pl.pallas_call(
-        functools.partial(qkv_back_kernel, parts=parts),
-        in_specs=[SMEM, VMEM, VMEM, VMEM, HBM] + [VMEM] * parts,
-        out_specs=[VMEM] * 3,
-        out_shape=[shape((rows, width), F32), shape((8, width), F32), shape((3 * width, rows), BF)],
+        functools.partial(qkv_back_kernel, parts=parts, shards=shards),
+        in_specs=[SMEM, VMEM, VMEM, VMEM, VMEM, HBM] + [VMEM] * parts,
+        out_specs=[VMEM, HBM, HBM],
+        out_shape=[shape((rows, width), BF), part, part],
         scratch_shapes=[
             pltpu.VMEM((width, 3 * width), BF),
             pltpu.VMEM((parts * pieces[0].shape[0], rows), BF),
-            pltpu.SemaphoreType.DMA((1,)),
+            pltpu.VMEM((width, total), BF),
+            pltpu.SemaphoreType.DMA((1 + 2 * shards,)),
         ],
         compiler_params=PARAMS,
         name="qkv_backward",
-    )(ids, x, ginner, vec, pack, *pieces)
-
-
-def late_kernel(x_ref, vec_ref, grad_ref, small_ref, pack_ref, scratch, sems):
-    width = x_ref.shape[1]
-    copies = []
-    unit, _ = normalised(x_ref[...].astype(F32))
-    normed = (unit * vec_ref[0:1] + vec_ref[2:3]).T.astype(BF)
-    for b in range(3):
-        cols = slice(b * width, (b + 1) * width)
-        rows = grad_ref[cols]
-        scratch[:, cols] = dot(normed, rows, 1, 1).astype(BF)
-        copy = pltpu.make_async_copy(scratch.at[:, cols], pack_ref.at[:, cols], sems.at[b])
-        copy.start()
-        copies.append(copy)
-    last = slice(3 * width, 3 * width + LANES)
-    scratch[:, last] = small_ref[...].astype(BF)
-    copy = pltpu.make_async_copy(scratch.at[:, last], pack_ref.at[:, last], sems.at[3])
-    copy.start()
-    copies.append(copy)
-    for copy in copies:
-        copy.wait()
-
-
-def late_grads(x, vec, grad_qkv, small):
+    )(ids, x, ginner, vec, table, weight, *pieces)
+
+
+def layer_forward(x, packs, rest, ids, order, parts, size, shards, ratio):
+    sent, weight, vec = qkv_project(ids, x, packs, parts, size, shards)
     width = x.shape[1]
-    return pl.pallas_call(
-        late_kernel,
-        in_specs=[VMEM] * 4,
-        out_specs=HBM,
-        out_shape=shape((width, 3 * width + LANES), BF),
-        scratch_shapes=[
-            pltpu.VMEM((width, 3 * width + LANES), BF),
-            pltpu.SemaphoreType.DMA((4,)),
-        ],
-        compiler_params=PARAMS,
-        name="late_grads",
-    )(x, vec, grad_qkv, small)
-
-
-def layer_forward(x, packs, vec, bias, ids, order, parts, size, shards, ratio):
-    sent = qkv_project(ids, x, vec, packs[0], parts, size)
+    depth = width // shards
+    bias = vec[8 : 8 + ratio].reshape(ratio, shards, depth).transpose(1, 0, 2).reshape(1, -1)
     mixed, attn_saved = attention_forward(exchange(sent), order, size)
     result, inner, hidden, mixed = mlp_forward(
-        ids, x, vec, bias, packs[1], exchange(mixed), shards, ratio
+        ids, x, vec, bias, rest, exchange(mixed), shards, ratio
     )
-    return result, (x, attn_saved, inner, hidden, mixed)
-
-
-def layer_backward(saved, grad, packs, vec, ids, order, parts, size, shards, ratio):
-    x, attn_saved, inner, hidden, mixed = saved
+    return result, (x, weight, vec, attn_saved, inner, hidden, mixed)
+
+
+def layer_backward(saved, grad, rest, ids, order, parts, size, shards, ratio, layer, background):
+    x, weight, vec, attn_saved, inner, hidden, mixed = saved
     width = x.shape[1]
     depth = width // shards
-    sent, (ginner, gattn, ghid, act, middle, small, sbias) = mlp_backward(
-        ids, grad, inner, hidden, vec, packs[1], parts, size, shards, ratio
+    last = layer == 0
+    sent, (ginner, gattn, ghid, act, middle, table) = mlp_backward(
+        ids, grad, inner, hidden, vec, rest, parts, size, shards, ratio
     )
-    early = early_grads(middle, ghid, act, grad, mixed, gattn, shards, ratio)
+    sent = background.slot(sent)
+    early = early_grads(ids, middle, ghid, mixed, gattn, act, grad, parts, shards, ratio, last)
     received = exchange(sent)
-    *received, early = lax.optimization_barrier((*received, early))
-    reduced = lax.psum_scatter(early, SHARDS, scatter_dimension=0, tiled=True)
+    both = background.slot([*received, *early])
+    received, early = both[:parts], both[parts:]
+    if last:
+        tasks = [
+            background.add(permuted_task(*early[:2], layer, (0, 1, 0), (0, 0, 0))),
+            background.add(permuted_task(*early[2:], layer, (0, 1, 1), (0, 0, 0))),
+        ]
+    else:
+        tasks = [background.add(offloaded_task(early[0], layer, 5, 1, (1, 1, 1)))]
     sent = attention_backward(received, attn_saved, order, size)
-    grad_x, small2, grad_qkv = qkv_backward(ids, x, ginner, vec, packs[0], exchange(sent))
-    sums = jnp.sum(grad_qkv.reshape(3, width, -1).astype(F32), axis=2)
-    table = jnp.concatenate(
-        [
-            jnp.stack([small2[0], small[0], small2[1], sums[0], sums[2], small[1], small[2], small[3]]),
-            sbias.reshape(shards, ratio, depth).transpose(1, 0, 2).reshape(ratio, width),
-        ]
+    sent = background.slot(sent)
+    received = background.slot(exchange(sent))
+    grad_x, keep, send = qkv_backward(
+        ids, x, ginner, vec, table, weight, received, shards
     )
-    table = jnp.pad(table, ((0, LANES - table.shape[0]), (0, 0))).T
-    late = late_grads(x, vec, grad_qkv, table)
-    return grad_x, reduced, late
+    grad_x, keep, send = background.slot([grad_x, keep, send])
+    slack = ((0, 0, 0), (0, 0, 0)) if last else ((0, 1, 0), (1, 0, 0))
+    tasks.append(background.add(permuted_task(keep, send, layer, *slack)))
+    return grad_x, tasks
 
 
 def blocks_to_columns(value, parts):
@@ -659,24 +726,108 @@
     return lax.all_gather(part, SHARDS, axis=0, tiled=True)
 
 
-def sum_over_ctx(value):
-    count = lax.axis_size("ctx")
-    index = lax.axis_index("ctx")
-    rows = value.shape[0] // count
-    pieces = value.reshape(count, rows, -1)
-
-    def turned(d):
-        return [(i, (i + d) % count) for i in range(count)]
-
-    total = lax.dynamic_index_in_dim(pieces, index, 0, keepdims=False).astype(F32)
-    for d in range(1, count):
-        piece = lax.dynamic_index_in_dim(pieces, (index + d) % count, 0, keepdims=False)
-        total = total + lax.ppermute(piece, "ctx", turned(d)).astype(F32)
-    total = total.astype(BF)
-    came = [lax.ppermute(total, "ctx", turned(d)) for d in range(count - 1, 0, -1)] + [total]
-    ring = jnp.stack(came + came)
-    start = (2 * count - 1 - index) % count
-    return lax.dynamic_slice_in_dim(ring, start, count, 0).reshape(value.shape)
+def across(value, bit):
+    count = lax.axis_size("fsdp")
+    return lax.ppermute(value, "fsdp", [(i, i ^ bit) for i in range(count)])
+
+
+def swap_cores(value):
+    return lax.ppermute(value, "section", [(0, 1), (1, 0)])
+
+
+def gather_pieces(part):
+    rows = part.shape[0] // 2
+    by_x, by_y = across(part, 1), across(part, 2)
+    pieces = [part, by_x, by_y, across(by_x[:rows], 2), across(by_y[rows:], 1)]
+    return pieces + [swap_cores(piece) for piece in pieces]
+
+
+class Background:
+    def __init__(self):
+        self.tasks = []
+
+    def add(self, task):
+        entry = {"task": task, "result": None}
+        entry["flight"] = next(task)
+        self.tasks.append(entry)
+        return entry
+
+    def slot(self, values):
+        waiting = [entry for entry in self.tasks if entry["flight"] is not None]
+        flat = list(values)
+        for entry in waiting:
+            flat += entry["flight"]
+        flat = list(lax.optimization_barrier(tuple(flat)))
+        values, flat = flat[: len(values)], flat[len(values) :]
+        for entry in waiting:
+            count = len(entry["flight"])
+            held, flat = flat[:count], flat[count:]
+            try:
+                entry["flight"] = entry["task"].send(held)
+            except StopIteration as stop:
+                entry["flight"], entry["result"] = None, stop.value
+        return values
+
+    def finish(self):
+        while any(entry["flight"] is not None for entry in self.tasks):
+            self.slot([])
+
+
+def held(flight, slots):
+    for _ in range(slots):
+        yield []
+    return (yield flight)
+
+
+def permuted_task(keep, send, layer, slack, ctx_slack):
+    (received,) = yield from held([swap_cores(send)], slack[0])
+    rows = keep.shape[1] // 2
+
+    def summed(slots, side):
+        return sum_pair(keep[slots, side], received[slots, side])
+
+    top, low = slice(0, rows), slice(rows, 2 * rows)
+    by_x, by_y = yield from held(
+        [across(summed(slice(1, 4, 2), top), 1), across(summed(slice(2, 4), low), 2)], slack[1]
+    )
+    first = sum_pair(summed(slice(0, 4, 2), top), by_x)
+    second = sum_pair(summed(slice(0, 2), low), by_y)
+    by_y, by_x = yield from held([across(first[1], 2), across(second[1], 1)], slack[2])
+    value = jnp.concatenate([sum_pair(first[0], by_y), sum_pair(second[0], by_x)])
+    return (yield from ctx_task(value, layer, ctx_slack))
+
+
+def offloaded_task(pack, layer, wait, pause, ctx_slack):
+    value = lax.psum_scatter(pack, SHARDS, scatter_dimension=0, tiled=True)
+    (value,) = yield from held([value], wait)
+    for _ in range(pause):
+        yield []
+    return (yield from ctx_task(value, layer, ctx_slack))
+
+
+def ctx_task(value, layer, slack):
+    if lax.axis_size("ctx") == 4:
+        index = lax.axis_index("ctx")
+        (received,) = yield from held([lax.ppermute(value, "ctx", [(0, 1), (3, 2)])], slack[0])
+        value = sum_pair(value, received)
+        (received,) = yield from held([lax.ppermute(value, "ctx", [(1, 2), (2, 1)])], slack[1])
+        value = sum_pair(value, received)
+        (received,) = yield from held([lax.ppermute(value, "ctx", [(1, 0), (2, 3)])], slack[2])
+        value = jnp.where((index == 0) | (index == 3), received, value)
+    else:
+        value = lax.psum(value, "ctx")
+    (other,) = yield [lax.ppermute(value, "section", [(1 - layer, layer)])]
+    return value, other
+
+
+def return_task(values, layers):
+    flight = [moved for value, layer in zip(values, layers) for moved in return_rows(value, layer)]
+    flight = yield flight
+    return flight
+
+
+def sum_pair(a, b):
+    return (a.astype(F32) + b.astype(F32)).astype(BF)
 
 
 def body(
@@ -697,7 +848,9 @@
 
     steps = jnp.arange(ctx, dtype=jnp.int32)
     came, goes = (member - steps) % ctx, (member + steps) % ctx
-    ids = jnp.concatenate([goes, came]).astype(jnp.int32)
+    shard = lax.axis_index("fsdp")
+    slots = [shard ^ k for k in range(shards)] + [core, 1 - core]
+    ids = jnp.concatenate([goes, came, jnp.stack(slots)]).astype(jnp.int32)
     order = jnp.concatenate([span_order[came], span_order[goes]])
 
     small = jnp.concatenate([norm_gains[0], bias_rows[0], bias_hidden[0].reshape(ratio, depth)]).T
@@ -707,64 +860,48 @@
     first0, first1 = split_layers(first, core)
     x = bring_rows(tokens[:, 0], core, base)
     rest0, rest1 = split_layers(rest, core)
-    packs = []
-    for a, b in ((first0, rest0), (first1, rest1)):
-        packs.append((gather(a), gather(b)))
-    vecs, biases = [], []
-    for a, _ in packs:
-        table = a[:, 3 * width :].T.astype(F32)
-        vecs.append(table[:16])
-        hidden = table[gain_count + shift_count : gain_count + shift_count + ratio]
-        biases.append(hidden.reshape(ratio, shards, depth).transpose(1, 0, 2).reshape(1, -1))
-
-    out0, saved0 = layer_forward(
-        x, packs[0], vecs[0], biases[0], ids, order, ctx, size, shards, ratio
-    )
-    out1, saved1 = layer_forward(
-        out0, packs[1], vecs[1], biases[1], ids, order, ctx, size, shards, ratio
-    )
-    cot = bring_rows(cotangent[:, 0], core, base)
-    grad1, early1, late1 = layer_backward(
-        saved1, cot, packs[1], vecs[1], ids, order, ctx, size, shards, ratio
-    )
-    late1 = lax.psum_scatter(late1, SHARDS, scatter_dimension=0, tiled=True)
-    grad1_low = grad1.astype(BF)
-    grad0, early0, late0 = layer_backward(
-        saved0, grad1_low, packs[0], vecs[0], ids, order, ctx, size, shards, ratio
-    )
-    late0 = lax.psum_scatter(late0, SHARDS, scatter_dimension=0, tiled=True)
-
-    def own_layer(value0, value1):
-        return [
-            jnp.where(core == 0, a, b)
-            for a, b in zip(return_rows(value0, 0), return_rows(value1, 1))
-        ]
-
-    layer_outputs = jnp.stack(own_layer(out0, out1))
-    input_grads = jnp.stack(own_layer(grad0.astype(BF), grad1_low)).astype(F32)
-
-    def joined(part0, part1):
-        part0, part1 = sum_over_ctx(part0), sum_over_ctx(part1)
-        other = jnp.where(
+    first0, first1 = gather_pieces(first0), gather_pieces(first1)
+    rest0, rest1 = gather(rest0), gather(rest1)
+    sizes = (ids, order, ctx, size, shards, ratio)
+    out0, saved0 = layer_forward(x, first0, rest0, *sizes)
+    late_cot, out0 = lax.optimization_barrier((cotangent[:, 0], out0))
+    out1, saved1 = layer_forward(out0, first1, rest1, *sizes)
+    cot = bring_rows(late_cot, core, base)
+    background = Background()
+    outs = background.add(return_task([out0, out1], [0, 1]))
+    grad1, reduced1 = layer_backward(saved1, cot, rest1, *sizes, 1, background)
+    back1 = background.add(return_task([grad1], [1]))
+    grad0, reduced0 = layer_backward(saved0, grad1, rest0, *sizes, 0, background)
+    back0 = background.add(return_task([grad0], [0]))
+    background.finish()
+
+    def chosen(values0, values1):
+        return jnp.stack([jnp.where(core == 0, a, b) for a, b in zip(values0, values1)])
+
+    layer_outputs = chosen(outs["result"][:cores], outs["result"][cores:])
+    input_grads = chosen(back0["result"], back1["result"]).astype(F32)
+
+    def joined(pair0, pair1):
+        return jnp.where(
             core == 0,
-            lax.ppermute(part0, "section", [(1, 0)]),
-            lax.ppermute(part1, "section", [(0, 1)]),
-        )
-        own = jnp.where(core == 0, part0, part1)
-        return jnp.where(
-            core == 0, jnp.concatenate([own, other]), jnp.concatenate([other, own])
+            jnp.concatenate([pair0[0], pair0[1]]),
+            jnp.concatenate([pair1[1], pair1[0]]),
         ).astype(F32)
 
-    early = joined(early0, early1)
+    (early0, down0, late0), (early1, late1) = [
+        [entry["result"] for entry in reduced] for reduced in (reduced0, reduced1)
+    ]
+    main = (1 + ratio) * width
+    early = joined(early0, [value[:, :main] for value in early1])
     late = joined(late0, late1)
-    down = early[:, width * (1 + ratio) :]
+    down = joined(down0, [value[:, main:] for value in early1])
     table = late[:, 3 * width :].T
     return (
         layer_outputs[None, :, None],
         input_grads[None, :, None],
         late[None, :, : 3 * width],
         early[None, :, :width],
-        early[None, :, width : width * (1 + ratio)],
+        early[None, :, width:],
         jnp.concatenate([down[:, j * width : (j + 1) * width] for j in range(ratio)])[None],
         table[None, :gain_count],
         table[None, gain_count : gain_count + shift_count],

time: 670 us -> 550 us (0.82)
  waiting for transfers between devices: 362 us -> 169 us
  starting transfers between devices: 103 us -> 165 us
  other arithmetic: 24.6 us -> 36.4 us
    all_gather x4 -> x2, waiting for transfers between devices: 108 us -> 12.1 us  [gather(): return lax.all_gather(part, SHARDS, axis=0, tiled=True)]
    reduce_scatter x4 -> x1, waiting for transfers between devices: 82.5 us -> 2.34 us  [offloaded_task(): value = lax.psum_scatter(pack, SHARDS, scatter_dimension=0, tiled=True)]
    ppermute x28 -> x58, starting transfers between devices: 63.8 us -> 122 us  [the longest x5 41.8 us: ctx_task(): lax.ppermute(value, 'ctx', [(0, 1), (3, 2)])]
    convert_element_type x11 -> x30, other arithmetic: 7.16 us -> 23.7 us  [the longest x26 21.6 us: sum_pair(): return (a.astype(F32) + b.astype(F32)).astype(BF)]
    ppermute x2, waiting for transfers between devices: 15 us -> 0.01 us  [bring_rows(): lax.ppermute(jnp.where(core == 0, both[1], both[0]), GROUP, pairs)]
    ppermute x8, waiting for transfers between devices: 12 us -> 0.02 us  [return_rows(): lax.ppermute(value, GROUP, [(place_of(z // half, m * half + z % half), pl...]
    ppermute x24, waiting for transfers between devices: 40.8 us -> 49.1 us  [exchange(): moved.append(lax.ppermute(pieces[d], GROUP, pairs))]
    unnamed x115 -> x153, local copies, waits for them, and re-layouts: 9.12 us -> 14.3 us
  transfers between devices with their start and end apart: 72 -> 97, of which waited for: 34 -> 31; matrix products, arithmetic and copies ran while one was open for 5% -> 7% of each run, Pallas kernels for 13% -> 24%
where the time goes in v3:
time: 550 us; the launch traced here: 540 us
  waiting for transfers between devices  169 us (31%)
  starting transfers between devices  165 us (30%)
  Pallas kernels  127 us (23%)
  other arithmetic  36.4 us (7%)
  local copies, waits for them, and re-layouts  27.3 us (5%)
  between operations  15.4 us (3%)
    ppermute x24, waiting for transfers between devices, across(): return lax.ppermute(value, 'fsdp', [(i, i ^ bit) for i in range(count)])  49.6 us
    ppermute x24, waiting for transfers between devices, exchange(): moved.append(lax.ppermute(pieces[d], GROUP, pairs))  49.1 us
    ppermute x5, starting transfers between devices, ctx_task(): lax.ppermute(value, 'ctx', [(0, 1), (3, 2)])  41.8 us
    ppermute x5, waiting for transfers between devices, ctx_task(): lax.ppermute(value, 'ctx', [(1, 0), (2, 3)])  35.3 us
    ppermute x5, starting transfers between devices, ctx_task(): other, = (yield [lax.ppermute(value, 'section', [(1 - layer, layer)])])  26.6 us
    pallas_call x2, Pallas kernels, mlp_backward(): pl.pallas_call(functools.partial(mlp_back_kernel, parts=parts, shards=sha...  26.5 us
    ppermute x24, starting transfers between devices, across(): return lax.ppermute(value, 'fsdp', [(i, i ^ bit) for i in range(count)])  24.4 us
    convert_element_type x26, other arithmetic, sum_pair(): return (a.astype(F32) + b.astype(F32)).astype(BF)  21.6 us
  transfers between devices with their start and end apart: 97, of which 31 were waited for; matrix products, arithmetic and copies ran while one was open for 7% of the time, Pallas kernels for 24%

profile of v3, /device:TPU:1, one launch (start us, length us, event | category | flops | bytes accessed | tf_op | source)
XLA Modules:
  0.0 540.5 jit_solution(1825417062938728545)
XLA Ops:
  27.4 7.1 %collective-permute-done.2.refs_1_ = bf16[96,2432]{1,0:T(8,128)(2,1)S(1)} collective-permute-done((bf16[96,2432]{1,0:T(8,128)(2,1)S(1)}, bf16[96,2432]{1,0:T(8,128)(2,1)S(1)}, u32[]{:S(2)}, u32[]{:S(2)}) %collective-permute-start.2) | collective-permute-done | bytes 466976 | tf_op jit(solution)/shard_map/ppermute | solution.py:731
  80.3 8.4 %attn_fwd.2 = (bf16[192,256]{1,0:T(8,128)(2,1)}, bf16[192,256]{1,0:T(8,128)(2,1)}, bf16[192,256]{1,0:T(8,128)(2,1)}, bf16[192,256]{1,0:T(8,128)(2,1)}, bf16[576,...) custom-call(s32[8]{0:T(128)} %pad_add_fusion.order_ref, ...), custom_call_target="tpu_custom_call" | custom-call | tf_op jit(solution)/shard_map/attn_fwd/pallas_call | solution.py:292
  101.1 9.7 %mlp_forward.2 = (bf16[256,768]{1,0:T(8,128)(2,1)}, f32[256,768]{1,0:T(8,128)}, f32[256,3072]{1,0:T(8,128)}, bf16[768,256]{1,0:T(8,128)(2,1)}) custom-call(s32[14]{0:T(128)} %concatenate.55.ids_ref, bf16[256,768]{1,0:T(8,128)(2,1)} %bitcast_select_fusion.1.x_ref, f32[16,768]{1,0:T(8,128)} %get-tuple-element.167.vec_ref, f32[1,3072]{1,0:T(1,128)} %reshape.195.bias_ref, ...), custom_call_target="tpu_custom_call" | custom-call | tf_op jit(solution)/shard_map/mlp_forward/pallas_call | solution.py:414
  121.5 10.5 %collective-permute-done.28.refs_1_ = bf16[576,256]{1,0:T(8,128)(2,1)S(1)} collective-permute-done((bf16[576,256]{1,0:T(8,128)(2,1)}, bf16[576,256]{1,0:T(8,128)(2,1)S(1)}, u32[]{:S(2)}, u32[]{:S(2)}) %collective-permute-start.28) | collective-permute-done | bytes 294944 | tf_op jit(solution)/shard_map/ppermute | solution.py:52
  138.3 8.4 %attn_fwd.3 = (bf16[192,256]{1,0:T(8,128)(2,1)}, bf16[192,256]{1,0:T(8,128)(2,1)}, bf16[192,256]{1,0:T(8,128)(2,1)}, bf16[192,256]{1,0:T(8,128)(2,1)}, bf16[576,...) custom-call(s32[8]{0:T(128)} %pad_add_fusion.order_ref, ...), custom_call_target="tpu_custom_call" | custom-call | tf_op jit(solution)/shard_map/attn_fwd/pallas_call | solution.py:292
  155.3 12.1 %all-gather.5.cloned.1.call-done.pack_ref = bf16[768,6912]{1,0:T(8,128)(2,1)} async-done(((bf16[96,6912]{1,0:T(8,128)(2,1)}), bf16[768,6912]{1,0:T(8,128)(2,1)}) %all-gather.5.cloned.1.call-update) | async-done | bytes 10616848 | tf_op jit(solution)/shard_map/all_gather | solution.py:726
  168.0 9.7 %mlp_forward.3 = (bf16[256,768]{1,0:T(8,128)(2,1)}, f32[256,768]{1,0:T(8,128)}, f32[256,3072]{1,0:T(8,128)}, bf16[768,256]{1,0:T(8,128)(2,1)}) custom-call(s32[14]{0:T(128)} %concatenate.55.ids_ref, bf16[256,768]{1,0:T(8,128)(2,1)} %get-tuple-element.178.x_ref, f32[16,768]{1,0:T(8,128)} %get-tuple-element.179.vec_ref, f32[1,3072]{1,0:T(1,128)} %reshape.197.bias_ref, ...), custom_call_target="tpu_custom_call" | custom-call | tf_op jit(solution)/shard_map/mlp_forward/pallas_call | solution.py:414
  183.9 13.1 %mlp_backward.2 = (bf16[192,256]{1,0:T(8,128)(2,1)}, bf16[192,256]{1,0:T(8,128)(2,1)}, bf16[192,256]{1,0:T(8,128)(2,1)}, bf16[192,256]{1,0:T(8,128)(2,1)}, f32[2...) custom-call(s32[14]{0:T(128)} %concatenate.55.ids_ref, ...), custom_call_target="tpu_custom_call" | custom-call | tf_op jit(solution)/shard_map/mlp_backward/pallas_call | solution.py:489
  199.0 8.1 %early_grads.2 = bf16[768,6912]{1,0:T(8,128)(2,1)} custom-call(s32[14]{0:T(128)} %concatenate.55.ids_ref, bf16[256,768]{1,0:T(8,128)(2,1)} %get-tuple-element.206.middle_ref, bf16[256,3072]{1,0:T(8,128)(2,1)} %get-tuple-element.207.ghid_ref, bf16[768,256]{1,0:T(8,128)(2,1)} %get-tuple-element.208.mixed_ref, bf16[256,768]{1,0:T(8,128)(2,1)} %get-tuple-element.209.gattn_ref, ...), custom_call_target="tpu_custom_call" | custom-call | tf_op jit(solution)/shard_map/early_grads/pallas_call | solution.py:589
  207.8 8.7 %attn_bwd.2 = (bf16[576,256]{1,0:T(8,128)(2,1)}, bf16[576,256]{1,0:T(8,128)(2,1)}, bf16[576,256]{1,0:T(8,128)(2,1)}, bf16[576,256]{1,0:T(8,128)(2,1)}) custom-call(s32[8]{0:T(128)} %pad_add_fusion.order_ref, bf16[192,256]{1,0:T(8,128)(2,1)} %get-tuple-element.211.refs_0_, bf16[192,256]{1,0:T(8,128)(2,1)} %copy-done.62, bf16[192,256]{1,0:T(8,128)(2,1)} %copy-done.63, ...), custom_call_target="tpu_custom_call" | custom-call | tf_op jit(solution)/shard_map/attn_bwd/pallas_call | solution.py:321
  218.8 7.3 %collective-permute-done.41.refs_1_ = bf16[576,256]{1,0:T(8,128)(2,1)S(1)} collective-permute-done((bf16[576,256]{1,0:T(8,128)(2,1)}, bf16[576,256]{1,0:T(8,128)(2,1)S(1)}, u32[]{:S(2)}, u32[]{:S(2)}) %collective-permute-start.41) | collective-permute-done | bytes 294944 | tf_op jit(solution)/shard_map/ppermute | solution.py:52
  233.0 9.4 %qkv_backward.2 = (bf16[256,768]{1,0:T(8,128)(2,1)}, bf16[4,96,2432]{2,1,0:T(8,128)(2,1)}, bf16[4,96,2432]{2,1,0:T(8,128)(2,1)}) custom-call(s32[14]{0:T(128)} %concatenate.55.ids_ref, bf16[256,768]{1,0:T(8,128)(2,1)} %get-tuple-element.178.x_ref, f32[256,768]{1,0:T(8,128)} %get-tuple-element.199.ginner_ref, f32[16,768]{1,0:T(8,128)} %get-tuple-element.179.vec_ref, ...), custom_call_target="tpu_custom_call" | custom-call | tf_op jit(solution)/shard_map/qkv_backward/pallas_call | solution.py:653
  249.9 13.5 %mlp_backward.3 = (bf16[192,256]{1,0:T(8,128)(2,1)}, bf16[192,256]{1,0:T(8,128)(2,1)}, bf16[192,256]{1,0:T(8,128)(2,1)}, bf16[192,256]{1,0:T(8,128)(2,1)}, f32[2...) custom-call(s32[14]{0:T(128)} %concatenate.55.ids_ref, ...), custom_call_target="tpu_custom_call" | custom-call | tf_op jit(solution)/shard_map/mlp_backward/pallas_call | solution.py:489
  265.2 8.2 %early_grads.3 = (bf16[4,96,3840]{2,1,0:T(8,128)(2,1)}, bf16[4,96,3840]{2,1,0:T(8,128)(2,1)}, bf16[4,96,3072]{2,1,0:T(8,128)(2,1)}, bf16[4,96,3072]{2,1,0:T(8,128)(2,1)}) custom-call(s32[14]{0:T(128)} %concatenate.55.ids_ref, bf16[256,768]{1,0:T(8,128)(2,1)} %get-tuple-element.238.middle_ref, bf16[256,3072]{1,0:T(8,128)(2,1)} %get-tuple-element.239.ghid_ref, ...), custom_call_target="tpu_custom_call" | custom-call | tf_op jit(solution)/shard_map/early_grads/pallas_call | solution.py:589
  276.5 8.6 %attn_bwd.3 = (bf16[576,256]{1,0:T(8,128)(2,1)}, bf16[576,256]{1,0:T(8,128)(2,1)}, bf16[576,256]{1,0:T(8,128)(2,1)}, bf16[576,256]{1,0:T(8,128)(2,1)}) custom-call(s32[8]{0:T(128)} %pad_add_fusion.order_ref, bf16[192,256]{1,0:T(8,128)(2,1)} %get-tuple-element.247.refs_0_, bf16[192,256]{1,0:T(8,128)(2,1)} %copy-done.59, bf16[192,256]{1,0:T(8,128)(2,1)} %copy-done.60, ...), custom_call_target="tpu_custom_call" | custom-call | tf_op jit(solution)/shard_map/attn_bwd/pallas_call | solution.py:321
  285.1 11.7 %collective-permute-done.50 = bf16[2,48,2432]{2,1,0:T(8,128)(2,1)S(1)} collective-permute-done((bf16[2,48,2432]{2,1,0:T(8,128)(2,1)S(1)}, bf16[2,48,2432]{2,1,0:T(8,128)(2,1)S(1)}, u32[]{:S(2)}, u32[]{:S(2)}) %collective-permute-start.50) | collective-permute-done | bytes 466976 | tf_op jit(solution)/shard_map/ppermute | solution.py:731
  325.6 8.8 %qkv_backward.3 = (bf16[256,768]{1,0:T(8,128)(2,1)}, bf16[4,96,2432]{2,1,0:T(8,128)(2,1)}, bf16[4,96,2432]{2,1,0:T(8,128)(2,1)}) custom-call(s32[14]{0:T(128)} %concatenate.55.ids_ref, bf16[256,768]{1,0:T(8,128)(2,1)} %bitcast_select_fusion.1.x_ref, f32[256,768]{1,0:T(8,128)} %get-tuple-element.274.ginner_ref, f32[16,768]{1,0:T(8,128)} %get-tuple-element.167.vec_ref, ...), custom_call_target="tpu_custom_call" | custom-call | tf_op jit(solution)/shard_map/qkv_backward/pallas_call | solution.py:653
  335.8 7.2 %collective-permute-done.61 = bf16[2,48,3840]{2,1,0:T(8,128)(2,1)} collective-permute-done((bf16[2,48,3840]{2,1,0:T(8,128)(2,1)}, bf16[2,48,3840]{2,1,0:T(8,128)(2,1)}, u32[]{:S(2)}, u32[]{:S(2)}) %collective-permute-start.61) | collective-permute-done | bytes 737312 | tf_op jit(solution)/shard_map/ppermute | solution.py:731
  354.0 9.3 %collective-permute-done.60 = bf16[96,2432]{1,0:T(8,128)(2,1)S(1)} collective-permute-done((bf16[96,2432]{1,0:T(8,128)(2,1)S(1)}, bf16[96,2432]{1,0:T(8,128)(2,1)S(1)}, u32[]{:S(2)}, u32[]{:S(2)}) %collective-permute-start.60) | collective-permute-done | bytes 466976 | tf_op jit(solution)/shard_map/ppermute | solution.py:811
  365.1 8.2 %collective-permute-done.66 = bf16[48,3840]{1,0:T(8,128)(2,1)S(1)} collective-permute-done((bf16[48,3840]{1,0:T(8,128)(2,1)S(1)}, bf16[48,3840]{1,0:T(8,128)(2,1)S(1)}, u32[]{:S(2)}, u32[]{:S(2)}) %collective-permute-start.66) | collective-permute-done | bytes 368672 | tf_op jit(solution)/shard_map/ppermute | solution.py:731
  419.9 26.5 %collective-permute-start.86 = (bf16[96,2432]{1,0:T(8,128)(2,1)S(1)}, bf16[96,2432]{1,0:T(8,128)(2,1)S(1)}, u32[]{:S(2)}, u32[]{:S(2)}) collective-permute-start(bf16[96,2432]{1,0:T(8,128)(2,1)S(1)} %pad_maximum_fusion.3), channel_id=1, source_target_pairs={{0,4},{12,8},{1,5},{13,9},{2,6},{14,10},{3,7},{15,11},{16,20},{28,... | collective-permute-start | bytes 1400840 | tf_op jit(solution)/shard_map/ppermute | solution.py:811
  458.4 7.2 %collective-permute-done.84 = bf16[96,3840]{1,0:T(8,128)(2,1)S(1)} collective-permute-done((bf16[96,3840]{1,0:T(8,128)(2,1)S(1)}, bf16[96,3840]{1,0:T(8,128)(2,1)S(1)}, u32[]{:S(2)}, u32[]{:S(2)}) %collective-permute-start.84) | collective-permute-done | bytes 737312 | tf_op jit(solution)/shard_map/ppermute | solution.py:815
  466.7 11.2 %collective-permute-start.87 = (bf16[96,3840]{1,0:T(8,128)(2,1)S(1)}, bf16[96,3840]{1,0:T(8,128)(2,1)S(1)}, u32[]{:S(2)}, u32[]{:S(2)}) collective-permute-start(bf16[96,3840]{1,0:T(8,128)(2,1)S(1)} %broadcast_select_fusion.4), channel_id=1, source_target_pairs={{16,0},{17,1},{18,2},{19,3},{20,4},{21,5},{22,6},{23,7},{24,8},{25... | collective-permute-start | bytes 2211848 | tf_op jit(solution)/shard_map/ppermute | solution.py:819
  482.5 24.2 %collective-permute-done.88 = bf16[96,3072]{1,0:T(8,128)(2,1)S(1)} collective-permute-done((bf16[96,3072]{1,0:T(8,128)(2,1)S(1)}, bf16[96,3072]{1,0:T(8,128)(2,1)S(1)}, u32[]{:S(2)}, u32[]{:S(2)}) %collective-permute-start.88) | collective-permute-done | bytes 589856 | tf_op jit(solution)/shard_map/ppermute | solution.py:815
  (442 shorter events, 268.2 us)
Async XLA Ops:
  7.2 93.9 %all-gather.3.cloned.1.call-start = ((), (), s32[]{:S(2)}) async-start(), calls=%async_computation.1 | async-start | bytes 11943936 | tf_op jit(solution)/shard_map/all_gather | solution.py:726
  14.9 152.5 %all-gather.5.cloned.1.call-start = ((), (), s32[]{:S(2)}) async-start(), calls=%async_computation.2 | async-start | bytes 11943936 | tf_op jit(solution)/shard_map/all_gather | solution.py:726
  15.6 285.5 %reduce-scatter.2.cloned.1.call-start = ((), (), s32[]{:S(2)}) async-start(), calls=%async_computation.3 | async-start | bytes 11943936 | tf_op jit(solution)/shard_map/reduce_scatter | solution.py:801
  65.8 22.9 %collective-permute-start.21 = (bf16[48,2432]{1,0:T(8,128)(2,1)S(1)}, bf16[48,2432]{1,0:T(8,128)(2,1)}, u32[]{:S(2)}, u32[]{:S(2)}) collective-permute-start(bf16[48,2432]{1,0:T(8,128)(2,1)S(1)} %slice.356), channel_id=1, source_target_pairs={{0,2},{1,3},{2,0},{3,1},{4,6},{5,7},{6,4},{7,5},{8,10},{9,11},{10,... | collective-permute-start | bytes 700424 | tf_op jit(solution)/shard_map/ppermute | solution.py:731
  67.3 22.8 %collective-permute-start.22 = (bf16[48,2432]{1,0:T(8,128)(2,1)}, bf16[48,2432]{1,0:T(8,128)(2,1)}, u32[]{:S(2)}, u32[]{:S(2)}) collective-permute-start(bf16[48,2432]{1,0:T(8,128)(2,1)} %slice.357), channel_id=1, source_target_pairs={{0,1},{1,0},{2,3},{3,2},{4,5},{5,4},{6,7},{7,6},{8,9},{9,8},{10,11... | collective-permute-start | bytes 700424 | tf_op jit(solution)/shard_map/ppermute | solution.py:731
  73.9 36.9 %collective-permute-start.23 = (bf16[96,2432]{1,0:T(8,128)(2,1)S(1)}, bf16[96,2432]{1,0:T(8,128)(2,1)S(1)}, u32[]{:S(2)}, u32[]{:S(2)}) collective-permute-start(bf16[96,2432]{1,0:T(8,128)(2,1)S(1)} %get-tuple-element.374.refs_0_), channel_id=1, source_target_pairs={{0,16},{16,0},{1,17},{17,1},{2,18},{18,2},{3,19},{19,3},{4,20},{20... | collective-permute-start | bytes 1400840 | tf_op jit(solution)/shard_map/ppermute | solution.py:735
  75.9 34.9 %collective-permute-start.24 = (bf16[96,2432]{1,0:T(8,128)(2,1)S(1)}, bf16[96,2432]{1,0:T(8,128)(2,1)S(1)}, u32[]{:S(2)}, u32[]{:S(2)}) collective-permute-start(bf16[96,2432]{1,0:T(8,128)(2,1)S(1)} %collective-permute-done.19.refs_1_), channel_id=1, source_target_pairs={{0,16},{16,0},{1,17},{17,1},{2,18},{18,2},{3,19},{19,3},{4,20},{20... | collective-permute-start | bytes 1400840 | tf_op jit(solution)/shard_map/ppermute | solution.py:735
  78.7 32.1 %collective-permute-start.25 = (bf16[96,2432]{1,0:T(8,128)(2,1)S(1)}, bf16[96,2432]{1,0:T(8,128)(2,1)}, u32[]{:S(2)}, u32[]{:S(2)}) collective-permute-start(bf16[96,2432]{1,0:T(8,128)(2,1)S(1)} %collective-permute-done.20.refs_2_), channel_id=1, source_target_pairs={{0,16},{16,0},{1,17},{17,1},{2,18},{18,2},{3,19},{19,3},{4,20},{20... | collective-permute-start | bytes 1400840 | tf_op jit(solution)/shard_map/ppermute | solution.py:735
  120.2 62.9 %collective-permute-start.18 = (bf16[256,768]{1,0:T(8,128)(2,1)S(1)}, bf16[256,768]{1,0:T(8,128)(2,1)S(1)}, u32[]{:S(2)}, u32[]{:S(2)}) collective-permute-start(bf16[256,768]{1,0:T(8,128)(2,1)S(1)} %select_bitcast_fusion.4), channel_id=1, source_target_pairs={{0,8},{4,12},{24,16},{28,20},{1,9},{5,13},{25,17},{29,21},{2,10},{... | collective-permute-start | bytes 1179656 | tf_op jit(solution)/shard_map/ppermute | solution.py:64
  149.2 47.7 %collective-permute-start.34 = (bf16[256,768]{1,0:T(8,128)(2,1)S(1)}, bf16[256,768]{1,0:T(8,128)(2,1)S(1)}, u32[]{:S(2)}, u32[]{:S(2)}) collective-permute-start(bf16[256,768]{1,0:T(8,128)(2,1)S(1)} %copy-done.2), channel_id=1, source_target_pairs={{0,0},{4,4},{16,8},{20,12},{1,1},{5,5},{17,9},{21,13},{2,2},{6,6},... | collective-permute-start | bytes 1179656 | tf_op jit(solution)/shard_map/ppermute | solution.py:73
  154.2 42.8 %collective-permute-start.35 = (bf16[256,768]{1,0:T(8,128)(2,1)S(1)}, bf16[256,768]{1,0:T(8,128)(2,1)S(1)}, u32[]{:S(2)}, u32[]{:S(2)}) collective-permute-start(bf16[256,768]{1,0:T(8,128)(2,1)S(1)} %copy-done.2), channel_id=1, source_target_pairs={{8,0},{12,4},{24,8},{28,12},{9,1},{13,5},{25,9},{29,13},{10,2},{14... | collective-permute-start | bytes 1179656 | tf_op jit(solution)/shard_map/ppermute | solution.py:73
  273.5 25.3 %collective-permute-start.52 = (bf16[4,96,3840]{2,1,0:T(8,128)(2,1)}, bf16[4,96,3840]{2,1,0:T(8,128)(2,1)S(1)}, u32[]{:S(2)}, u32[]{:S(2)}) collective-permute-start(bf16[4,96,3840]{2,1,0:T(8,128)(2,1)} %get-tuple-element.261), channel_id=1, source_target_pairs={{0,16},{16,0},{1,17},{17,1},{2,18},{18,2},{3,19},{19,3},{4,20},{20... | collective-permute-start | bytes 8847368 | tf_op jit(solution)/shard_map/ppermute | solution.py:735
  274.1 24.7 %collective-permute-start.53 = (bf16[4,96,3072]{2,1,0:T(8,128)(2,1)}, bf16[4,96,3072]{2,1,0:T(8,128)(2,1)}, u32[]{:S(2)}, u32[]{:S(2)}) collective-permute-start(bf16[4,96,3072]{2,1,0:T(8,128)(2,1)} %get-tuple-element.262), channel_id=1, source_target_pairs={{0,16},{16,0},{1,17},{17,1},{2,18},{18,2},{3,19},{19,3},{4,20},{20... | collective-permute-start | bytes 7077896 | tf_op jit(solution)/shard_map/ppermute | solution.py:735
  315.0 28.0 %collective-permute-start.61 = (bf16[2,48,3840]{2,1,0:T(8,128)(2,1)}, bf16[2,48,3840]{2,1,0:T(8,128)(2,1)}, u32[]{:S(2)}, u32[]{:S(2)}) collective-permute-start(bf16[2,48,3840]{2,1,0:T(8,128)(2,1)} %get-tuple-element.355), channel_id=1, source_target_pairs={{0,1},{1,0},{2,3},{3,2},{4,5},{5,4},{6,7},{7,6},{8,9},{9,8},{10,11... | collective-permute-start | bytes 2211848 | tf_op jit(solution)/shard_map/ppermute | solution.py:731
  316.0 27.7 %collective-permute-start.62 = (bf16[2,48,3840]{2,1,0:T(8,128)(2,1)}, bf16[2,48,3840]{2,1,0:T(8,128)(2,1)}, u32[]{:S(2)}, u32[]{:S(2)}) collective-permute-start(bf16[2,48,3840]{2,1,0:T(8,128)(2,1)} %get-tuple-element.354), channel_id=1, source_target_pairs={{0,2},{1,3},{2,0},{3,1},{4,6},{5,7},{6,4},{7,5},{8,10},{9,11},{10,... | collective-permute-start | bytes 2211848 | tf_op jit(solution)/shard_map/ppermute | solution.py:731
  322.1 52.7 %collective-permute-start.54 = (bf16[96,6912]{1,0:T(8,128)(2,1)}, bf16[96,6912]{1,0:T(8,128)(2,1)}, u32[]{:S(2)}, u32[]{:S(2)}) collective-permute-start(bf16[96,6912]{1,0:T(8,128)(2,1)} %reduce-scatter.2.cloned.1.call-done), channel_id=1, source_target_pairs={{0,4},{12,8},{1,5},{13,9},{2,6},{14,10},{3,7},{15,11},{16,20},{28,... | collective-permute-start | bytes 3981320 | tf_op jit(solution)/shard_map/ppermute | solution.py:811
  334.4 28.9 %collective-permute-start.60 = (bf16[96,2432]{1,0:T(8,128)(2,1)S(1)}, bf16[96,2432]{1,0:T(8,128)(2,1)S(1)}, u32[]{:S(2)}, u32[]{:S(2)}) collective-permute-start(bf16[96,2432]{1,0:T(8,128)(2,1)S(1)} %pad_maximum_fusion.2), channel_id=1, source_target_pairs={{0,4},{12,8},{1,5},{13,9},{2,6},{14,10},{3,7},{15,11},{16,20},{28,... | collective-permute-start | bytes 1400840 | tf_op jit(solution)/shard_map/ppermute | solution.py:811
  346.3 29.3 %collective-permute-start.67 = (bf16[4,96,2432]{2,1,0:T(8,128)(2,1)S(1)}, bf16[4,96,2432]{2,1,0:T(8,128)(2,1)S(1)}, u32[]{:S(2)}, u32[]{:S(2)}) collective-permute-start(bf16[4,96,2432]{2,1,0:T(8,128)(2,1)S(1)} %copy-done.68), channel_id=1, source_target_pairs={{0,16},{16,0},{1,17},{17,1},{2,18},{18,2},{3,19},{19,3},{4,20},{20... | collective-permute-start | bytes 5603336 | tf_op jit(solution)/shard_map/ppermute | solution.py:735
  347.8 26.5 %collective-permute-start.68 = (bf16[256,768]{1,0:T(8,128)(2,1)S(1)}, bf16[256,768]{1,0:T(8,128)(2,1)S(1)}, u32[]{:S(2)}, u32[]{:S(2)}) collective-permute-start(bf16[256,768]{1,0:T(8,128)(2,1)S(1)} %copy-done.69), channel_id=1, source_target_pairs={{0,0},{4,4},{16,8},{20,12},{1,1},{5,5},{17,9},{21,13},{2,2},{6,6},... | collective-permute-start | bytes 1179656 | tf_op jit(solution)/shard_map/ppermute | solution.py:73
  384.3 33.4 %collective-permute-start.70 = (bf16[96,6912]{1,0:T(8,128)(2,1)S(1)}, bf16[96,6912]{1,0:T(8,128)(2,1)}, u32[]{:S(2)}, u32[]{:S(2)}) collective-permute-start(bf16[96,6912]{1,0:T(8,128)(2,1)S(1)} %add_convert_fusion.1), channel_id=1, source_target_pairs={{4,8},{8,4},{5,9},{9,5},{6,10},{10,6},{7,11},{11,7},{20,24},{24,20... | collective-permute-start | bytes 3981320 | tf_op jit(solution)/shard_map/ppermute | solution.py:813
  419.9 36.3 %collective-permute-start.86 = (bf16[96,2432]{1,0:T(8,128)(2,1)S(1)}, bf16[96,2432]{1,0:T(8,128)(2,1)S(1)}, u32[]{:S(2)}, u32[]{:S(2)}) collective-permute-start(bf16[96,2432]{1,0:T(8,128)(2,1)S(1)} %pad_maximum_fusion.3), channel_id=1, source_target_pairs={{0,4},{12,8},{1,5},{13,9},{2,6},{14,10},{3,7},{15,11},{16,20},{28,... | collective-permute-start | bytes 1400840 | tf_op jit(solution)/shard_map/ppermute | solution.py:811
  454.9 51.8 %collective-permute-start.82 = (bf16[96,6912]{1,0:T(8,128)(2,1)S(1)}, bf16[96,6912]{1,0:T(8,128)(2,1)S(1)}, u32[]{:S(2)}, u32[]{:S(2)}) collective-permute-start(bf16[96,6912]{1,0:T(8,128)(2,1)S(1)} %add_convert_fusion), channel_id=1, source_target_pairs={{4,0},{8,12},{5,1},{9,13},{6,2},{10,14},{7,3},{11,15},{20,16},{24,... | collective-permute-start | bytes 3981320 | tf_op jit(solution)/shard_map/ppermute | solution.py:815
  466.7 40.0 %collective-permute-start.87 = (bf16[96,3840]{1,0:T(8,128)(2,1)S(1)}, bf16[96,3840]{1,0:T(8,128)(2,1)S(1)}, u32[]{:S(2)}, u32[]{:S(2)}) collective-permute-start(bf16[96,3840]{1,0:T(8,128)(2,1)S(1)} %broadcast_select_fusion.4), channel_id=1, source_target_pairs={{16,0},{17,1},{18,2},{19,3},{20,4},{21,5},{22,6},{23,7},{24,8},{25... | collective-permute-start | bytes 2211848 | tf_op jit(solution)/shard_map/ppermute | solution.py:819
  478.1 28.6 %collective-permute-start.88 = (bf16[96,3072]{1,0:T(8,128)(2,1)S(1)}, bf16[96,3072]{1,0:T(8,128)(2,1)S(1)}, u32[]{:S(2)}, u32[]{:S(2)}) collective-permute-start(bf16[96,3072]{1,0:T(8,128)(2,1)S(1)} %add_convert_fusion.10), channel_id=1, source_target_pairs={{4,0},{8,12},{5,1},{9,13},{6,2},{10,14},{7,3},{11,15},{20,16},{24,... | collective-permute-start | bytes 1769480 | tf_op jit(solution)/shard_map/ppermute | solution.py:815
  (147 other events, 1519.1 us)
Sparse Core Ops, SparseCore 0:
  15.0 83.9 all-gather.2
  101.5 65.8 all-gather.4
  207.3 93.7 reduce-scatter.1

commit v4 on v3

--- a/solution.py
+++ b/solution.py
@@ -547,7 +547,7 @@
     ids_ref, middle_ref, ghid_ref, mixed_ref, gattn_ref, act_ref, glow_ref, *refs, parts, shards, ratio, apart
 ):
     if apart:
-        outs, (scratch, sems) = refs[:4], refs[4:]
+        outs, (scratch, sems) = refs[:2], refs[2:]
     else:
         pack_ref, scratch, sems = refs
     width = middle_ref.shape[1]
@@ -564,16 +564,12 @@
         cols = slice(i * width, (i + 1) * width)
         block = dot(middle_ref[...], ghid_ref[:, cols], 0, 0).astype(BF)
         scratch[:, (i + 1) * width : (i + 2) * width] = block
-    if apart:
-        copies += send_sides(
-            ids_ref, 2 * parts, scratch, 0, main, outs[:2], sems, 0, shards
-        )
-    else:
+    if not apart:
         send(slice(0, main), 0)
     write_down(act_ref, glow_ref, scratch, main, shards, ratio)
     if apart:
         copies += send_sides(
-            ids_ref, 2 * parts, scratch, main, ratio * width, outs[2:], sems, 2 * shards, shards
+            ids_ref, 2 * parts, scratch, 0, main + ratio * width, outs, sems, 0, shards
         )
     else:
         send(slice(main, main + ratio * width), 1)
@@ -585,15 +581,15 @@
     width = middle.shape[1]
     main, hidden = (1 + ratio) * width, ratio * width
     rows = width // shards // 2
-    up, down = shape((shards, rows, main), BF), shape((shards, rows, hidden), BF)
+    side = shape((shards, rows, main + hidden), BF)
     return pl.pallas_call(
         functools.partial(early_kernel, parts=parts, shards=shards, ratio=ratio, apart=apart),
         in_specs=[SMEM] + [VMEM] * 6,
-        out_specs=[HBM] * (4 if apart else 1),
-        out_shape=[up, up, down, down] if apart else [shape((width, main + hidden), BF)],
+        out_specs=[HBM] * (2 if apart else 1),
+        out_shape=[side, side] if apart else [shape((width, main + hidden), BF)],
         scratch_shapes=[
             pltpu.VMEM((width, main + hidden), BF),
-            pltpu.SemaphoreType.DMA((4 * shards,)),
+            pltpu.SemaphoreType.DMA((2 + 2 * shards,)),
         ],
         compiler_params=PARAMS,
         name="early_grads",
@@ -601,10 +597,10 @@
 
 
 def qkv_back_kernel(
-    ids_ref, x_ref, ginner_ref, vec_ref, table_ref, weight_hbm, *refs, parts, shards
+    ids_ref, x_ref, ginner_ref, vec_ref, table_ref, weight_hbm, *refs, parts, shards, apart
 ):
     pieces, refs = refs[:parts], refs[parts:]
-    gx_ref, keep_ref, send_ref, weight, whole, pack, sem = refs
+    gx_ref, *outs, weight, whole, pack, sem = refs
     width = x_ref.shape[1]
     main = 3 * width + LANES
     copies = []
@@ -638,23 +634,26 @@
     lane = lax.broadcasted_iota(jnp.int32, table.shape, 1)
     table = jnp.where(lane == 3, sums[0], jnp.where(lane == 4, sums[2], table))
     pack[:, 3 * width : main] = table.astype(BF)
-    copies += send_sides(
-        ids_ref, 2 * parts, pack, 0, main, (keep_ref, send_ref), sem, 1, shards
-    )
+    if apart:
+        copies += send_sides(ids_ref, 2 * parts, pack, 0, main, outs, sem, 1, shards)
+    else:
+        copies.append(pltpu.make_async_copy(pack, outs[0], sem.at[1]))
+        copies[0].start()
     for copy in copies:
         copy.wait()
 
 
-def qkv_backward(ids, x, ginner, vec, table, weight, pieces, shards):
+def qkv_backward(ids, x, ginner, vec, table, weight, pieces, shards, apart):
     parts = len(pieces)
     rows, width = x.shape
     total = 3 * width + LANES
     part = shape((shards, width // shards // 2, total), BF)
+    outs = [part, part] if apart else [shape((width, total), BF)]
     return pl.pallas_call(
-        functools.partial(qkv_back_kernel, parts=parts, shards=shards),
+        functools.partial(qkv_back_kernel, parts=parts, shards=shards, apart=apart),
         in_specs=[SMEM, VMEM, VMEM, VMEM, VMEM, HBM] + [VMEM] * parts,
-        out_specs=[VMEM, HBM, HBM],
-        out_shape=[shape((rows, width), BF), part, part],
+        out_specs=[VMEM] + [HBM] * len(outs),
+        out_shape=[shape((rows, width), BF)] + outs,
         scratch_shapes=[
             pltpu.VMEM((width, 3 * width), BF),
             pltpu.VMEM((parts * pieces[0].shape[0], rows), BF),
@@ -666,48 +665,52 @@
     )(ids, x, ginner, vec, table, weight, *pieces)
 
 
-def layer_forward(x, packs, rest, ids, order, parts, size, shards, ratio):
+def layer_forward(x, packs, rest, ids, order, parts, size, shards, ratio, back=None):
     sent, weight, vec = qkv_project(ids, x, packs, parts, size, shards)
     width = x.shape[1]
     depth = width // shards
     bias = vec[8 : 8 + ratio].reshape(ratio, shards, depth).transpose(1, 0, 2).reshape(1, -1)
-    mixed, attn_saved = attention_forward(exchange(sent), order, size)
+    received = exchange(sent)
+    returned = None
+    if back is not None:
+        *received, back = lax.optimization_barrier((*received, back))
+        returned = return_rows(back, 0)
+    mixed, attn_saved = attention_forward(received, order, size)
+    received = exchange(mixed)
+    if back is not None:
+        tied = lax.optimization_barrier((*received, *returned))
+        received, returned = tied[:parts], tied[parts:]
     result, inner, hidden, mixed = mlp_forward(
-        ids, x, vec, bias, rest, exchange(mixed), shards, ratio
+        ids, x, vec, bias, rest, received, shards, ratio
     )
-    return result, (x, weight, vec, attn_saved, inner, hidden, mixed)
+    return result, (x, weight, vec, attn_saved, inner, hidden, mixed), returned
 
 
 def layer_backward(saved, grad, rest, ids, order, parts, size, shards, ratio, layer, background):
     x, weight, vec, attn_saved, inner, hidden, mixed = saved
-    width = x.shape[1]
-    depth = width // shards
     last = layer == 0
+    column = (1 + ratio) * x.shape[1]
     sent, (ginner, gattn, ghid, act, middle, table) = mlp_backward(
         ids, grad, inner, hidden, vec, rest, parts, size, shards, ratio
     )
-    sent = background.slot(sent)
+    received = exchange(background.slot("A", sent))
     early = early_grads(ids, middle, ghid, mixed, gattn, act, grad, parts, shards, ratio, last)
-    received = exchange(sent)
-    both = background.slot([*received, *early])
-    received, early = both[:parts], both[parts:]
+    tied = lax.optimization_barrier((*received, *early))
+    received, early = tied[:parts], tied[parts:]
     if last:
-        tasks = [
-            background.add(permuted_task(*early[:2], layer, (0, 1, 0), (0, 0, 0))),
-            background.add(permuted_task(*early[2:], layer, (0, 1, 1), (0, 0, 0))),
-        ]
+        first = background.add("B", permuted_task(*early, layer, background, "B", column))
     else:
-        tasks = [background.add(offloaded_task(early[0], layer, 5, 1, (1, 1, 1)))]
+        first = background.add("C", offloaded_task(*early, layer, background, "C", column))
     sent = attention_backward(received, attn_saved, order, size)
-    sent = background.slot(sent)
-    received = background.slot(exchange(sent))
-    grad_x, keep, send = qkv_backward(
-        ids, x, ginner, vec, table, weight, received, shards
-    )
-    grad_x, keep, send = background.slot([grad_x, keep, send])
-    slack = ((0, 0, 0), (0, 0, 0)) if last else ((0, 1, 0), (1, 0, 0))
-    tasks.append(background.add(permuted_task(keep, send, layer, *slack)))
-    return grad_x, tasks
+    received = background.slot("BC" if last else "", exchange(sent))
+    results = qkv_backward(ids, x, ginner, vec, table, weight, received, shards, last)
+    grad_x, *late = lax.optimization_barrier(tuple(results))
+    if last:
+        (grad_x,) = background.slot("BC", [grad_x])
+        second = background.add("A", permuted_task(*late, layer, background, "A", None))
+    else:
+        second = background.add("D", offloaded_task(*late, layer, background, "D", None))
+    return grad_x, first, second
 
 
 def blocks_to_columns(value, parts):
@@ -746,18 +749,19 @@
     def __init__(self):
         self.tasks = []
 
-    def add(self, task):
-        entry = {"task": task, "result": None}
+    def add(self, lane, task):
+        entry = {"lane": lane, "task": task, "result": None}
         entry["flight"] = next(task)
         self.tasks.append(entry)
         return entry
 
-    def slot(self, values):
-        waiting = [entry for entry in self.tasks if entry["flight"] is not None]
+    def slot(self, lanes, values=()):
+        waiting = [e for e in self.tasks if e["flight"] is not None and e["lane"] in lanes]
         flat = list(values)
         for entry in waiting:
             flat += entry["flight"]
-        flat = list(lax.optimization_barrier(tuple(flat)))
+        if len(flat) > 0:
+            flat = list(lax.optimization_barrier(tuple(flat)))
         values, flat = flat[: len(values)], flat[len(values) :]
         for entry in waiting:
             count = len(entry["flight"])
@@ -768,51 +772,52 @@
                 entry["flight"], entry["result"] = None, stop.value
         return values
 
-    def finish(self):
+    def finish(self, lanes):
         while any(entry["flight"] is not None for entry in self.tasks):
-            self.slot([])
-
-
-def held(flight, slots):
-    for _ in range(slots):
-        yield []
-    return (yield flight)
-
-
-def permuted_task(keep, send, layer, slack, ctx_slack):
-    (received,) = yield from held([swap_cores(send)], slack[0])
+            for lane in lanes:
+                self.slot(lane)
+
+
+def permuted_task(keep, send, layer, background, lane, column):
+    (received,) = yield [swap_cores(send)]
     rows = keep.shape[1] // 2
 
     def summed(slots, side):
         return sum_pair(keep[slots, side], received[slots, side])
 
     top, low = slice(0, rows), slice(rows, 2 * rows)
-    by_x, by_y = yield from held(
-        [across(summed(slice(1, 4, 2), top), 1), across(summed(slice(2, 4), low), 2)], slack[1]
-    )
+    by_x, by_y = yield [
+        across(summed(slice(1, 4, 2), top), 1),
+        across(summed(slice(2, 4), low), 2),
+    ]
     first = sum_pair(summed(slice(0, 4, 2), top), by_x)
     second = sum_pair(summed(slice(0, 2), low), by_y)
-    by_y, by_x = yield from held([across(first[1], 2), across(second[1], 1)], slack[2])
+    by_y, by_x = yield [across(first[1], 2), across(second[1], 1)]
     value = jnp.concatenate([sum_pair(first[0], by_y), sum_pair(second[0], by_x)])
-    return (yield from ctx_task(value, layer, ctx_slack))
-
-
-def offloaded_task(pack, layer, wait, pause, ctx_slack):
-    value = lax.psum_scatter(pack, SHARDS, scatter_dimension=0, tiled=True)
-    (value,) = yield from held([value], wait)
-    for _ in range(pause):
-        yield []
-    return (yield from ctx_task(value, layer, ctx_slack))
-
-
-def ctx_task(value, layer, slack):
+    return (yield from split_task(value, layer, background, lane, column))
+
+
+def offloaded_task(pack, layer, background, lane, column):
+    (value,) = yield [lax.psum_scatter(pack, SHARDS, scatter_dimension=0, tiled=True)]
+    return (yield from split_task(value, layer, background, lane, column))
+
+
+def split_task(value, layer, background, lane, column):
+    if column is None:
+        return (yield from ctx_task(value, layer))
+    other = background.add(lane, ctx_task(value[:, column:], layer))
+    mine = yield from ctx_task(value[:, :column], layer)
+    return mine, other
+
+
+def ctx_task(value, layer):
     if lax.axis_size("ctx") == 4:
         index = lax.axis_index("ctx")
-        (received,) = yield from held([lax.ppermute(value, "ctx", [(0, 1), (3, 2)])], slack[0])
+        (received,) = yield [lax.ppermute(value, "ctx", [(0, 1), (3, 2)])]
         value = sum_pair(value, received)
-        (received,) = yield from held([lax.ppermute(value, "ctx", [(1, 2), (2, 1)])], slack[1])
+        (received,) = yield [lax.ppermute(value, "ctx", [(1, 2), (2, 1)])]
         value = sum_pair(value, received)
-        (received,) = yield from held([lax.ppermute(value, "ctx", [(1, 0), (2, 3)])], slack[2])
+        (received,) = yield [lax.ppermute(value, "ctx", [(1, 0), (2, 3)])]
         value = jnp.where((index == 0) | (index == 3), received, value)
     else:
         value = lax.psum(value, "ctx")
@@ -820,9 +825,10 @@
     return value, other
 
 
-def return_task(values, layers):
-    flight = [moved for value, layer in zip(values, layers) for moved in return_rows(value, layer)]
-    flight = yield flight
+def return_task(value, layer, pause):
+    for _ in range(pause):
+        yield []
+    flight = yield return_rows(value, layer)
     return flight
 
 
@@ -863,23 +869,24 @@
     first0, first1 = gather_pieces(first0), gather_pieces(first1)
     rest0, rest1 = gather(rest0), gather(rest1)
     sizes = (ids, order, ctx, size, shards, ratio)
-    out0, saved0 = layer_forward(x, first0, rest0, *sizes)
+    out0, saved0, _ = layer_forward(x, first0, rest0, *sizes)
     late_cot, out0 = lax.optimization_barrier((cotangent[:, 0], out0))
-    out1, saved1 = layer_forward(out0, first1, rest1, *sizes)
+    out1, saved1, back_out0 = layer_forward(out0, first1, rest1, *sizes, out0)
     cot = bring_rows(late_cot, core, base)
     background = Background()
-    outs = background.add(return_task([out0, out1], [0, 1]))
-    grad1, reduced1 = layer_backward(saved1, cot, rest1, *sizes, 1, background)
-    back1 = background.add(return_task([grad1], [1]))
-    grad0, reduced0 = layer_backward(saved0, grad1, rest0, *sizes, 0, background)
-    back0 = background.add(return_task([grad0], [0]))
-    background.finish()
+    grad1, early1, late1 = layer_backward(saved1, cot, rest1, *sizes, 1, background)
+    back1 = background.add("A", return_task(jnp.concatenate([out1, grad1], axis=1), 1, 0))
+    grad0, early0, late0 = layer_backward(saved0, grad1, rest0, *sizes, 0, background)
+    back0 = background.add("A", return_task(grad0, 0, 2))
+    background.finish(("A", "BD", "C"))
 
     def chosen(values0, values1):
         return jnp.stack([jnp.where(core == 0, a, b) for a, b in zip(values0, values1)])
 
-    layer_outputs = chosen(outs["result"][:cores], outs["result"][cores:])
-    input_grads = chosen(back0["result"], back1["result"]).astype(F32)
+    layer_outputs = chosen(back_out0, [value[:, :width] for value in back1["result"]])
+    input_grads = chosen(
+        back0["result"], [value[:, width:] for value in back1["result"]]
+    ).astype(F32)
 
     def joined(pair0, pair1):
         return jnp.where(
@@ -888,13 +895,10 @@
             jnp.concatenate([pair1[1], pair1[0]]),
         ).astype(F32)
 
-    (early0, down0, late0), (early1, late1) = [
-        [entry["result"] for entry in reduced] for reduced in (reduced0, reduced1)
-    ]
-    main = (1 + ratio) * width
-    early = joined(early0, [value[:, :main] for value in early1])
-    late = joined(late0, late1)
-    down = joined(down0, [value[:, main:] for value in early1])
+    (up0, down0), (up1, down1) = early0["result"], early1["result"]
+    early = joined(up0, up1)
+    late = joined(late0["result"], late1["result"])
+    down = joined(down0["result"], down1["result"])
     table = late[:, 3 * width :].T
     return (
         layer_outputs[None, :, None],

time: 550 us -> 560 us (1.018)
  waiting for transfers between devices: 169 us -> 206 us
  starting transfers between devices: 165 us -> 142 us
  other arithmetic: 36.4 us -> 30.3 us
    ppermute x15 -> x18, waiting for transfers between devices: 48.1 us -> 98.5 us  [the longest x6 56.2 us: ctx_task(): received, = (yield [lax.ppermute(value, 'ctx', [(1, 0), (2, 3)])])]
    ppermute x24 -> x16, waiting for transfers between devices: 49.6 us -> 28.9 us  [across(): return lax.ppermute(value, 'fsdp', [(i, i ^ bit) for i in range(count)])]
    ppermute x24, waiting for transfers between devices: 49.1 us -> 60.4 us  [exchange(): moved.append(lax.ppermute(pieces[d], GROUP, pairs))]
    ppermute x15 -> x18, starting transfers between devices: 53.7 us -> 43.7 us  [the longest x6 30.2 us: ctx_task(): received, = (yield [lax.ppermute(value, 'ctx', [(0, 1), (3, 2)])])]
    ppermute x24 -> x16, starting transfers between devices: 24.4 us -> 16.3 us  [across(): return lax.ppermute(value, 'fsdp', [(i, i ^ bit) for i in range(count)])]
    ppermute x14 -> x12, starting transfers between devices: 17.7 us -> 12.7 us  [swap_cores(): return lax.ppermute(value, 'section', [(0, 1), (1, 0)])]
    unnamed x153 -> x130, local copies, waits for them, and re-layouts: 14.3 us -> 12.1 us
    convert_element_type x26 -> x20, other arithmetic: 21.6 us -> 20.4 us  [sum_pair(): return (a.astype(F32) + b.astype(F32)).astype(BF)]
  transfers between devices with their start and end apart: 97 -> 90, of which waited for: 31 -> 28; matrix products, arithmetic and copies ran while one was open for 7% -> 6% of each run, Pallas kernels for 24% -> 19%
where the time goes in v4:
time: 560 us; the launch traced here: 549 us
  waiting for transfers between devices  206 us (37%)
  starting transfers between devices  142 us (25%)
  Pallas kernels  129 us (23%)
  other arithmetic  30.3 us (5%)
  local copies, waits for them, and re-layouts  27.5 us (5%)
  between operations  15.4 us (3%)
    ppermute x24, waiting for transfers between devices, exchange(): moved.append(lax.ppermute(pieces[d], GROUP, pairs))  60.4 us
    ppermute x6, waiting for transfers between devices, ctx_task(): received, = (yield [lax.ppermute(value, 'ctx', [(1, 0), (2, 3)])])  56.2 us
    ppermute x6, waiting for transfers between devices, ctx_task(): received, = (yield [lax.ppermute(value, 'ctx', [(0, 1), (3, 2)])])  42.3 us
    ppermute x6, starting transfers between devices, ctx_task(): received, = (yield [lax.ppermute(value, 'ctx', [(0, 1), (3, 2)])])  30.2 us
    ppermute x16, waiting for transfers between devices, across(): return lax.ppermute(value, 'fsdp', [(i, i ^ bit) for i in range(count)])  28.9 us
    ppermute x6, starting transfers between devices, ctx_task(): other, = (yield [lax.ppermute(value, 'section', [(1 - layer, layer)])])  26.9 us
    pallas_call x2, Pallas kernels, mlp_backward(): pl.pallas_call(functools.partial(mlp_back_kernel, parts=parts, shards=sha...  26.7 us
    ppermute x6, starting transfers between devices, return_rows(): lax.ppermute(value, GROUP, [(place_of(z // half, m * half + z % half), pl...  21.3 us
  transfers between devices with their start and end apart: 90, of which 28 were waited for; matrix products, arithmetic and copies ran while one was open for 6% of the time, Pallas kernels for 19%

profile of v4, /device:TPU:1, one launch (start us, length us, event | category | flops | bytes accessed | tf_op | source)
XLA Modules:
  0.0 549.4 jit_solution(5686226361706165726)
XLA Ops:
  78.8 8.4 %attn_fwd.2 = (bf16[192,256]{1,0:T(8,128)(2,1)}, bf16[192,256]{1,0:T(8,128)(2,1)}, bf16[192,256]{1,0:T(8,128)(2,1)}, bf16[192,256]{1,0:T(8,128)(2,1)}, bf16[576,...) custom-call(s32[8]{0:T(128)} %pad_add_fusion.order_ref, ...), custom_call_target="tpu_custom_call" | custom-call | tf_op jit(solution)/shard_map/attn_fwd/pallas_call | solution.py:292
  99.8 9.7 %mlp_forward.2 = (bf16[256,768]{1,0:T(8,128)(2,1)}, f32[256,768]{1,0:T(8,128)}, f32[256,3072]{1,0:T(8,128)}, bf16[768,256]{1,0:T(8,128)(2,1)}) custom-call(s32[14]{0:T(128)} %concatenate.53.ids_ref, bf16[256,768]{1,0:T(8,128)(2,1)} %bitcast_select_fusion.1.x_ref, f32[16,768]{1,0:T(8,128)} %get-tuple-element.154.vec_ref, f32[1,3072]{1,0:T(1,128)} %reshape.187.bias_ref, ...), custom_call_target="tpu_custom_call" | custom-call | tf_op jit(solution)/shard_map/mlp_forward/pallas_call | solution.py:414
  120.3 10.6 %collective-permute-done.27.refs_1_ = bf16[576,256]{1,0:T(8,128)(2,1)S(1)} collective-permute-done((bf16[576,256]{1,0:T(8,128)(2,1)}, bf16[576,256]{1,0:T(8,128)(2,1)S(1)}, u32[]{:S(2)}, u32[]{:S(2)}) %collective-permute-start.27) | collective-permute-done | bytes 294944 | tf_op jit(solution)/shard_map/ppermute | solution.py:52
  145.8 8.4 %attn_fwd.3 = (bf16[192,256]{1,0:T(8,128)(2,1)}, bf16[192,256]{1,0:T(8,128)(2,1)}, bf16[192,256]{1,0:T(8,128)(2,1)}, bf16[192,256]{1,0:T(8,128)(2,1)}, bf16[576,...) custom-call(s32[8]{0:T(128)} %pad_add_fusion.order_ref, ...), custom_call_target="tpu_custom_call" | custom-call | tf_op jit(solution)/shard_map/attn_fwd/pallas_call | solution.py:292
  159.9 7.0 %all-gather.5.cloned.1.call-done.pack_ref = bf16[768,6912]{1,0:T(8,128)(2,1)} async-done(((bf16[96,6912]{1,0:T(8,128)(2,1)}), bf16[768,6912]{1,0:T(8,128)(2,1)}) %all-gather.5.cloned.1.call-update) | async-done | bytes 10616848 | tf_op jit(solution)/shard_map/all_gather | solution.py:729
  166.9 9.8 %mlp_forward.3 = (bf16[256,768]{1,0:T(8,128)(2,1)}, f32[256,768]{1,0:T(8,128)}, f32[256,3072]{1,0:T(8,128)}, bf16[768,256]{1,0:T(8,128)(2,1)}) custom-call(s32[14]{0:T(128)} %concatenate.53.ids_ref, bf16[256,768]{1,0:T(8,128)(2,1)} %get-tuple-element.177.x_ref, f32[16,768]{1,0:T(8,128)} %get-tuple-element.180.vec_ref, f32[1,3072]{1,0:T(1,128)} %reshape.189.bias_ref, ...), custom_call_target="tpu_custom_call" | custom-call | tf_op jit(solution)/shard_map/mlp_forward/pallas_call | solution.py:414
  176.7 13.1 %mlp_backward.2 = (bf16[192,256]{1,0:T(8,128)(2,1)}, bf16[192,256]{1,0:T(8,128)(2,1)}, bf16[192,256]{1,0:T(8,128)(2,1)}, bf16[192,256]{1,0:T(8,128)(2,1)}, f32[2...) custom-call(s32[14]{0:T(128)} %concatenate.53.ids_ref, ...), custom_call_target="tpu_custom_call" | custom-call | tf_op jit(solution)/shard_map/mlp_backward/pallas_call | solution.py:489
  191.9 8.1 %early_grads.2 = bf16[768,6912]{1,0:T(8,128)(2,1)} custom-call(s32[14]{0:T(128)} %concatenate.53.ids_ref, bf16[256,768]{1,0:T(8,128)(2,1)} %get-tuple-element.198.middle_ref, bf16[256,3072]{1,0:T(8,128)(2,1)} %get-tuple-element.199.ghid_ref, bf16[768,256]{1,0:T(8,128)(2,1)} %get-tuple-element.200.mixed_ref, bf16[256,768]{1,0:T(8,128)(2,1)} %get-tuple-element.201.gattn_ref, ...), custom_call_target="tpu_custom_call" | custom-call | tf_op jit(solution)/shard_map/early_grads/pallas_call | solution.py:585
  200.9 8.7 %attn_bwd.2 = (bf16[576,256]{1,0:T(8,128)(2,1)}, bf16[576,256]{1,0:T(8,128)(2,1)}, bf16[576,256]{1,0:T(8,128)(2,1)}, bf16[576,256]{1,0:T(8,128)(2,1)}) custom-call(s32[8]{0:T(128)} %pad_add_fusion.order_ref, bf16[192,256]{1,0:T(8,128)(2,1)} %get-tuple-element.203.refs_0_, bf16[192,256]{1,0:T(8,128)(2,1)} %copy-done.52, bf16[192,256]{1,0:T(8,128)(2,1)} %copy-done.54, ...), custom_call_target="tpu_custom_call" | custom-call | tf_op jit(solution)/shard_map/attn_bwd/pallas_call | solution.py:321
  211.7 7.4 %collective-permute-done.39.refs_1_ = bf16[576,256]{1,0:T(8,128)(2,1)S(1)} collective-permute-done((bf16[576,256]{1,0:T(8,128)(2,1)}, bf16[576,256]{1,0:T(8,128)(2,1)S(1)}, u32[]{:S(2)}, u32[]{:S(2)}) %collective-permute-start.39) | collective-permute-done | bytes 294944 | tf_op jit(solution)/shard_map/ppermute | solution.py:52
  225.7 9.1 %qkv_backward.2 = (bf16[256,768]{1,0:T(8,128)(2,1)}, bf16[768,2432]{1,0:T(8,128)(2,1)}) custom-call(s32[14]{0:T(128)} %concatenate.53.ids_ref, bf16[256,768]{1,0:T(8,128)(2,1)} %get-tuple-element.177.x_ref, f32[256,768]{1,0:T(8,128)} %get-tuple-element.187.ginner_ref, f32[16,768]{1,0:T(8,128)} %get-tuple-element.180.vec_ref, ...), custom_call_target="tpu_custom_call" | custom-call | tf_op jit(solution)/shard_map/qkv_backward/pallas_call | solution.py:652
  240.4 13.6 %mlp_backward.3 = (bf16[192,256]{1,0:T(8,128)(2,1)}, bf16[192,256]{1,0:T(8,128)(2,1)}, bf16[192,256]{1,0:T(8,128)(2,1)}, bf16[192,256]{1,0:T(8,128)(2,1)}, f32[2...) custom-call(s32[14]{0:T(128)} %concatenate.53.ids_ref, ...), custom_call_target="tpu_custom_call" | custom-call | tf_op jit(solution)/shard_map/mlp_backward/pallas_call | solution.py:489
  260.7 9.3 %early_grads.3 = (bf16[4,96,6912]{2,1,0:T(8,128)(2,1)}, bf16[4,96,6912]{2,1,0:T(8,128)(2,1)}) custom-call(s32[14]{0:T(128)} %concatenate.53.ids_ref, bf16[256,768]{1,0:T(8,128)(2,1)} %get-tuple-element.236.middle_ref, bf16[256,3072]{1,0:T(8,128)(2,1)} %get-tuple-element.237.ghid_ref, bf16[768,256]{1,0:T(8,128)(2,1)} %get-tuple-element.238.mixed_ref, ...), custom_call_target="tpu_custom_call" | custom-call | tf_op jit(solution)/shard_map/early_grads/pallas_call | solution.py:585
  270.8 8.7 %attn_bwd.3 = (bf16[576,256]{1,0:T(8,128)(2,1)}, bf16[576,256]{1,0:T(8,128)(2,1)}, bf16[576,256]{1,0:T(8,128)(2,1)}, bf16[576,256]{1,0:T(8,128)(2,1)}) custom-call(s32[8]{0:T(128)} %pad_add_fusion.order_ref, bf16[192,256]{1,0:T(8,128)(2,1)} %get-tuple-element.243.refs_0_, bf16[192,256]{1,0:T(8,128)(2,1)} %copy-done.53, bf16[192,256]{1,0:T(8,128)(2,1)} %copy-done.55, ...), custom_call_target="tpu_custom_call" | custom-call | tf_op jit(solution)/shard_map/attn_bwd/pallas_call | solution.py:321
  281.8 7.3 %collective-permute-done.47.refs_1_ = bf16[576,256]{1,0:T(8,128)(2,1)} collective-permute-done((bf16[576,256]{1,0:T(8,128)(2,1)}, bf16[576,256]{1,0:T(8,128)(2,1)}, u32[]{:S(2)}, u32[]{:S(2)}) %collective-permute-start.47) | collective-permute-done | bytes 294944 | tf_op jit(solution)/shard_map/ppermute | solution.py:52
  308.0 8.8 %qkv_backward.3 = (bf16[256,768]{1,0:T(8,128)(2,1)}, bf16[4,96,2432]{2,1,0:T(8,128)(2,1)}, bf16[4,96,2432]{2,1,0:T(8,128)(2,1)}) custom-call(s32[14]{0:T(128)} %concatenate.53.ids_ref, bf16[256,768]{1,0:T(8,128)(2,1)} %bitcast_select_fusion.1.x_ref, f32[256,768]{1,0:T(8,128)} %get-tuple-element.229.ginner_ref, f32[16,768]{1,0:T(8,128)} %get-tuple-element.154.vec_ref, ...), custom_call_target="tpu_custom_call" | custom-call | tf_op jit(solution)/shard_map/qkv_backward/pallas_call | solution.py:652
  317.5 14.8 %collective-permute-done.59 = bf16[96,3072]{1,0:T(8,128)(2,1)} collective-permute-done((bf16[96,3072]{1,0:T(8,128)(2,1)}, bf16[96,3072]{1,0:T(8,128)(2,1)}, u32[]{:S(2)}, u32[]{:S(2)}) %collective-permute-start.59) | collective-permute-done | bytes 589856 | tf_op jit(solution)/shard_map/ppermute | solution.py:816
  333.7 7.9 %collective-permute-start.60 = (bf16[256,768]{1,0:T(8,128)(2,1)}, bf16[256,768]{1,0:T(8,128)(2,1)}, u32[]{:S(2)}, u32[]{:S(2)}) collective-permute-start(bf16[256,768]{1,0:T(8,128)(2,1)} %get-tuple-element.268), channel_id=1, source_target_pairs={{0,0},{4,4},{16,8},{20,12},{1,1},{5,5},{17,9},{21,13},{2,2},{6,6},... | collective-permute-start | bytes 1179656 | tf_op jit(solution)/shard_map/ppermute | solution.py:73
  354.3 16.7 %collective-permute-done.66 = bf16[48,6912]{1,0:T(8,128)(2,1)S(1)} collective-permute-done((bf16[48,6912]{1,0:T(8,128)(2,1)S(1)}, bf16[48,6912]{1,0:T(8,128)(2,1)S(1)}, u32[]{:S(2)}, u32[]{:S(2)}) %collective-permute-start.66) | collective-permute-done | bytes 663584 | tf_op jit(solution)/shard_map/ppermute | solution.py:734
  377.0 18.4 %collective-permute-start.68 = (bf16[96,2432]{1,0:T(8,128)(2,1)S(1)}, bf16[96,2432]{1,0:T(8,128)(2,1)S(1)}, u32[]{:S(2)}, u32[]{:S(2)}) collective-permute-start(bf16[96,2432]{1,0:T(8,128)(2,1)S(1)} %copy-done.28), channel_id=1, source_target_pairs={{0,4},{12,8},{1,5},{13,9},{2,6},{14,10},{3,7},{15,11},{16,20},{28,... | collective-permute-start | bytes 1400840 | tf_op jit(solution)/shard_map/ppermute | solution.py:816
  416.9 15.8 %collective-permute-done.69 = bf16[96,3840]{1,0:T(8,128)(2,1)S(1)} collective-permute-done((bf16[96,3840]{1,0:T(8,128)(2,1)S(1)}, bf16[96,3840]{1,0:T(8,128)(2,1)S(1)}, u32[]{:S(2)}, u32[]{:S(2)}) %collective-permute-start.69) | collective-permute-done | bytes 737312 | tf_op jit(solution)/shard_map/ppermute | solution.py:816
  449.3 47.5 %collective-permute-done.64 = bf16[96,2432]{1,0:T(8,128)(2,1)S(1)} collective-permute-done((bf16[96,2432]{1,0:T(8,128)(2,1)S(1)}, bf16[96,2432]{1,0:T(8,128)(2,1)S(1)}, u32[]{:S(2)}, u32[]{:S(2)}) %collective-permute-start.64) | collective-permute-done | bytes 466976 | tf_op jit(solution)/shard_map/ppermute | solution.py:820
  498.2 8.7 %collective-permute-done.74 = bf16[96,2432]{1,0:T(8,128)(2,1)S(1)} collective-permute-done((bf16[96,2432]{1,0:T(8,128)(2,1)S(1)}, bf16[96,2432]{1,0:T(8,128)(2,1)S(1)}, u32[]{:S(2)}, u32[]{:S(2)}) %collective-permute-start.74) | collective-permute-done | bytes 466976 | tf_op jit(solution)/shard_map/ppermute | solution.py:820
  506.9 15.2 %collective-permute-start.65 = (bf16[96,2432]{1,0:T(8,128)(2,1)S(1)}, bf16[96,2432]{1,0:T(8,128)(2,1)S(1)}, u32[]{:S(2)}, u32[]{:S(2)}) collective-permute-start(bf16[96,2432]{1,0:T(8,128)(2,1)S(1)} %broadcast_select_fusion.8), channel_id=1, source_target_pairs={{16,0},{17,1},{18,2},{19,3},{20,4},{21,5},{22,6},{23,7},{24,8},{25... | collective-permute-start | bytes 1400840 | tf_op jit(solution)/shard_map/ppermute | solution.py:824
  (392 shorter events, 241.2 us)
Async XLA Ops:
  7.2 92.6 %all-gather.3.cloned.1.call-start = ((), (), s32[]{:S(2)}) async-start(), calls=%async_computation.2 | async-start | bytes 11943936 | tf_op jit(solution)/shard_map/all_gather | solution.py:729
  14.8 152.1 %all-gather.5.cloned.1.call-start = ((), (), s32[]{:S(2)}) async-start(), calls=%async_computation.3 | async-start | bytes 11943936 | tf_op jit(solution)/shard_map/all_gather | solution.py:729
  15.6 279.9 %reduce-scatter.3.cloned.1.call-start = ((), (), s32[]{:S(2)}) async-start(), calls=%async_computation.4 | async-start | bytes 11943936 | tf_op jit(solution)/shard_map/reduce_scatter | solution.py:801
  72.0 37.5 %collective-permute-start.22 = (bf16[96,2432]{1,0:T(8,128)(2,1)S(1)}, bf16[96,2432]{1,0:T(8,128)(2,1)S(1)}, u32[]{:S(2)}, u32[]{:S(2)}) collective-permute-start(bf16[96,2432]{1,0:T(8,128)(2,1)S(1)} %get-tuple-element.340.refs_0_), channel_id=1, source_target_pairs={{0,16},{16,0},{1,17},{17,1},{2,18},{18,2},{3,19},{19,3},{4,20},{20... | collective-permute-start | bytes 1400840 | tf_op jit(solution)/shard_map/ppermute | solution.py:738
  73.1 36.4 %collective-permute-start.24 = (bf16[96,2432]{1,0:T(8,128)(2,1)S(1)}, bf16[96,2432]{1,0:T(8,128)(2,1)S(1)}, u32[]{:S(2)}, u32[]{:S(2)}) collective-permute-start(bf16[96,2432]{1,0:T(8,128)(2,1)S(1)} %collective-permute-done.19.refs_2_), channel_id=1, source_target_pairs={{0,16},{16,0},{1,17},{17,1},{2,18},{18,2},{3,19},{19,3},{4,20},{20... | collective-permute-start | bytes 1400840 | tf_op jit(solution)/shard_map/ppermute | solution.py:738
  77.5 32.1 %collective-permute-start.23 = (bf16[96,2432]{1,0:T(8,128)(2,1)S(1)}, bf16[96,2432]{1,0:T(8,128)(2,1)}, u32[]{:S(2)}, u32[]{:S(2)}) collective-permute-start(bf16[96,2432]{1,0:T(8,128)(2,1)S(1)} %collective-permute-done.18.refs_1_), channel_id=1, source_target_pairs={{0,16},{16,0},{1,17},{17,1},{2,18},{18,2},{3,19},{19,3},{4,20},{20... | collective-permute-start | bytes 1400840 | tf_op jit(solution)/shard_map/ppermute | solution.py:738
  119.0 35.3 %collective-permute-start.35 = (bf16[256,768]{1,0:T(8,128)(2,1)S(1)}, bf16[256,768]{1,0:T(8,128)(2,1)S(1)}, u32[]{:S(2)}, u32[]{:S(2)}) collective-permute-start(bf16[256,768]{1,0:T(8,128)(2,1)S(1)} %select_bitcast_fusion.4), channel_id=1, source_target_pairs={{0,8},{4,12},{24,16},{28,20},{1,9},{5,13},{25,17},{29,21},{2,10},{... | collective-permute-start | bytes 1179656 | tf_op jit(solution)/shard_map/ppermute | solution.py:64
  200.7 173.2 %reduce-scatter.5.cloned.1.call-start = ((), (), s32[]{:S(2)}) async-start(), calls=%async_computation.5 | async-start | bytes 4202496 | tf_op jit(solution)/shard_map/reduce_scatter | solution.py:801
  300.2 32.1 %collective-permute-start.58 = (bf16[2,48,6912]{2,1,0:T(8,128)(2,1)}, bf16[2,48,6912]{2,1,0:T(8,128)(2,1)S(1)}, u32[]{:S(2)}, u32[]{:S(2)}) collective-permute-start(bf16[2,48,6912]{2,1,0:T(8,128)(2,1)} %get-tuple-element.328), channel_id=1, source_target_pairs={{0,2},{1,3},{2,0},{3,1},{4,6},{5,7},{6,4},{7,5},{8,10},{9,11},{10,... | collective-permute-start | bytes 3981320 | tf_op jit(solution)/shard_map/ppermute | solution.py:734
  300.9 31.4 %collective-permute-start.57 = (bf16[2,48,6912]{2,1,0:T(8,128)(2,1)}, bf16[2,48,6912]{2,1,0:T(8,128)(2,1)}, u32[]{:S(2)}, u32[]{:S(2)}) collective-permute-start(bf16[2,48,6912]{2,1,0:T(8,128)(2,1)} %get-tuple-element.329), channel_id=1, source_target_pairs={{0,1},{1,0},{2,3},{3,2},{4,5},{5,4},{6,7},{7,6},{8,9},{9,8},{10,11... | collective-permute-start | bytes 3981320 | tf_op jit(solution)/shard_map/ppermute | solution.py:734
  302.0 30.2 %collective-permute-start.56 = (bf16[96,3840]{1,0:T(8,128)(2,1)S(1)}, bf16[96,3840]{1,0:T(8,128)(2,1)}, u32[]{:S(2)}, u32[]{:S(2)}) collective-permute-start(bf16[96,3840]{1,0:T(8,128)(2,1)S(1)} %slice.235), channel_id=1, source_target_pairs={{0,4},{12,8},{1,5},{13,9},{2,6},{14,10},{3,7},{15,11},{16,20},{28,... | collective-permute-start | bytes 2211848 | tf_op jit(solution)/shard_map/ppermute | solution.py:816
  316.8 34.6 %collective-permute-start.51 = (bf16[4,96,2432]{2,1,0:T(8,128)(2,1)}, bf16[4,96,2432]{2,1,0:T(8,128)(2,1)S(1)}, u32[]{:S(2)}, u32[]{:S(2)}) collective-permute-start(bf16[4,96,2432]{2,1,0:T(8,128)(2,1)} %get-tuple-element.261), channel_id=1, source_target_pairs={{0,16},{16,0},{1,17},{17,1},{2,18},{18,2},{3,19},{19,3},{4,20},{20... | collective-permute-start | bytes 5603336 | tf_op jit(solution)/shard_map/ppermute | solution.py:738
  332.2 68.9 %collective-permute-start.61 = (bf16[256,768]{1,0:T(8,128)(2,1)}, bf16[256,768]{1,0:T(8,128)(2,1)}, u32[]{:S(2)}, u32[]{:S(2)}) collective-permute-start(bf16[256,768]{1,0:T(8,128)(2,1)} %get-tuple-element.268), channel_id=1, source_target_pairs={{8,0},{12,4},{24,8},{28,12},{9,1},{13,5},{25,9},{29,13},{10,2},{14... | collective-permute-start | bytes 1179656 | tf_op jit(solution)/shard_map/ppermute | solution.py:73
  333.7 68.8 %collective-permute-start.60 = (bf16[256,768]{1,0:T(8,128)(2,1)}, bf16[256,768]{1,0:T(8,128)(2,1)}, u32[]{:S(2)}, u32[]{:S(2)}) collective-permute-start(bf16[256,768]{1,0:T(8,128)(2,1)} %get-tuple-element.268), channel_id=1, source_target_pairs={{0,0},{4,4},{16,8},{20,12},{1,1},{5,5},{17,9},{21,13},{2,2},{6,6},... | collective-permute-start | bytes 1179656 | tf_op jit(solution)/shard_map/ppermute | solution.py:73
  345.0 30.6 %collective-permute-start.81 = (bf16[96,3072]{1,0:T(8,128)(2,1)}, bf16[96,3072]{1,0:T(8,128)(2,1)}, u32[]{:S(2)}, u32[]{:S(2)}) collective-permute-start(bf16[96,3072]{1,0:T(8,128)(2,1)} %add_convert_fusion.11), channel_id=1, source_target_pairs={{4,8},{8,4},{5,9},{9,5},{6,10},{10,6},{7,11},{11,7},{20,24},{24,20... | collective-permute-start | bytes 1769480 | tf_op jit(solution)/shard_map/ppermute | solution.py:818
  377.0 30.0 %collective-permute-start.68 = (bf16[96,2432]{1,0:T(8,128)(2,1)S(1)}, bf16[96,2432]{1,0:T(8,128)(2,1)S(1)}, u32[]{:S(2)}, u32[]{:S(2)}) collective-permute-start(bf16[96,2432]{1,0:T(8,128)(2,1)S(1)} %copy-done.28), channel_id=1, source_target_pairs={{0,4},{12,8},{1,5},{13,9},{2,6},{14,10},{3,7},{15,11},{16,20},{28,... | collective-permute-start | bytes 1400840 | tf_op jit(solution)/shard_map/ppermute | solution.py:816
  402.5 30.2 %collective-permute-start.69 = (bf16[96,3840]{1,0:T(8,128)(2,1)S(1)}, bf16[96,3840]{1,0:T(8,128)(2,1)S(1)}, u32[]{:S(2)}, u32[]{:S(2)}) collective-permute-start(bf16[96,3840]{1,0:T(8,128)(2,1)S(1)} %fusion.7), channel_id=1, source_target_pairs={{0,4},{12,8},{1,5},{13,9},{2,6},{14,10},{3,7},{15,11},{16,20},{28,... | collective-permute-start | bytes 2211848 | tf_op jit(solution)/shard_map/ppermute | solution.py:816
  404.1 30.5 %collective-permute-start.83 = (bf16[96,3072]{1,0:T(8,128)(2,1)S(1)}, bf16[96,3072]{1,0:T(8,128)(2,1)S(1)}, u32[]{:S(2)}, u32[]{:S(2)}) collective-permute-start(bf16[96,3072]{1,0:T(8,128)(2,1)S(1)} %add_convert_fusion.10), channel_id=1, source_target_pairs={{4,0},{8,12},{5,1},{9,13},{6,2},{10,14},{7,3},{11,15},{20,16},{24,... | collective-permute-start | bytes 1769480 | tf_op jit(solution)/shard_map/ppermute | solution.py:820
  407.0 35.7 %collective-permute-start.62 = (bf16[96,2432]{1,0:T(8,128)(2,1)S(1)}, bf16[96,2432]{1,0:T(8,128)(2,1)S(1)}, u32[]{:S(2)}, u32[]{:S(2)}) collective-permute-start(bf16[96,2432]{1,0:T(8,128)(2,1)S(1)} %pad_maximum_fusion.1), channel_id=1, source_target_pairs={{0,4},{12,8},{1,5},{13,9},{2,6},{14,10},{3,7},{15,11},{16,20},{28,... | collective-permute-start | bytes 1400840 | tf_op jit(solution)/shard_map/ppermute | solution.py:816
  435.5 94.7 %collective-permute-start.85 = (bf16[96,3072]{1,0:T(8,128)(2,1)S(1)}, bf16[96,3072]{1,0:T(8,128)(2,1)S(1)}, u32[]{:S(2)}, u32[]{:S(2)}) collective-permute-start(bf16[96,3072]{1,0:T(8,128)(2,1)S(1)} %broadcast_select_fusion.5), channel_id=1, source_target_pairs={{0,16},{1,17},{2,18},{3,19},{4,20},{5,21},{6,22},{7,23},{8,24},{9,... | collective-permute-start | bytes 1769480 | tf_op jit(solution)/shard_map/ppermute | solution.py:824
  442.7 91.2 %collective-permute-start.84 = (bf16[96,3840]{1,0:T(8,128)(2,1)S(1)}, bf16[96,3840]{1,0:T(8,128)(2,1)S(1)}, u32[]{:S(2)}, u32[]{:S(2)}) collective-permute-start(bf16[96,3840]{1,0:T(8,128)(2,1)S(1)} %broadcast_select_fusion.3), channel_id=1, source_target_pairs={{0,16},{1,17},{2,18},{3,19},{4,20},{5,21},{6,22},{7,23},{8,24},{9,... | collective-permute-start | bytes 2211848 | tf_op jit(solution)/shard_map/ppermute | solution.py:824
  445.0 77.1 %collective-permute-start.75 = (bf16[96,3840]{1,0:T(8,128)(2,1)S(1)}, bf16[96,3840]{1,0:T(8,128)(2,1)S(1)}, u32[]{:S(2)}, u32[]{:S(2)}) collective-permute-start(bf16[96,3840]{1,0:T(8,128)(2,1)S(1)} %add_convert_fusion.8), channel_id=1, source_target_pairs={{4,0},{8,12},{5,1},{9,13},{6,2},{10,14},{7,3},{11,15},{20,16},{24,... | collective-permute-start | bytes 2211848 | tf_op jit(solution)/shard_map/ppermute | solution.py:820
  446.6 50.2 %collective-permute-start.64 = (bf16[96,2432]{1,0:T(8,128)(2,1)S(1)}, bf16[96,2432]{1,0:T(8,128)(2,1)S(1)}, u32[]{:S(2)}, u32[]{:S(2)}) collective-permute-start(bf16[96,2432]{1,0:T(8,128)(2,1)S(1)} %add_convert_fusion.16), channel_id=1, source_target_pairs={{4,0},{8,12},{5,1},{9,13},{6,2},{10,14},{7,3},{11,15},{20,16},{24,... | collective-permute-start | bytes 1400840 | tf_op jit(solution)/shard_map/ppermute | solution.py:820
  448.0 58.8 %collective-permute-start.74 = (bf16[96,2432]{1,0:T(8,128)(2,1)S(1)}, bf16[96,2432]{1,0:T(8,128)(2,1)S(1)}, u32[]{:S(2)}, u32[]{:S(2)}) collective-permute-start(bf16[96,2432]{1,0:T(8,128)(2,1)S(1)} %add_convert_fusion.14), channel_id=1, source_target_pairs={{4,0},{8,12},{5,1},{9,13},{6,2},{10,14},{7,3},{11,15},{20,16},{24,... | collective-permute-start | bytes 1400840 | tf_op jit(solution)/shard_map/ppermute | solution.py:820
  (127 other events, 1445.7 us)
Sparse Core Ops, SparseCore 0:
  15.0 83.3 all-gather.2
  100.8 66.0 all-gather.4
  200.2 81.8 reduce-scatter.2
  308.1 56.3 reduce-scatter.4

commit v5 on v4

--- a/solution.py
+++ b/solution.py
@@ -597,7 +597,7 @@
 
 
 def qkv_back_kernel(
-    ids_ref, x_ref, ginner_ref, vec_ref, table_ref, weight_hbm, *refs, parts, shards, apart
+    ids_ref, x_ref, ginner_ref, vec_ref, table_ref, weight_hbm, *refs, parts, shards
 ):
     pieces, refs = refs[:parts], refs[parts:]
     gx_ref, *outs, weight, whole, pack, sem = refs
@@ -634,26 +634,21 @@
     lane = lax.broadcasted_iota(jnp.int32, table.shape, 1)
     table = jnp.where(lane == 3, sums[0], jnp.where(lane == 4, sums[2], table))
     pack[:, 3 * width : main] = table.astype(BF)
-    if apart:
-        copies += send_sides(ids_ref, 2 * parts, pack, 0, main, outs, sem, 1, shards)
-    else:
-        copies.append(pltpu.make_async_copy(pack, outs[0], sem.at[1]))
-        copies[0].start()
+    copies += send_sides(ids_ref, 2 * parts, pack, 0, main, outs, sem, 1, shards)
     for copy in copies:
         copy.wait()
 
 
-def qkv_backward(ids, x, ginner, vec, table, weight, pieces, shards, apart):
+def qkv_backward(ids, x, ginner, vec, table, weight, pieces, shards):
     parts = len(pieces)
     rows, width = x.shape
     total = 3 * width + LANES
     part = shape((shards, width // shards // 2, total), BF)
-    outs = [part, part] if apart else [shape((width, total), BF)]
     return pl.pallas_call(
-        functools.partial(qkv_back_kernel, parts=parts, shards=shards, apart=apart),
+        functools.partial(qkv_back_kernel, parts=parts, shards=shards),
         in_specs=[SMEM, VMEM, VMEM, VMEM, VMEM, HBM] + [VMEM] * parts,
-        out_specs=[VMEM] + [HBM] * len(outs),
-        out_shape=[shape((rows, width), BF)] + outs,
+        out_specs=[VMEM, HBM, HBM],
+        out_shape=[shape((rows, width), BF), part, part],
         scratch_shapes=[
             pltpu.VMEM((width, 3 * width), BF),
             pltpu.VMEM((parts * pieces[0].shape[0], rows), BF),
@@ -693,23 +688,27 @@
     sent, (ginner, gattn, ghid, act, middle, table) = mlp_backward(
         ids, grad, inner, hidden, vec, rest, parts, size, shards, ratio
     )
-    received = exchange(background.slot("A", sent))
+    received = exchange(background.slot("AD", sent))
     early = early_grads(ids, middle, ghid, mixed, gattn, act, grad, parts, shards, ratio, last)
     tied = lax.optimization_barrier((*received, *early))
     received, early = tied[:parts], tied[parts:]
     if last:
-        first = background.add("B", permuted_task(*early, layer, background, "B", column))
+        first = background.add("B", permuted_task(*early, layer, background, column))
     else:
-        first = background.add("C", offloaded_task(*early, layer, background, "C", column))
+        first = background.add("C", offloaded_task(*early, layer, background, column, 1))
     sent = attention_backward(received, attn_saved, order, size)
-    received = background.slot("BC" if last else "", exchange(sent))
-    results = qkv_backward(ids, x, ginner, vec, table, weight, received, shards, last)
+    if last:
+        sent = background.slot("BCD", sent)
+    received = exchange(sent)
+    if last:
+        received = background.slot("CD", received)
+    results = qkv_backward(ids, x, ginner, vec, table, weight, received, shards)
     grad_x, *late = lax.optimization_barrier(tuple(results))
     if last:
-        (grad_x,) = background.slot("BC", [grad_x])
-        second = background.add("A", permuted_task(*late, layer, background, "A", None))
+        (grad_x,) = background.slot("ABCD", [grad_x])
+        second = background.add("A", permuted_task(*late, layer, background, None))
     else:
-        second = background.add("D", offloaded_task(*late, layer, background, "D", None))
+        second = background.add("D", permuted_task(*late, layer, background, None, 1, 4))
     return grad_x, first, second
 
 
@@ -772,13 +771,18 @@
                 entry["flight"], entry["result"] = None, stop.value
         return values
 
-    def finish(self, lanes):
+    def finish(self):
         while any(entry["flight"] is not None for entry in self.tasks):
-            for lane in lanes:
-                self.slot(lane)
-
-
-def permuted_task(keep, send, layer, background, lane, column):
+            self.slot("ABCD")
+
+
+def idle(values, slots):
+    for _ in range(slots):
+        values = yield list(values)
+    return values
+
+
+def permuted_task(keep, send, layer, background, column, hold=0, before=0):
     (received,) = yield [swap_cores(send)]
     rows = keep.shape[1] // 2
 
@@ -790,27 +794,32 @@
         across(summed(slice(1, 4, 2), top), 1),
         across(summed(slice(2, 4), low), 2),
     ]
+    by_x, by_y = yield from idle([by_x, by_y], hold)
     first = sum_pair(summed(slice(0, 4, 2), top), by_x)
     second = sum_pair(summed(slice(0, 2), low), by_y)
     by_y, by_x = yield [across(first[1], 2), across(second[1], 1)]
     value = jnp.concatenate([sum_pair(first[0], by_y), sum_pair(second[0], by_x)])
-    return (yield from split_task(value, layer, background, lane, column))
-
-
-def offloaded_task(pack, layer, background, lane, column):
-    (value,) = yield [lax.psum_scatter(pack, SHARDS, scatter_dimension=0, tiled=True)]
-    return (yield from split_task(value, layer, background, lane, column))
-
-
-def split_task(value, layer, background, lane, column):
+    (value,) = yield from idle([value], before)
+    return (yield from split_task(value, layer, background, column))
+
+
+def offloaded_task(pack, layer, background, column, after):
+    value = lax.psum_scatter(pack, SHARDS, scatter_dimension=0, tiled=True)
+    (value,) = yield [value]
+    (value,) = yield from idle([value], after)
+    return (yield from split_task(value, layer, background, column))
+
+
+def split_task(value, layer, background, column):
     if column is None:
         return (yield from ctx_task(value, layer))
-    other = background.add(lane, ctx_task(value[:, column:], layer))
+    other = background.add("D", ctx_task(value[:, column:], layer, 1))
     mine = yield from ctx_task(value[:, :column], layer)
     return mine, other
 
 
-def ctx_task(value, layer):
+def ctx_task(value, layer, before=0):
+    (value,) = yield from idle([value], before)
     if lax.axis_size("ctx") == 4:
         index = lax.axis_index("ctx")
         (received,) = yield [lax.ppermute(value, "ctx", [(0, 1), (3, 2)])]
@@ -826,8 +835,7 @@
 
 
 def return_task(value, layer, pause):
-    for _ in range(pause):
-        yield []
+    (value,) = yield from idle([value], pause)
     flight = yield return_rows(value, layer)
     return flight
 
@@ -877,8 +885,8 @@
     grad1, early1, late1 = layer_backward(saved1, cot, rest1, *sizes, 1, background)
     back1 = background.add("A", return_task(jnp.concatenate([out1, grad1], axis=1), 1, 0))
     grad0, early0, late0 = layer_backward(saved0, grad1, rest0, *sizes, 0, background)
-    back0 = background.add("A", return_task(grad0, 0, 2))
-    background.finish(("A", "BD", "C"))
+    back0 = background.add("A", return_task(grad0, 0, 5))
+    background.finish()
 
     def chosen(values0, values1):
         return jnp.stack([jnp.where(core == 0, a, b) for a, b in zip(values0, values1)])

time: 560 us -> 522 us (0.932)
  waiting for transfers between devices: 206 us -> 172 us
    ppermute x6, waiting for transfers between devices: 56.2 us -> 27.1 us  [ctx_task(): received, = (yield [lax.ppermute(value, 'ctx', [(1, 0), (2, 3)])])]
    ppermute x16 -> x20, waiting for transfers between devices: 28.9 us -> 55.1 us  [across(): return lax.ppermute(value, 'fsdp', [(i, i ^ bit) for i in range(count)])]
    ppermute x6, waiting for transfers between devices: 42.3 us -> 17.3 us  [ctx_task(): received, = (yield [lax.ppermute(value, 'ctx', [(0, 1), (3, 2)])])]
    ppermute x6, starting transfers between devices: 26.9 us -> 14.7 us  [ctx_task(): other, = (yield [lax.ppermute(value, 'section', [(1 - layer, layer)])])]
    ppermute x16 -> x20, starting transfers between devices: 16.3 us -> 22.6 us  [across(): return lax.ppermute(value, 'fsdp', [(i, i ^ bit) for i in range(count)])]
    ppermute x24, waiting for transfers between devices: 60.4 us -> 54.3 us  [exchange(): moved.append(lax.ppermute(pieces[d], GROUP, pairs))]
    unnamed x130 -> x140, local copies, waits for them, and re-layouts: 12.1 us -> 9.58 us
    ppermute x12 -> x13, starting transfers between devices: 12.7 us -> 13.6 us  [swap_cores(): return lax.ppermute(value, 'section', [(0, 1), (1, 0)])]
  transfers between devices with their start and end apart: 90 -> 94, of which waited for: 28 -> 37; matrix products, arithmetic and copies ran while one was open for 6% -> 7% of each run, Pallas kernels for 19% -> 21%
where the time goes in v5:
time: 522 us; the launch traced here: 513 us
  waiting for transfers between devices  172 us (33%)
  starting transfers between devices  139 us (27%)
  Pallas kernels  128 us (25%)
  other arithmetic  32 us (6%)
  local copies, waits for them, and re-layouts  25.6 us (5%)
  between operations  15.3 us (3%)
    ppermute x20, waiting for transfers between devices, across(): return lax.ppermute(value, 'fsdp', [(i, i ^ bit) for i in range(count)])  55.1 us
    ppermute x24, waiting for transfers between devices, exchange(): moved.append(lax.ppermute(pieces[d], GROUP, pairs))  54.3 us
    ppermute x6, starting transfers between devices, ctx_task(): received, = (yield [lax.ppermute(value, 'ctx', [(0, 1), (3, 2)])])  35.6 us
    ppermute x6, waiting for transfers between devices, ctx_task(): received, = (yield [lax.ppermute(value, 'ctx', [(1, 0), (2, 3)])])  27.1 us
    pallas_call x2, Pallas kernels, mlp_backward(): pl.pallas_call(functools.partial(mlp_back_kernel, parts=parts, shards=sha...  26.3 us
    ppermute x20, starting transfers between devices, across(): return lax.ppermute(value, 'fsdp', [(i, i ^ bit) for i in range(count)])  22.6 us
    convert_element_type x24, other arithmetic, sum_pair(): return (a.astype(F32) + b.astype(F32)).astype(BF)  20.3 us
    pallas_call x2, Pallas kernels, mlp_forward(): pl.pallas_call(functools.partial(mlp_kernel, parts=parts, shards=shards,...  19.3 us
  transfers between devices with their start and end apart: 94, of which 37 were waited for; matrix products, arithmetic and copies ran while one was open for 7% of the time, Pallas kernels for 21%

profile of v5, /device:TPU:1, one launch (start us, length us, event | category | flops | bytes accessed | tf_op | source)
XLA Modules:
  0.0 512.9 jit_solution(15693299671043823019)
XLA Ops:
  78.7 8.4 %attn_fwd.2 = (bf16[192,256]{1,0:T(8,128)(2,1)}, bf16[192,256]{1,0:T(8,128)(2,1)}, bf16[192,256]{1,0:T(8,128)(2,1)}, bf16[192,256]{1,0:T(8,128)(2,1)}, bf16[576,...) custom-call(s32[8]{0:T(128)} %pad_add_fusion.order_ref, ...), custom_call_target="tpu_custom_call" | custom-call | tf_op jit(solution)/shard_map/attn_fwd/pallas_call | solution.py:292
  99.5 9.6 %mlp_forward.2 = (bf16[256,768]{1,0:T(8,128)(2,1)}, f32[256,768]{1,0:T(8,128)}, f32[256,3072]{1,0:T(8,128)}, bf16[768,256]{1,0:T(8,128)(2,1)}) custom-call(s32[14]{0:T(128)} %concatenate.56.ids_ref, bf16[256,768]{1,0:T(8,128)(2,1)} %bitcast_select_fusion.1.x_ref, f32[16,768]{1,0:T(8,128)} %get-tuple-element.177.vec_ref, f32[1,3072]{1,0:T(1,128)} %reshape.191.bias_ref, ...), custom_call_target="tpu_custom_call" | custom-call | tf_op jit(solution)/shard_map/mlp_forward/pallas_call | solution.py:414
  119.8 10.6 %collective-permute-done.27.refs_1_ = bf16[576,256]{1,0:T(8,128)(2,1)S(1)} collective-permute-done((bf16[576,256]{1,0:T(8,128)(2,1)}, bf16[576,256]{1,0:T(8,128)(2,1)S(1)}, u32[]{:S(2)}, u32[]{:S(2)}) %collective-permute-start.27) | collective-permute-done | bytes 294944 | tf_op jit(solution)/shard_map/ppermute | solution.py:52
  145.3 8.4 %attn_fwd.3 = (bf16[192,256]{1,0:T(8,128)(2,1)}, bf16[192,256]{1,0:T(8,128)(2,1)}, bf16[192,256]{1,0:T(8,128)(2,1)}, bf16[192,256]{1,0:T(8,128)(2,1)}, bf16[576,...) custom-call(s32[8]{0:T(128)} %pad_add_fusion.order_ref, ...), custom_call_target="tpu_custom_call" | custom-call | tf_op jit(solution)/shard_map/attn_fwd/pallas_call | solution.py:292
  159.6 7.3 %all-gather.5.cloned.1.call-done.pack_ref = bf16[768,6912]{1,0:T(8,128)(2,1)} async-done(((bf16[96,6912]{1,0:T(8,128)(2,1)}), bf16[768,6912]{1,0:T(8,128)(2,1)}) %all-gather.5.cloned.1.call-update) | async-done | bytes 10616848 | tf_op jit(solution)/shard_map/all_gather | solution.py:728
  166.9 9.6 %mlp_forward.3 = (bf16[256,768]{1,0:T(8,128)(2,1)}, f32[256,768]{1,0:T(8,128)}, f32[256,3072]{1,0:T(8,128)}, bf16[768,256]{1,0:T(8,128)(2,1)}) custom-call(s32[14]{0:T(128)} %concatenate.56.ids_ref, bf16[256,768]{1,0:T(8,128)(2,1)} %get-tuple-element.200.x_ref, f32[16,768]{1,0:T(8,128)} %get-tuple-element.203.vec_ref, f32[1,3072]{1,0:T(1,128)} %reshape.193.bias_ref, ...), custom_call_target="tpu_custom_call" | custom-call | tf_op jit(solution)/shard_map/mlp_forward/pallas_call | solution.py:414
  176.6 13.1 %mlp_backward.2 = (bf16[192,256]{1,0:T(8,128)(2,1)}, bf16[192,256]{1,0:T(8,128)(2,1)}, bf16[192,256]{1,0:T(8,128)(2,1)}, bf16[192,256]{1,0:T(8,128)(2,1)}, f32[2...) custom-call(s32[14]{0:T(128)} %concatenate.56.ids_ref, ...), custom_call_target="tpu_custom_call" | custom-call | tf_op jit(solution)/shard_map/mlp_backward/pallas_call | solution.py:489
  191.8 8.1 %early_grads.2 = bf16[768,6912]{1,0:T(8,128)(2,1)} custom-call(s32[14]{0:T(128)} %concatenate.56.ids_ref, bf16[256,768]{1,0:T(8,128)(2,1)} %get-tuple-element.221.middle_ref, bf16[256,3072]{1,0:T(8,128)(2,1)} %get-tuple-element.222.ghid_ref, bf16[768,256]{1,0:T(8,128)(2,1)} %get-tuple-element.223.mixed_ref, bf16[256,768]{1,0:T(8,128)(2,1)} %get-tuple-element.224.gattn_ref, ...), custom_call_target="tpu_custom_call" | custom-call | tf_op jit(solution)/shard_map/early_grads/pallas_call | solution.py:585
  200.7 8.6 %attn_bwd.2 = (bf16[576,256]{1,0:T(8,128)(2,1)}, bf16[576,256]{1,0:T(8,128)(2,1)}, bf16[576,256]{1,0:T(8,128)(2,1)}, bf16[576,256]{1,0:T(8,128)(2,1)}) custom-call(s32[8]{0:T(128)} %pad_add_fusion.order_ref, bf16[192,256]{1,0:T(8,128)(2,1)} %get-tuple-element.226.refs_0_, bf16[192,256]{1,0:T(8,128)(2,1)} %copy-done.57, bf16[192,256]{1,0:T(8,128)(2,1)} %copy-done.58, ...), custom_call_target="tpu_custom_call" | custom-call | tf_op jit(solution)/shard_map/attn_bwd/pallas_call | solution.py:321
  211.3 7.4 %collective-permute-done.39.refs_1_ = bf16[576,256]{1,0:T(8,128)(2,1)S(1)} collective-permute-done((bf16[576,256]{1,0:T(8,128)(2,1)}, bf16[576,256]{1,0:T(8,128)(2,1)S(1)}, u32[]{:S(2)}, u32[]{:S(2)}) %collective-permute-start.39) | collective-permute-done | bytes 294944 | tf_op jit(solution)/shard_map/ppermute | solution.py:52
  225.4 9.1 %qkv_backward.2 = (bf16[256,768]{1,0:T(8,128)(2,1)}, bf16[4,96,2432]{2,1,0:T(8,128)(2,1)}, bf16[4,96,2432]{2,1,0:T(8,128)(2,1)}) custom-call(s32[14]{0:T(128)} %concatenate.56.ids_ref, bf16[256,768]{1,0:T(8,128)(2,1)} %get-tuple-element.200.x_ref, f32[256,768]{1,0:T(8,128)} %get-tuple-element.210.ginner_ref, f32[16,768]{1,0:T(8,128)} %get-tuple-element.203.vec_ref, ...), custom_call_target="tpu_custom_call" | custom-call | tf_op jit(solution)/shard_map/qkv_backward/pallas_call | solution.py:647
  241.7 13.3 %mlp_backward.3 = (bf16[192,256]{1,0:T(8,128)(2,1)}, bf16[192,256]{1,0:T(8,128)(2,1)}, bf16[192,256]{1,0:T(8,128)(2,1)}, bf16[192,256]{1,0:T(8,128)(2,1)}, f32[2...) custom-call(s32[14]{0:T(128)} %concatenate.56.ids_ref, ...), custom_call_target="tpu_custom_call" | custom-call | tf_op jit(solution)/shard_map/mlp_backward/pallas_call | solution.py:489
  261.2 9.4 %early_grads.3 = (bf16[4,96,6912]{2,1,0:T(8,128)(2,1)}, bf16[4,96,6912]{2,1,0:T(8,128)(2,1)}) custom-call(s32[14]{0:T(128)} %concatenate.56.ids_ref, bf16[256,768]{1,0:T(8,128)(2,1)} %get-tuple-element.253.middle_ref, bf16[256,3072]{1,0:T(8,128)(2,1)} %get-tuple-element.254.ghid_ref, bf16[768,256]{1,0:T(8,128)(2,1)} %get-tuple-element.255.mixed_ref, ...), custom_call_target="tpu_custom_call" | custom-call | tf_op jit(solution)/shard_map/early_grads/pallas_call | solution.py:585
  273.1 8.6 %attn_bwd.3 = (bf16[576,256]{1,0:T(8,128)(2,1)}, bf16[576,256]{1,0:T(8,128)(2,1)}, bf16[576,256]{1,0:T(8,128)(2,1)}, bf16[576,256]{1,0:T(8,128)(2,1)}) custom-call(s32[8]{0:T(128)} %pad_add_fusion.order_ref, bf16[192,256]{1,0:T(8,128)(2,1)} %get-tuple-element.260.refs_0_, bf16[192,256]{1,0:T(8,128)(2,1)} %copy-done.54, bf16[192,256]{1,0:T(8,128)(2,1)} %copy-done.55, ...), custom_call_target="tpu_custom_call" | custom-call | tf_op jit(solution)/shard_map/attn_bwd/pallas_call | solution.py:321
  281.7 8.8 %collective-permute-done.49 = bf16[2,48,2432]{2,1,0:T(8,128)(2,1)S(1)} collective-permute-done((bf16[2,48,2432]{2,1,0:T(8,128)(2,1)S(1)}, bf16[2,48,2432]{2,1,0:T(8,128)(2,1)S(1)}, u32[]{:S(2)}, u32[]{:S(2)}) %collective-permute-start.49) | collective-permute-done | bytes 466976 | tf_op jit(solution)/shard_map/ppermute | solution.py:733
  315.8 8.8 %qkv_backward.3 = (bf16[256,768]{1,0:T(8,128)(2,1)}, bf16[4,96,2432]{2,1,0:T(8,128)(2,1)}, bf16[4,96,2432]{2,1,0:T(8,128)(2,1)}) custom-call(s32[14]{0:T(128)} %concatenate.56.ids_ref, bf16[256,768]{1,0:T(8,128)(2,1)} %bitcast_select_fusion.1.x_ref, f32[256,768]{1,0:T(8,128)} %get-tuple-element.283.ginner_ref, f32[16,768]{1,0:T(8,128)} %get-tuple-element.177.vec_ref, ...), custom_call_target="tpu_custom_call" | custom-call | tf_op jit(solution)/shard_map/qkv_backward/pallas_call | solution.py:647
  324.6 9.1 %collective-permute-done.55 = bf16[48,2432]{1,0:T(8,128)(2,1)} collective-permute-done((bf16[48,2432]{1,0:T(8,128)(2,1)}, bf16[48,2432]{1,0:T(8,128)(2,1)}, u32[]{:S(2)}, u32[]{:S(2)}) %collective-permute-start.55) | collective-permute-done | bytes 233504 | tf_op jit(solution)/shard_map/ppermute | solution.py:733
  349.1 8.7 %collective-permute-done.60 = bf16[48,6912]{1,0:T(8,128)(2,1)S(1)} collective-permute-done((bf16[48,6912]{1,0:T(8,128)(2,1)S(1)}, bf16[48,6912]{1,0:T(8,128)(2,1)S(1)}, u32[]{:S(2)}, u32[]{:S(2)}) %collective-permute-start.60) | collective-permute-done | bytes 663584 | tf_op jit(solution)/shard_map/ppermute | solution.py:733
  373.2 8.1 %collective-permute-done.68 = bf16[2,48,2432]{2,1,0:T(8,128)(2,1)} collective-permute-done((bf16[2,48,2432]{2,1,0:T(8,128)(2,1)}, bf16[2,48,2432]{2,1,0:T(8,128)(2,1)}, u32[]{:S(2)}, u32[]{:S(2)}) %collective-permute-start.68) | collective-permute-done | bytes 466976 | tf_op jit(solution)/shard_map/ppermute | solution.py:733
  410.2 11.5 %collective-permute-start.77 = (bf16[96,2432]{1,0:T(8,128)(2,1)S(1)}, bf16[96,2432]{1,0:T(8,128)(2,1)S(1)}, u32[]{:S(2)}, u32[]{:S(2)}) collective-permute-start(bf16[96,2432]{1,0:T(8,128)(2,1)S(1)} %pad_maximum_fusion.2), channel_id=1, source_target_pairs={{0,4},{12,8},{1,5},{13,9},{2,6},{14,10},{3,7},{15,11},{16,20},{28,... | collective-permute-start | bytes 1400840 | tf_op jit(solution)/shard_map/ppermute | solution.py:825
  433.0 8.1 %collective-permute-start.80 = (bf16[96,3840]{1,0:T(8,128)(2,1)S(1)}, bf16[96,3840]{1,0:T(8,128)(2,1)S(1)}, u32[]{:S(2)}, u32[]{:S(2)}) collective-permute-start(bf16[96,3840]{1,0:T(8,128)(2,1)S(1)} %broadcast_select_fusion.3), channel_id=1, source_target_pairs={{16,0},{17,1},{18,2},{19,3},{20,4},{21,5},{22,6},{23,7},{24,8},{25... | collective-permute-start | bytes 2211848 | tf_op jit(solution)/shard_map/ppermute | solution.py:833
  448.7 10.4 %collective-permute-done.79 = bf16[96,2432]{1,0:T(8,128)(2,1)S(1)} collective-permute-done((bf16[96,2432]{1,0:T(8,128)(2,1)S(1)}, bf16[96,2432]{1,0:T(8,128)(2,1)S(1)}, u32[]{:S(2)}, u32[]{:S(2)}) %collective-permute-start.79) | collective-permute-done | bytes 466976 | tf_op jit(solution)/shard_map/ppermute | solution.py:825
  472.4 7.0 %collective-permute-done.84 = bf16[96,2432]{1,0:T(8,128)(2,1)S(1)} collective-permute-done((bf16[96,2432]{1,0:T(8,128)(2,1)S(1)}, bf16[96,2432]{1,0:T(8,128)(2,1)S(1)}, u32[]{:S(2)}, u32[]{:S(2)}) %collective-permute-start.84) | collective-permute-done | bytes 466976 | tf_op jit(solution)/shard_map/ppermute | solution.py:829
  485.2 13.3 %collective-permute-done.88 = bf16[96,2432]{1,0:T(8,128)(2,1)S(1)} collective-permute-done((bf16[96,2432]{1,0:T(8,128)(2,1)S(1)}, bf16[96,2432]{1,0:T(8,128)(2,1)S(1)}, u32[]{:S(2)}, u32[]{:S(2)}) %collective-permute-start.88) | collective-permute-done | bytes 466976 | tf_op jit(solution)/shard_map/ppermute | solution.py:829
  (417 shorter events, 272.3 us)
Async XLA Ops:
  7.2 92.3 %all-gather.3.cloned.1.call-start = ((), (), s32[]{:S(2)}) async-start(), calls=%async_computation.1 | async-start | bytes 11943936 | tf_op jit(solution)/shard_map/all_gather | solution.py:728
  14.8 152.1 %all-gather.5.cloned.1.call-start = ((), (), s32[]{:S(2)}) async-start(), calls=%async_computation.2 | async-start | bytes 11943936 | tf_op jit(solution)/shard_map/all_gather | solution.py:728
  15.6 274.9 %reduce-scatter.2.cloned.1.call-start = ((), (), s32[]{:S(2)}) async-start(), calls=%async_computation.3 | async-start | bytes 11943936 | tf_op jit(solution)/shard_map/reduce_scatter | solution.py:807
  64.1 23.0 %collective-permute-start.21 = (bf16[48,2432]{1,0:T(8,128)(2,1)S(1)}, bf16[48,2432]{1,0:T(8,128)(2,1)}, u32[]{:S(2)}, u32[]{:S(2)}) collective-permute-start(bf16[48,2432]{1,0:T(8,128)(2,1)S(1)} %slice.325), channel_id=1, source_target_pairs={{0,1},{1,0},{2,3},{3,2},{4,5},{5,4},{6,7},{7,6},{8,9},{9,8},{10,11... | collective-permute-start | bytes 700424 | tf_op jit(solution)/shard_map/ppermute | solution.py:733
  65.7 22.5 %collective-permute-start.20 = (bf16[48,2432]{1,0:T(8,128)(2,1)S(1)}, bf16[48,2432]{1,0:T(8,128)(2,1)}, u32[]{:S(2)}, u32[]{:S(2)}) collective-permute-start(bf16[48,2432]{1,0:T(8,128)(2,1)S(1)} %slice.324), channel_id=1, source_target_pairs={{0,2},{1,3},{2,0},{3,1},{4,6},{5,7},{6,4},{7,5},{8,10},{9,11},{10,... | collective-permute-start | bytes 700424 | tf_op jit(solution)/shard_map/ppermute | solution.py:733
  71.9 37.2 %collective-permute-start.22 = (bf16[96,2432]{1,0:T(8,128)(2,1)S(1)}, bf16[96,2432]{1,0:T(8,128)(2,1)S(1)}, u32[]{:S(2)}, u32[]{:S(2)}) collective-permute-start(bf16[96,2432]{1,0:T(8,128)(2,1)S(1)} %get-tuple-element.390.refs_0_), channel_id=1, source_target_pairs={{0,16},{16,0},{1,17},{17,1},{2,18},{18,2},{3,19},{19,3},{4,20},{20... | collective-permute-start | bytes 1400840 | tf_op jit(solution)/shard_map/ppermute | solution.py:737
  72.6 36.6 %collective-permute-start.24 = (bf16[96,2432]{1,0:T(8,128)(2,1)S(1)}, bf16[96,2432]{1,0:T(8,128)(2,1)}, u32[]{:S(2)}, u32[]{:S(2)}) collective-permute-start(bf16[96,2432]{1,0:T(8,128)(2,1)S(1)} %collective-permute-done.19.refs_2_), channel_id=1, source_target_pairs={{0,16},{16,0},{1,17},{17,1},{2,18},{18,2},{3,19},{19,3},{4,20},{20... | collective-permute-start | bytes 1400840 | tf_op jit(solution)/shard_map/ppermute | solution.py:737
  77.4 31.8 %collective-permute-start.23 = (bf16[96,2432]{1,0:T(8,128)(2,1)S(1)}, bf16[96,2432]{1,0:T(8,128)(2,1)}, u32[]{:S(2)}, u32[]{:S(2)}) collective-permute-start(bf16[96,2432]{1,0:T(8,128)(2,1)S(1)} %collective-permute-done.18.refs_1_), channel_id=1, source_target_pairs={{0,16},{16,0},{1,17},{17,1},{2,18},{18,2},{3,19},{19,3},{4,20},{20... | collective-permute-start | bytes 1400840 | tf_op jit(solution)/shard_map/ppermute | solution.py:737
  118.5 35.3 %collective-permute-start.35 = (bf16[256,768]{1,0:T(8,128)(2,1)S(1)}, bf16[256,768]{1,0:T(8,128)(2,1)S(1)}, u32[]{:S(2)}, u32[]{:S(2)}) collective-permute-start(bf16[256,768]{1,0:T(8,128)(2,1)S(1)} %select_bitcast_fusion.4), channel_id=1, source_target_pairs={{0,8},{4,12},{24,16},{28,20},{1,9},{5,13},{25,17},{29,21},{2,10},{... | collective-permute-start | bytes 1179656 | tf_op jit(solution)/shard_map/ppermute | solution.py:64
  136.3 23.3 %collective-permute-start.34 = (bf16[256,768]{1,0:T(8,128)(2,1)S(1)}, bf16[256,768]{1,0:T(8,128)(2,1)S(1)}, u32[]{:S(2)}, u32[]{:S(2)}) collective-permute-start(bf16[256,768]{1,0:T(8,128)(2,1)S(1)} %copy-done.2), channel_id=1, source_target_pairs={{8,0},{12,4},{24,8},{28,12},{9,1},{13,5},{25,9},{29,13},{10,2},{14... | collective-permute-start | bytes 1179656 | tf_op jit(solution)/shard_map/ppermute | solution.py:73
  137.0 22.6 %collective-permute-start.33 = (bf16[256,768]{1,0:T(8,128)(2,1)S(1)}, bf16[256,768]{1,0:T(8,128)(2,1)S(1)}, u32[]{:S(2)}, u32[]{:S(2)}) collective-permute-start(bf16[256,768]{1,0:T(8,128)(2,1)S(1)} %copy-done.2), channel_id=1, source_target_pairs={{0,0},{4,4},{16,8},{20,12},{1,1},{5,5},{17,9},{21,13},{2,2},{6,6},... | collective-permute-start | bytes 1179656 | tf_op jit(solution)/shard_map/ppermute | solution.py:73
  234.6 24.8 %collective-permute-start.42 = (bf16[4,96,2432]{2,1,0:T(8,128)(2,1)}, bf16[4,96,2432]{2,1,0:T(8,128)(2,1)S(1)}, u32[]{:S(2)}, u32[]{:S(2)}) collective-permute-start(bf16[4,96,2432]{2,1,0:T(8,128)(2,1)} %get-tuple-element.244), channel_id=1, source_target_pairs={{0,16},{16,0},{1,17},{17,1},{2,18},{18,2},{3,19},{19,3},{4,20},{20... | collective-permute-start | bytes 5603336 | tf_op jit(solution)/shard_map/ppermute | solution.py:737
  236.9 22.5 %collective-permute-start.44 = (bf16[256,1536]{1,0:T(8,128)(2,1)S(1)}, bf16[256,1536]{1,0:T(8,128)(2,1)S(1)}, u32[]{:S(2)}, u32[]{:S(2)}) collective-permute-start(bf16[256,1536]{1,0:T(8,128)(2,1)S(1)} %constant_dynamic-update-slice_fusion), channel_id=1, source_target_pairs={{8,16},{12,20},{24,24},{28,28},{9,17},{13,21},{25,25},{29,29},{10,... | collective-permute-start | bytes 2359304 | tf_op jit(solution)/shard_map/ppermute | solution.py:73
  238.2 21.2 %collective-permute-start.43 = (bf16[256,1536]{1,0:T(8,128)(2,1)S(1)}, bf16[256,1536]{1,0:T(8,128)(2,1)S(1)}, u32[]{:S(2)}, u32[]{:S(2)}) collective-permute-start(bf16[256,1536]{1,0:T(8,128)(2,1)S(1)} %constant_dynamic-update-slice_fusion), channel_id=1, source_target_pairs={{0,16},{4,20},{16,24},{20,28},{1,17},{5,21},{17,25},{21,29},{2,18}... | collective-permute-start | bytes 2359304 | tf_op jit(solution)/shard_map/ppermute | solution.py:73
  297.6 37.0 %collective-permute-start.58 = (bf16[2,48,6912]{2,1,0:T(8,128)(2,1)}, bf16[2,48,6912]{2,1,0:T(8,128)(2,1)}, u32[]{:S(2)}, u32[]{:S(2)}) collective-permute-start(bf16[2,48,6912]{2,1,0:T(8,128)(2,1)} %get-tuple-element.374), channel_id=1, source_target_pairs={{0,2},{1,3},{2,0},{3,1},{4,6},{5,7},{6,4},{7,5},{8,10},{9,11},{10,... | collective-permute-start | bytes 3981320 | tf_op jit(solution)/shard_map/ppermute | solution.py:733
  298.8 35.8 %collective-permute-start.57 = (bf16[2,48,6912]{2,1,0:T(8,128)(2,1)}, bf16[2,48,6912]{2,1,0:T(8,128)(2,1)}, u32[]{:S(2)}, u32[]{:S(2)}) collective-permute-start(bf16[2,48,6912]{2,1,0:T(8,128)(2,1)} %get-tuple-element.375), channel_id=1, source_target_pairs={{0,1},{1,0},{2,3},{3,2},{4,5},{5,4},{6,7},{7,6},{8,9},{9,8},{10,11... | collective-permute-start | bytes 3981320 | tf_op jit(solution)/shard_map/ppermute | solution.py:733
  308.7 25.0 %collective-permute-start.55 = (bf16[48,2432]{1,0:T(8,128)(2,1)}, bf16[48,2432]{1,0:T(8,128)(2,1)}, u32[]{:S(2)}, u32[]{:S(2)}) collective-permute-start(bf16[48,2432]{1,0:T(8,128)(2,1)} %slice_bitcast_fusion.14), channel_id=1, source_target_pairs={{0,2},{1,3},{2,0},{3,1},{4,6},{5,7},{6,4},{7,5},{8,10},{9,11},{10,... | collective-permute-start | bytes 700424 | tf_op jit(solution)/shard_map/ppermute | solution.py:733
  311.0 23.6 %collective-permute-start.54 = (bf16[96,3840]{1,0:T(8,128)(2,1)}, bf16[96,3840]{1,0:T(8,128)(2,1)}, u32[]{:S(2)}, u32[]{:S(2)}) collective-permute-start(bf16[96,3840]{1,0:T(8,128)(2,1)} %slice.265), channel_id=1, source_target_pairs={{0,4},{12,8},{1,5},{13,9},{2,6},{14,10},{3,7},{15,11},{16,20},{28,... | collective-permute-start | bytes 2211848 | tf_op jit(solution)/shard_map/ppermute | solution.py:825
  333.7 25.9 %collective-permute-start.63 = (bf16[4,96,2432]{2,1,0:T(8,128)(2,1)}, bf16[4,96,2432]{2,1,0:T(8,128)(2,1)S(1)}, u32[]{:S(2)}, u32[]{:S(2)}) collective-permute-start(bf16[4,96,2432]{2,1,0:T(8,128)(2,1)} %get-tuple-element.301), channel_id=1, source_target_pairs={{0,16},{16,0},{1,17},{17,1},{2,18},{18,2},{3,19},{19,3},{4,20},{20... | collective-permute-start | bytes 5603336 | tf_op jit(solution)/shard_map/ppermute | solution.py:737
  360.3 22.5 %collective-permute-start.66 = (bf16[96,3072]{1,0:T(8,128)(2,1)S(1)}, bf16[96,3072]{1,0:T(8,128)(2,1)}, u32[]{:S(2)}, u32[]{:S(2)}) collective-permute-start(bf16[96,3072]{1,0:T(8,128)(2,1)S(1)} %add_convert_fusion.13), channel_id=1, source_target_pairs={{4,8},{8,4},{5,9},{9,5},{6,10},{10,6},{7,11},{11,7},{20,24},{24,20... | collective-permute-start | bytes 1769480 | tf_op jit(solution)/shard_map/ppermute | solution.py:827
  361.9 20.9 %collective-permute-start.65 = (bf16[96,3840]{1,0:T(8,128)(2,1)S(1)}, bf16[96,3840]{1,0:T(8,128)(2,1)}, u32[]{:S(2)}, u32[]{:S(2)}) collective-permute-start(bf16[96,3840]{1,0:T(8,128)(2,1)S(1)} %fusion.7), channel_id=1, source_target_pairs={{0,4},{12,8},{1,5},{13,9},{2,6},{14,10},{3,7},{15,11},{16,20},{28,... | collective-permute-start | bytes 2211848 | tf_op jit(solution)/shard_map/ppermute | solution.py:825
  408.9 22.4 %collective-permute-start.75 = (bf16[96,3840]{1,0:T(8,128)(2,1)S(1)}, bf16[96,3840]{1,0:T(8,128)(2,1)S(1)}, u32[]{:S(2)}, u32[]{:S(2)}) collective-permute-start(bf16[96,3840]{1,0:T(8,128)(2,1)S(1)} %add_convert_fusion.6), channel_id=1, source_target_pairs={{4,0},{8,12},{5,1},{9,13},{6,2},{10,14},{7,3},{11,15},{20,16},{24,... | collective-permute-start | bytes 2211848 | tf_op jit(solution)/shard_map/ppermute | solution.py:829
  431.6 27.5 %collective-permute-start.82 = (bf16[96,3072]{1,0:T(8,128)(2,1)S(1)}, bf16[96,3072]{1,0:T(8,128)(2,1)S(1)}, u32[]{:S(2)}, u32[]{:S(2)}) collective-permute-start(bf16[96,3072]{1,0:T(8,128)(2,1)S(1)} %add_convert_fusion.10), channel_id=1, source_target_pairs={{4,0},{8,12},{5,1},{9,13},{6,2},{10,14},{7,3},{11,15},{20,16},{24,... | collective-permute-start | bytes 1769480 | tf_op jit(solution)/shard_map/ppermute | solution.py:829
  433.0 26.0 %collective-permute-start.80 = (bf16[96,3840]{1,0:T(8,128)(2,1)S(1)}, bf16[96,3840]{1,0:T(8,128)(2,1)S(1)}, u32[]{:S(2)}, u32[]{:S(2)}) collective-permute-start(bf16[96,3840]{1,0:T(8,128)(2,1)S(1)} %broadcast_select_fusion.3), channel_id=1, source_target_pairs={{16,0},{17,1},{18,2},{19,3},{20,4},{21,5},{22,6},{23,7},{24,8},{25... | collective-permute-start | bytes 2211848 | tf_op jit(solution)/shard_map/ppermute | solution.py:833
  (136 other events, 1574.3 us)
Sparse Core Ops, SparseCore 0:
  15.0 83.3 all-gather.2
  100.8 66.0 all-gather.4
  200.2 87.5 reduce-scatter.1

commit v6 on v5

--- a/solution.py
+++ b/solution.py
@@ -693,9 +693,9 @@
     tied = lax.optimization_barrier((*received, *early))
     received, early = tied[:parts], tied[parts:]
     if last:
-        first = background.add("B", permuted_task(*early, layer, background, column))
+        first = background.add("B", early_task0(*early, background, column))
     else:
-        first = background.add("C", offloaded_task(*early, layer, background, column, 1))
+        first = background.add("C", early_task1(*early, background, column))
     sent = attention_backward(received, attn_saved, order, size)
     if last:
         sent = background.slot("BCD", sent)
@@ -705,10 +705,11 @@
     results = qkv_backward(ids, x, ginner, vec, table, weight, received, shards)
     grad_x, *late = lax.optimization_barrier(tuple(results))
     if last:
-        (grad_x,) = background.slot("ABCD", [grad_x])
-        second = background.add("A", permuted_task(*late, layer, background, None))
+        for lane in "DCB":
+            background.slot(lane, [grad_x])
+        second = background.add("A", late_task0(*late, background))
     else:
-        second = background.add("D", permuted_task(*late, layer, background, None, 1, 4))
+        second = background.add("D", late_task1(*late, background))
     return grad_x, first, second
 
 
@@ -747,12 +748,31 @@
 class Background:
     def __init__(self):
         self.tasks = []
+        self.links = {}
+        self.shared = {}
+
+    def send(self, link, value, axis, pairs):
+        if link in self.links:
+            value, _ = lax.optimization_barrier((value, self.links[link]))
+        moved = lax.ppermute(value, axis, pairs)
+        self.links[link] = moved
+        return moved
+
+    def across(self, value, bit):
+        count = lax.axis_size("fsdp")
+        return self.send(bit, value, "fsdp", [(i, i ^ bit) for i in range(count)])
 
     def add(self, lane, task):
         entry = {"lane": lane, "task": task, "result": None}
         entry["flight"] = next(task)
         self.tasks.append(entry)
         return entry
+
+    def resume(self, entry, flight):
+        try:
+            entry["flight"] = entry["task"].send(flight)
+        except StopIteration as stop:
+            entry["flight"], entry["result"] = None, stop.value
 
     def slot(self, lanes, values=()):
         waiting = [e for e in self.tasks if e["flight"] is not None and e["lane"] in lanes]
@@ -764,16 +784,15 @@
         values, flat = flat[: len(values)], flat[len(values) :]
         for entry in waiting:
             count = len(entry["flight"])
-            held, flat = flat[:count], flat[count:]
-            try:
-                entry["flight"] = entry["task"].send(held)
-            except StopIteration as stop:
-                entry["flight"], entry["result"] = None, stop.value
+            self.resume(entry, flat[:count])
+            flat = flat[count:]
         return values
 
     def finish(self):
         while any(entry["flight"] is not None for entry in self.tasks):
-            self.slot("ABCD")
+            for entry in list(self.tasks):
+                if entry["flight"] is not None:
+                    self.resume(entry, entry["flight"])
 
 
 def idle(values, slots):
@@ -782,7 +801,7 @@
     return values
 
 
-def permuted_task(keep, send, layer, background, column, hold=0, before=0):
+def permuted_value(keep, send, background, hold):
     (received,) = yield [swap_cores(send)]
     rows = keep.shape[1] // 2
 
@@ -791,42 +810,51 @@
 
     top, low = slice(0, rows), slice(rows, 2 * rows)
     by_x, by_y = yield [
-        across(summed(slice(1, 4, 2), top), 1),
-        across(summed(slice(2, 4), low), 2),
+        background.across(summed(slice(1, 4, 2), top), 1),
+        background.across(summed(slice(2, 4), low), 2),
     ]
     by_x, by_y = yield from idle([by_x, by_y], hold)
     first = sum_pair(summed(slice(0, 4, 2), top), by_x)
     second = sum_pair(summed(slice(0, 2), low), by_y)
-    by_y, by_x = yield [across(first[1], 2), across(second[1], 1)]
-    value = jnp.concatenate([sum_pair(first[0], by_y), sum_pair(second[0], by_x)])
-    (value,) = yield from idle([value], before)
-    return (yield from split_task(value, layer, background, column))
-
-
-def offloaded_task(pack, layer, background, column, after):
+    by_y, by_x = yield [background.across(first[1], 2), background.across(second[1], 1)]
+    return jnp.concatenate([sum_pair(first[0], by_y), sum_pair(second[0], by_x)])
+
+
+def early_task0(keep, send, background, column):
+    value = yield from permuted_value(keep, send, background, 0)
+    other = background.add("D", ctx_task(value[:, column:], 0, background, 1))
+    mine = yield from ctx_task(value[:, :column], 0, background)
+    return mine, other
+
+
+def late_task0(keep, send, background):
+    value = yield from permuted_value(keep, send, background, 0)
+    return (yield from ctx_task(value, 0, background))
+
+
+def early_task1(pack, background, column):
     value = lax.psum_scatter(pack, SHARDS, scatter_dimension=0, tiled=True)
     (value,) = yield [value]
-    (value,) = yield from idle([value], after)
-    return (yield from split_task(value, layer, background, column))
-
-
-def split_task(value, layer, background, column):
-    if column is None:
-        return (yield from ctx_task(value, layer))
-    other = background.add("D", ctx_task(value[:, column:], layer, 1))
-    mine = yield from ctx_task(value[:, :column], layer)
-    return mine, other
-
-
-def ctx_task(value, layer, before=0):
+    (value,) = yield [value]
+    background.shared["down"] = value[:, column:]
+    return (yield from ctx_task(value[:, :column], 1, background))
+
+
+def late_task1(keep, send, background):
+    value = yield from permuted_value(keep, send, background, 1)
+    value = jnp.concatenate([background.shared["down"], value], axis=1)
+    return (yield from ctx_task(value, 1, background))
+
+
+def ctx_task(value, layer, background, before=0):
     (value,) = yield from idle([value], before)
     if lax.axis_size("ctx") == 4:
         index = lax.axis_index("ctx")
-        (received,) = yield [lax.ppermute(value, "ctx", [(0, 1), (3, 2)])]
+        (received,) = yield [background.send("in", value, "ctx", [(0, 1), (3, 2)])]
         value = sum_pair(value, received)
-        (received,) = yield [lax.ppermute(value, "ctx", [(1, 2), (2, 1)])]
+        (received,) = yield [background.send("mid", value, "ctx", [(1, 2), (2, 1)])]
         value = sum_pair(value, received)
-        (received,) = yield [lax.ppermute(value, "ctx", [(1, 0), (2, 3)])]
+        (received,) = yield [background.send("out", value, "ctx", [(1, 0), (2, 3)])]
         value = jnp.where((index == 0) | (index == 3), received, value)
     else:
         value = lax.psum(value, "ctx")
@@ -903,10 +931,11 @@
             jnp.concatenate([pair1[1], pair1[0]]),
         ).astype(F32)
 
-    (up0, down0), (up1, down1) = early0["result"], early1["result"]
+    (up0, down0), up1, rest1 = early0["result"], early1["result"], late1["result"]
+    hidden = ratio * width
     early = joined(up0, up1)
-    late = joined(late0["result"], late1["result"])
-    down = joined(down0["result"], down1["result"])
+    late = joined(late0["result"], [value[:, hidden:] for value in rest1])
+    down = joined(down0["result"], [value[:, :hidden] for value in rest1])
     table = late[:, 3 * width :].T
     return (
         layer_outputs[None, :, None],

time: 522 us -> 505 us (0.967)
  other arithmetic: 32 us -> 22.7 us
  starting transfers between devices: 139 us -> 130 us
    ppermute x18 -> x27, waiting for transfers between devices: 44.4 us -> 91.4 us  [send(): moved = lax.ppermute(value, axis, pairs)]
    ppermute x20 -> x8, waiting for transfers between devices: 55.1 us -> 11.9 us  [across(): return lax.ppermute(value, 'fsdp', [(i, i ^ bit) for i in range(count)])]
    ppermute x20 -> x8, starting transfers between devices: 22.6 us -> 11.1 us  [across(): return lax.ppermute(value, 'fsdp', [(i, i ^ bit) for i in range(count)])]
    ppermute x18 -> x27, starting transfers between devices: 48.6 us -> 39.9 us  [send(): moved = lax.ppermute(value, axis, pairs)]
    convert_element_type x24 -> x22, other arithmetic: 20.3 us -> 12.8 us  [sum_pair(): return (a.astype(F32) + b.astype(F32)).astype(BF)]
    ppermute x6 -> x5, starting transfers between devices: 14.7 us -> 21.2 us  [ctx_task(): other, = (yield [lax.ppermute(value, 'section', [(1 - layer, layer)])])]
  transfers between devices with their start and end apart: 94 -> 90, of which waited for: 37 -> 36; matrix products, arithmetic and copies ran while one was open for 7% -> 7% of each run, Pallas kernels for 21% -> 21%
where the time goes in v6:
time: 505 us; the launch traced here: 497 us
  waiting for transfers between devices  176 us (35%)
  starting transfers between devices  130 us (26%)
  Pallas kernels  129 us (26%)
  local copies, waits for them, and re-layouts  24.4 us (5%)
  other arithmetic  22.7 us (4%)
  between operations  15.4 us (3%)
    ppermute x27, waiting for transfers between devices, send(): moved = lax.ppermute(value, axis, pairs)  91.4 us
    ppermute x24, waiting for transfers between devices, exchange(): moved.append(lax.ppermute(pieces[d], GROUP, pairs))  53.9 us
    ppermute x27, starting transfers between devices, send(): moved = lax.ppermute(value, axis, pairs)  39.9 us
    pallas_call x2, Pallas kernels, mlp_backward(): pl.pallas_call(functools.partial(mlp_back_kernel, parts=parts, shards=sha...  26.3 us
    ppermute x5, starting transfers between devices, ctx_task(): other, = (yield [lax.ppermute(value, 'section', [(1 - layer, layer)])])  21.2 us
    ppermute x6, starting transfers between devices, return_rows(): lax.ppermute(value, GROUP, [(place_of(z // half, m * half + z % half), pl...  19.3 us
    pallas_call x2, Pallas kernels, mlp_forward(): pl.pallas_call(functools.partial(mlp_kernel, parts=parts, shards=shards,...  19.3 us
    pallas_call x2, Pallas kernels, qkv_backward(): pl.pallas_call(functools.partial(qkv_back_kernel, parts=parts, shards=sha...  18 us
  transfers between devices with their start and end apart: 90, of which 36 were waited for; matrix products, arithmetic and copies ran while one was open for 7% of the time, Pallas kernels for 21%

profile of v6, /device:TPU:1, one launch (start us, length us, event | category | flops | bytes accessed | tf_op | source)
XLA Modules:
  0.0 496.6 jit_solution(12890508507361531272)
XLA Ops:
  78.7 8.4 %attn_fwd.2 = (bf16[192,256]{1,0:T(8,128)(2,1)}, bf16[192,256]{1,0:T(8,128)(2,1)}, bf16[192,256]{1,0:T(8,128)(2,1)}, bf16[192,256]{1,0:T(8,128)(2,1)}, bf16[576,...) custom-call(s32[8]{0:T(128)} %pad_add_fusion.order_ref, ...), custom_call_target="tpu_custom_call" | custom-call | tf_op jit(solution)/shard_map/attn_fwd/pallas_call | solution.py:292
  99.4 9.6 %mlp_forward.2 = (bf16[256,768]{1,0:T(8,128)(2,1)}, f32[256,768]{1,0:T(8,128)}, f32[256,3072]{1,0:T(8,128)}, bf16[768,256]{1,0:T(8,128)(2,1)}) custom-call(s32[14]{0:T(128)} %concatenate.59.ids_ref, bf16[256,768]{1,0:T(8,128)(2,1)} %bitcast_select_fusion.1.x_ref, f32[16,768]{1,0:T(8,128)} %get-tuple-element.156.vec_ref, f32[1,3072]{1,0:T(1,128)} %reshape.191.bias_ref, ...), custom_call_target="tpu_custom_call" | custom-call | tf_op jit(solution)/shard_map/mlp_forward/pallas_call | solution.py:414
  119.9 10.6 %collective-permute-done.27.refs_1_ = bf16[576,256]{1,0:T(8,128)(2,1)S(1)} collective-permute-done((bf16[576,256]{1,0:T(8,128)(2,1)}, bf16[576,256]{1,0:T(8,128)(2,1)S(1)}, u32[]{:S(2)}, u32[]{:S(2)}) %collective-permute-start.27) | collective-permute-done | bytes 294944 | tf_op jit(solution)/shard_map/ppermute | solution.py:52
  137.1 6.8 %collective-permute-start.33 = (bf16[256,768]{1,0:T(8,128)(2,1)S(1)}, bf16[256,768]{1,0:T(8,128)(2,1)S(1)}, u32[]{:S(2)}, u32[]{:S(2)}) collective-permute-start(bf16[256,768]{1,0:T(8,128)(2,1)S(1)} %copy-done.2), channel_id=1, source_target_pairs={{0,0},{4,4},{16,8},{20,12},{1,1},{5,5},{17,9},{21,13},{2,2},{6,6},... | collective-permute-start | bytes 1179656 | tf_op jit(solution)/shard_map/ppermute | solution.py:73
  145.4 8.4 %attn_fwd.3 = (bf16[192,256]{1,0:T(8,128)(2,1)}, bf16[192,256]{1,0:T(8,128)(2,1)}, bf16[192,256]{1,0:T(8,128)(2,1)}, bf16[192,256]{1,0:T(8,128)(2,1)}, bf16[576,...) custom-call(s32[8]{0:T(128)} %pad_add_fusion.order_ref, ...), custom_call_target="tpu_custom_call" | custom-call | tf_op jit(solution)/shard_map/attn_fwd/pallas_call | solution.py:292
  159.7 7.2 %all-gather.5.cloned.1.call-done.pack_ref = bf16[768,6912]{1,0:T(8,128)(2,1)} async-done(((bf16[96,6912]{1,0:T(8,128)(2,1)}), bf16[768,6912]{1,0:T(8,128)(2,1)}) %all-gather.5.cloned.1.call-update) | async-done | bytes 10616848 | tf_op jit(solution)/shard_map/all_gather | solution.py:729
  166.9 9.6 %mlp_forward.3 = (bf16[256,768]{1,0:T(8,128)(2,1)}, f32[256,768]{1,0:T(8,128)}, f32[256,3072]{1,0:T(8,128)}, bf16[768,256]{1,0:T(8,128)(2,1)}) custom-call(s32[14]{0:T(128)} %concatenate.59.ids_ref, bf16[256,768]{1,0:T(8,128)(2,1)} %get-tuple-element.179.x_ref, f32[16,768]{1,0:T(8,128)} %get-tuple-element.182.vec_ref, f32[1,3072]{1,0:T(1,128)} %reshape.193.bias_ref, ...), custom_call_target="tpu_custom_call" | custom-call | tf_op jit(solution)/shard_map/mlp_forward/pallas_call | solution.py:414
  176.6 13.0 %mlp_backward.2 = (bf16[192,256]{1,0:T(8,128)(2,1)}, bf16[192,256]{1,0:T(8,128)(2,1)}, bf16[192,256]{1,0:T(8,128)(2,1)}, bf16[192,256]{1,0:T(8,128)(2,1)}, f32[2...) custom-call(s32[14]{0:T(128)} %concatenate.59.ids_ref, ...), custom_call_target="tpu_custom_call" | custom-call | tf_op jit(solution)/shard_map/mlp_backward/pallas_call | solution.py:489
  191.8 8.2 %early_grads.2 = bf16[768,6912]{1,0:T(8,128)(2,1)} custom-call(s32[14]{0:T(128)} %concatenate.59.ids_ref, bf16[256,768]{1,0:T(8,128)(2,1)} %get-tuple-element.200.middle_ref, bf16[256,3072]{1,0:T(8,128)(2,1)} %get-tuple-element.201.ghid_ref, bf16[768,256]{1,0:T(8,128)(2,1)} %get-tuple-element.202.mixed_ref, bf16[256,768]{1,0:T(8,128)(2,1)} %get-tuple-element.203.gattn_ref, ...), custom_call_target="tpu_custom_call" | custom-call | tf_op jit(solution)/shard_map/early_grads/pallas_call | solution.py:585
  200.7 8.6 %attn_bwd.2 = (bf16[576,256]{1,0:T(8,128)(2,1)}, bf16[576,256]{1,0:T(8,128)(2,1)}, bf16[576,256]{1,0:T(8,128)(2,1)}, bf16[576,256]{1,0:T(8,128)(2,1)}) custom-call(s32[8]{0:T(128)} %pad_add_fusion.order_ref, bf16[192,256]{1,0:T(8,128)(2,1)} %get-tuple-element.205.refs_0_, bf16[192,256]{1,0:T(8,128)(2,1)} %copy-done.56, bf16[192,256]{1,0:T(8,128)(2,1)} %copy-done.57, ...), custom_call_target="tpu_custom_call" | custom-call | tf_op jit(solution)/shard_map/attn_bwd/pallas_call | solution.py:321
  211.4 7.4 %collective-permute-done.39.refs_1_ = bf16[576,256]{1,0:T(8,128)(2,1)S(1)} collective-permute-done((bf16[576,256]{1,0:T(8,128)(2,1)}, bf16[576,256]{1,0:T(8,128)(2,1)S(1)}, u32[]{:S(2)}, u32[]{:S(2)}) %collective-permute-start.39) | collective-permute-done | bytes 294944 | tf_op jit(solution)/shard_map/ppermute | solution.py:52
  225.5 9.1 %qkv_backward.2 = (bf16[256,768]{1,0:T(8,128)(2,1)}, bf16[4,96,2432]{2,1,0:T(8,128)(2,1)}, bf16[4,96,2432]{2,1,0:T(8,128)(2,1)}) custom-call(s32[14]{0:T(128)} %concatenate.59.ids_ref, bf16[256,768]{1,0:T(8,128)(2,1)} %get-tuple-element.179.x_ref, f32[256,768]{1,0:T(8,128)} %get-tuple-element.189.ginner_ref, f32[16,768]{1,0:T(8,128)} %get-tuple-element.182.vec_ref, ...), custom_call_target="tpu_custom_call" | custom-call | tf_op jit(solution)/shard_map/qkv_backward/pallas_call | solution.py:647
  241.8 13.2 %mlp_backward.3 = (bf16[192,256]{1,0:T(8,128)(2,1)}, bf16[192,256]{1,0:T(8,128)(2,1)}, bf16[192,256]{1,0:T(8,128)(2,1)}, bf16[192,256]{1,0:T(8,128)(2,1)}, f32[2...) custom-call(s32[14]{0:T(128)} %concatenate.59.ids_ref, ...), custom_call_target="tpu_custom_call" | custom-call | tf_op jit(solution)/shard_map/mlp_backward/pallas_call | solution.py:489
  261.3 9.4 %early_grads.3 = (bf16[4,96,6912]{2,1,0:T(8,128)(2,1)}, bf16[4,96,6912]{2,1,0:T(8,128)(2,1)}) custom-call(s32[14]{0:T(128)} %concatenate.59.ids_ref, bf16[256,768]{1,0:T(8,128)(2,1)} %get-tuple-element.235.middle_ref, bf16[256,3072]{1,0:T(8,128)(2,1)} %get-tuple-element.236.ghid_ref, bf16[768,256]{1,0:T(8,128)(2,1)} %get-tuple-element.237.mixed_ref, ...), custom_call_target="tpu_custom_call" | custom-call | tf_op jit(solution)/shard_map/early_grads/pallas_call | solution.py:585
  273.8 8.7 %attn_bwd.3 = (bf16[576,256]{1,0:T(8,128)(2,1)}, bf16[576,256]{1,0:T(8,128)(2,1)}, bf16[576,256]{1,0:T(8,128)(2,1)}, bf16[576,256]{1,0:T(8,128)(2,1)}) custom-call(s32[8]{0:T(128)} %pad_add_fusion.order_ref, bf16[192,256]{1,0:T(8,128)(2,1)} %get-tuple-element.242.refs_0_, bf16[192,256]{1,0:T(8,128)(2,1)} %copy-done.53, bf16[192,256]{1,0:T(8,128)(2,1)} %copy-done.54, ...), custom_call_target="tpu_custom_call" | custom-call | tf_op jit(solution)/shard_map/attn_bwd/pallas_call | solution.py:321
  282.6 7.9 %collective-permute-done.49 = bf16[2,48,2432]{2,1,0:T(8,128)(2,1)S(1)} collective-permute-done((bf16[2,48,2432]{2,1,0:T(8,128)(2,1)}, bf16[2,48,2432]{2,1,0:T(8,128)(2,1)S(1)}, u32[]{:S(2)}, u32[]{:S(2)}) %collective-permute-start.49) | collective-permute-done | bytes 466976 | tf_op jit(solution)/shard_map/ppermute | solution.py:757
  307.1 8.9 %qkv_backward.3 = (bf16[256,768]{1,0:T(8,128)(2,1)}, bf16[4,96,2432]{2,1,0:T(8,128)(2,1)}, bf16[4,96,2432]{2,1,0:T(8,128)(2,1)}) custom-call(s32[14]{0:T(128)} %concatenate.59.ids_ref, bf16[256,768]{1,0:T(8,128)(2,1)} %bitcast_select_fusion.1.x_ref, f32[256,768]{1,0:T(8,128)} %get-tuple-element.228.ginner_ref, f32[16,768]{1,0:T(8,128)} %get-tuple-element.156.vec_ref, ...), custom_call_target="tpu_custom_call" | custom-call | tf_op jit(solution)/shard_map/qkv_backward/pallas_call | solution.py:647
  334.2 9.6 %collective-permute-done.67 = bf16[96,3840]{1,0:T(8,128)(2,1)S(1)} collective-permute-done((bf16[96,3840]{1,0:T(8,128)(2,1)S(1)}, bf16[96,3840]{1,0:T(8,128)(2,1)S(1)}, u32[]{:S(2)}, u32[]{:S(2)}) %collective-permute-start.67) | collective-permute-done | bytes 737312 | tf_op jit(solution)/shard_map/ppermute | solution.py:757
  352.6 7.7 %collective-permute-start.68 = (bf16[96,5504]{1,0:T(8,128)(2,1)S(1)}, bf16[96,5504]{1,0:T(8,128)(2,1)S(1)}, u32[]{:S(2)}, u32[]{:S(2)}) collective-permute-start(bf16[96,5504]{1,0:T(8,128)(2,1)S(1)} %maximum_maximum_fusion), channel_id=1, source_target_pairs={{0,4},{12,8},{1,5},{13,9},{2,6},{14,10},{3,7},{15,11},{16,20},{28,... | collective-permute-start | bytes 3170312 | tf_op jit(solution)/shard_map/ppermute | solution.py:757
  368.9 13.3 %collective-permute-done.77 = bf16[96,3840]{1,0:T(8,128)(2,1)S(1)} collective-permute-done((bf16[96,3840]{1,0:T(8,128)(2,1)S(1)}, bf16[96,3840]{1,0:T(8,128)(2,1)S(1)}, u32[]{:S(2)}, u32[]{:S(2)}) %collective-permute-start.77) | collective-permute-done | bytes 737312 | tf_op jit(solution)/shard_map/ppermute | solution.py:757
  393.5 7.2 %collective-permute-done.69 = bf16[96,3840]{1,0:T(8,128)(2,1)S(1)} collective-permute-done((bf16[96,3840]{1,0:T(8,128)(2,1)S(1)}, bf16[96,3840]{1,0:T(8,128)(2,1)S(1)}, u32[]{:S(2)}, u32[]{:S(2)}) %collective-permute-start.69) | collective-permute-done | bytes 737312 | tf_op jit(solution)/shard_map/ppermute | solution.py:757
  407.3 7.5 %collective-permute-done.70 = bf16[96,3072]{1,0:T(8,128)(2,1)S(1)} collective-permute-done((bf16[96,3072]{1,0:T(8,128)(2,1)S(1)}, bf16[96,3072]{1,0:T(8,128)(2,1)S(1)}, u32[]{:S(2)}, u32[]{:S(2)}) %collective-permute-start.70) | collective-permute-done | bytes 589856 | tf_op jit(solution)/shard_map/ppermute | solution.py:757
  426.4 10.3 %collective-permute-done.78 = bf16[96,5504]{1,0:T(8,128)(2,1)S(1)} collective-permute-done((bf16[96,5504]{1,0:T(8,128)(2,1)S(1)}, bf16[96,5504]{1,0:T(8,128)(2,1)S(1)}, u32[]{:S(2)}, u32[]{:S(2)}) %collective-permute-start.78) | collective-permute-done | bytes 1056800 | tf_op jit(solution)/shard_map/ppermute | solution.py:757
  440.7 13.1 %collective-permute-done.79 = bf16[96,3840]{1,0:T(8,128)(2,1)S(1)} collective-permute-done((bf16[96,3840]{1,0:T(8,128)(2,1)S(1)}, bf16[96,3840]{1,0:T(8,128)(2,1)S(1)}, u32[]{:S(2)}, u32[]{:S(2)}) %collective-permute-start.79) | collective-permute-done | bytes 737312 | tf_op jit(solution)/shard_map/ppermute | solution.py:757
  (410 shorter events, 257.2 us)
Async XLA Ops:
  7.2 92.2 %all-gather.3.cloned.1.call-start = ((), (), s32[]{:S(2)}) async-start(), calls=%async_computation.1 | async-start | bytes 11943936 | tf_op jit(solution)/shard_map/all_gather | solution.py:729
  14.8 152.1 %all-gather.5.cloned.1.call-start = ((), (), s32[]{:S(2)}) async-start(), calls=%async_computation.2 | async-start | bytes 11943936 | tf_op jit(solution)/shard_map/all_gather | solution.py:729
  15.6 274.9 %reduce-scatter.2.cloned.1.call-start = ((), (), s32[]{:S(2)}) async-start(), calls=%async_computation.3 | async-start | bytes 11943936 | tf_op jit(solution)/shard_map/reduce_scatter | solution.py:836
  21.9 20.5 %collective-permute-start = (bf16[256,768]{1,0:T(8,128)(2,1)S(1)}, bf16[256,768]{1,0:T(8,128)(2,1)S(1)}, u32[]{:S(2)}, u32[]{:S(2)}) collective-permute-start(bf16[256,768]{1,0:T(8,128)(2,1)S(1)} %select_bitcast_fusion.5), channel_id=1, source_target_pairs={{0,8},{4,12},{24,16},{28,20},{1,9},{5,13},{25,17},{29,21},{2,10},{... | collective-permute-start | bytes 1179656 | tf_op jit(solution)/shard_map/ppermute | solution.py:64
  64.1 23.0 %collective-permute-start.21 = (bf16[48,2432]{1,0:T(8,128)(2,1)S(1)}, bf16[48,2432]{1,0:T(8,128)(2,1)}, u32[]{:S(2)}, u32[]{:S(2)}) collective-permute-start(bf16[48,2432]{1,0:T(8,128)(2,1)S(1)} %slice.341), channel_id=1, source_target_pairs={{0,1},{1,0},{2,3},{3,2},{4,5},{5,4},{6,7},{7,6},{8,9},{9,8},{10,11... | collective-permute-start | bytes 700424 | tf_op jit(solution)/shard_map/ppermute | solution.py:734
  66.5 21.7 %collective-permute-start.20 = (bf16[48,2432]{1,0:T(8,128)(2,1)}, bf16[48,2432]{1,0:T(8,128)(2,1)}, u32[]{:S(2)}, u32[]{:S(2)}) collective-permute-start(bf16[48,2432]{1,0:T(8,128)(2,1)} %slice.340), channel_id=1, source_target_pairs={{0,2},{1,3},{2,0},{3,1},{4,6},{5,7},{6,4},{7,5},{8,10},{9,11},{10,... | collective-permute-start | bytes 700424 | tf_op jit(solution)/shard_map/ppermute | solution.py:734
  71.9 37.2 %collective-permute-start.22 = (bf16[96,2432]{1,0:T(8,128)(2,1)S(1)}, bf16[96,2432]{1,0:T(8,128)(2,1)S(1)}, u32[]{:S(2)}, u32[]{:S(2)}) collective-permute-start(bf16[96,2432]{1,0:T(8,128)(2,1)S(1)} %get-tuple-element.348.refs_0_), channel_id=1, source_target_pairs={{0,16},{16,0},{1,17},{17,1},{2,18},{18,2},{3,19},{19,3},{4,20},{20... | collective-permute-start | bytes 1400840 | tf_op jit(solution)/shard_map/ppermute | solution.py:738
  73.2 35.9 %collective-permute-start.24 = (bf16[96,2432]{1,0:T(8,128)(2,1)S(1)}, bf16[96,2432]{1,0:T(8,128)(2,1)S(1)}, u32[]{:S(2)}, u32[]{:S(2)}) collective-permute-start(bf16[96,2432]{1,0:T(8,128)(2,1)S(1)} %collective-permute-done.19.refs_2_), channel_id=1, source_target_pairs={{0,16},{16,0},{1,17},{17,1},{2,18},{18,2},{3,19},{19,3},{4,20},{20... | collective-permute-start | bytes 1400840 | tf_op jit(solution)/shard_map/ppermute | solution.py:738
  77.4 31.8 %collective-permute-start.23 = (bf16[96,2432]{1,0:T(8,128)(2,1)S(1)}, bf16[96,2432]{1,0:T(8,128)(2,1)}, u32[]{:S(2)}, u32[]{:S(2)}) collective-permute-start(bf16[96,2432]{1,0:T(8,128)(2,1)S(1)} %collective-permute-done.18.refs_1_), channel_id=1, source_target_pairs={{0,16},{16,0},{1,17},{17,1},{2,18},{18,2},{3,19},{19,3},{4,20},{20... | collective-permute-start | bytes 1400840 | tf_op jit(solution)/shard_map/ppermute | solution.py:738
  118.6 35.3 %collective-permute-start.35 = (bf16[256,768]{1,0:T(8,128)(2,1)S(1)}, bf16[256,768]{1,0:T(8,128)(2,1)S(1)}, u32[]{:S(2)}, u32[]{:S(2)}) collective-permute-start(bf16[256,768]{1,0:T(8,128)(2,1)S(1)} %select_bitcast_fusion.4), channel_id=1, source_target_pairs={{0,8},{4,12},{24,16},{28,20},{1,9},{5,13},{25,17},{29,21},{2,10},{... | collective-permute-start | bytes 1179656 | tf_op jit(solution)/shard_map/ppermute | solution.py:64
  136.4 23.3 %collective-permute-start.34 = (bf16[256,768]{1,0:T(8,128)(2,1)S(1)}, bf16[256,768]{1,0:T(8,128)(2,1)S(1)}, u32[]{:S(2)}, u32[]{:S(2)}) collective-permute-start(bf16[256,768]{1,0:T(8,128)(2,1)S(1)} %copy-done.2), channel_id=1, source_target_pairs={{8,0},{12,4},{24,8},{28,12},{9,1},{13,5},{25,9},{29,13},{10,2},{14... | collective-permute-start | bytes 1179656 | tf_op jit(solution)/shard_map/ppermute | solution.py:73
  137.1 22.6 %collective-permute-start.33 = (bf16[256,768]{1,0:T(8,128)(2,1)S(1)}, bf16[256,768]{1,0:T(8,128)(2,1)S(1)}, u32[]{:S(2)}, u32[]{:S(2)}) collective-permute-start(bf16[256,768]{1,0:T(8,128)(2,1)S(1)} %copy-done.2), channel_id=1, source_target_pairs={{0,0},{4,4},{16,8},{20,12},{1,1},{5,5},{17,9},{21,13},{2,2},{6,6},... | collective-permute-start | bytes 1179656 | tf_op jit(solution)/shard_map/ppermute | solution.py:73
  234.6 24.8 %collective-permute-start.42 = (bf16[4,96,2432]{2,1,0:T(8,128)(2,1)}, bf16[4,96,2432]{2,1,0:T(8,128)(2,1)S(1)}, u32[]{:S(2)}, u32[]{:S(2)}) collective-permute-start(bf16[4,96,2432]{2,1,0:T(8,128)(2,1)} %get-tuple-element.223), channel_id=1, source_target_pairs={{0,16},{16,0},{1,17},{17,1},{2,18},{18,2},{3,19},{19,3},{4,20},{20... | collective-permute-start | bytes 5603336 | tf_op jit(solution)/shard_map/ppermute | solution.py:738
  237.0 22.5 %collective-permute-start.44 = (bf16[256,1536]{1,0:T(8,128)(2,1)S(1)}, bf16[256,1536]{1,0:T(8,128)(2,1)S(1)}, u32[]{:S(2)}, u32[]{:S(2)}) collective-permute-start(bf16[256,1536]{1,0:T(8,128)(2,1)S(1)} %constant_dynamic-update-slice_fusion), channel_id=1, source_target_pairs={{8,16},{12,20},{24,24},{28,28},{9,17},{13,21},{25,25},{29,29},{10,... | collective-permute-start | bytes 2359304 | tf_op jit(solution)/shard_map/ppermute | solution.py:73
  238.3 21.2 %collective-permute-start.43 = (bf16[256,1536]{1,0:T(8,128)(2,1)S(1)}, bf16[256,1536]{1,0:T(8,128)(2,1)S(1)}, u32[]{:S(2)}, u32[]{:S(2)}) collective-permute-start(bf16[256,1536]{1,0:T(8,128)(2,1)S(1)} %constant_dynamic-update-slice_fusion), channel_id=1, source_target_pairs={{0,16},{4,20},{16,24},{20,28},{1,17},{5,21},{17,25},{21,29},{2,18}... | collective-permute-start | bytes 2359304 | tf_op jit(solution)/shard_map/ppermute | solution.py:73
  297.6 47.0 %collective-permute-start.57 = (bf16[2,48,6912]{2,1,0:T(8,128)(2,1)}, bf16[2,48,6912]{2,1,0:T(8,128)(2,1)S(1)}, u32[]{:S(2)}, u32[]{:S(2)}) collective-permute-start(bf16[2,48,6912]{2,1,0:T(8,128)(2,1)} %get-tuple-element.273), channel_id=1, source_target_pairs={{0,1},{1,0},{2,3},{3,2},{4,5},{5,4},{6,7},{7,6},{8,9},{9,8},{10,11... | collective-permute-start | bytes 3981320 | tf_op jit(solution)/shard_map/ppermute | solution.py:757
  298.8 47.1 %collective-permute-start.58 = (bf16[2,48,6912]{2,1,0:T(8,128)(2,1)}, bf16[2,48,6912]{2,1,0:T(8,128)(2,1)S(1)}, u32[]{:S(2)}, u32[]{:S(2)}) collective-permute-start(bf16[2,48,6912]{2,1,0:T(8,128)(2,1)} %get-tuple-element.274), channel_id=1, source_target_pairs={{0,2},{1,3},{2,0},{3,1},{4,6},{5,7},{6,4},{7,5},{8,10},{9,11},{10,... | collective-permute-start | bytes 3981320 | tf_op jit(solution)/shard_map/ppermute | solution.py:757
  326.9 34.9 %collective-permute-start.56 = (bf16[4,96,2432]{2,1,0:T(8,128)(2,1)S(1)}, bf16[4,96,2432]{2,1,0:T(8,128)(2,1)S(1)}, u32[]{:S(2)}, u32[]{:S(2)}) collective-permute-start(bf16[4,96,2432]{2,1,0:T(8,128)(2,1)S(1)} %copy-done.62), channel_id=1, source_target_pairs={{0,16},{16,0},{1,17},{17,1},{2,18},{18,2},{3,19},{19,3},{4,20},{20... | collective-permute-start | bytes 5603336 | tf_op jit(solution)/shard_map/ppermute | solution.py:738
  352.6 31.0 %collective-permute-start.68 = (bf16[96,5504]{1,0:T(8,128)(2,1)S(1)}, bf16[96,5504]{1,0:T(8,128)(2,1)S(1)}, u32[]{:S(2)}, u32[]{:S(2)}) collective-permute-start(bf16[96,5504]{1,0:T(8,128)(2,1)S(1)} %maximum_maximum_fusion), channel_id=1, source_target_pairs={{0,4},{12,8},{1,5},{13,9},{2,6},{14,10},{3,7},{15,11},{16,20},{28,... | collective-permute-start | bytes 3170312 | tf_op jit(solution)/shard_map/ppermute | solution.py:757
  360.5 21.8 %collective-permute-start.77 = (bf16[96,3840]{1,0:T(8,128)(2,1)S(1)}, bf16[96,3840]{1,0:T(8,128)(2,1)S(1)}, u32[]{:S(2)}, u32[]{:S(2)}) collective-permute-start(bf16[96,3840]{1,0:T(8,128)(2,1)S(1)} %add_convert_fusion.8), channel_id=1, source_target_pairs={{4,0},{8,12},{5,1},{9,13},{6,2},{10,14},{7,3},{11,15},{20,16},{24,... | collective-permute-start | bytes 2211848 | tf_op jit(solution)/shard_map/ppermute | solution.py:757
  382.3 92.4 %collective-permute-start.85 = (bf16[96,3840]{1,0:T(8,128)(2,1)S(1)}, bf16[96,3840]{1,0:T(8,128)(2,1)S(1)}, u32[]{:S(2)}, u32[]{:S(2)}) collective-permute-start(bf16[96,3840]{1,0:T(8,128)(2,1)S(1)} %broadcast_select_fusion.4), channel_id=1, source_target_pairs={{0,16},{1,17},{2,18},{3,19},{4,20},{5,21},{6,22},{7,23},{8,24},{9,... | collective-permute-start | bytes 2211848 | tf_op jit(solution)/shard_map/ppermute | solution.py:861
  406.0 30.8 %collective-permute-start.78 = (bf16[96,5504]{1,0:T(8,128)(2,1)S(1)}, bf16[96,5504]{1,0:T(8,128)(2,1)S(1)}, u32[]{:S(2)}, u32[]{:S(2)}) collective-permute-start(bf16[96,5504]{1,0:T(8,128)(2,1)S(1)} %add_convert_fusion.6), channel_id=1, source_target_pairs={{4,0},{8,12},{5,1},{9,13},{6,2},{10,14},{7,3},{11,15},{20,16},{24,... | collective-permute-start | bytes 3170312 | tf_op jit(solution)/shard_map/ppermute | solution.py:757
  438.5 22.5 %collective-permute-start.83 = (bf16[96,5504]{1,0:T(8,128)(2,1)S(1)}, bf16[96,5504]{1,0:T(8,128)(2,1)S(1)}, u32[]{:S(2)}, u32[]{:S(2)}) collective-permute-start(bf16[96,5504]{1,0:T(8,128)(2,1)S(1)} %broadcast_select_fusion.3), channel_id=1, source_target_pairs={{0,16},{1,17},{2,18},{3,19},{4,20},{5,21},{6,22},{7,23},{8,24},{9,... | collective-permute-start | bytes 3170312 | tf_op jit(solution)/shard_map/ppermute | solution.py:861
  439.8 21.1 %collective-permute-start.76 = (bf16[96,2432]{1,0:T(8,128)(2,1)S(1)}, bf16[96,2432]{1,0:T(8,128)(2,1)S(1)}, u32[]{:S(2)}, u32[]{:S(2)}) collective-permute-start(bf16[96,2432]{1,0:T(8,128)(2,1)S(1)} %add_convert_fusion.15), channel_id=1, source_target_pairs={{4,8},{8,4},{5,9},{9,5},{6,10},{10,6},{7,11},{11,7},{20,24},{24,20... | collective-permute-start | bytes 1400840 | tf_op jit(solution)/shard_map/ppermute | solution.py:757
  (133 other events, 1469.2 us)
Sparse Core Ops, SparseCore 0:
  15.0 83.3 all-gather.2
  100.8 66.0 all-gather.4
  200.2 86.6 reduce-scatter.1

commit v7 on v6

--- a/solution.py
+++ b/solution.py
@@ -66,9 +66,11 @@
     return jnp.where(core == base, own, received)
 
 
-def return_rows(value, layer):
+def return_rows(value, layer, background=None):
     ctx, cores = lax.axis_size("ctx"), lax.axis_size("section")
     half = ctx // cores
+    if background is not None and "mid" in background.links:
+        value, _ = lax.optimization_barrier((value, background.links["mid"]))
     return [
         lax.ppermute(
             value,
@@ -681,7 +683,9 @@
     return result, (x, weight, vec, attn_saved, inner, hidden, mixed), returned
 
 
-def layer_backward(saved, grad, rest, ids, order, parts, size, shards, ratio, layer, background):
+def layer_backward(
+    saved, grad, rest, ids, order, parts, size, shards, ratio, layer, background, result=None
+):
     x, weight, vec, attn_saved, inner, hidden, mixed = saved
     last = layer == 0
     column = (1 + ratio) * x.shape[1]
@@ -690,27 +694,29 @@
     )
     received = exchange(background.slot("AD", sent))
     early = early_grads(ids, middle, ghid, mixed, gattn, act, grad, parts, shards, ratio, last)
-    tied = lax.optimization_barrier((*received, *early))
-    received, early = tied[:parts], tied[parts:]
+    tied = lax.optimization_barrier((*received, *early, result if result is not None else grad))
+    received, early = tied[:parts], tied[parts:-1]
+    returned = None
     if last:
         first = background.add("B", early_task0(*early, background, column))
     else:
         first = background.add("C", early_task1(*early, background, column))
+        returned = background.add("A", return_task(tied[-1], layer, 0))
     sent = attention_backward(received, attn_saved, order, size)
-    if last:
-        sent = background.slot("BCD", sent)
+    sent = background.slot("BC" if last else "A", sent)
     received = exchange(sent)
     if last:
         received = background.slot("CD", received)
-    results = qkv_backward(ids, x, ginner, vec, table, weight, received, shards)
-    grad_x, *late = lax.optimization_barrier(tuple(results))
+    grad_x, *late = lax.optimization_barrier(
+        tuple(qkv_backward(ids, x, ginner, vec, table, weight, received, shards))
+    )
     if last:
-        for lane in "DCB":
+        for lane in "EB":
             background.slot(lane, [grad_x])
         second = background.add("A", late_task0(*late, background))
     else:
         second = background.add("D", late_task1(*late, background))
-    return grad_x, first, second
+    return grad_x, first, second, returned
 
 
 def blocks_to_columns(value, parts):
@@ -749,7 +755,6 @@
     def __init__(self):
         self.tasks = []
         self.links = {}
-        self.shared = {}
 
     def send(self, link, value, axis, pairs):
         if link in self.links:
@@ -803,6 +808,7 @@
 
 def permuted_value(keep, send, background, hold):
     (received,) = yield [swap_cores(send)]
+    (received,) = yield from idle([received], hold)
     rows = keep.shape[1] // 2
 
     def summed(slots, side):
@@ -813,7 +819,6 @@
         background.across(summed(slice(1, 4, 2), top), 1),
         background.across(summed(slice(2, 4), low), 2),
     ]
-    by_x, by_y = yield from idle([by_x, by_y], hold)
     first = sum_pair(summed(slice(0, 4, 2), top), by_x)
     second = sum_pair(summed(slice(0, 2), low), by_y)
     by_y, by_x = yield [background.across(first[1], 2), background.across(second[1], 1)]
@@ -836,13 +841,13 @@
     value = lax.psum_scatter(pack, SHARDS, scatter_dimension=0, tiled=True)
     (value,) = yield [value]
     (value,) = yield [value]
-    background.shared["down"] = value[:, column:]
-    return (yield from ctx_task(value[:, :column], 1, background))
+    other = background.add("E", ctx_task(value[:, column:], 1, background))
+    mine = yield from ctx_task(value[:, :column], 1, background)
+    return mine, other
 
 
 def late_task1(keep, send, background):
-    value = yield from permuted_value(keep, send, background, 1)
-    value = jnp.concatenate([background.shared["down"], value], axis=1)
+    value = yield from permuted_value(keep, send, background, 2)
     return (yield from ctx_task(value, 1, background))
 
 
@@ -862,9 +867,9 @@
     return value, other
 
 
-def return_task(value, layer, pause):
+def return_task(value, layer, pause, background=None):
     (value,) = yield from idle([value], pause)
-    flight = yield return_rows(value, layer)
+    flight = yield return_rows(value, layer, background)
     return flight
 
 
@@ -910,19 +915,19 @@
     out1, saved1, back_out0 = layer_forward(out0, first1, rest1, *sizes, out0)
     cot = bring_rows(late_cot, core, base)
     background = Background()
-    grad1, early1, late1 = layer_backward(saved1, cot, rest1, *sizes, 1, background)
-    back1 = background.add("A", return_task(jnp.concatenate([out1, grad1], axis=1), 1, 0))
-    grad0, early0, late0 = layer_backward(saved0, grad1, rest0, *sizes, 0, background)
-    back0 = background.add("A", return_task(grad0, 0, 5))
+    grad1, early1, late1, back_out1 = layer_backward(
+        saved1, cot, rest1, *sizes, 1, background, out1
+    )
+    back1 = background.add("A", return_task(grad1, 1, 0))
+    grad0, early0, late0, _ = layer_backward(saved0, grad1, rest0, *sizes, 0, background)
+    back0 = background.add("A", return_task(grad0, 0, 5, background))
     background.finish()
 
     def chosen(values0, values1):
         return jnp.stack([jnp.where(core == 0, a, b) for a, b in zip(values0, values1)])
 
-    layer_outputs = chosen(back_out0, [value[:, :width] for value in back1["result"]])
-    input_grads = chosen(
-        back0["result"], [value[:, width:] for value in back1["result"]]
-    ).astype(F32)
+    layer_outputs = chosen(back_out0, back_out1["result"])
+    input_grads = chosen(back0["result"], back1["result"]).astype(F32)
 
     def joined(pair0, pair1):
         return jnp.where(
@@ -931,11 +936,10 @@
             jnp.concatenate([pair1[1], pair1[0]]),
         ).astype(F32)
 
-    (up0, down0), up1, rest1 = early0["result"], early1["result"], late1["result"]
-    hidden = ratio * width
+    (up0, down0), (up1, down1) = early0["result"], early1["result"]
     early = joined(up0, up1)
-    late = joined(late0["result"], [value[:, hidden:] for value in rest1])
-    down = joined(down0["result"], [value[:, :hidden] for value in rest1])
+    late = joined(late0["result"], late1["result"])
+    down = joined(down0["result"], down1["result"])
     table = late[:, 3 * width :].T
     return (
         layer_outputs[None, :, None],

time: 505 us -> 483 us (0.956)
  waiting for transfers between devices: 176 us -> 145 us
  starting transfers between devices: 130 us -> 137 us
    ppermute x27 -> x30, waiting for transfers between devices: 91.4 us -> 60.7 us  [send(): moved = lax.ppermute(value, axis, pairs)]
    ppermute x13, starting transfers between devices: 17.7 us -> 12.6 us  [swap_cores(): return lax.ppermute(value, 'section', [(0, 1), (1, 0)])]
    ppermute x6 -> x8, starting transfers between devices: 19.3 us -> 24 us  [return_rows(): lax.ppermute(value, GROUP, [(place_of(z // half, m * half + z % half), pl...]
    ppermute x5 -> x6, starting transfers between devices: 21.2 us -> 25 us  [ctx_task(): other, = (yield [lax.ppermute(value, 'section', [(1 - layer, layer)])])]
    ppermute x27 -> x30, starting transfers between devices: 39.9 us -> 43 us  [send(): moved = lax.ppermute(value, axis, pairs)]
    convert_element_type x22 -> x24, other arithmetic: 12.8 us -> 12.9 us  [sum_pair(): return (a.astype(F32) + b.astype(F32)).astype(BF)]
  transfers between devices with their start and end apart: 90 -> 96, of which waited for: 36 -> 34; matrix products, arithmetic and copies ran while one was open for 7% -> 7% of each run, Pallas kernels for 21% -> 22%
where the time goes in v7:
time: 483 us; the launch traced here: 474 us
  waiting for transfers between devices  145 us (30%)
  starting transfers between devices  137 us (28%)
  Pallas kernels  129 us (27%)
  local copies, waits for them, and re-layouts  24.4 us (5%)
  other arithmetic  22.7 us (5%)
  between operations  15.4 us (3%)
    ppermute x30, waiting for transfers between devices, send(): moved = lax.ppermute(value, axis, pairs)  60.7 us
    ppermute x24, waiting for transfers between devices, exchange(): moved.append(lax.ppermute(pieces[d], GROUP, pairs))  54 us
    ppermute x30, starting transfers between devices, send(): moved = lax.ppermute(value, axis, pairs)  43 us
    pallas_call x2, Pallas kernels, mlp_backward(): pl.pallas_call(functools.partial(mlp_back_kernel, parts=parts, shards=sha...  26.5 us
    ppermute x6, starting transfers between devices, ctx_task(): other, = (yield [lax.ppermute(value, 'section', [(1 - layer, layer)])])  25 us
    ppermute x8, starting transfers between devices, return_rows(): lax.ppermute(value, GROUP, [(place_of(z // half, m * half + z % half), pl...  24 us
    pallas_call x2, Pallas kernels, mlp_forward(): pl.pallas_call(functools.partial(mlp_kernel, parts=parts, shards=shards,...  19.3 us
    ppermute x24, starting transfers between devices, exchange(): moved.append(lax.ppermute(pieces[d], GROUP, pairs))  18.4 us
  transfers between devices with their start and end apart: 96, of which 34 were waited for; matrix products, arithmetic and copies ran while one was open for 7% of the time, Pallas kernels for 22%

profile of v7, /device:TPU:1, one launch (start us, length us, event | category | flops | bytes accessed | tf_op | source)
XLA Modules:
  0.0 474.1 jit_solution(15804537621424388359)
XLA Ops:
  55.4 6.6 %qkv_project.2 = (bf16[576,256]{1,0:T(8,128)(2,1)}, bf16[576,256]{1,0:T(8,128)(2,1)}, bf16[576,256]{1,0:T(8,128)(2,1)}, bf16[576,256]{1,0:T(8,128)(2,1)}, bf16[768,2304]{1,0:T(8,128)(2,1)}, /*index=5*/f32[16,768]{1,0:T(8,128)}) custom-call(s32[14]{0:T(128)} %concatenate.53.ids_ref, bf16[256,768]{1,0:T(8,128)(2,1)} %bitcast_select_fusion.1.x_ref, ...), custom_call_target="tpu_custom_call" | custom-call | tf_op jit(solution)/shard_map/qkv_project/pallas_call | solution.py:161
  78.7 8.4 %attn_fwd.2 = (bf16[192,256]{1,0:T(8,128)(2,1)}, bf16[192,256]{1,0:T(8,128)(2,1)}, bf16[192,256]{1,0:T(8,128)(2,1)}, bf16[192,256]{1,0:T(8,128)(2,1)}, bf16[576,...) custom-call(s32[8]{0:T(128)} %pad_add_fusion.order_ref, ...), custom_call_target="tpu_custom_call" | custom-call | tf_op jit(solution)/shard_map/attn_fwd/pallas_call | solution.py:294
  99.4 9.6 %mlp_forward.2 = (bf16[256,768]{1,0:T(8,128)(2,1)}, f32[256,768]{1,0:T(8,128)}, f32[256,3072]{1,0:T(8,128)}, bf16[768,256]{1,0:T(8,128)(2,1)}) custom-call(s32[14]{0:T(128)} %concatenate.53.ids_ref, bf16[256,768]{1,0:T(8,128)(2,1)} %bitcast_select_fusion.1.x_ref, f32[16,768]{1,0:T(8,128)} %get-tuple-element.162.vec_ref, f32[1,3072]{1,0:T(1,128)} %reshape.191.bias_ref, ...), custom_call_target="tpu_custom_call" | custom-call | tf_op jit(solution)/shard_map/mlp_forward/pallas_call | solution.py:416
  119.8 10.6 %collective-permute-done.27.refs_1_ = bf16[576,256]{1,0:T(8,128)(2,1)S(1)} collective-permute-done((bf16[576,256]{1,0:T(8,128)(2,1)}, bf16[576,256]{1,0:T(8,128)(2,1)S(1)}, u32[]{:S(2)}, u32[]{:S(2)}) %collective-permute-start.27) | collective-permute-done | bytes 294944 | tf_op jit(solution)/shard_map/ppermute | solution.py:52
  137.0 6.8 %collective-permute-start.33 = (bf16[256,768]{1,0:T(8,128)(2,1)S(1)}, bf16[256,768]{1,0:T(8,128)(2,1)S(1)}, u32[]{:S(2)}, u32[]{:S(2)}) collective-permute-start(bf16[256,768]{1,0:T(8,128)(2,1)S(1)} %copy-done.3), channel_id=1, source_target_pairs={{0,0},{4,4},{16,8},{20,12},{1,1},{5,5},{17,9},{21,13},{2,2},{6,6},... | collective-permute-start | bytes 1179656 | tf_op jit(solution)/shard_map/ppermute | solution.py:75
  145.3 8.4 %attn_fwd.3 = (bf16[192,256]{1,0:T(8,128)(2,1)}, bf16[192,256]{1,0:T(8,128)(2,1)}, bf16[192,256]{1,0:T(8,128)(2,1)}, bf16[192,256]{1,0:T(8,128)(2,1)}, bf16[576,...) custom-call(s32[8]{0:T(128)} %pad_add_fusion.order_ref, ...), custom_call_target="tpu_custom_call" | custom-call | tf_op jit(solution)/shard_map/attn_fwd/pallas_call | solution.py:294
  159.6 7.3 %all-gather.5.cloned.1.call-done.pack_ref = bf16[768,6912]{1,0:T(8,128)(2,1)} async-done(((bf16[96,6912]{1,0:T(8,128)(2,1)}), bf16[768,6912]{1,0:T(8,128)(2,1)}) %all-gather.5.cloned.1.call-update) | async-done | bytes 10616848 | tf_op jit(solution)/shard_map/all_gather | solution.py:735
  166.9 9.7 %mlp_forward.3 = (bf16[256,768]{1,0:T(8,128)(2,1)}, f32[256,768]{1,0:T(8,128)}, f32[256,3072]{1,0:T(8,128)}, bf16[768,256]{1,0:T(8,128)(2,1)}) custom-call(s32[14]{0:T(128)} %concatenate.53.ids_ref, bf16[256,768]{1,0:T(8,128)(2,1)} %get-tuple-element.185.x_ref, f32[16,768]{1,0:T(8,128)} %get-tuple-element.188.vec_ref, f32[1,3072]{1,0:T(1,128)} %reshape.193.bias_ref, ...), custom_call_target="tpu_custom_call" | custom-call | tf_op jit(solution)/shard_map/mlp_forward/pallas_call | solution.py:416
  176.6 13.1 %mlp_backward.2 = (bf16[192,256]{1,0:T(8,128)(2,1)}, bf16[192,256]{1,0:T(8,128)(2,1)}, bf16[192,256]{1,0:T(8,128)(2,1)}, bf16[192,256]{1,0:T(8,128)(2,1)}, f32[2...) custom-call(s32[14]{0:T(128)} %concatenate.53.ids_ref, ...), custom_call_target="tpu_custom_call" | custom-call | tf_op jit(solution)/shard_map/mlp_backward/pallas_call | solution.py:491
  191.8 8.2 %early_grads.2 = bf16[768,6912]{1,0:T(8,128)(2,1)} custom-call(s32[14]{0:T(128)} %concatenate.53.ids_ref, bf16[256,768]{1,0:T(8,128)(2,1)} %get-tuple-element.203.middle_ref, bf16[256,3072]{1,0:T(8,128)(2,1)} %get-tuple-element.204.ghid_ref, bf16[768,256]{1,0:T(8,128)(2,1)} %get-tuple-element.205.mixed_ref, bf16[256,768]{1,0:T(8,128)(2,1)} %get-tuple-element.206.gattn_ref, ...), custom_call_target="tpu_custom_call" | custom-call | tf_op jit(solution)/shard_map/early_grads/pallas_call | solution.py:587
  206.0 8.7 %attn_bwd.2 = (bf16[576,256]{1,0:T(8,128)(2,1)}, bf16[576,256]{1,0:T(8,128)(2,1)}, bf16[576,256]{1,0:T(8,128)(2,1)}, bf16[576,256]{1,0:T(8,128)(2,1)}) custom-call(s32[8]{0:T(128)} %pad_add_fusion.order_ref, bf16[192,256]{1,0:T(8,128)(2,1)} %get-tuple-element.209.refs_0_, bf16[192,256]{1,0:T(8,128)(2,1)} %copy-done.48, bf16[192,256]{1,0:T(8,128)(2,1)} %copy-done.49, ...), custom_call_target="tpu_custom_call" | custom-call | tf_op jit(solution)/shard_map/attn_bwd/pallas_call | solution.py:323
  217.0 7.8 %collective-permute-done.41.refs_1_ = bf16[576,256]{1,0:T(8,128)(2,1)S(1)} collective-permute-done((bf16[576,256]{1,0:T(8,128)(2,1)}, bf16[576,256]{1,0:T(8,128)(2,1)S(1)}, u32[]{:S(2)}, u32[]{:S(2)}) %collective-permute-start.41) | collective-permute-done | bytes 294944 | tf_op jit(solution)/shard_map/ppermute | solution.py:52
  229.9 8.8 %qkv_backward.2 = (bf16[256,768]{1,0:T(8,128)(2,1)}, bf16[4,96,2432]{2,1,0:T(8,128)(2,1)}, bf16[4,96,2432]{2,1,0:T(8,128)(2,1)}) custom-call(s32[14]{0:T(128)} %concatenate.53.ids_ref, bf16[256,768]{1,0:T(8,128)(2,1)} %get-tuple-element.185.x_ref, f32[256,768]{1,0:T(8,128)} %get-tuple-element.224.ginner_ref, f32[16,768]{1,0:T(8,128)} %get-tuple-element.188.vec_ref, ...), custom_call_target="tpu_custom_call" | custom-call | tf_op jit(solution)/shard_map/qkv_backward/pallas_call | solution.py:649
  243.6 13.5 %mlp_backward.3 = (bf16[192,256]{1,0:T(8,128)(2,1)}, bf16[192,256]{1,0:T(8,128)(2,1)}, bf16[192,256]{1,0:T(8,128)(2,1)}, bf16[192,256]{1,0:T(8,128)(2,1)}, f32[2...) custom-call(s32[14]{0:T(128)} %concatenate.53.ids_ref, ...), custom_call_target="tpu_custom_call" | custom-call | tf_op jit(solution)/shard_map/mlp_backward/pallas_call | solution.py:491
  260.0 9.3 %early_grads.3 = (bf16[4,96,6912]{2,1,0:T(8,128)(2,1)}, bf16[4,96,6912]{2,1,0:T(8,128)(2,1)}) custom-call(s32[14]{0:T(128)} %concatenate.53.ids_ref, bf16[256,768]{1,0:T(8,128)(2,1)} %get-tuple-element.246.middle_ref, bf16[256,3072]{1,0:T(8,128)(2,1)} %get-tuple-element.247.ghid_ref, bf16[768,256]{1,0:T(8,128)(2,1)} %get-tuple-element.248.mixed_ref, ...), custom_call_target="tpu_custom_call" | custom-call | tf_op jit(solution)/shard_map/early_grads/pallas_call | solution.py:587
  270.6 8.7 %attn_bwd.3 = (bf16[576,256]{1,0:T(8,128)(2,1)}, bf16[576,256]{1,0:T(8,128)(2,1)}, bf16[576,256]{1,0:T(8,128)(2,1)}, bf16[576,256]{1,0:T(8,128)(2,1)}) custom-call(s32[8]{0:T(128)} %pad_add_fusion.order_ref, bf16[192,256]{1,0:T(8,128)(2,1)} %get-tuple-element.253.refs_0_, bf16[192,256]{1,0:T(8,128)(2,1)} %copy-done.45, bf16[192,256]{1,0:T(8,128)(2,1)} %copy-done.46, ...), custom_call_target="tpu_custom_call" | custom-call | tf_op jit(solution)/shard_map/attn_bwd/pallas_call | solution.py:323
  300.8 9.4 %qkv_backward.3 = (bf16[256,768]{1,0:T(8,128)(2,1)}, bf16[4,96,2432]{2,1,0:T(8,128)(2,1)}, bf16[4,96,2432]{2,1,0:T(8,128)(2,1)}) custom-call(s32[14]{0:T(128)} %concatenate.53.ids_ref, bf16[256,768]{1,0:T(8,128)(2,1)} %bitcast_select_fusion.1.x_ref, f32[256,768]{1,0:T(8,128)} %get-tuple-element.234.ginner_ref, f32[16,768]{1,0:T(8,128)} %get-tuple-element.162.vec_ref, ...), custom_call_target="tpu_custom_call" | custom-call | tf_op jit(solution)/shard_map/qkv_backward/pallas_call | solution.py:649
  314.6 11.2 %collective-permute-done.67 = bf16[96,3072]{1,0:T(8,128)(2,1)S(1)} collective-permute-done((bf16[96,3072]{1,0:T(8,128)(2,1)}, bf16[96,3072]{1,0:T(8,128)(2,1)S(1)}, u32[]{:S(2)}, u32[]{:S(2)}) %collective-permute-start.67) | collective-permute-done | bytes 589856 | tf_op jit(solution)/shard_map/ppermute | solution.py:762
  339.7 7.9 %collective-permute-done.68 = bf16[96,3840]{1,0:T(8,128)(2,1)S(1)} collective-permute-done((bf16[96,3840]{1,0:T(8,128)(2,1)S(1)}, bf16[96,3840]{1,0:T(8,128)(2,1)S(1)}, u32[]{:S(2)}, u32[]{:S(2)}) %collective-permute-start.68) | collective-permute-done | bytes 737312 | tf_op jit(solution)/shard_map/ppermute | solution.py:762
  363.7 8.1 %collective-permute-done.69 = bf16[96,3840]{1,0:T(8,128)(2,1)S(1)} collective-permute-done((bf16[96,3840]{1,0:T(8,128)(2,1)S(1)}, bf16[96,3840]{1,0:T(8,128)(2,1)S(1)}, u32[]{:S(2)}, u32[]{:S(2)}) %collective-permute-start.69) | collective-permute-done | bytes 737312 | tf_op jit(solution)/shard_map/ppermute | solution.py:762
  412.9 10.9 %collective-permute-start.89 = (bf16[96,3840]{1,0:T(8,128)(2,1)S(1)}, bf16[96,3840]{1,0:T(8,128)(2,1)S(1)}, u32[]{:S(2)}, u32[]{:S(2)}) collective-permute-start(bf16[96,3840]{1,0:T(8,128)(2,1)S(1)} %broadcast_select_fusion.4), channel_id=1, source_target_pairs={{16,0},{17,1},{18,2},{19,3},{20,4},{21,5},{22,6},{23,7},{24,8},{25... | collective-permute-start | bytes 2211848 | tf_op jit(solution)/shard_map/ppermute | solution.py:866
  426.2 8.9 %collective-permute-start.91 = (bf16[96,3072]{1,0:T(8,128)(2,1)S(1)}, bf16[96,3072]{1,0:T(8,128)(2,1)S(1)}, u32[]{:S(2)}, u32[]{:S(2)}) collective-permute-start(bf16[96,3072]{1,0:T(8,128)(2,1)S(1)} %broadcast_select_fusion.6), channel_id=1, source_target_pairs={{16,0},{17,1},{18,2},{19,3},{20,4},{21,5},{22,6},{23,7},{24,8},{25... | collective-permute-start | bytes 1769480 | tf_op jit(solution)/shard_map/ppermute | solution.py:866
  438.8 7.4 %collective-permute-start.79 = (bf16[256,768]{1,0:T(8,128)(2,1)S(1)}, bf16[256,768]{1,0:T(8,128)(2,1)S(1)}, u32[]{:S(2)}, u32[]{:S(2)}) collective-permute-start(bf16[256,768]{1,0:T(8,128)(2,1)S(1)} %copy-done.54), channel_id=1, source_target_pairs={{0,0},{4,4},{16,8},{20,12},{1,1},{5,5},{17,9},{21,13},{2,2},{6,6},... | collective-permute-start | bytes 1179656 | tf_op jit(solution)/shard_map/ppermute | solution.py:75
  452.5 7.9 %collective-permute-done.86 = bf16[96,2432]{1,0:T(8,128)(2,1)S(1)} collective-permute-done((bf16[96,2432]{1,0:T(8,128)(2,1)S(1)}, bf16[96,2432]{1,0:T(8,128)(2,1)S(1)}, u32[]{:S(2)}, u32[]{:S(2)}) %collective-permute-start.86) | collective-permute-done | bytes 466976 | tf_op jit(solution)/shard_map/ppermute | solution.py:762
  (405 shorter events, 241.7 us)
Async XLA Ops:
  7.2 92.2 %all-gather.3.cloned.1.call-start = ((), (), s32[]{:S(2)}) async-start(), calls=%async_computation.1 | async-start | bytes 11943936 | tf_op jit(solution)/shard_map/all_gather | solution.py:735
  14.8 152.1 %all-gather.5.cloned.1.call-start = ((), (), s32[]{:S(2)}) async-start(), calls=%async_computation.2 | async-start | bytes 11943936 | tf_op jit(solution)/shard_map/all_gather | solution.py:735
  15.6 266.4 %reduce-scatter.2.cloned.1.call-start = ((), (), s32[]{:S(2)}) async-start(), calls=%async_computation.3 | async-start | bytes 11943936 | tf_op jit(solution)/shard_map/reduce_scatter | solution.py:841
  21.9 20.5 %collective-permute-start = (bf16[256,768]{1,0:T(8,128)(2,1)S(1)}, bf16[256,768]{1,0:T(8,128)(2,1)S(1)}, u32[]{:S(2)}, u32[]{:S(2)}) collective-permute-start(bf16[256,768]{1,0:T(8,128)(2,1)S(1)} %select_bitcast_fusion.5), channel_id=1, source_target_pairs={{0,8},{4,12},{24,16},{28,20},{1,9},{5,13},{25,17},{29,21},{2,10},{... | collective-permute-start | bytes 1179656 | tf_op jit(solution)/shard_map/ppermute | solution.py:64
  23.2 19.8 %collective-permute-start.6 = (bf16[96,2432]{1,0:T(8,128)(2,1)S(1)}, bf16[96,2432]{1,0:T(8,128)(2,1)S(1)}, u32[]{:S(2)}, u32[]{:S(2)}) collective-permute-start(bf16[96,2432]{1,0:T(8,128)(2,1)S(1)} %get-tuple-element.361.refs_0_), channel_id=1, source_target_pairs={{0,16},{16,0},{1,17},{17,1},{2,18},{18,2},{3,19},{19,3},{4,20},{20... | collective-permute-start | bytes 1400840 | tf_op jit(solution)/shard_map/ppermute | solution.py:744
  43.7 20.3 %collective-permute-start.19 = (bf16[96,2432]{1,0:T(8,128)(2,1)S(1)}, bf16[96,2432]{1,0:T(8,128)(2,1)S(1)}, u32[]{:S(2)}, u32[]{:S(2)}) collective-permute-start(bf16[96,2432]{1,0:T(8,128)(2,1)S(1)} %get-tuple-element.360.refs_0_), channel_id=1, source_target_pairs={{0,2},{1,3},{2,0},{3,1},{4,6},{5,7},{6,4},{7,5},{8,10},{9,11},{10,... | collective-permute-start | bytes 1400840 | tf_op jit(solution)/shard_map/ppermute | solution.py:740
  64.1 23.0 %collective-permute-start.21 = (bf16[48,2432]{1,0:T(8,128)(2,1)S(1)}, bf16[48,2432]{1,0:T(8,128)(2,1)}, u32[]{:S(2)}, u32[]{:S(2)}) collective-permute-start(bf16[48,2432]{1,0:T(8,128)(2,1)S(1)} %slice.309), channel_id=1, source_target_pairs={{0,1},{1,0},{2,3},{3,2},{4,5},{5,4},{6,7},{7,6},{8,9},{9,8},{10,11... | collective-permute-start | bytes 700424 | tf_op jit(solution)/shard_map/ppermute | solution.py:740
  65.8 22.4 %collective-permute-start.20 = (bf16[48,2432]{1,0:T(8,128)(2,1)S(1)}, bf16[48,2432]{1,0:T(8,128)(2,1)}, u32[]{:S(2)}, u32[]{:S(2)}) collective-permute-start(bf16[48,2432]{1,0:T(8,128)(2,1)S(1)} %slice.308), channel_id=1, source_target_pairs={{0,2},{1,3},{2,0},{3,1},{4,6},{5,7},{6,4},{7,5},{8,10},{9,11},{10,... | collective-permute-start | bytes 700424 | tf_op jit(solution)/shard_map/ppermute | solution.py:740
  71.9 37.2 %collective-permute-start.22 = (bf16[96,2432]{1,0:T(8,128)(2,1)S(1)}, bf16[96,2432]{1,0:T(8,128)(2,1)S(1)}, u32[]{:S(2)}, u32[]{:S(2)}) collective-permute-start(bf16[96,2432]{1,0:T(8,128)(2,1)S(1)} %get-tuple-element.360.refs_0_), channel_id=1, source_target_pairs={{0,16},{16,0},{1,17},{17,1},{2,18},{18,2},{3,19},{19,3},{4,20},{20... | collective-permute-start | bytes 1400840 | tf_op jit(solution)/shard_map/ppermute | solution.py:744
  72.5 36.6 %collective-permute-start.24 = (bf16[96,2432]{1,0:T(8,128)(2,1)S(1)}, bf16[96,2432]{1,0:T(8,128)(2,1)}, u32[]{:S(2)}, u32[]{:S(2)}) collective-permute-start(bf16[96,2432]{1,0:T(8,128)(2,1)S(1)} %collective-permute-done.19.refs_2_), channel_id=1, source_target_pairs={{0,16},{16,0},{1,17},{17,1},{2,18},{18,2},{3,19},{19,3},{4,20},{20... | collective-permute-start | bytes 1400840 | tf_op jit(solution)/shard_map/ppermute | solution.py:744
  77.4 31.7 %collective-permute-start.23 = (bf16[96,2432]{1,0:T(8,128)(2,1)S(1)}, bf16[96,2432]{1,0:T(8,128)(2,1)}, u32[]{:S(2)}, u32[]{:S(2)}) collective-permute-start(bf16[96,2432]{1,0:T(8,128)(2,1)S(1)} %collective-permute-done.18.refs_1_), channel_id=1, source_target_pairs={{0,16},{16,0},{1,17},{17,1},{2,18},{18,2},{3,19},{19,3},{4,20},{20... | collective-permute-start | bytes 1400840 | tf_op jit(solution)/shard_map/ppermute | solution.py:744
  118.5 35.3 %collective-permute-start.35 = (bf16[256,768]{1,0:T(8,128)(2,1)S(1)}, bf16[256,768]{1,0:T(8,128)(2,1)S(1)}, u32[]{:S(2)}, u32[]{:S(2)}) collective-permute-start(bf16[256,768]{1,0:T(8,128)(2,1)S(1)} %select_bitcast_fusion.4), channel_id=1, source_target_pairs={{0,8},{4,12},{24,16},{28,20},{1,9},{5,13},{25,17},{29,21},{2,10},{... | collective-permute-start | bytes 1179656 | tf_op jit(solution)/shard_map/ppermute | solution.py:64
  136.3 23.3 %collective-permute-start.34 = (bf16[256,768]{1,0:T(8,128)(2,1)S(1)}, bf16[256,768]{1,0:T(8,128)(2,1)S(1)}, u32[]{:S(2)}, u32[]{:S(2)}) collective-permute-start(bf16[256,768]{1,0:T(8,128)(2,1)S(1)} %copy-done.3), channel_id=1, source_target_pairs={{8,0},{12,4},{24,8},{28,12},{9,1},{13,5},{25,9},{29,13},{10,2},{14... | collective-permute-start | bytes 1179656 | tf_op jit(solution)/shard_map/ppermute | solution.py:75
  137.0 22.6 %collective-permute-start.33 = (bf16[256,768]{1,0:T(8,128)(2,1)S(1)}, bf16[256,768]{1,0:T(8,128)(2,1)S(1)}, u32[]{:S(2)}, u32[]{:S(2)}) collective-permute-start(bf16[256,768]{1,0:T(8,128)(2,1)S(1)} %copy-done.3), channel_id=1, source_target_pairs={{0,0},{4,4},{16,8},{20,12},{1,1},{5,5},{17,9},{21,13},{2,2},{6,6},... | collective-permute-start | bytes 1179656 | tf_op jit(solution)/shard_map/ppermute | solution.py:75
  289.4 43.8 %collective-permute-start.56 = (bf16[2,48,6912]{2,1,0:T(8,128)(2,1)}, bf16[2,48,6912]{2,1,0:T(8,128)(2,1)S(1)}, u32[]{:S(2)}, u32[]{:S(2)}) collective-permute-start(bf16[2,48,6912]{2,1,0:T(8,128)(2,1)} %get-tuple-element.344), channel_id=1, source_target_pairs={{0,2},{1,3},{2,0},{3,1},{4,6},{5,7},{6,4},{7,5},{8,10},{9,11},{10,... | collective-permute-start | bytes 3981320 | tf_op jit(solution)/shard_map/ppermute | solution.py:762
  290.5 42.8 %collective-permute-start.55 = (bf16[2,48,6912]{2,1,0:T(8,128)(2,1)}, bf16[2,48,6912]{2,1,0:T(8,128)(2,1)}, u32[]{:S(2)}, u32[]{:S(2)}) collective-permute-start(bf16[2,48,6912]{2,1,0:T(8,128)(2,1)} %get-tuple-element.345), channel_id=1, source_target_pairs={{0,1},{1,0},{2,3},{3,2},{4,5},{5,4},{6,7},{7,6},{8,9},{9,8},{10,11... | collective-permute-start | bytes 3981320 | tf_op jit(solution)/shard_map/ppermute | solution.py:762
  312.7 45.7 %collective-permute-start.54 = (bf16[4,96,2432]{2,1,0:T(8,128)(2,1)}, bf16[4,96,2432]{2,1,0:T(8,128)(2,1)S(1)}, u32[]{:S(2)}, u32[]{:S(2)}) collective-permute-start(bf16[4,96,2432]{2,1,0:T(8,128)(2,1)} %get-tuple-element.278), channel_id=1, source_target_pairs={{0,16},{16,0},{1,17},{17,1},{2,18},{18,2},{3,19},{19,3},{4,20},{20... | collective-permute-start | bytes 5603336 | tf_op jit(solution)/shard_map/ppermute | solution.py:744
  326.6 20.9 %collective-permute-start.68 = (bf16[96,3840]{1,0:T(8,128)(2,1)S(1)}, bf16[96,3840]{1,0:T(8,128)(2,1)S(1)}, u32[]{:S(2)}, u32[]{:S(2)}) collective-permute-start(bf16[96,3840]{1,0:T(8,128)(2,1)S(1)} %copy-done.17), channel_id=1, source_target_pairs={{0,4},{12,8},{1,5},{13,9},{2,6},{14,10},{3,7},{15,11},{16,20},{28,... | collective-permute-start | bytes 2211848 | tf_op jit(solution)/shard_map/ppermute | solution.py:762
  358.5 93.7 %collective-permute-start.92 = (bf16[96,3072]{1,0:T(8,128)(2,1)S(1)}, bf16[96,3072]{1,0:T(8,128)(2,1)S(1)}, u32[]{:S(2)}, u32[]{:S(2)}) collective-permute-start(bf16[96,3072]{1,0:T(8,128)(2,1)S(1)} %broadcast_select_fusion.5), channel_id=1, source_target_pairs={{0,16},{1,17},{2,18},{3,19},{4,20},{5,21},{6,22},{7,23},{8,24},{9,... | collective-permute-start | bytes 1769480 | tf_op jit(solution)/shard_map/ppermute | solution.py:866
  360.2 22.1 %collective-permute-start.82 = (bf16[96,3840]{1,0:T(8,128)(2,1)S(1)}, bf16[96,3840]{1,0:T(8,128)(2,1)S(1)}, u32[]{:S(2)}, u32[]{:S(2)}) collective-permute-start(bf16[96,3840]{1,0:T(8,128)(2,1)S(1)} %add_convert_fusion.6), channel_id=1, source_target_pairs={{4,0},{8,12},{5,1},{9,13},{6,2},{10,14},{7,3},{11,15},{20,16},{24,... | collective-permute-start | bytes 2211848 | tf_op jit(solution)/shard_map/ppermute | solution.py:762
  383.6 42.6 %collective-permute-start.90 = (bf16[96,3840]{1,0:T(8,128)(2,1)S(1)}, bf16[96,3840]{1,0:T(8,128)(2,1)S(1)}, u32[]{:S(2)}, u32[]{:S(2)}) collective-permute-start(bf16[96,3840]{1,0:T(8,128)(2,1)S(1)} %broadcast_select_fusion.3), channel_id=1, source_target_pairs={{0,16},{1,17},{2,18},{3,19},{4,20},{5,21},{6,22},{7,23},{8,24},{9,... | collective-permute-start | bytes 2211848 | tf_op jit(solution)/shard_map/ppermute | solution.py:866
  412.9 22.2 %collective-permute-start.89 = (bf16[96,3840]{1,0:T(8,128)(2,1)S(1)}, bf16[96,3840]{1,0:T(8,128)(2,1)S(1)}, u32[]{:S(2)}, u32[]{:S(2)}) collective-permute-start(bf16[96,3840]{1,0:T(8,128)(2,1)S(1)} %broadcast_select_fusion.4), channel_id=1, source_target_pairs={{16,0},{17,1},{18,2},{19,3},{20,4},{21,5},{22,6},{23,7},{24,8},{25... | collective-permute-start | bytes 2211848 | tf_op jit(solution)/shard_map/ppermute | solution.py:866
  424.8 21.5 %collective-permute-start.85 = (bf16[96,2432]{1,0:T(8,128)(2,1)S(1)}, bf16[96,2432]{1,0:T(8,128)(2,1)S(1)}, u32[]{:S(2)}, u32[]{:S(2)}) collective-permute-start(bf16[96,2432]{1,0:T(8,128)(2,1)S(1)} %add_convert_fusion.14), channel_id=1, source_target_pairs={{4,0},{8,12},{5,1},{9,13},{6,2},{10,14},{7,3},{11,15},{20,16},{24,... | collective-permute-start | bytes 1400840 | tf_op jit(solution)/shard_map/ppermute | solution.py:762
  426.2 26.0 %collective-permute-start.91 = (bf16[96,3072]{1,0:T(8,128)(2,1)S(1)}, bf16[96,3072]{1,0:T(8,128)(2,1)S(1)}, u32[]{:S(2)}, u32[]{:S(2)}) collective-permute-start(bf16[96,3072]{1,0:T(8,128)(2,1)S(1)} %broadcast_select_fusion.6), channel_id=1, source_target_pairs={{16,0},{17,1},{18,2},{19,3},{20,4},{21,5},{22,6},{23,7},{24,8},{25... | collective-permute-start | bytes 1769480 | tf_op jit(solution)/shard_map/ppermute | solution.py:866
  (130 other events, 1420.0 us)
Sparse Core Ops, SparseCore 0:
  15.0 83.3 all-gather.2
  100.8 66.0 all-gather.4
  200.2 81.8 reduce-scatter.1

commit v8 on v7

--- a/solution.py
+++ b/solution.py
@@ -706,13 +706,12 @@
     sent = background.slot("BC" if last else "A", sent)
     received = exchange(sent)
     if last:
-        received = background.slot("CD", received)
+        received = background.slot("E", background.slot("CD", received))
     grad_x, *late = lax.optimization_barrier(
         tuple(qkv_backward(ids, x, ginner, vec, table, weight, received, shards))
     )
     if last:
-        for lane in "EB":
-            background.slot(lane, [grad_x])
+        background.slot("B", [grad_x])
         second = background.add("A", late_task0(*late, background))
     else:
         second = background.add("D", late_task1(*late, background))

time: 483 us -> 492 us (1.019)
  waiting for transfers between devices: 145 us -> 153 us
    ppermute x30, waiting for transfers between devices: 60.7 us -> 70.4 us  [send(): moved = lax.ppermute(value, axis, pairs)]
    unnamed x123 -> x129, local copies, waits for them, and re-layouts: 9.88 us -> 9.44 us
  transfers between devices with their start and end apart: 96 -> 96, of which waited for: 34 -> 37; matrix products, arithmetic and copies ran while one was open for 7% -> 7% of each run, Pallas kernels for 22% -> 22%
where the time goes in v8:
time: 492 us; the launch traced here: 483 us
  waiting for transfers between devices  153 us (31%)
  starting transfers between devices  138 us (28%)
  Pallas kernels  128 us (26%)
  other arithmetic  24.5 us (5%)
  local copies, waits for them, and re-layouts  23.1 us (5%)
  between operations  15.4 us (3%)
    ppermute x30, waiting for transfers between devices, send(): moved = lax.ppermute(value, axis, pairs)  70.4 us
    ppermute x24, waiting for transfers between devices, exchange(): moved.append(lax.ppermute(pieces[d], GROUP, pairs))  53 us
    ppermute x30, starting transfers between devices, send(): moved = lax.ppermute(value, axis, pairs)  42.1 us
    ppermute x6, starting transfers between devices, ctx_task(): other, = (yield [lax.ppermute(value, 'section', [(1 - layer, layer)])])  27.1 us
    pallas_call x2, Pallas kernels, mlp_backward(): pl.pallas_call(functools.partial(mlp_back_kernel, parts=parts, shards=sha...  26.5 us
    ppermute x8, starting transfers between devices, return_rows(): lax.ppermute(value, GROUP, [(place_of(z // half, m * half + z % half), pl...  21.6 us
    pallas_call x2, Pallas kernels, mlp_forward(): pl.pallas_call(functools.partial(mlp_kernel, parts=parts, shards=shards,...  19.3 us
    ppermute x24, starting transfers between devices, exchange(): moved.append(lax.ppermute(pieces[d], GROUP, pairs))  18.3 us
  transfers between devices with their start and end apart: 96, of which 37 were waited for; matrix products, arithmetic and copies ran while one was open for 7% of the time, Pallas kernels for 22%

profile of v8, /device:TPU:1, one launch (start us, length us, event | category | flops | bytes accessed | tf_op | source)
XLA Modules:
  0.0 483.1 jit_solution(1257004847204586667)
XLA Ops:
  78.7 8.4 %attn_fwd.2 = (bf16[192,256]{1,0:T(8,128)(2,1)}, bf16[192,256]{1,0:T(8,128)(2,1)}, bf16[192,256]{1,0:T(8,128)(2,1)}, bf16[192,256]{1,0:T(8,128)(2,1)}, bf16[576,...) custom-call(s32[8]{0:T(128)} %pad_add_fusion.order_ref, ...), custom_call_target="tpu_custom_call" | custom-call | tf_op jit(solution)/shard_map/attn_fwd/pallas_call | solution.py:294
  99.6 9.6 %mlp_forward.2 = (bf16[256,768]{1,0:T(8,128)(2,1)}, f32[256,768]{1,0:T(8,128)}, f32[256,3072]{1,0:T(8,128)}, bf16[768,256]{1,0:T(8,128)(2,1)}) custom-call(s32[14]{0:T(128)} %concatenate.53.ids_ref, bf16[256,768]{1,0:T(8,128)(2,1)} %bitcast_select_fusion.1.x_ref, f32[16,768]{1,0:T(8,128)} %get-tuple-element.166.vec_ref, f32[1,3072]{1,0:T(1,128)} %reshape.191.bias_ref, ...), custom_call_target="tpu_custom_call" | custom-call | tf_op jit(solution)/shard_map/mlp_forward/pallas_call | solution.py:416
  110.2 6.7 %qkv_project.3 = (bf16[576,256]{1,0:T(8,128)(2,1)}, bf16[576,256]{1,0:T(8,128)(2,1)}, bf16[576,256]{1,0:T(8,128)(2,1)}, bf16[576,256]{1,0:T(8,128)(2,1)}, bf16[768,2304]{1,0:T(8,128)(2,1)}, /*index=5*/f32[16,768]{1,0:T(8,128)}) custom-call(s32[14]{0:T(128)} %concatenate.53.ids_ref, bf16[256,768]{1,0:T(8,128)(2,1)} %get-tuple-element.189.x_ref, ...), custom_call_target="tpu_custom_call" | custom-call | tf_op jit(solution)/shard_map/qkv_project/pallas_call | solution.py:161
  120.1 10.6 %collective-permute-done.27.refs_1_ = bf16[576,256]{1,0:T(8,128)(2,1)S(1)} collective-permute-done((bf16[576,256]{1,0:T(8,128)(2,1)}, bf16[576,256]{1,0:T(8,128)(2,1)S(1)}, u32[]{:S(2)}, u32[]{:S(2)}) %collective-permute-start.27) | collective-permute-done | bytes 294944 | tf_op jit(solution)/shard_map/ppermute | solution.py:52
  136.6 6.8 %collective-permute-start.33 = (bf16[256,768]{1,0:T(8,128)(2,1)S(1)}, bf16[256,768]{1,0:T(8,128)(2,1)S(1)}, u32[]{:S(2)}, u32[]{:S(2)}) collective-permute-start(bf16[256,768]{1,0:T(8,128)(2,1)S(1)} %copy-done.3), channel_id=1, source_target_pairs={{0,0},{4,4},{16,8},{20,12},{1,1},{5,5},{17,9},{21,13},{2,2},{6,6},... | collective-permute-start | bytes 1179656 | tf_op jit(solution)/shard_map/ppermute | solution.py:75
  144.9 8.4 %attn_fwd.3 = (bf16[192,256]{1,0:T(8,128)(2,1)}, bf16[192,256]{1,0:T(8,128)(2,1)}, bf16[192,256]{1,0:T(8,128)(2,1)}, bf16[192,256]{1,0:T(8,128)(2,1)}, bf16[576,...) custom-call(s32[8]{0:T(128)} %pad_add_fusion.order_ref, ...), custom_call_target="tpu_custom_call" | custom-call | tf_op jit(solution)/shard_map/attn_fwd/pallas_call | solution.py:294
  159.3 7.6 %all-gather.5.cloned.1.call-done.pack_ref = bf16[768,6912]{1,0:T(8,128)(2,1)} async-done(((bf16[96,6912]{1,0:T(8,128)(2,1)}), bf16[768,6912]{1,0:T(8,128)(2,1)}) %all-gather.5.cloned.1.call-update) | async-done | bytes 10616848 | tf_op jit(solution)/shard_map/all_gather | solution.py:734
  166.9 9.7 %mlp_forward.3 = (bf16[256,768]{1,0:T(8,128)(2,1)}, f32[256,768]{1,0:T(8,128)}, f32[256,3072]{1,0:T(8,128)}, bf16[768,256]{1,0:T(8,128)(2,1)}) custom-call(s32[14]{0:T(128)} %concatenate.53.ids_ref, bf16[256,768]{1,0:T(8,128)(2,1)} %get-tuple-element.189.x_ref, f32[16,768]{1,0:T(8,128)} %get-tuple-element.192.vec_ref, f32[1,3072]{1,0:T(1,128)} %reshape.193.bias_ref, ...), custom_call_target="tpu_custom_call" | custom-call | tf_op jit(solution)/shard_map/mlp_forward/pallas_call | solution.py:416
  176.6 13.1 %mlp_backward.2 = (bf16[192,256]{1,0:T(8,128)(2,1)}, bf16[192,256]{1,0:T(8,128)(2,1)}, bf16[192,256]{1,0:T(8,128)(2,1)}, bf16[192,256]{1,0:T(8,128)(2,1)}, f32[2...) custom-call(s32[14]{0:T(128)} %concatenate.53.ids_ref, ...), custom_call_target="tpu_custom_call" | custom-call | tf_op jit(solution)/shard_map/mlp_backward/pallas_call | solution.py:491
  191.7 8.1 %early_grads.2 = bf16[768,6912]{1,0:T(8,128)(2,1)} custom-call(s32[14]{0:T(128)} %concatenate.53.ids_ref, bf16[256,768]{1,0:T(8,128)(2,1)} %get-tuple-element.207.middle_ref, bf16[256,3072]{1,0:T(8,128)(2,1)} %get-tuple-element.208.ghid_ref, bf16[768,256]{1,0:T(8,128)(2,1)} %get-tuple-element.209.mixed_ref, bf16[256,768]{1,0:T(8,128)(2,1)} %get-tuple-element.210.gattn_ref, ...), custom_call_target="tpu_custom_call" | custom-call | tf_op jit(solution)/shard_map/early_grads/pallas_call | solution.py:587
  205.9 8.7 %attn_bwd.2 = (bf16[576,256]{1,0:T(8,128)(2,1)}, bf16[576,256]{1,0:T(8,128)(2,1)}, bf16[576,256]{1,0:T(8,128)(2,1)}, bf16[576,256]{1,0:T(8,128)(2,1)}) custom-call(s32[8]{0:T(128)} %pad_add_fusion.order_ref, bf16[192,256]{1,0:T(8,128)(2,1)} %get-tuple-element.213.refs_0_, bf16[192,256]{1,0:T(8,128)(2,1)} %copy-done.51, bf16[192,256]{1,0:T(8,128)(2,1)} %copy-done.52, ...), custom_call_target="tpu_custom_call" | custom-call | tf_op jit(solution)/shard_map/attn_bwd/pallas_call | solution.py:323
  216.9 7.8 %collective-permute-done.41.refs_1_ = bf16[576,256]{1,0:T(8,128)(2,1)S(1)} collective-permute-done((bf16[576,256]{1,0:T(8,128)(2,1)}, bf16[576,256]{1,0:T(8,128)(2,1)S(1)}, u32[]{:S(2)}, u32[]{:S(2)}) %collective-permute-start.41) | collective-permute-done | bytes 294944 | tf_op jit(solution)/shard_map/ppermute | solution.py:52
  229.8 8.8 %qkv_backward.2 = (bf16[256,768]{1,0:T(8,128)(2,1)}, bf16[4,96,2432]{2,1,0:T(8,128)(2,1)}, bf16[4,96,2432]{2,1,0:T(8,128)(2,1)}) custom-call(s32[14]{0:T(128)} %concatenate.53.ids_ref, bf16[256,768]{1,0:T(8,128)(2,1)} %get-tuple-element.189.x_ref, f32[256,768]{1,0:T(8,128)} %get-tuple-element.228.ginner_ref, f32[16,768]{1,0:T(8,128)} %get-tuple-element.192.vec_ref, ...), custom_call_target="tpu_custom_call" | custom-call | tf_op jit(solution)/shard_map/qkv_backward/pallas_call | solution.py:649
  243.6 13.4 %mlp_backward.3 = (bf16[192,256]{1,0:T(8,128)(2,1)}, bf16[192,256]{1,0:T(8,128)(2,1)}, bf16[192,256]{1,0:T(8,128)(2,1)}, bf16[192,256]{1,0:T(8,128)(2,1)}, f32[2...) custom-call(s32[14]{0:T(128)} %concatenate.53.ids_ref, ...), custom_call_target="tpu_custom_call" | custom-call | tf_op jit(solution)/shard_map/mlp_backward/pallas_call | solution.py:491
  260.0 9.3 %early_grads.3 = (bf16[4,96,6912]{2,1,0:T(8,128)(2,1)}, bf16[4,96,6912]{2,1,0:T(8,128)(2,1)}) custom-call(s32[14]{0:T(128)} %concatenate.53.ids_ref, bf16[256,768]{1,0:T(8,128)(2,1)} %get-tuple-element.250.middle_ref, bf16[256,3072]{1,0:T(8,128)(2,1)} %get-tuple-element.251.ghid_ref, bf16[768,256]{1,0:T(8,128)(2,1)} %get-tuple-element.252.mixed_ref, ...), custom_call_target="tpu_custom_call" | custom-call | tf_op jit(solution)/shard_map/early_grads/pallas_call | solution.py:587
  271.6 8.7 %attn_bwd.3 = (bf16[576,256]{1,0:T(8,128)(2,1)}, bf16[576,256]{1,0:T(8,128)(2,1)}, bf16[576,256]{1,0:T(8,128)(2,1)}, bf16[576,256]{1,0:T(8,128)(2,1)}) custom-call(s32[8]{0:T(128)} %pad_add_fusion.order_ref, bf16[192,256]{1,0:T(8,128)(2,1)} %get-tuple-element.257.refs_0_, bf16[192,256]{1,0:T(8,128)(2,1)} %copy-done.48, bf16[192,256]{1,0:T(8,128)(2,1)} %copy-done.49, ...), custom_call_target="tpu_custom_call" | custom-call | tf_op jit(solution)/shard_map/attn_bwd/pallas_call | solution.py:323
  303.3 10.3 %collective-permute-done.54 = bf16[96,3072]{1,0:T(8,128)(2,1)} collective-permute-done((bf16[96,3072]{1,0:T(8,128)(2,1)S(1)}, bf16[96,3072]{1,0:T(8,128)(2,1)}, u32[]{:S(2)}, u32[]{:S(2)}) %collective-permute-start.54) | collective-permute-done | bytes 589856 | tf_op jit(solution)/shard_map/ppermute | solution.py:761
  313.5 8.9 %qkv_backward.3 = (bf16[256,768]{1,0:T(8,128)(2,1)}, bf16[4,96,2432]{2,1,0:T(8,128)(2,1)}, bf16[4,96,2432]{2,1,0:T(8,128)(2,1)}) custom-call(s32[14]{0:T(128)} %concatenate.53.ids_ref, bf16[256,768]{1,0:T(8,128)(2,1)} %bitcast_select_fusion.1.x_ref, f32[256,768]{1,0:T(8,128)} %get-tuple-element.238.ginner_ref, f32[16,768]{1,0:T(8,128)} %get-tuple-element.166.vec_ref, ...), custom_call_target="tpu_custom_call" | custom-call | tf_op jit(solution)/shard_map/qkv_backward/pallas_call | solution.py:649
  324.3 6.8 %collective-permute-start.68 = (bf16[96,3840]{1,0:T(8,128)(2,1)S(1)}, bf16[96,3840]{1,0:T(8,128)(2,1)S(1)}, u32[]{:S(2)}, u32[]{:S(2)}) collective-permute-start(bf16[96,3840]{1,0:T(8,128)(2,1)S(1)} %slice.286), channel_id=1, source_target_pairs={{0,4},{12,8},{1,5},{13,9},{2,6},{14,10},{3,7},{15,11},{16,20},{28,... | collective-permute-start | bytes 2211848 | tf_op jit(solution)/shard_map/ppermute | solution.py:761
  346.3 6.9 %collective-permute-done.61 = bf16[48,6912]{1,0:T(8,128)(2,1)S(1)} collective-permute-done((bf16[48,6912]{1,0:T(8,128)(2,1)S(1)}, bf16[48,6912]{1,0:T(8,128)(2,1)S(1)}, u32[]{:S(2)}, u32[]{:S(2)}) %collective-permute-start.61) | collective-permute-done | bytes 663584 | tf_op jit(solution)/shard_map/ppermute | solution.py:761
  412.9 7.0 %collective-permute-done.83 = bf16[96,3840]{1,0:T(8,128)(2,1)S(1)} collective-permute-done((bf16[96,3840]{1,0:T(8,128)(2,1)S(1)}, bf16[96,3840]{1,0:T(8,128)(2,1)S(1)}, u32[]{:S(2)}, u32[]{:S(2)}) %collective-permute-start.83) | collective-permute-done | bytes 737312 | tf_op jit(solution)/shard_map/ppermute | solution.py:761
  421.3 11.6 %collective-permute-start.89 = (bf16[96,3840]{1,0:T(8,128)(2,1)S(1)}, bf16[96,3840]{1,0:T(8,128)(2,1)S(1)}, u32[]{:S(2)}, u32[]{:S(2)}) collective-permute-start(bf16[96,3840]{1,0:T(8,128)(2,1)S(1)} %broadcast_select_fusion.4), channel_id=1, source_target_pairs={{16,0},{17,1},{18,2},{19,3},{20,4},{21,5},{22,6},{23,7},{24,8},{25... | collective-permute-start | bytes 2211848 | tf_op jit(solution)/shard_map/ppermute | solution.py:865
  435.3 10.4 %collective-permute-start.91 = (bf16[96,3072]{1,0:T(8,128)(2,1)S(1)}, bf16[96,3072]{1,0:T(8,128)(2,1)S(1)}, u32[]{:S(2)}, u32[]{:S(2)}) collective-permute-start(bf16[96,3072]{1,0:T(8,128)(2,1)S(1)} %broadcast_select_fusion.6), channel_id=1, source_target_pairs={{16,0},{17,1},{18,2},{19,3},{20,4},{21,5},{22,6},{23,7},{24,8},{25... | collective-permute-start | bytes 1769480 | tf_op jit(solution)/shard_map/ppermute | solution.py:865
  460.7 8.7 %collective-permute-done.86 = bf16[96,2432]{1,0:T(8,128)(2,1)S(1)} collective-permute-done((bf16[96,2432]{1,0:T(8,128)(2,1)S(1)}, bf16[96,2432]{1,0:T(8,128)(2,1)S(1)}, u32[]{:S(2)}, u32[]{:S(2)}) %collective-permute-start.86) | collective-permute-done | bytes 466976 | tf_op jit(solution)/shard_map/ppermute | solution.py:761
  (411 shorter events, 251.5 us)
Async XLA Ops:
  7.2 92.4 %all-gather.3.cloned.1.call-start = ((), (), s32[]{:S(2)}) async-start(), calls=%async_computation.1 | async-start | bytes 11943936 | tf_op jit(solution)/shard_map/all_gather | solution.py:734
  14.8 152.1 %all-gather.5.cloned.1.call-start = ((), (), s32[]{:S(2)}) async-start(), calls=%async_computation.2 | async-start | bytes 11943936 | tf_op jit(solution)/shard_map/all_gather | solution.py:734
  15.6 266.3 %reduce-scatter.2.cloned.1.call-start = ((), (), s32[]{:S(2)}) async-start(), calls=%async_computation.3 | async-start | bytes 11943936 | tf_op jit(solution)/shard_map/reduce_scatter | solution.py:840
  21.9 20.5 %collective-permute-start = (bf16[256,768]{1,0:T(8,128)(2,1)S(1)}, bf16[256,768]{1,0:T(8,128)(2,1)S(1)}, u32[]{:S(2)}, u32[]{:S(2)}) collective-permute-start(bf16[256,768]{1,0:T(8,128)(2,1)S(1)} %select_bitcast_fusion.5), channel_id=1, source_target_pairs={{0,8},{4,12},{24,16},{28,20},{1,9},{5,13},{25,17},{29,21},{2,10},{... | collective-permute-start | bytes 1179656 | tf_op jit(solution)/shard_map/ppermute | solution.py:64
  64.1 23.1 %collective-permute-start.21 = (bf16[48,2432]{1,0:T(8,128)(2,1)S(1)}, bf16[48,2432]{1,0:T(8,128)(2,1)}, u32[]{:S(2)}, u32[]{:S(2)}) collective-permute-start(bf16[48,2432]{1,0:T(8,128)(2,1)S(1)} %slice.309), channel_id=1, source_target_pairs={{0,1},{1,0},{2,3},{3,2},{4,5},{5,4},{6,7},{7,6},{8,9},{9,8},{10,11... | collective-permute-start | bytes 700424 | tf_op jit(solution)/shard_map/ppermute | solution.py:739
  66.5 21.7 %collective-permute-start.20 = (bf16[48,2432]{1,0:T(8,128)(2,1)}, bf16[48,2432]{1,0:T(8,128)(2,1)}, u32[]{:S(2)}, u32[]{:S(2)}) collective-permute-start(bf16[48,2432]{1,0:T(8,128)(2,1)} %slice.308), channel_id=1, source_target_pairs={{0,2},{1,3},{2,0},{3,1},{4,6},{5,7},{6,4},{7,5},{8,10},{9,11},{10,... | collective-permute-start | bytes 700424 | tf_op jit(solution)/shard_map/ppermute | solution.py:739
  71.9 37.4 %collective-permute-start.22 = (bf16[96,2432]{1,0:T(8,128)(2,1)S(1)}, bf16[96,2432]{1,0:T(8,128)(2,1)S(1)}, u32[]{:S(2)}, u32[]{:S(2)}) collective-permute-start(bf16[96,2432]{1,0:T(8,128)(2,1)S(1)} %get-tuple-element.368.refs_0_), channel_id=1, source_target_pairs={{0,16},{16,0},{1,17},{17,1},{2,18},{18,2},{3,19},{19,3},{4,20},{20... | collective-permute-start | bytes 1400840 | tf_op jit(solution)/shard_map/ppermute | solution.py:743
  73.2 36.1 %collective-permute-start.24 = (bf16[96,2432]{1,0:T(8,128)(2,1)S(1)}, bf16[96,2432]{1,0:T(8,128)(2,1)S(1)}, u32[]{:S(2)}, u32[]{:S(2)}) collective-permute-start(bf16[96,2432]{1,0:T(8,128)(2,1)S(1)} %collective-permute-done.19.refs_2_), channel_id=1, source_target_pairs={{0,16},{16,0},{1,17},{17,1},{2,18},{18,2},{3,19},{19,3},{4,20},{20... | collective-permute-start | bytes 1400840 | tf_op jit(solution)/shard_map/ppermute | solution.py:743
  77.4 31.9 %collective-permute-start.23 = (bf16[96,2432]{1,0:T(8,128)(2,1)S(1)}, bf16[96,2432]{1,0:T(8,128)(2,1)}, u32[]{:S(2)}, u32[]{:S(2)}) collective-permute-start(bf16[96,2432]{1,0:T(8,128)(2,1)S(1)} %collective-permute-done.18.refs_1_), channel_id=1, source_target_pairs={{0,16},{16,0},{1,17},{17,1},{2,18},{18,2},{3,19},{19,3},{4,20},{20... | collective-permute-start | bytes 1400840 | tf_op jit(solution)/shard_map/ppermute | solution.py:743
  118.8 34.6 %collective-permute-start.35 = (bf16[256,768]{1,0:T(8,128)(2,1)S(1)}, bf16[256,768]{1,0:T(8,128)(2,1)S(1)}, u32[]{:S(2)}, u32[]{:S(2)}) collective-permute-start(bf16[256,768]{1,0:T(8,128)(2,1)S(1)} %select_bitcast_fusion.4), channel_id=1, source_target_pairs={{0,8},{4,12},{24,16},{28,20},{1,9},{5,13},{25,17},{29,21},{2,10},{... | collective-permute-start | bytes 1179656 | tf_op jit(solution)/shard_map/ppermute | solution.py:64
  135.9 23.4 %collective-permute-start.34 = (bf16[256,768]{1,0:T(8,128)(2,1)S(1)}, bf16[256,768]{1,0:T(8,128)(2,1)S(1)}, u32[]{:S(2)}, u32[]{:S(2)}) collective-permute-start(bf16[256,768]{1,0:T(8,128)(2,1)S(1)} %copy-done.3), channel_id=1, source_target_pairs={{8,0},{12,4},{24,8},{28,12},{9,1},{13,5},{25,9},{29,13},{10,2},{14... | collective-permute-start | bytes 1179656 | tf_op jit(solution)/shard_map/ppermute | solution.py:75
  136.6 22.7 %collective-permute-start.33 = (bf16[256,768]{1,0:T(8,128)(2,1)S(1)}, bf16[256,768]{1,0:T(8,128)(2,1)S(1)}, u32[]{:S(2)}, u32[]{:S(2)}) collective-permute-start(bf16[256,768]{1,0:T(8,128)(2,1)S(1)} %copy-done.3), channel_id=1, source_target_pairs={{0,0},{4,4},{16,8},{20,12},{1,1},{5,5},{17,9},{21,13},{2,2},{6,6},... | collective-permute-start | bytes 1179656 | tf_op jit(solution)/shard_map/ppermute | solution.py:75
  288.9 44.0 %collective-permute-start.57 = (bf16[2,48,6912]{2,1,0:T(8,128)(2,1)}, bf16[2,48,6912]{2,1,0:T(8,128)(2,1)}, u32[]{:S(2)}, u32[]{:S(2)}) collective-permute-start(bf16[2,48,6912]{2,1,0:T(8,128)(2,1)} %get-tuple-element.352), channel_id=1, source_target_pairs={{0,2},{1,3},{2,0},{3,1},{4,6},{5,7},{6,4},{7,5},{8,10},{9,11},{10,... | collective-permute-start | bytes 3981320 | tf_op jit(solution)/shard_map/ppermute | solution.py:761
  290.0 43.0 %collective-permute-start.56 = (bf16[2,48,6912]{2,1,0:T(8,128)(2,1)}, bf16[2,48,6912]{2,1,0:T(8,128)(2,1)}, u32[]{:S(2)}, u32[]{:S(2)}) collective-permute-start(bf16[2,48,6912]{2,1,0:T(8,128)(2,1)} %get-tuple-element.353), channel_id=1, source_target_pairs={{0,1},{1,0},{2,3},{3,2},{4,5},{5,4},{6,7},{7,6},{8,9},{9,8},{10,11... | collective-permute-start | bytes 3981320 | tf_op jit(solution)/shard_map/ppermute | solution.py:761
  324.3 21.1 %collective-permute-start.68 = (bf16[96,3840]{1,0:T(8,128)(2,1)S(1)}, bf16[96,3840]{1,0:T(8,128)(2,1)S(1)}, u32[]{:S(2)}, u32[]{:S(2)}) collective-permute-start(bf16[96,3840]{1,0:T(8,128)(2,1)S(1)} %slice.286), channel_id=1, source_target_pairs={{0,4},{12,8},{1,5},{13,9},{2,6},{14,10},{3,7},{15,11},{16,20},{28,... | collective-permute-start | bytes 2211848 | tf_op jit(solution)/shard_map/ppermute | solution.py:761
  331.2 46.5 %collective-permute-start.55 = (bf16[4,96,2432]{2,1,0:T(8,128)(2,1)}, bf16[4,96,2432]{2,1,0:T(8,128)(2,1)S(1)}, u32[]{:S(2)}, u32[]{:S(2)}) collective-permute-start(bf16[4,96,2432]{2,1,0:T(8,128)(2,1)} %get-tuple-element.287), channel_id=1, source_target_pairs={{0,16},{16,0},{1,17},{17,1},{2,18},{18,2},{3,19},{19,3},{4,20},{20... | collective-permute-start | bytes 5603336 | tf_op jit(solution)/shard_map/ppermute | solution.py:743
  358.2 102.1 %collective-permute-start.92 = (bf16[96,3072]{1,0:T(8,128)(2,1)S(1)}, bf16[96,3072]{1,0:T(8,128)(2,1)S(1)}, u32[]{:S(2)}, u32[]{:S(2)}) collective-permute-start(bf16[96,3072]{1,0:T(8,128)(2,1)S(1)} %broadcast_select_fusion.5), channel_id=1, source_target_pairs={{0,16},{1,17},{2,18},{3,19},{4,20},{5,21},{6,22},{7,23},{8,24},{9,... | collective-permute-start | bytes 1769480 | tf_op jit(solution)/shard_map/ppermute | solution.py:865
  372.8 21.6 %collective-permute-start.70 = (bf16[96,3072]{1,0:T(8,128)(2,1)S(1)}, bf16[96,3072]{1,0:T(8,128)(2,1)S(1)}, u32[]{:S(2)}, u32[]{:S(2)}) collective-permute-start(bf16[96,3072]{1,0:T(8,128)(2,1)S(1)} %pad_maximum_fusion.1), channel_id=1, source_target_pairs={{0,4},{12,8},{1,5},{13,9},{2,6},{14,10},{3,7},{15,11},{16,20},{28,... | collective-permute-start | bytes 1769480 | tf_op jit(solution)/shard_map/ppermute | solution.py:761
  376.9 23.4 %collective-permute-start.75 = (bf16[96,3840]{1,0:T(8,128)(2,1)S(1)}, bf16[96,3840]{1,0:T(8,128)(2,1)S(1)}, u32[]{:S(2)}, u32[]{:S(2)}) collective-permute-start(bf16[96,3840]{1,0:T(8,128)(2,1)S(1)} %add_convert_fusion.9), channel_id=1, source_target_pairs={{4,8},{8,4},{5,9},{9,5},{6,10},{10,6},{7,11},{11,7},{20,24},{24,20... | collective-permute-start | bytes 2211848 | tf_op jit(solution)/shard_map/ppermute | solution.py:761
  387.6 47.6 %collective-permute-start.90 = (bf16[96,3840]{1,0:T(8,128)(2,1)S(1)}, bf16[96,3840]{1,0:T(8,128)(2,1)S(1)}, u32[]{:S(2)}, u32[]{:S(2)}) collective-permute-start(bf16[96,3840]{1,0:T(8,128)(2,1)S(1)} %broadcast_select_fusion.3), channel_id=1, source_target_pairs={{0,16},{1,17},{2,18},{3,19},{4,20},{5,21},{6,22},{7,23},{8,24},{9,... | collective-permute-start | bytes 2211848 | tf_op jit(solution)/shard_map/ppermute | solution.py:865
  412.1 21.0 %collective-permute-start.77 = (bf16[96,2432]{1,0:T(8,128)(2,1)S(1)}, bf16[96,2432]{1,0:T(8,128)(2,1)S(1)}, u32[]{:S(2)}, u32[]{:S(2)}) collective-permute-start(bf16[96,2432]{1,0:T(8,128)(2,1)S(1)} %add_convert_fusion.16), channel_id=1, source_target_pairs={{4,8},{8,4},{5,9},{9,5},{6,10},{10,6},{7,11},{11,7},{20,24},{24,20... | collective-permute-start | bytes 1400840 | tf_op jit(solution)/shard_map/ppermute | solution.py:761
  421.3 24.3 %collective-permute-start.89 = (bf16[96,3840]{1,0:T(8,128)(2,1)S(1)}, bf16[96,3840]{1,0:T(8,128)(2,1)S(1)}, u32[]{:S(2)}, u32[]{:S(2)}) collective-permute-start(bf16[96,3840]{1,0:T(8,128)(2,1)S(1)} %broadcast_select_fusion.4), channel_id=1, source_target_pairs={{16,0},{17,1},{18,2},{19,3},{20,4},{21,5},{22,6},{23,7},{24,8},{25... | collective-permute-start | bytes 2211848 | tf_op jit(solution)/shard_map/ppermute | solution.py:865
  433.9 20.6 %collective-permute-start.85 = (bf16[96,2432]{1,0:T(8,128)(2,1)S(1)}, bf16[96,2432]{1,0:T(8,128)(2,1)S(1)}, u32[]{:S(2)}, u32[]{:S(2)}) collective-permute-start(bf16[96,2432]{1,0:T(8,128)(2,1)S(1)} %add_convert_fusion.14), channel_id=1, source_target_pairs={{4,0},{8,12},{5,1},{9,13},{6,2},{10,14},{7,3},{11,15},{20,16},{24,... | collective-permute-start | bytes 1400840 | tf_op jit(solution)/shard_map/ppermute | solution.py:761
  435.3 25.1 %collective-permute-start.91 = (bf16[96,3072]{1,0:T(8,128)(2,1)S(1)}, bf16[96,3072]{1,0:T(8,128)(2,1)S(1)}, u32[]{:S(2)}, u32[]{:S(2)}) collective-permute-start(bf16[96,3072]{1,0:T(8,128)(2,1)S(1)} %broadcast_select_fusion.6), channel_id=1, source_target_pairs={{16,0},{17,1},{18,2},{19,3},{20,4},{21,5},{22,6},{23,7},{24,8},{25... | collective-permute-start | bytes 1769480 | tf_op jit(solution)/shard_map/ppermute | solution.py:865
  (133 other events, 1496.9 us)
Sparse Core Ops, SparseCore 0:
  15.0 83.3 all-gather.2
  100.8 66.1 all-gather.4
  200.0 81.8 reduce-scatter.1

commit v9 on v8

--- a/solution.py
+++ b/solution.py
@@ -706,7 +706,7 @@
     sent = background.slot("BC" if last else "A", sent)
     received = exchange(sent)
     if last:
-        received = background.slot("E", background.slot("CD", received))
+        received = background.slot("CD", received)
     grad_x, *late = lax.optimization_barrier(
         tuple(qkv_backward(ids, x, ginner, vec, table, weight, received, shards))
     )
@@ -756,8 +756,9 @@
         self.links = {}
 
     def send(self, link, value, axis, pairs):
-        if link in self.links:
-            value, _ = lax.optimization_barrier((value, self.links[link]))
+        before = [self.links[name] for name in (link, "sums") if name in self.links]
+        if len(before) > 0:
+            value, *_ = lax.optimization_barrier((value, *before))
         moved = lax.ppermute(value, axis, pairs)
         self.links[link] = moved
         return moved
@@ -820,7 +821,9 @@
     ]
     first = sum_pair(summed(slice(0, 4, 2), top), by_x)
     second = sum_pair(summed(slice(0, 2), low), by_y)
-    by_y, by_x = yield [background.across(first[1], 2), background.across(second[1], 1)]
+    flight = [background.across(first[1], 2), background.across(second[1], 1)]
+    background.links.setdefault("sums", first)
+    by_y, by_x = yield flight
     return jnp.concatenate([sum_pair(first[0], by_y), sum_pair(second[0], by_x)])
 
 
@@ -841,7 +844,7 @@
     (value,) = yield [value]
     (value,) = yield [value]
     other = background.add("E", ctx_task(value[:, column:], 1, background))
-    mine = yield from ctx_task(value[:, :column], 1, background)
+    mine = yield from ctx_task(value[:, :column], 1, background, 1)
     return mine, other
 
 

time: 492 us -> 483 us (0.982)
  waiting for transfers between devices: 153 us -> 143 us
    ppermute x30, waiting for transfers between devices: 70.4 us -> 58.5 us  [send(): moved = lax.ppermute(value, axis, pairs)]
    unnamed x129 -> x123, local copies, waits for them, and re-layouts: 9.44 us -> 9.88 us
  transfers between devices with their start and end apart: 96 -> 96, of which waited for: 37 -> 36; matrix products, arithmetic and copies ran while one was open for 7% -> 7% of each run, Pallas kernels for 22% -> 22%
where the time goes in v9:
time: 483 us; the launch traced here: 475 us
  waiting for transfers between devices  143 us (30%)
  starting transfers between devices  140 us (29%)
  Pallas kernels  129 us (27%)
  local copies, waits for them, and re-layouts  24.4 us (5%)
  other arithmetic  22.6 us (5%)
  between operations  15.4 us (3%)
    ppermute x30, waiting for transfers between devices, send(): moved = lax.ppermute(value, axis, pairs)  58.5 us
    ppermute x24, waiting for transfers between devices, exchange(): moved.append(lax.ppermute(pieces[d], GROUP, pairs))  54 us
    ppermute x30, starting transfers between devices, send(): moved = lax.ppermute(value, axis, pairs)  46.7 us
    pallas_call x2, Pallas kernels, mlp_backward(): pl.pallas_call(functools.partial(mlp_back_kernel, parts=parts, shards=sha...  26.5 us
    ppermute x6, starting transfers between devices, ctx_task(): other, = (yield [lax.ppermute(value, 'section', [(1 - layer, layer)])])  26.3 us
    ppermute x8, starting transfers between devices, return_rows(): lax.ppermute(value, GROUP, [(place_of(z // half, m * half + z % half), pl...  22.3 us
    pallas_call x2, Pallas kernels, mlp_forward(): pl.pallas_call(functools.partial(mlp_kernel, parts=parts, shards=shards,...  19.3 us
    ppermute x24, starting transfers between devices, exchange(): moved.append(lax.ppermute(pieces[d], GROUP, pairs))  18.4 us
  transfers between devices with their start and end apart: 96, of which 36 were waited for; matrix products, arithmetic and copies ran while one was open for 7% of the time, Pallas kernels for 22%

profile of v9, /device:TPU:1, one launch (start us, length us, event | category | flops | bytes accessed | tf_op | source)
XLA Modules:
  0.0 475.0 jit_solution(15576617610960823729)
XLA Ops:
  55.4 6.6 %qkv_project.2 = (bf16[576,256]{1,0:T(8,128)(2,1)}, bf16[576,256]{1,0:T(8,128)(2,1)}, bf16[576,256]{1,0:T(8,128)(2,1)}, bf16[576,256]{1,0:T(8,128)(2,1)}, bf16[768,2304]{1,0:T(8,128)(2,1)}, /*index=5*/f32[16,768]{1,0:T(8,128)}) custom-call(s32[14]{0:T(128)} %concatenate.53.ids_ref, bf16[256,768]{1,0:T(8,128)(2,1)} %bitcast_select_fusion.1.x_ref, ...), custom_call_target="tpu_custom_call" | custom-call | tf_op jit(solution)/shard_map/qkv_project/pallas_call | solution.py:161
  78.7 8.4 %attn_fwd.2 = (bf16[192,256]{1,0:T(8,128)(2,1)}, bf16[192,256]{1,0:T(8,128)(2,1)}, bf16[192,256]{1,0:T(8,128)(2,1)}, bf16[192,256]{1,0:T(8,128)(2,1)}, bf16[576,...) custom-call(s32[8]{0:T(128)} %pad_add_fusion.order_ref, ...), custom_call_target="tpu_custom_call" | custom-call | tf_op jit(solution)/shard_map/attn_fwd/pallas_call | solution.py:294
  99.4 9.6 %mlp_forward.2 = (bf16[256,768]{1,0:T(8,128)(2,1)}, f32[256,768]{1,0:T(8,128)}, f32[256,3072]{1,0:T(8,128)}, bf16[768,256]{1,0:T(8,128)(2,1)}) custom-call(s32[14]{0:T(128)} %concatenate.53.ids_ref, bf16[256,768]{1,0:T(8,128)(2,1)} %bitcast_select_fusion.1.x_ref, f32[16,768]{1,0:T(8,128)} %get-tuple-element.163.vec_ref, f32[1,3072]{1,0:T(1,128)} %reshape.191.bias_ref, ...), custom_call_target="tpu_custom_call" | custom-call | tf_op jit(solution)/shard_map/mlp_forward/pallas_call | solution.py:416
  110.0 6.6 %qkv_project.3 = (bf16[576,256]{1,0:T(8,128)(2,1)}, bf16[576,256]{1,0:T(8,128)(2,1)}, bf16[576,256]{1,0:T(8,128)(2,1)}, bf16[576,256]{1,0:T(8,128)(2,1)}, bf16[768,2304]{1,0:T(8,128)(2,1)}, /*index=5*/f32[16,768]{1,0:T(8,128)}) custom-call(s32[14]{0:T(128)} %concatenate.53.ids_ref, bf16[256,768]{1,0:T(8,128)(2,1)} %get-tuple-element.186.x_ref, ...), custom_call_target="tpu_custom_call" | custom-call | tf_op jit(solution)/shard_map/qkv_project/pallas_call | solution.py:161
  119.8 10.6 %collective-permute-done.27.refs_1_ = bf16[576,256]{1,0:T(8,128)(2,1)S(1)} collective-permute-done((bf16[576,256]{1,0:T(8,128)(2,1)}, bf16[576,256]{1,0:T(8,128)(2,1)S(1)}, u32[]{:S(2)}, u32[]{:S(2)}) %collective-permute-start.27) | collective-permute-done | bytes 294944 | tf_op jit(solution)/shard_map/ppermute | solution.py:52
  137.0 6.8 %collective-permute-start.33 = (bf16[256,768]{1,0:T(8,128)(2,1)S(1)}, bf16[256,768]{1,0:T(8,128)(2,1)S(1)}, u32[]{:S(2)}, u32[]{:S(2)}) collective-permute-start(bf16[256,768]{1,0:T(8,128)(2,1)S(1)} %copy-done.3), channel_id=1, source_target_pairs={{0,0},{4,4},{16,8},{20,12},{1,1},{5,5},{17,9},{21,13},{2,2},{6,6},... | collective-permute-start | bytes 1179656 | tf_op jit(solution)/shard_map/ppermute | solution.py:75
  145.3 8.4 %attn_fwd.3 = (bf16[192,256]{1,0:T(8,128)(2,1)}, bf16[192,256]{1,0:T(8,128)(2,1)}, bf16[192,256]{1,0:T(8,128)(2,1)}, bf16[192,256]{1,0:T(8,128)(2,1)}, bf16[576,...) custom-call(s32[8]{0:T(128)} %pad_add_fusion.order_ref, ...), custom_call_target="tpu_custom_call" | custom-call | tf_op jit(solution)/shard_map/attn_fwd/pallas_call | solution.py:294
  159.6 7.3 %all-gather.5.cloned.1.call-done.pack_ref = bf16[768,6912]{1,0:T(8,128)(2,1)} async-done(((bf16[96,6912]{1,0:T(8,128)(2,1)}), bf16[768,6912]{1,0:T(8,128)(2,1)}) %all-gather.5.cloned.1.call-update) | async-done | bytes 10616848 | tf_op jit(solution)/shard_map/all_gather | solution.py:734
  166.9 9.7 %mlp_forward.3 = (bf16[256,768]{1,0:T(8,128)(2,1)}, f32[256,768]{1,0:T(8,128)}, f32[256,3072]{1,0:T(8,128)}, bf16[768,256]{1,0:T(8,128)(2,1)}) custom-call(s32[14]{0:T(128)} %concatenate.53.ids_ref, bf16[256,768]{1,0:T(8,128)(2,1)} %get-tuple-element.186.x_ref, f32[16,768]{1,0:T(8,128)} %get-tuple-element.189.vec_ref, f32[1,3072]{1,0:T(1,128)} %reshape.193.bias_ref, ...), custom_call_target="tpu_custom_call" | custom-call | tf_op jit(solution)/shard_map/mlp_forward/pallas_call | solution.py:416
  176.6 13.1 %mlp_backward.2 = (bf16[192,256]{1,0:T(8,128)(2,1)}, bf16[192,256]{1,0:T(8,128)(2,1)}, bf16[192,256]{1,0:T(8,128)(2,1)}, bf16[192,256]{1,0:T(8,128)(2,1)}, f32[2...) custom-call(s32[14]{0:T(128)} %concatenate.53.ids_ref, ...), custom_call_target="tpu_custom_call" | custom-call | tf_op jit(solution)/shard_map/mlp_backward/pallas_call | solution.py:491
  191.8 8.2 %early_grads.2 = bf16[768,6912]{1,0:T(8,128)(2,1)} custom-call(s32[14]{0:T(128)} %concatenate.53.ids_ref, bf16[256,768]{1,0:T(8,128)(2,1)} %get-tuple-element.204.middle_ref, bf16[256,3072]{1,0:T(8,128)(2,1)} %get-tuple-element.205.ghid_ref, bf16[768,256]{1,0:T(8,128)(2,1)} %get-tuple-element.206.mixed_ref, bf16[256,768]{1,0:T(8,128)(2,1)} %get-tuple-element.207.gattn_ref, ...), custom_call_target="tpu_custom_call" | custom-call | tf_op jit(solution)/shard_map/early_grads/pallas_call | solution.py:587
  206.0 8.7 %attn_bwd.2 = (bf16[576,256]{1,0:T(8,128)(2,1)}, bf16[576,256]{1,0:T(8,128)(2,1)}, bf16[576,256]{1,0:T(8,128)(2,1)}, bf16[576,256]{1,0:T(8,128)(2,1)}) custom-call(s32[8]{0:T(128)} %pad_add_fusion.order_ref, bf16[192,256]{1,0:T(8,128)(2,1)} %get-tuple-element.210.refs_0_, bf16[192,256]{1,0:T(8,128)(2,1)} %copy-done.48, bf16[192,256]{1,0:T(8,128)(2,1)} %copy-done.49, ...), custom_call_target="tpu_custom_call" | custom-call | tf_op jit(solution)/shard_map/attn_bwd/pallas_call | solution.py:323
  217.0 7.8 %collective-permute-done.41.refs_1_ = bf16[576,256]{1,0:T(8,128)(2,1)S(1)} collective-permute-done((bf16[576,256]{1,0:T(8,128)(2,1)}, bf16[576,256]{1,0:T(8,128)(2,1)S(1)}, u32[]{:S(2)}, u32[]{:S(2)}) %collective-permute-start.41) | collective-permute-done | bytes 294944 | tf_op jit(solution)/shard_map/ppermute | solution.py:52
  229.9 8.8 %qkv_backward.2 = (bf16[256,768]{1,0:T(8,128)(2,1)}, bf16[4,96,2432]{2,1,0:T(8,128)(2,1)}, bf16[4,96,2432]{2,1,0:T(8,128)(2,1)}) custom-call(s32[14]{0:T(128)} %concatenate.53.ids_ref, bf16[256,768]{1,0:T(8,128)(2,1)} %get-tuple-element.186.x_ref, f32[256,768]{1,0:T(8,128)} %get-tuple-element.225.ginner_ref, f32[16,768]{1,0:T(8,128)} %get-tuple-element.189.vec_ref, ...), custom_call_target="tpu_custom_call" | custom-call | tf_op jit(solution)/shard_map/qkv_backward/pallas_call | solution.py:649
  243.6 13.5 %mlp_backward.3 = (bf16[192,256]{1,0:T(8,128)(2,1)}, bf16[192,256]{1,0:T(8,128)(2,1)}, bf16[192,256]{1,0:T(8,128)(2,1)}, bf16[192,256]{1,0:T(8,128)(2,1)}, f32[2...) custom-call(s32[14]{0:T(128)} %concatenate.53.ids_ref, ...), custom_call_target="tpu_custom_call" | custom-call | tf_op jit(solution)/shard_map/mlp_backward/pallas_call | solution.py:491
  260.0 9.3 %early_grads.3 = (bf16[4,96,6912]{2,1,0:T(8,128)(2,1)}, bf16[4,96,6912]{2,1,0:T(8,128)(2,1)}) custom-call(s32[14]{0:T(128)} %concatenate.53.ids_ref, bf16[256,768]{1,0:T(8,128)(2,1)} %get-tuple-element.247.middle_ref, bf16[256,3072]{1,0:T(8,128)(2,1)} %get-tuple-element.248.ghid_ref, bf16[768,256]{1,0:T(8,128)(2,1)} %get-tuple-element.249.mixed_ref, ...), custom_call_target="tpu_custom_call" | custom-call | tf_op jit(solution)/shard_map/early_grads/pallas_call | solution.py:587
  270.6 8.7 %attn_bwd.3 = (bf16[576,256]{1,0:T(8,128)(2,1)}, bf16[576,256]{1,0:T(8,128)(2,1)}, bf16[576,256]{1,0:T(8,128)(2,1)}, bf16[576,256]{1,0:T(8,128)(2,1)}) custom-call(s32[8]{0:T(128)} %pad_add_fusion.order_ref, bf16[192,256]{1,0:T(8,128)(2,1)} %get-tuple-element.254.refs_0_, bf16[192,256]{1,0:T(8,128)(2,1)} %copy-done.45, bf16[192,256]{1,0:T(8,128)(2,1)} %copy-done.46, ...), custom_call_target="tpu_custom_call" | custom-call | tf_op jit(solution)/shard_map/attn_bwd/pallas_call | solution.py:323
  300.8 9.4 %qkv_backward.3 = (bf16[256,768]{1,0:T(8,128)(2,1)}, bf16[4,96,2432]{2,1,0:T(8,128)(2,1)}, bf16[4,96,2432]{2,1,0:T(8,128)(2,1)}) custom-call(s32[14]{0:T(128)} %concatenate.53.ids_ref, bf16[256,768]{1,0:T(8,128)(2,1)} %bitcast_select_fusion.1.x_ref, f32[256,768]{1,0:T(8,128)} %get-tuple-element.235.ginner_ref, f32[16,768]{1,0:T(8,128)} %get-tuple-element.163.vec_ref, ...), custom_call_target="tpu_custom_call" | custom-call | tf_op jit(solution)/shard_map/qkv_backward/pallas_call | solution.py:649
  314.5 11.3 %collective-permute-done.67 = bf16[96,3072]{1,0:T(8,128)(2,1)S(1)} collective-permute-done((bf16[96,3072]{1,0:T(8,128)(2,1)}, bf16[96,3072]{1,0:T(8,128)(2,1)S(1)}, u32[]{:S(2)}, u32[]{:S(2)}) %collective-permute-start.67) | collective-permute-done | bytes 589856 | tf_op jit(solution)/shard_map/ppermute | solution.py:762
  339.8 6.9 %collective-permute-done.60 = bf16[48,6912]{1,0:T(8,128)(2,1)S(1)} collective-permute-done((bf16[48,6912]{1,0:T(8,128)(2,1)S(1)}, bf16[48,6912]{1,0:T(8,128)(2,1)S(1)}, u32[]{:S(2)}, u32[]{:S(2)}) %collective-permute-start.60) | collective-permute-done | bytes 663584 | tf_op jit(solution)/shard_map/ppermute | solution.py:762
  361.9 7.5 %collective-permute-done.69 = bf16[96,3840]{1,0:T(8,128)(2,1)S(1)} collective-permute-done((bf16[96,3840]{1,0:T(8,128)(2,1)S(1)}, bf16[96,3840]{1,0:T(8,128)(2,1)S(1)}, u32[]{:S(2)}, u32[]{:S(2)}) %collective-permute-start.69) | collective-permute-done | bytes 737312 | tf_op jit(solution)/shard_map/ppermute | solution.py:762
  414.4 11.9 %collective-permute-start.89 = (bf16[96,3840]{1,0:T(8,128)(2,1)S(1)}, bf16[96,3840]{1,0:T(8,128)(2,1)S(1)}, u32[]{:S(2)}, u32[]{:S(2)}) collective-permute-start(bf16[96,3840]{1,0:T(8,128)(2,1)S(1)} %broadcast_select_fusion.4), channel_id=1, source_target_pairs={{16,0},{17,1},{18,2},{19,3},{20,4},{21,5},{22,6},{23,7},{24,8},{25... | collective-permute-start | bytes 2211848 | tf_op jit(solution)/shard_map/ppermute | solution.py:868
  428.7 9.2 %collective-permute-start.91 = (bf16[96,3072]{1,0:T(8,128)(2,1)S(1)}, bf16[96,3072]{1,0:T(8,128)(2,1)S(1)}, u32[]{:S(2)}, u32[]{:S(2)}) collective-permute-start(bf16[96,3072]{1,0:T(8,128)(2,1)S(1)} %broadcast_select_fusion.6), channel_id=1, source_target_pairs={{16,0},{17,1},{18,2},{19,3},{20,4},{21,5},{22,6},{23,7},{24,8},{25... | collective-permute-start | bytes 1769480 | tf_op jit(solution)/shard_map/ppermute | solution.py:868
  453.5 7.8 %collective-permute-done.86 = bf16[96,2432]{1,0:T(8,128)(2,1)S(1)} collective-permute-done((bf16[96,2432]{1,0:T(8,128)(2,1)S(1)}, bf16[96,2432]{1,0:T(8,128)(2,1)S(1)}, u32[]{:S(2)}, u32[]{:S(2)}) %collective-permute-start.86) | collective-permute-done | bytes 466976 | tf_op jit(solution)/shard_map/ppermute | solution.py:762
  (405 shorter events, 243.6 us)
Async XLA Ops:
  7.2 92.2 %all-gather.3.cloned.1.call-start = ((), (), s32[]{:S(2)}) async-start(), calls=%async_computation.1 | async-start | bytes 11943936 | tf_op jit(solution)/shard_map/all_gather | solution.py:734
  14.8 152.1 %all-gather.5.cloned.1.call-start = ((), (), s32[]{:S(2)}) async-start(), calls=%async_computation.2 | async-start | bytes 11943936 | tf_op jit(solution)/shard_map/all_gather | solution.py:734
  15.6 266.4 %reduce-scatter.2.cloned.1.call-start = ((), (), s32[]{:S(2)}) async-start(), calls=%async_computation.3 | async-start | bytes 11943936 | tf_op jit(solution)/shard_map/reduce_scatter | solution.py:843
  21.9 20.5 %collective-permute-start = (bf16[256,768]{1,0:T(8,128)(2,1)S(1)}, bf16[256,768]{1,0:T(8,128)(2,1)S(1)}, u32[]{:S(2)}, u32[]{:S(2)}) collective-permute-start(bf16[256,768]{1,0:T(8,128)(2,1)S(1)} %select_bitcast_fusion.5), channel_id=1, source_target_pairs={{0,8},{4,12},{24,16},{28,20},{1,9},{5,13},{25,17},{29,21},{2,10},{... | collective-permute-start | bytes 1179656 | tf_op jit(solution)/shard_map/ppermute | solution.py:64
  64.1 23.0 %collective-permute-start.21 = (bf16[48,2432]{1,0:T(8,128)(2,1)S(1)}, bf16[48,2432]{1,0:T(8,128)(2,1)}, u32[]{:S(2)}, u32[]{:S(2)}) collective-permute-start(bf16[48,2432]{1,0:T(8,128)(2,1)S(1)} %slice.309), channel_id=1, source_target_pairs={{0,1},{1,0},{2,3},{3,2},{4,5},{5,4},{6,7},{7,6},{8,9},{9,8},{10,11... | collective-permute-start | bytes 700424 | tf_op jit(solution)/shard_map/ppermute | solution.py:739
  65.8 22.4 %collective-permute-start.20 = (bf16[48,2432]{1,0:T(8,128)(2,1)S(1)}, bf16[48,2432]{1,0:T(8,128)(2,1)}, u32[]{:S(2)}, u32[]{:S(2)}) collective-permute-start(bf16[48,2432]{1,0:T(8,128)(2,1)S(1)} %slice.308), channel_id=1, source_target_pairs={{0,2},{1,3},{2,0},{3,1},{4,6},{5,7},{6,4},{7,5},{8,10},{9,11},{10,... | collective-permute-start | bytes 700424 | tf_op jit(solution)/shard_map/ppermute | solution.py:739
  71.9 37.2 %collective-permute-start.22 = (bf16[96,2432]{1,0:T(8,128)(2,1)S(1)}, bf16[96,2432]{1,0:T(8,128)(2,1)S(1)}, u32[]{:S(2)}, u32[]{:S(2)}) collective-permute-start(bf16[96,2432]{1,0:T(8,128)(2,1)S(1)} %get-tuple-element.362.refs_0_), channel_id=1, source_target_pairs={{0,16},{16,0},{1,17},{17,1},{2,18},{18,2},{3,19},{19,3},{4,20},{20... | collective-permute-start | bytes 1400840 | tf_op jit(solution)/shard_map/ppermute | solution.py:743
  72.5 36.6 %collective-permute-start.24 = (bf16[96,2432]{1,0:T(8,128)(2,1)S(1)}, bf16[96,2432]{1,0:T(8,128)(2,1)}, u32[]{:S(2)}, u32[]{:S(2)}) collective-permute-start(bf16[96,2432]{1,0:T(8,128)(2,1)S(1)} %collective-permute-done.19.refs_2_), channel_id=1, source_target_pairs={{0,16},{16,0},{1,17},{17,1},{2,18},{18,2},{3,19},{19,3},{4,20},{20... | collective-permute-start | bytes 1400840 | tf_op jit(solution)/shard_map/ppermute | solution.py:743
  77.4 31.7 %collective-permute-start.23 = (bf16[96,2432]{1,0:T(8,128)(2,1)S(1)}, bf16[96,2432]{1,0:T(8,128)(2,1)}, u32[]{:S(2)}, u32[]{:S(2)}) collective-permute-start(bf16[96,2432]{1,0:T(8,128)(2,1)S(1)} %collective-permute-done.18.refs_1_), channel_id=1, source_target_pairs={{0,16},{16,0},{1,17},{17,1},{2,18},{18,2},{3,19},{19,3},{4,20},{20... | collective-permute-start | bytes 1400840 | tf_op jit(solution)/shard_map/ppermute | solution.py:743
  118.5 35.3 %collective-permute-start.35 = (bf16[256,768]{1,0:T(8,128)(2,1)S(1)}, bf16[256,768]{1,0:T(8,128)(2,1)S(1)}, u32[]{:S(2)}, u32[]{:S(2)}) collective-permute-start(bf16[256,768]{1,0:T(8,128)(2,1)S(1)} %select_bitcast_fusion.4), channel_id=1, source_target_pairs={{0,8},{4,12},{24,16},{28,20},{1,9},{5,13},{25,17},{29,21},{2,10},{... | collective-permute-start | bytes 1179656 | tf_op jit(solution)/shard_map/ppermute | solution.py:64
  136.3 23.3 %collective-permute-start.34 = (bf16[256,768]{1,0:T(8,128)(2,1)S(1)}, bf16[256,768]{1,0:T(8,128)(2,1)S(1)}, u32[]{:S(2)}, u32[]{:S(2)}) collective-permute-start(bf16[256,768]{1,0:T(8,128)(2,1)S(1)} %copy-done.3), channel_id=1, source_target_pairs={{8,0},{12,4},{24,8},{28,12},{9,1},{13,5},{25,9},{29,13},{10,2},{14... | collective-permute-start | bytes 1179656 | tf_op jit(solution)/shard_map/ppermute | solution.py:75
  137.0 22.6 %collective-permute-start.33 = (bf16[256,768]{1,0:T(8,128)(2,1)S(1)}, bf16[256,768]{1,0:T(8,128)(2,1)S(1)}, u32[]{:S(2)}, u32[]{:S(2)}) collective-permute-start(bf16[256,768]{1,0:T(8,128)(2,1)S(1)} %copy-done.3), channel_id=1, source_target_pairs={{0,0},{4,4},{16,8},{20,12},{1,1},{5,5},{17,9},{21,13},{2,2},{6,6},... | collective-permute-start | bytes 1179656 | tf_op jit(solution)/shard_map/ppermute | solution.py:75
  289.4 36.5 %collective-permute-start.56 = (bf16[2,48,6912]{2,1,0:T(8,128)(2,1)}, bf16[2,48,6912]{2,1,0:T(8,128)(2,1)S(1)}, u32[]{:S(2)}, u32[]{:S(2)}) collective-permute-start(bf16[2,48,6912]{2,1,0:T(8,128)(2,1)} %get-tuple-element.346), channel_id=1, source_target_pairs={{0,2},{1,3},{2,0},{3,1},{4,6},{5,7},{6,4},{7,5},{8,10},{9,11},{10,... | collective-permute-start | bytes 3981320 | tf_op jit(solution)/shard_map/ppermute | solution.py:762
  290.5 35.4 %collective-permute-start.55 = (bf16[2,48,6912]{2,1,0:T(8,128)(2,1)}, bf16[2,48,6912]{2,1,0:T(8,128)(2,1)}, u32[]{:S(2)}, u32[]{:S(2)}) collective-permute-start(bf16[2,48,6912]{2,1,0:T(8,128)(2,1)} %get-tuple-element.347), channel_id=1, source_target_pairs={{0,1},{1,0},{2,3},{3,2},{4,5},{5,4},{6,7},{7,6},{8,9},{9,8},{10,11... | collective-permute-start | bytes 3981320 | tf_op jit(solution)/shard_map/ppermute | solution.py:762
  312.7 43.9 %collective-permute-start.54 = (bf16[4,96,2432]{2,1,0:T(8,128)(2,1)}, bf16[4,96,2432]{2,1,0:T(8,128)(2,1)S(1)}, u32[]{:S(2)}, u32[]{:S(2)}) collective-permute-start(bf16[4,96,2432]{2,1,0:T(8,128)(2,1)} %get-tuple-element.279), channel_id=1, source_target_pairs={{0,16},{16,0},{1,17},{17,1},{2,18},{18,2},{3,19},{19,3},{4,20},{20... | collective-permute-start | bytes 5603336 | tf_op jit(solution)/shard_map/ppermute | solution.py:743
  331.7 20.4 %collective-permute-start.68 = (bf16[96,3840]{1,0:T(8,128)(2,1)S(1)}, bf16[96,3840]{1,0:T(8,128)(2,1)S(1)}, u32[]{:S(2)}, u32[]{:S(2)}) collective-permute-start(bf16[96,3840]{1,0:T(8,128)(2,1)S(1)} %copy-done.17), channel_id=1, source_target_pairs={{0,4},{12,8},{1,5},{13,9},{2,6},{14,10},{3,7},{15,11},{16,20},{28,... | collective-permute-start | bytes 2211848 | tf_op jit(solution)/shard_map/ppermute | solution.py:762
  338.5 22.1 %collective-permute-start.81 = (bf16[96,3072]{1,0:T(8,128)(2,1)S(1)}, bf16[96,3072]{1,0:T(8,128)(2,1)S(1)}, u32[]{:S(2)}, u32[]{:S(2)}) collective-permute-start(bf16[96,3072]{1,0:T(8,128)(2,1)S(1)} %add_convert_fusion.10), channel_id=1, source_target_pairs={{4,0},{8,12},{5,1},{9,13},{6,2},{10,14},{7,3},{11,15},{20,16},{24,... | collective-permute-start | bytes 1769480 | tf_op jit(solution)/shard_map/ppermute | solution.py:762
  360.6 92.6 %collective-permute-start.92 = (bf16[96,3072]{1,0:T(8,128)(2,1)S(1)}, bf16[96,3072]{1,0:T(8,128)(2,1)S(1)}, u32[]{:S(2)}, u32[]{:S(2)}) collective-permute-start(bf16[96,3072]{1,0:T(8,128)(2,1)S(1)} %broadcast_select_fusion.5), channel_id=1, source_target_pairs={{0,16},{1,17},{2,18},{3,19},{4,20},{5,21},{6,22},{7,23},{8,24},{9,... | collective-permute-start | bytes 1769480 | tf_op jit(solution)/shard_map/ppermute | solution.py:868
  369.5 22.6 %collective-permute-start.70 = (bf16[96,3072]{1,0:T(8,128)(2,1)S(1)}, bf16[96,3072]{1,0:T(8,128)(2,1)S(1)}, u32[]{:S(2)}, u32[]{:S(2)}) collective-permute-start(bf16[96,3072]{1,0:T(8,128)(2,1)S(1)} %pad_maximum_fusion.1), channel_id=1, source_target_pairs={{0,4},{12,8},{1,5},{13,9},{2,6},{14,10},{3,7},{15,11},{16,20},{28,... | collective-permute-start | bytes 1769480 | tf_op jit(solution)/shard_map/ppermute | solution.py:762
  374.0 21.8 %collective-permute-start.75 = (bf16[96,3840]{1,0:T(8,128)(2,1)S(1)}, bf16[96,3840]{1,0:T(8,128)(2,1)S(1)}, u32[]{:S(2)}, u32[]{:S(2)}) collective-permute-start(bf16[96,3840]{1,0:T(8,128)(2,1)S(1)} %add_convert_fusion.9), channel_id=1, source_target_pairs={{4,8},{8,4},{5,9},{9,5},{6,10},{10,6},{7,11},{11,7},{20,24},{24,20... | collective-permute-start | bytes 2211848 | tf_op jit(solution)/shard_map/ppermute | solution.py:762
  398.1 30.6 %collective-permute-start.90 = (bf16[96,3840]{1,0:T(8,128)(2,1)S(1)}, bf16[96,3840]{1,0:T(8,128)(2,1)S(1)}, u32[]{:S(2)}, u32[]{:S(2)}) collective-permute-start(bf16[96,3840]{1,0:T(8,128)(2,1)S(1)} %broadcast_select_fusion.3), channel_id=1, source_target_pairs={{0,16},{1,17},{2,18},{3,19},{4,20},{5,21},{6,22},{7,23},{8,24},{9,... | collective-permute-start | bytes 2211848 | tf_op jit(solution)/shard_map/ppermute | solution.py:868
  405.1 21.4 %collective-permute-start.77 = (bf16[96,2432]{1,0:T(8,128)(2,1)S(1)}, bf16[96,2432]{1,0:T(8,128)(2,1)S(1)}, u32[]{:S(2)}, u32[]{:S(2)}) collective-permute-start(bf16[96,2432]{1,0:T(8,128)(2,1)S(1)} %add_convert_fusion.16), channel_id=1, source_target_pairs={{4,8},{8,4},{5,9},{9,5},{6,10},{10,6},{7,11},{11,7},{20,24},{24,20... | collective-permute-start | bytes 1400840 | tf_op jit(solution)/shard_map/ppermute | solution.py:762
  414.4 23.5 %collective-permute-start.89 = (bf16[96,3840]{1,0:T(8,128)(2,1)S(1)}, bf16[96,3840]{1,0:T(8,128)(2,1)S(1)}, u32[]{:S(2)}, u32[]{:S(2)}) collective-permute-start(bf16[96,3840]{1,0:T(8,128)(2,1)S(1)} %broadcast_select_fusion.4), channel_id=1, source_target_pairs={{16,0},{17,1},{18,2},{19,3},{20,4},{21,5},{22,6},{23,7},{24,8},{25... | collective-permute-start | bytes 2211848 | tf_op jit(solution)/shard_map/ppermute | solution.py:868
  428.7 24.5 %collective-permute-start.91 = (bf16[96,3072]{1,0:T(8,128)(2,1)S(1)}, bf16[96,3072]{1,0:T(8,128)(2,1)S(1)}, u32[]{:S(2)}, u32[]{:S(2)}) collective-permute-start(bf16[96,3072]{1,0:T(8,128)(2,1)S(1)} %broadcast_select_fusion.6), channel_id=1, source_target_pairs={{16,0},{17,1},{18,2},{19,3},{20,4},{21,5},{22,6},{23,7},{24,8},{25... | collective-permute-start | bytes 1769480 | tf_op jit(solution)/shard_map/ppermute | solution.py:868
  (130 other events, 1416.4 us)
Sparse Core Ops, SparseCore 0:
  15.0 83.3 all-gather.2
  100.8 66.0 all-gather.4
  200.2 81.8 reduce-scatter.1

commit v10 on v7

--- a/solution.py
+++ b/solution.py
@@ -920,7 +920,7 @@
     )
     back1 = background.add("A", return_task(grad1, 1, 0))
     grad0, early0, late0, _ = layer_backward(saved0, grad1, rest0, *sizes, 0, background)
-    back0 = background.add("A", return_task(grad0, 0, 5, background))
+    back0 = background.add("A", return_task(grad0, 0, 1, background))
     background.finish()
 
     def chosen(values0, values1):

time: 483 us -> 492 us (1.019)
    ppermute x8, starting transfers between devices: 24 us -> 29.7 us  [return_rows(): lax.ppermute(value, GROUP, [(place_of(z // half, m * half + z % half), pl...]
  transfers between devices with their start and end apart: 96 -> 96, of which waited for: 34 -> 36; matrix products, arithmetic and copies ran while one was open for 7% -> 7% of each run, Pallas kernels for 22% -> 22%
where the time goes in v10:
time: 492 us; the launch traced here: 483 us
  waiting for transfers between devices  149 us (30%)
  starting transfers between devices  141 us (29%)
  Pallas kernels  129 us (26%)
  local copies, waits for them, and re-layouts  25 us (5%)
  other arithmetic  22.8 us (5%)
  between operations  15.4 us (3%)
    ppermute x30, waiting for transfers between devices, send(): moved = lax.ppermute(value, axis, pairs)  65.4 us
    ppermute x24, waiting for transfers between devices, exchange(): moved.append(lax.ppermute(pieces[d], GROUP, pairs))  53.9 us
    ppermute x30, starting transfers between devices, send(): moved = lax.ppermute(value, axis, pairs)  45.2 us
    ppermute x8, starting transfers between devices, return_rows(): lax.ppermute(value, GROUP, [(place_of(z // half, m * half + z % half), pl...  29.7 us
    pallas_call x2, Pallas kernels, mlp_backward(): pl.pallas_call(functools.partial(mlp_back_kernel, parts=parts, shards=sha...  26.5 us
    ppermute x6, starting transfers between devices, ctx_task(): other, = (yield [lax.ppermute(value, 'section', [(1 - layer, layer)])])  21.4 us
    pallas_call x2, Pallas kernels, mlp_forward(): pl.pallas_call(functools.partial(mlp_kernel, parts=parts, shards=shards,...  19.3 us
    ppermute x24, starting transfers between devices, exchange(): moved.append(lax.ppermute(pieces[d], GROUP, pairs))  18.4 us
  transfers between devices with their start and end apart: 96, of which 36 were waited for; matrix products, arithmetic and copies ran while one was open for 7% of the time, Pallas kernels for 22%

profile of v10, /device:TPU:1, one launch (start us, length us, event | category | flops | bytes accessed | tf_op | source)
XLA Modules:
  0.0 483.0 jit_solution(7923231352821079097)
XLA Ops:
  55.4 6.6 %qkv_project.2 = (bf16[576,256]{1,0:T(8,128)(2,1)}, bf16[576,256]{1,0:T(8,128)(2,1)}, bf16[576,256]{1,0:T(8,128)(2,1)}, bf16[576,256]{1,0:T(8,128)(2,1)}, bf16[768,2304]{1,0:T(8,128)(2,1)}, /*index=5*/f32[16,768]{1,0:T(8,128)}) custom-call(s32[14]{0:T(128)} %concatenate.53.ids_ref, bf16[256,768]{1,0:T(8,128)(2,1)} %bitcast_select_fusion.1.x_ref, ...), custom_call_target="tpu_custom_call" | custom-call | tf_op jit(solution)/shard_map/qkv_project/pallas_call | solution.py:161
  78.7 8.4 %attn_fwd.2 = (bf16[192,256]{1,0:T(8,128)(2,1)}, bf16[192,256]{1,0:T(8,128)(2,1)}, bf16[192,256]{1,0:T(8,128)(2,1)}, bf16[192,256]{1,0:T(8,128)(2,1)}, bf16[576,...) custom-call(s32[8]{0:T(128)} %pad_add_fusion.order_ref, ...), custom_call_target="tpu_custom_call" | custom-call | tf_op jit(solution)/shard_map/attn_fwd/pallas_call | solution.py:294
  99.4 9.6 %mlp_forward.2 = (bf16[256,768]{1,0:T(8,128)(2,1)}, f32[256,768]{1,0:T(8,128)}, f32[256,3072]{1,0:T(8,128)}, bf16[768,256]{1,0:T(8,128)(2,1)}) custom-call(s32[14]{0:T(128)} %concatenate.53.ids_ref, bf16[256,768]{1,0:T(8,128)(2,1)} %bitcast_select_fusion.1.x_ref, f32[16,768]{1,0:T(8,128)} %get-tuple-element.162.vec_ref, f32[1,3072]{1,0:T(1,128)} %reshape.191.bias_ref, ...), custom_call_target="tpu_custom_call" | custom-call | tf_op jit(solution)/shard_map/mlp_forward/pallas_call | solution.py:416
  119.8 10.6 %collective-permute-done.27.refs_1_ = bf16[576,256]{1,0:T(8,128)(2,1)S(1)} collective-permute-done((bf16[576,256]{1,0:T(8,128)(2,1)}, bf16[576,256]{1,0:T(8,128)(2,1)S(1)}, u32[]{:S(2)}, u32[]{:S(2)}) %collective-permute-start.27) | collective-permute-done | bytes 294944 | tf_op jit(solution)/shard_map/ppermute | solution.py:52
  137.0 6.8 %collective-permute-start.33 = (bf16[256,768]{1,0:T(8,128)(2,1)S(1)}, bf16[256,768]{1,0:T(8,128)(2,1)S(1)}, u32[]{:S(2)}, u32[]{:S(2)}) collective-permute-start(bf16[256,768]{1,0:T(8,128)(2,1)S(1)} %copy-done.3), channel_id=1, source_target_pairs={{0,0},{4,4},{16,8},{20,12},{1,1},{5,5},{17,9},{21,13},{2,2},{6,6},... | collective-permute-start | bytes 1179656 | tf_op jit(solution)/shard_map/ppermute | solution.py:75
  145.3 8.4 %attn_fwd.3 = (bf16[192,256]{1,0:T(8,128)(2,1)}, bf16[192,256]{1,0:T(8,128)(2,1)}, bf16[192,256]{1,0:T(8,128)(2,1)}, bf16[192,256]{1,0:T(8,128)(2,1)}, bf16[576,...) custom-call(s32[8]{0:T(128)} %pad_add_fusion.order_ref, ...), custom_call_target="tpu_custom_call" | custom-call | tf_op jit(solution)/shard_map/attn_fwd/pallas_call | solution.py:294
  159.6 7.3 %all-gather.5.cloned.1.call-done.pack_ref = bf16[768,6912]{1,0:T(8,128)(2,1)} async-done(((bf16[96,6912]{1,0:T(8,128)(2,1)}), bf16[768,6912]{1,0:T(8,128)(2,1)}) %all-gather.5.cloned.1.call-update) | async-done | bytes 10616848 | tf_op jit(solution)/shard_map/all_gather | solution.py:735
  166.9 9.7 %mlp_forward.3 = (bf16[256,768]{1,0:T(8,128)(2,1)}, f32[256,768]{1,0:T(8,128)}, f32[256,3072]{1,0:T(8,128)}, bf16[768,256]{1,0:T(8,128)(2,1)}) custom-call(s32[14]{0:T(128)} %concatenate.53.ids_ref, bf16[256,768]{1,0:T(8,128)(2,1)} %get-tuple-element.185.x_ref, f32[16,768]{1,0:T(8,128)} %get-tuple-element.188.vec_ref, f32[1,3072]{1,0:T(1,128)} %reshape.193.bias_ref, ...), custom_call_target="tpu_custom_call" | custom-call | tf_op jit(solution)/shard_map/mlp_forward/pallas_call | solution.py:416
  176.6 13.1 %mlp_backward.2 = (bf16[192,256]{1,0:T(8,128)(2,1)}, bf16[192,256]{1,0:T(8,128)(2,1)}, bf16[192,256]{1,0:T(8,128)(2,1)}, bf16[192,256]{1,0:T(8,128)(2,1)}, f32[2...) custom-call(s32[14]{0:T(128)} %concatenate.53.ids_ref, ...), custom_call_target="tpu_custom_call" | custom-call | tf_op jit(solution)/shard_map/mlp_backward/pallas_call | solution.py:491
  191.7 8.2 %early_grads.2 = bf16[768,6912]{1,0:T(8,128)(2,1)} custom-call(s32[14]{0:T(128)} %concatenate.53.ids_ref, bf16[256,768]{1,0:T(8,128)(2,1)} %get-tuple-element.203.middle_ref, bf16[256,3072]{1,0:T(8,128)(2,1)} %get-tuple-element.204.ghid_ref, bf16[768,256]{1,0:T(8,128)(2,1)} %get-tuple-element.205.mixed_ref, bf16[256,768]{1,0:T(8,128)(2,1)} %get-tuple-element.206.gattn_ref, ...), custom_call_target="tpu_custom_call" | custom-call | tf_op jit(solution)/shard_map/early_grads/pallas_call | solution.py:587
  206.0 8.7 %attn_bwd.2 = (bf16[576,256]{1,0:T(8,128)(2,1)}, bf16[576,256]{1,0:T(8,128)(2,1)}, bf16[576,256]{1,0:T(8,128)(2,1)}, bf16[576,256]{1,0:T(8,128)(2,1)}) custom-call(s32[8]{0:T(128)} %pad_add_fusion.order_ref, bf16[192,256]{1,0:T(8,128)(2,1)} %get-tuple-element.209.refs_0_, bf16[192,256]{1,0:T(8,128)(2,1)} %copy-done.48, bf16[192,256]{1,0:T(8,128)(2,1)} %copy-done.49, ...), custom_call_target="tpu_custom_call" | custom-call | tf_op jit(solution)/shard_map/attn_bwd/pallas_call | solution.py:323
  217.0 7.8 %collective-permute-done.41.refs_1_ = bf16[576,256]{1,0:T(8,128)(2,1)S(1)} collective-permute-done((bf16[576,256]{1,0:T(8,128)(2,1)}, bf16[576,256]{1,0:T(8,128)(2,1)S(1)}, u32[]{:S(2)}, u32[]{:S(2)}) %collective-permute-start.41) | collective-permute-done | bytes 294944 | tf_op jit(solution)/shard_map/ppermute | solution.py:52
  229.9 8.8 %qkv_backward.2 = (bf16[256,768]{1,0:T(8,128)(2,1)}, bf16[4,96,2432]{2,1,0:T(8,128)(2,1)}, bf16[4,96,2432]{2,1,0:T(8,128)(2,1)}) custom-call(s32[14]{0:T(128)} %concatenate.53.ids_ref, bf16[256,768]{1,0:T(8,128)(2,1)} %get-tuple-element.185.x_ref, f32[256,768]{1,0:T(8,128)} %get-tuple-element.224.ginner_ref, f32[16,768]{1,0:T(8,128)} %get-tuple-element.188.vec_ref, ...), custom_call_target="tpu_custom_call" | custom-call | tf_op jit(solution)/shard_map/qkv_backward/pallas_call | solution.py:649
  243.6 13.5 %mlp_backward.3 = (bf16[192,256]{1,0:T(8,128)(2,1)}, bf16[192,256]{1,0:T(8,128)(2,1)}, bf16[192,256]{1,0:T(8,128)(2,1)}, bf16[192,256]{1,0:T(8,128)(2,1)}, f32[2...) custom-call(s32[14]{0:T(128)} %concatenate.53.ids_ref, ...), custom_call_target="tpu_custom_call" | custom-call | tf_op jit(solution)/shard_map/mlp_backward/pallas_call | solution.py:491
  260.0 9.3 %early_grads.3 = (bf16[4,96,6912]{2,1,0:T(8,128)(2,1)}, bf16[4,96,6912]{2,1,0:T(8,128)(2,1)}) custom-call(s32[14]{0:T(128)} %concatenate.53.ids_ref, bf16[256,768]{1,0:T(8,128)(2,1)} %get-tuple-element.246.middle_ref, bf16[256,3072]{1,0:T(8,128)(2,1)} %get-tuple-element.247.ghid_ref, bf16[768,256]{1,0:T(8,128)(2,1)} %get-tuple-element.248.mixed_ref, ...), custom_call_target="tpu_custom_call" | custom-call | tf_op jit(solution)/shard_map/early_grads/pallas_call | solution.py:587
  270.6 8.7 %attn_bwd.3 = (bf16[576,256]{1,0:T(8,128)(2,1)}, bf16[576,256]{1,0:T(8,128)(2,1)}, bf16[576,256]{1,0:T(8,128)(2,1)}, bf16[576,256]{1,0:T(8,128)(2,1)}) custom-call(s32[8]{0:T(128)} %pad_add_fusion.order_ref, bf16[192,256]{1,0:T(8,128)(2,1)} %get-tuple-element.253.refs_0_, bf16[192,256]{1,0:T(8,128)(2,1)} %copy-done.45, bf16[192,256]{1,0:T(8,128)(2,1)} %copy-done.46, ...), custom_call_target="tpu_custom_call" | custom-call | tf_op jit(solution)/shard_map/attn_bwd/pallas_call | solution.py:323
  300.7 9.4 %qkv_backward.3 = (bf16[256,768]{1,0:T(8,128)(2,1)}, bf16[4,96,2432]{2,1,0:T(8,128)(2,1)}, bf16[4,96,2432]{2,1,0:T(8,128)(2,1)}) custom-call(s32[14]{0:T(128)} %concatenate.53.ids_ref, bf16[256,768]{1,0:T(8,128)(2,1)} %bitcast_select_fusion.1.x_ref, f32[256,768]{1,0:T(8,128)} %get-tuple-element.234.ginner_ref, f32[16,768]{1,0:T(8,128)} %get-tuple-element.162.vec_ref, ...), custom_call_target="tpu_custom_call" | custom-call | tf_op jit(solution)/shard_map/qkv_backward/pallas_call | solution.py:649
  314.6 11.2 %collective-permute-done.54 = bf16[96,3072]{1,0:T(8,128)(2,1)S(1)} collective-permute-done((bf16[96,3072]{1,0:T(8,128)(2,1)}, bf16[96,3072]{1,0:T(8,128)(2,1)S(1)}, u32[]{:S(2)}, u32[]{:S(2)}) %collective-permute-start.54) | collective-permute-done | bytes 589856 | tf_op jit(solution)/shard_map/ppermute | solution.py:762
  339.6 7.9 %collective-permute-done.55 = bf16[96,3840]{1,0:T(8,128)(2,1)S(1)} collective-permute-done((bf16[96,3840]{1,0:T(8,128)(2,1)S(1)}, bf16[96,3840]{1,0:T(8,128)(2,1)S(1)}, u32[]{:S(2)}, u32[]{:S(2)}) %collective-permute-start.55) | collective-permute-done | bytes 737312 | tf_op jit(solution)/shard_map/ppermute | solution.py:762
  361.5 13.1 %collective-permute-start.58 = (bf16[256,768]{1,0:T(8,128)(2,1)S(1)}, bf16[256,768]{1,0:T(8,128)(2,1)S(1)}, u32[]{:S(2)}, u32[]{:S(2)}) collective-permute-start(bf16[256,768]{1,0:T(8,128)(2,1)S(1)} %copy-done.54), channel_id=1, source_target_pairs={{0,0},{4,4},{16,8},{20,12},{1,1},{5,5},{17,9},{21,13},{2,2},{6,6},... | collective-permute-start | bytes 1179656 | tf_op jit(solution)/shard_map/ppermute | solution.py:75
  379.3 7.3 %collective-permute-start.74 = (bf16[96,3072]{1,0:T(8,128)(2,1)S(1)}, bf16[96,3072]{1,0:T(8,128)(2,1)S(1)}, u32[]{:S(2)}, u32[]{:S(2)}) collective-permute-start(bf16[96,3072]{1,0:T(8,128)(2,1)S(1)} %pad_maximum_fusion.1), channel_id=1, source_target_pairs={{0,4},{12,8},{1,5},{13,9},{2,6},{14,10},{3,7},{15,11},{16,20},{28,... | collective-permute-start | bytes 1769480 | tf_op jit(solution)/shard_map/ppermute | solution.py:762
  436.1 6.9 %collective-permute-done.84 = bf16[96,3072]{1,0:T(8,128)(2,1)S(1)} collective-permute-done((bf16[96,3072]{1,0:T(8,128)(2,1)S(1)}, bf16[96,3072]{1,0:T(8,128)(2,1)S(1)}, u32[]{:S(2)}, u32[]{:S(2)}) %collective-permute-start.84) | collective-permute-done | bytes 589856 | tf_op jit(solution)/shard_map/ppermute | solution.py:762
  456.6 6.7 %collective-permute-done.86 = bf16[96,2432]{1,0:T(8,128)(2,1)S(1)} collective-permute-done((bf16[96,2432]{1,0:T(8,128)(2,1)S(1)}, bf16[96,2432]{1,0:T(8,128)(2,1)S(1)}, u32[]{:S(2)}, u32[]{:S(2)}) %collective-permute-start.86) | collective-permute-done | bytes 466976 | tf_op jit(solution)/shard_map/ppermute | solution.py:762
  463.4 7.2 %collective-permute-start.87 = (bf16[96,2432]{1,0:T(8,128)(2,1)S(1)}, bf16[96,2432]{1,0:T(8,128)(2,1)S(1)}, u32[]{:S(2)}, u32[]{:S(2)}) collective-permute-start(bf16[96,2432]{1,0:T(8,128)(2,1)S(1)} %broadcast_select_fusion.8), channel_id=1, source_target_pairs={{16,0},{17,1},{18,2},{19,3},{20,4},{21,5},{22,6},{23,7},{24,8},{25... | collective-permute-start | bytes 1400840 | tf_op jit(solution)/shard_map/ppermute | solution.py:866
  (405 shorter events, 252.5 us)
Async XLA Ops:
  7.2 92.2 %all-gather.3.cloned.1.call-start = ((), (), s32[]{:S(2)}) async-start(), calls=%async_computation.1 | async-start | bytes 11943936 | tf_op jit(solution)/shard_map/all_gather | solution.py:735
  14.8 152.1 %all-gather.5.cloned.1.call-start = ((), (), s32[]{:S(2)}) async-start(), calls=%async_computation.2 | async-start | bytes 11943936 | tf_op jit(solution)/shard_map/all_gather | solution.py:735
  15.6 266.4 %reduce-scatter.2.cloned.1.call-start = ((), (), s32[]{:S(2)}) async-start(), calls=%async_computation.3 | async-start | bytes 11943936 | tf_op jit(solution)/shard_map/reduce_scatter | solution.py:841
  21.9 20.5 %collective-permute-start = (bf16[256,768]{1,0:T(8,128)(2,1)S(1)}, bf16[256,768]{1,0:T(8,128)(2,1)S(1)}, u32[]{:S(2)}, u32[]{:S(2)}) collective-permute-start(bf16[256,768]{1,0:T(8,128)(2,1)S(1)} %select_bitcast_fusion.5), channel_id=1, source_target_pairs={{0,8},{4,12},{24,16},{28,20},{1,9},{5,13},{25,17},{29,21},{2,10},{... | collective-permute-start | bytes 1179656 | tf_op jit(solution)/shard_map/ppermute | solution.py:64
  23.2 19.8 %collective-permute-start.6 = (bf16[96,2432]{1,0:T(8,128)(2,1)S(1)}, bf16[96,2432]{1,0:T(8,128)(2,1)S(1)}, u32[]{:S(2)}, u32[]{:S(2)}) collective-permute-start(bf16[96,2432]{1,0:T(8,128)(2,1)S(1)} %get-tuple-element.361.refs_0_), channel_id=1, source_target_pairs={{0,16},{16,0},{1,17},{17,1},{2,18},{18,2},{3,19},{19,3},{4,20},{20... | collective-permute-start | bytes 1400840 | tf_op jit(solution)/shard_map/ppermute | solution.py:744
  43.7 20.3 %collective-permute-start.19 = (bf16[96,2432]{1,0:T(8,128)(2,1)S(1)}, bf16[96,2432]{1,0:T(8,128)(2,1)S(1)}, u32[]{:S(2)}, u32[]{:S(2)}) collective-permute-start(bf16[96,2432]{1,0:T(8,128)(2,1)S(1)} %get-tuple-element.360.refs_0_), channel_id=1, source_target_pairs={{0,2},{1,3},{2,0},{3,1},{4,6},{5,7},{6,4},{7,5},{8,10},{9,11},{10,... | collective-permute-start | bytes 1400840 | tf_op jit(solution)/shard_map/ppermute | solution.py:740
  64.1 23.0 %collective-permute-start.21 = (bf16[48,2432]{1,0:T(8,128)(2,1)S(1)}, bf16[48,2432]{1,0:T(8,128)(2,1)}, u32[]{:S(2)}, u32[]{:S(2)}) collective-permute-start(bf16[48,2432]{1,0:T(8,128)(2,1)S(1)} %slice.309), channel_id=1, source_target_pairs={{0,1},{1,0},{2,3},{3,2},{4,5},{5,4},{6,7},{7,6},{8,9},{9,8},{10,11... | collective-permute-start | bytes 700424 | tf_op jit(solution)/shard_map/ppermute | solution.py:740
  65.8 22.4 %collective-permute-start.20 = (bf16[48,2432]{1,0:T(8,128)(2,1)S(1)}, bf16[48,2432]{1,0:T(8,128)(2,1)}, u32[]{:S(2)}, u32[]{:S(2)}) collective-permute-start(bf16[48,2432]{1,0:T(8,128)(2,1)S(1)} %slice.308), channel_id=1, source_target_pairs={{0,2},{1,3},{2,0},{3,1},{4,6},{5,7},{6,4},{7,5},{8,10},{9,11},{10,... | collective-permute-start | bytes 700424 | tf_op jit(solution)/shard_map/ppermute | solution.py:740
  71.9 37.2 %collective-permute-start.22 = (bf16[96,2432]{1,0:T(8,128)(2,1)S(1)}, bf16[96,2432]{1,0:T(8,128)(2,1)S(1)}, u32[]{:S(2)}, u32[]{:S(2)}) collective-permute-start(bf16[96,2432]{1,0:T(8,128)(2,1)S(1)} %get-tuple-element.360.refs_0_), channel_id=1, source_target_pairs={{0,16},{16,0},{1,17},{17,1},{2,18},{18,2},{3,19},{19,3},{4,20},{20... | collective-permute-start | bytes 1400840 | tf_op jit(solution)/shard_map/ppermute | solution.py:744
  72.5 36.6 %collective-permute-start.24 = (bf16[96,2432]{1,0:T(8,128)(2,1)S(1)}, bf16[96,2432]{1,0:T(8,128)(2,1)}, u32[]{:S(2)}, u32[]{:S(2)}) collective-permute-start(bf16[96,2432]{1,0:T(8,128)(2,1)S(1)} %collective-permute-done.19.refs_2_), channel_id=1, source_target_pairs={{0,16},{16,0},{1,17},{17,1},{2,18},{18,2},{3,19},{19,3},{4,20},{20... | collective-permute-start | bytes 1400840 | tf_op jit(solution)/shard_map/ppermute | solution.py:744
  77.4 31.7 %collective-permute-start.23 = (bf16[96,2432]{1,0:T(8,128)(2,1)S(1)}, bf16[96,2432]{1,0:T(8,128)(2,1)}, u32[]{:S(2)}, u32[]{:S(2)}) collective-permute-start(bf16[96,2432]{1,0:T(8,128)(2,1)S(1)} %collective-permute-done.18.refs_1_), channel_id=1, source_target_pairs={{0,16},{16,0},{1,17},{17,1},{2,18},{18,2},{3,19},{19,3},{4,20},{20... | collective-permute-start | bytes 1400840 | tf_op jit(solution)/shard_map/ppermute | solution.py:744
  118.5 35.3 %collective-permute-start.35 = (bf16[256,768]{1,0:T(8,128)(2,1)S(1)}, bf16[256,768]{1,0:T(8,128)(2,1)S(1)}, u32[]{:S(2)}, u32[]{:S(2)}) collective-permute-start(bf16[256,768]{1,0:T(8,128)(2,1)S(1)} %select_bitcast_fusion.4), channel_id=1, source_target_pairs={{0,8},{4,12},{24,16},{28,20},{1,9},{5,13},{25,17},{29,21},{2,10},{... | collective-permute-start | bytes 1179656 | tf_op jit(solution)/shard_map/ppermute | solution.py:64
  136.3 23.3 %collective-permute-start.34 = (bf16[256,768]{1,0:T(8,128)(2,1)S(1)}, bf16[256,768]{1,0:T(8,128)(2,1)S(1)}, u32[]{:S(2)}, u32[]{:S(2)}) collective-permute-start(bf16[256,768]{1,0:T(8,128)(2,1)S(1)} %copy-done.3), channel_id=1, source_target_pairs={{8,0},{12,4},{24,8},{28,12},{9,1},{13,5},{25,9},{29,13},{10,2},{14... | collective-permute-start | bytes 1179656 | tf_op jit(solution)/shard_map/ppermute | solution.py:75
  137.0 22.6 %collective-permute-start.33 = (bf16[256,768]{1,0:T(8,128)(2,1)S(1)}, bf16[256,768]{1,0:T(8,128)(2,1)S(1)}, u32[]{:S(2)}, u32[]{:S(2)}) collective-permute-start(bf16[256,768]{1,0:T(8,128)(2,1)S(1)} %copy-done.3), channel_id=1, source_target_pairs={{0,0},{4,4},{16,8},{20,12},{1,1},{5,5},{17,9},{21,13},{2,2},{6,6},... | collective-permute-start | bytes 1179656 | tf_op jit(solution)/shard_map/ppermute | solution.py:75
  289.4 43.8 %collective-permute-start.62 = (bf16[2,48,6912]{2,1,0:T(8,128)(2,1)}, bf16[2,48,6912]{2,1,0:T(8,128)(2,1)S(1)}, u32[]{:S(2)}, u32[]{:S(2)}) collective-permute-start(bf16[2,48,6912]{2,1,0:T(8,128)(2,1)} %get-tuple-element.344), channel_id=1, source_target_pairs={{0,2},{1,3},{2,0},{3,1},{4,6},{5,7},{6,4},{7,5},{8,10},{9,11},{10,... | collective-permute-start | bytes 3981320 | tf_op jit(solution)/shard_map/ppermute | solution.py:762
  290.5 42.7 %collective-permute-start.61 = (bf16[2,48,6912]{2,1,0:T(8,128)(2,1)}, bf16[2,48,6912]{2,1,0:T(8,128)(2,1)}, u32[]{:S(2)}, u32[]{:S(2)}) collective-permute-start(bf16[2,48,6912]{2,1,0:T(8,128)(2,1)} %get-tuple-element.345), channel_id=1, source_target_pairs={{0,1},{1,0},{2,3},{3,2},{4,5},{5,4},{6,7},{7,6},{8,9},{9,8},{10,11... | collective-permute-start | bytes 3981320 | tf_op jit(solution)/shard_map/ppermute | solution.py:762
  312.7 45.7 %collective-permute-start.60 = (bf16[4,96,2432]{2,1,0:T(8,128)(2,1)}, bf16[4,96,2432]{2,1,0:T(8,128)(2,1)S(1)}, u32[]{:S(2)}, u32[]{:S(2)}) collective-permute-start(bf16[4,96,2432]{2,1,0:T(8,128)(2,1)} %get-tuple-element.285), channel_id=1, source_target_pairs={{0,16},{16,0},{1,17},{17,1},{2,18},{18,2},{3,19},{19,3},{4,20},{20... | collective-permute-start | bytes 5603336 | tf_op jit(solution)/shard_map/ppermute | solution.py:744
  326.6 20.9 %collective-permute-start.55 = (bf16[96,3840]{1,0:T(8,128)(2,1)S(1)}, bf16[96,3840]{1,0:T(8,128)(2,1)S(1)}, u32[]{:S(2)}, u32[]{:S(2)}) collective-permute-start(bf16[96,3840]{1,0:T(8,128)(2,1)S(1)} %copy-done.17), channel_id=1, source_target_pairs={{0,4},{12,8},{1,5},{13,9},{2,6},{14,10},{3,7},{15,11},{16,20},{28,... | collective-permute-start | bytes 2211848 | tf_op jit(solution)/shard_map/ppermute | solution.py:762
  352.5 22.1 %collective-permute-start.64 = (bf16[2,48,2432]{2,1,0:T(8,128)(2,1)S(1)}, bf16[2,48,2432]{2,1,0:T(8,128)(2,1)S(1)}, u32[]{:S(2)}, u32[]{:S(2)}) collective-permute-start(bf16[2,48,2432]{2,1,0:T(8,128)(2,1)S(1)} %get-tuple-element.292), channel_id=1, source_target_pairs={{0,1},{1,0},{2,3},{3,2},{4,5},{5,4},{6,7},{7,6},{8,9},{9,8},{10,11... | collective-permute-start | bytes 1400840 | tf_op jit(solution)/shard_map/ppermute | solution.py:762
  358.4 97.9 %collective-permute-start.92 = (bf16[96,3072]{1,0:T(8,128)(2,1)S(1)}, bf16[96,3072]{1,0:T(8,128)(2,1)S(1)}, u32[]{:S(2)}, u32[]{:S(2)}) collective-permute-start(bf16[96,3072]{1,0:T(8,128)(2,1)S(1)} %broadcast_select_fusion.5), channel_id=1, source_target_pairs={{0,16},{1,17},{2,18},{3,19},{4,20},{5,21},{6,22},{7,23},{8,24},{9,... | collective-permute-start | bytes 1769480 | tf_op jit(solution)/shard_map/ppermute | solution.py:866
  379.3 22.6 %collective-permute-start.74 = (bf16[96,3072]{1,0:T(8,128)(2,1)S(1)}, bf16[96,3072]{1,0:T(8,128)(2,1)S(1)}, u32[]{:S(2)}, u32[]{:S(2)}) collective-permute-start(bf16[96,3072]{1,0:T(8,128)(2,1)S(1)} %pad_maximum_fusion.1), channel_id=1, source_target_pairs={{0,4},{12,8},{1,5},{13,9},{2,6},{14,10},{3,7},{15,11},{16,20},{28,... | collective-permute-start | bytes 1769480 | tf_op jit(solution)/shard_map/ppermute | solution.py:762
  388.1 21.5 %collective-permute-start.77 = (bf16[96,3840]{1,0:T(8,128)(2,1)S(1)}, bf16[96,3840]{1,0:T(8,128)(2,1)S(1)}, u32[]{:S(2)}, u32[]{:S(2)}) collective-permute-start(bf16[96,3840]{1,0:T(8,128)(2,1)S(1)} %add_convert_fusion.8), channel_id=1, source_target_pairs={{4,8},{8,4},{5,9},{9,5},{6,10},{10,6},{7,11},{11,7},{20,24},{24,20... | collective-permute-start | bytes 2211848 | tf_op jit(solution)/shard_map/ppermute | solution.py:762
  395.1 49.3 %collective-permute-start.90 = (bf16[96,3840]{1,0:T(8,128)(2,1)S(1)}, bf16[96,3840]{1,0:T(8,128)(2,1)S(1)}, u32[]{:S(2)}, u32[]{:S(2)}) collective-permute-start(bf16[96,3840]{1,0:T(8,128)(2,1)S(1)} %broadcast_select_fusion.3), channel_id=1, source_target_pairs={{0,16},{1,17},{2,18},{3,19},{4,20},{5,21},{6,22},{7,23},{8,24},{9,... | collective-permute-start | bytes 2211848 | tf_op jit(solution)/shard_map/ppermute | solution.py:866
  430.3 19.5 %collective-permute-start.89 = (bf16[96,3840]{1,0:T(8,128)(2,1)S(1)}, bf16[96,3840]{1,0:T(8,128)(2,1)S(1)}, u32[]{:S(2)}, u32[]{:S(2)}) collective-permute-start(bf16[96,3840]{1,0:T(8,128)(2,1)S(1)} %broadcast_select_fusion.4), channel_id=1, source_target_pairs={{16,0},{17,1},{18,2},{19,3},{20,4},{21,5},{22,6},{23,7},{24,8},{25... | collective-permute-start | bytes 2211848 | tf_op jit(solution)/shard_map/ppermute | solution.py:866
  (130 other events, 1453.6 us)
Sparse Core Ops, SparseCore 0:
  15.0 83.3 all-gather.2
  100.8 66.0 all-gather.4
  200.2 81.8 reduce-scatter.1
